TPU v7x, 32 devices: a whole 2x2x4 slice. The times are simulated.
32 devices in a mesh: dp: 16 (over z, y, x), fsdp: 2 (over core).
Axes of the slice: x: 2, y: 2, z: 4, core: 2. Of those that a mesh axis runs over, the one named last changes fastest.
Arguments:
- tokens: bfloat16 [16384, 768], P(('dp', 'fsdp')), may hold values from -6 to 6
- upstream: bfloat16 [16384, 768], P(('dp', 'fsdp')), may hold values from -6 to 6
- lengths: int32 [32], P(('dp', 'fsdp')), may hold values from 1 to 512, 12288 in all
- qkv_weight: bfloat16 [768, 2304], P(('dp', 'fsdp')), may hold values from -0.21875 to 0.21875
- proj_weight: bfloat16 [768, 768], P(('dp', 'fsdp')), may hold values from -1.75 to 1.75
- up_weight: bfloat16 [768, 3072], P(('dp', 'fsdp')), may hold values from -0.21875 to 0.21875
- down_weight: bfloat16 [3072, 768], P(('dp', 'fsdp')), may hold values from -0.109375 to 0.109375
- gains: bfloat16 [768, 2], P(('dp', 'fsdp')), may hold values from 0.099609375 to 1.8984375
- shifts: bfloat16 [768, 6], P(('dp', 'fsdp')), may hold values from -3 to 3
- up_bias: bfloat16 [3072], P(('dp', 'fsdp')), may hold values from -3 to 3
Outputs:
- output: bfloat16 [16384, 768], P(('dp', 'fsdp'))
- grad_tokens: bfloat16 [16384, 768], P(('dp', 'fsdp'))
- grad_qkv: float32 [768, 2304], P(('dp', 'fsdp'))
- grad_proj: float32 [768, 768], P(('dp', 'fsdp'))
- grad_up: float32 [768, 3072], P(('dp', 'fsdp'))
- grad_down: float32 [3072, 768], P(('dp', 'fsdp'))
- grad_gains: float32 [768, 2], P(('dp', 'fsdp'))
- grad_shifts: float32 [768, 6], P(('dp', 'fsdp'))
- grad_bias_up: float32 [3072], P(('dp', 'fsdp'))
Inputs may be any that keep to these rules, and one draw needn't show every extreme that they name: lengths[c] tokens of clip c are live, in its first slots; some clip fills all 512 slots.
All inputs are finite; a program needn't handle non-finite values. No bound on the sum of `lengths` on one device may be relied on, other than what follows from the above.
Results may differ from a plain program's by a relative error of at most 0.012.
Values may be sent and summed in bfloat16 or wider, within the bound.
No kernel may reach another device: no remote copies, remote signals or barrier semaphores. Data moves between devices by JAX's collectives and lax.ppermute only.
A program may use at most 192 MiB of HBM per device.

v0:
```python
from functools import partial

import jax
import jax.numpy as jnp
from jax import lax
from jax.sharding import PartitionSpec as P

HEADS = 12


EPS = 1e-06
NEG = -1e30


def collect(qkv_weight, proj_weight, up_weight, down_weight, gains, shifts, up_bias):
    gathered = (
        lax.all_gather(qkv_weight, ("dp", "fsdp"), axis=0, tiled=True),
        lax.all_gather(proj_weight, ("dp", "fsdp"), axis=0, tiled=True),
        lax.all_gather(up_weight, ("dp", "fsdp"), axis=0, tiled=True),
        lax.all_gather(down_weight, ("dp", "fsdp"), axis=0, tiled=True),
        lax.all_gather(gains, ("dp", "fsdp"), axis=0, tiled=True),
        lax.all_gather(shifts, ("dp", "fsdp"), axis=0, tiled=True),
        lax.all_gather(up_bias, ("dp", "fsdp"), axis=0, tiled=True),
    )
    return gathered


def give_back(grad_qkv, grad_proj, grad_up, grad_down, grad_gains, grad_shifts, grad_bias_up):
    owned = (
        lax.psum_scatter(grad_qkv, ("dp", "fsdp"), scatter_dimension=0, tiled=True),
        lax.psum_scatter(grad_proj, ("dp", "fsdp"), scatter_dimension=0, tiled=True),
        lax.psum_scatter(grad_up, ("dp", "fsdp"), scatter_dimension=0, tiled=True),
        lax.psum_scatter(grad_down, ("dp", "fsdp"), scatter_dimension=0, tiled=True),
        lax.psum_scatter(grad_gains, ("dp", "fsdp"), scatter_dimension=0, tiled=True),
        lax.psum_scatter(grad_shifts, ("dp", "fsdp"), scatter_dimension=0, tiled=True),
        lax.psum_scatter(grad_bias_up, ("dp", "fsdp"), scatter_dimension=0, tiled=True),
    )
    return owned


def normalize(values):
    centred = values - jnp.mean(values, axis=-1, keepdims=True)
    inverse = lax.rsqrt(jnp.mean(centred * centred, axis=-1, keepdims=True) + EPS)
    return (centred * inverse, inverse)


def norm_back(grad_norm, normed, inverse):
    return inverse * (
        grad_norm
        - jnp.mean(grad_norm, axis=-1, keepdims=True)
        - normed * jnp.mean(grad_norm * normed, axis=-1, keepdims=True)
    )


def block_scores(query_blk, key_rows, live_mask, scaling):
    raw = (
        jnp.einsum("qhd,khd->hqk", query_blk, key_rows, preferred_element_type=jnp.float32)
        * scaling
    )
    return jnp.where(live_mask[None, None, :], raw, NEG)


def local(
    tokens,
    upstream,
    lengths,
    qkv_weight,
    proj_weight,
    up_weight,
    down_weight,
    gains,
    shifts,
    up_bias,
):
    tok_rows, feat_width = tokens.shape
    n_heads = HEADS
    head_size = feat_width // n_heads
    scaling = head_size ** (-0.5)
    block_rows = min(512, tok_rows)
    group_heads = 4
    head_starts = list(range(0, n_heads, group_heads))
    gathered = collect(qkv_weight, proj_weight, up_weight, down_weight, gains, shifts, up_bias)
    qkv_full, proj_full, up_full, down_full, gain_full, shift_full, bias_full = gathered
    gain_f = gain_full.astype(jnp.float32)
    shift_f = shift_full.astype(jnp.float32)
    bias_f = bias_full.astype(jnp.float32)
    live_mask = lax.iota(jnp.int32, tok_rows) < lengths[0]
    source = tokens.astype(jnp.float32)
    norm_one, inv_one = normalize(source)
    first = (norm_one * gain_f[:, 0] + shift_f[:, 0]).astype(jnp.bfloat16)
    joint_bias = jnp.concatenate([shift_f[:, 1], jnp.zeros_like(shift_f[:, 1]), shift_f[:, 2]])
    joint = (jnp.dot(first, qkv_full, preferred_element_type=jnp.float32) + joint_bias).astype(
        jnp.bfloat16
    )
    queries = joint[:, :feat_width].reshape(tok_rows, n_heads, head_size)
    key_rows = joint[:, feat_width : 2 * feat_width].reshape(tok_rows, n_heads, head_size)
    value_rows = joint[:, 2 * feat_width :].reshape(tok_rows, n_heads, head_size)
    log_sums = {}
    offset = 0
    group_parts = []
    for head_lo in head_starts:
        head_hi = head_lo + group_heads
        scores = block_scores(
            queries[offset : offset + block_rows, head_lo:head_hi],
            key_rows[:, head_lo:head_hi],
            live_mask,
            scaling,
        )
        row_max = jnp.max(scores, axis=-1, keepdims=True)
        expd = jnp.exp(scores - row_max)
        row_sum = jnp.sum(expd, axis=-1, keepdims=True)
        attn_low = (expd / row_sum).astype(jnp.bfloat16)
        log_sums[offset, head_lo] = row_max + jnp.log(row_sum)
        group_parts.append(
            jnp.einsum(
                "hqk,khd->qhd",
                attn_low,
                value_rows[:, head_lo:head_hi],
                preferred_element_type=jnp.float32,
            )
        )
    mixed_parts = jnp.concatenate(group_parts, axis=1)
    mixed = mixed_parts.reshape(tok_rows, feat_width).astype(jnp.bfloat16)
    after = source + jnp.dot(mixed, proj_full, preferred_element_type=jnp.float32) + shift_f[:, 3]
    norm_two, inv_two = normalize(after)
    second = (norm_two * gain_f[:, 1] + shift_f[:, 4]).astype(jnp.bfloat16)
    hidden = jnp.dot(second, up_full, preferred_element_type=jnp.float32) + bias_f
    gelu_exact = partial(jax.nn.gelu, approximate=False)
    active = gelu_exact(hidden).astype(jnp.bfloat16)
    output = (
        after + jnp.dot(active, down_full, preferred_element_type=jnp.float32) + shift_f[:, 5]
    ).astype(jnp.bfloat16)
    regathered = collect(qkv_weight, proj_weight, up_weight, down_weight, gains, shifts, up_bias)
    qkv_full, proj_full, up_full, down_full, gain_full, shift_full, bias_full = regathered
    grad_y = jnp.where(live_mask[:, None], upstream, jnp.zeros_like(upstream))
    sum_y = jnp.sum(grad_y, axis=0, dtype=jnp.float32)
    grad_down = jnp.einsum("tf,td->fd", active, grad_y, preferred_element_type=jnp.float32)
    grad_active = jnp.einsum("td,fd->tf", grad_y, down_full, preferred_element_type=jnp.float32)
    gelu_value, gelu_pull = jax.vjp(gelu_exact, hidden)
    grad_hidden = gelu_pull(grad_active)[0].astype(jnp.bfloat16)
    grad_bias_up = jnp.sum(grad_hidden, axis=0, dtype=jnp.float32)
    grad_up = jnp.einsum("td,tf->df", second, grad_hidden, preferred_element_type=jnp.float32)
    grad_second = jnp.einsum("tf,df->td", grad_hidden, up_full, preferred_element_type=jnp.float32)
    gain_two_grad = jnp.sum(grad_second * norm_two, axis=0)
    shift_two_grad = jnp.sum(grad_second, axis=0)
    grad_after = grad_y.astype(jnp.float32) + norm_back(
        grad_second * gain_f[:, 1], norm_two, inv_two
    )
    grad_attn = grad_after.astype(jnp.bfloat16)
    sum_attn = jnp.sum(grad_attn, axis=0, dtype=jnp.float32)
    grad_proj = jnp.einsum("td,te->de", mixed, grad_attn, preferred_element_type=jnp.float32)
    grad_mixed = jnp.einsum("te,de->td", grad_attn, proj_full, preferred_element_type=jnp.float32)
    grad_mixed = grad_mixed.astype(jnp.bfloat16).reshape(tok_rows, n_heads, head_size)
    key_groups = {}
    value_groups = {}
    for head_lo in head_starts:
        key_groups[head_lo] = jnp.zeros((tok_rows, group_heads, head_size), jnp.float32)
        value_groups[head_lo] = jnp.zeros((tok_rows, group_heads, head_size), jnp.float32)
    offset = 0
    query_groups = []
    for head_lo in head_starts:
        head_hi = head_lo + group_heads
        query_blk = queries[offset : offset + block_rows, head_lo:head_hi]
        grad_blk = grad_mixed[offset : offset + block_rows, head_lo:head_hi]
        key_part = key_rows[:, head_lo:head_hi]
        scores = block_scores(query_blk, key_part, live_mask, scaling)
        attn_p = jnp.exp(scores - log_sums[offset, head_lo])
        value_groups[head_lo] = jnp.einsum(
            "hqk,qhd->khd",
            attn_p.astype(jnp.bfloat16),
            grad_blk,
            preferred_element_type=jnp.float32,
        )
        grad_prob = jnp.einsum(
            "qhd,khd->hqk",
            grad_blk,
            value_rows[:, head_lo:head_hi],
            preferred_element_type=jnp.float32,
        )
        grad_score = attn_p * (grad_prob - jnp.sum(attn_p * grad_prob, axis=-1, keepdims=True))
        score_low = grad_score.astype(jnp.bfloat16)
        query_groups.append(
            jnp.einsum("hqk,khd->qhd", score_low, key_part, preferred_element_type=jnp.float32)
            * scaling
        )
        key_groups[head_lo] = (
            jnp.einsum("hqk,qhd->khd", score_low, query_blk, preferred_element_type=jnp.float32)
            * scaling
        )
    grad_query_parts = jnp.concatenate(query_groups, axis=1)
    grad_keys = jnp.concatenate([key_groups[head_lo] for head_lo in head_starts], axis=1)
    grad_vals = jnp.concatenate([value_groups[head_lo] for head_lo in head_starts], axis=1)
    grad_joint = jnp.concatenate(
        [
            grad_query_parts.reshape(tok_rows, feat_width),
            grad_keys.reshape(tok_rows, feat_width),
            grad_vals.reshape(tok_rows, feat_width),
        ],
        axis=1,
    ).astype(jnp.bfloat16)
    joint_sums = jnp.sum(grad_joint, axis=0, dtype=jnp.float32)
    grad_qkv = jnp.einsum("td,te->de", first, grad_joint, preferred_element_type=jnp.float32)
    grad_first = jnp.einsum("te,de->td", grad_joint, qkv_full, preferred_element_type=jnp.float32)
    gain_one_grad = jnp.sum(grad_first * norm_one, axis=0)
    shift_one_grad = jnp.sum(grad_first, axis=0)
    grad_tokens = (grad_after + norm_back(grad_first * gain_f[:, 0], norm_one, inv_one)).astype(
        jnp.bfloat16
    )
    grad_gains = jnp.stack([gain_one_grad, gain_two_grad], axis=1)
    grad_shifts = jnp.stack(
        [
            shift_one_grad,
            joint_sums[:feat_width],
            joint_sums[2 * feat_width :],
            sum_attn,
            shift_two_grad,
            sum_y,
        ],
        axis=1,
    )
    owned = give_back(
        grad_qkv, grad_proj, grad_up, grad_down, grad_gains, grad_shifts, grad_bias_up
    )
    own_qkv, own_proj, own_up, own_down, own_gains, own_shifts, own_bias = owned
    return (
        output,
        grad_tokens,
        own_qkv,
        own_proj,
        own_up,
        own_down,
        own_gains,
        own_shifts,
        own_bias,
    )


def solution(mesh):
    placed = (
        P(("dp", "fsdp"), None),
        P(("dp", "fsdp"), None),
        P(("dp", "fsdp")),
        P(("dp", "fsdp"), None),
        P(("dp", "fsdp"), None),
        P(("dp", "fsdp"), None),
        P(("dp", "fsdp"), None),
        P(("dp", "fsdp"), None),
        P(("dp", "fsdp"), None),
        P(("dp", "fsdp")),
    )
    return jax.shard_map(
        local,
        mesh=mesh,
        in_specs=placed,
        out_specs=(
            P(("dp", "fsdp"), None),
            P(("dp", "fsdp"), None),
            P(("dp", "fsdp"), None),
            P(("dp", "fsdp"), None),
            P(("dp", "fsdp"), None),
            P(("dp", "fsdp"), None),
            P(("dp", "fsdp"), None),
            P(("dp", "fsdp"), None),
            P(("dp", "fsdp")),
        ),
        check_vma=False,
    )
```

profile of v0, /device:TPU:0, one launch (start us, length us, event | category | flops | bytes accessed | tf_op | source)
XLA Modules:
  0.0 809.8 jit_solution(5188915780798190231)
XLA Ops:
  14.4 42.3 %all-reduce = bf16[3072]{0:T(1024)(128)(2,1)S(1)} all-reduce(bf16[3072]{0:T(1024)(128)(2,1)S(1)} %dynamic-update-slice), channel_id=1, replica_groups=mesh['dp'=16,'fsdp'=2] {'dp','fsdp'}, use_global_device_ids=true, to_apply=%add | all-reduce | flops 3072 | bytes 12288
  56.7 40.2 %all-gather = bf16[32,24,2]{1,2,0:T(2,128)(2,1)S(1)} all-gather(bf16[1,24,2]{1,2,0:T(2,128)(2,1)} %bitcast.118), channel_id=1, replica_groups=mesh['dp'=16,'fsdp'=2] {'dp','fsdp'}, dimensions={0}, use_global_device_ids=true | all-gather | bytes 3168 | tf_op jit(solution)/shard_map/all_gather | solution.py:21
  97.2 37.3 %all-gather.1 = bf16[32,24,6]{1,2,0:T(8,128)(2,1)S(1)} all-gather(bf16[1,24,6]{1,2,0:T(8,128)(2,1)} %bitcast.117), channel_id=1, replica_groups=mesh['dp'=16,'fsdp'=2] {'dp','fsdp'}, dimensions={0}, use_global_device_ids=true | all-gather | bytes 9504 | tf_op jit(solution)/shard_map/all_gather | solution.py:22
  135.5 4.4 fusion.6
  141.7 3.2 fusion.101
  145.8 3.0 fusion.8
  150.5 3.1 copy-done.7
  157.8 2.2 fusion.103
  160.4 34.9 %all-gather.11.cloned.1.call-done = bf16[768,3072]{1,0:T(8,128)(2,1)} async-done(((bf16[24,3072]{1,0:T(8,128)(2,1)}), bf16[768,3072]{1,0:T(8,128)(2,1)}) %all-gather.11.cloned.1.call-update) | async-done | bytes 4718608 | tf_op jit(solution)/shard_map/all_gather | solution.py:19
  195.2 20.0 %multiply_convert_fusion = (bf16[512,3072]{1,0:T(8,128)(2,1)}, f32[512,3072]{1,0:T(8,128)}, f32[512,3072]{1,0:T(8,128)}) fusion(f32[3072]{0:T(1024)S(1)} %convert_element_type.94, bf16[768,3072]{1,0:T(8,128)(2,1)} %all-gather.11.cloned.1.call-done, f32[512,768]{1,0:T(8,128)S(1)} %get-tuple-element.45, f32[768]{0:T(1024)S(1)} %get-tuple-element.18, ...), kind=kOutput, calls=%fused_computation.4 | convolution fusion | flops 2521694208 | bytes 22042624 | tf_op jit(solution)/shard_map/dot_general | solution.py:127
  215.2 45.3 %all-gather.13.cloned.1.call-done = bf16[3072,768]{1,0:T(8,128)(2,1)} async-done(((bf16[96,768]{1,0:T(8,128)(2,1)}), bf16[3072,768]{1,0:T(8,128)(2,1)}) %all-gather.13.cloned.1.call-update) | async-done | bytes 4718608 | tf_op jit(solution)/shard_map/all_gather | solution.py:20
  260.5 10.8 %convert_reduce_fusion = (f32[3072]{0:T(1024)S(1)}, bf16[512,3072]{1,0:T(8,128)(2,1)S(1)}) fusion(f32[512,3072]{1,0:T(8,128)} %get-tuple-element.31, bf16[3072,768]{1,0:T(8,128)(2,1)} %all-gather.13.cloned.1.call-done, bf16[512,768]{1,0:T(8,128)(2,1)} %param.11, pred[512]{0:T(512)(128)(4,1)S(1)} %iota_compare_fusion, f32[512,3072]{1,0:T(8,128)} %get-tuple-element.46, ...), kind=kOutput, calls=%fused_computation.2 | convolution fusion | flops 2443047936 | bytes 21258752 | tf_op jit(solution)/shard_map/td,fd->tf/dot_general | solution.py:138
  271.3 3.0 multiply_reduce_fusion.3
  274.4 2.2 convert_reduce_fusion.4
  276.6 2.2 fusion.86
  278.8 3.0 convolution_convert_fusion
  283.2 3.1 fusion.59
  286.8 3.0 multiply_reduce_fusion
  291.4 3.0 multiply_reduce_fusion.1
  295.9 4.8 multiply_convert_fusion.1
  304.0 1.9 copy-done.2
  305.9 2.1 multiply_reduce_fusion.2
  313.6 5.2 fusion.89
  319.1 8.9 %fusion.95 = f32[768,3072]{1,0:T(8,128)} fusion(bf16[512,3072]{1,0:T(8,128)(2,1)} %copy-done.32, f32[512,768]{1,0:T(8,128)} %copy-done.11, f32[768]{0:T(1024)S(1)} %get-tuple-element.18, f32[768]{0:T(1024)S(1)} %get-tuple-element.23, f32[512]{0:T(512)S(1)} %add_rsqrt_fusion, f32[512]{0:T(512)S(1)} %broadcast_multiply_fusion.4), kind=kOutput, calls=%fused_computation.161 | convolution fusion | flops 2417885184 | bytes 14166016 | tf_op jit(solution)/shard_map/td,tf->df/dot_general | solution.py:142
  329.2 8.3 %fusion.93 = f32[3072,768]{1,0:T(8,128)} fusion(bf16[512,3072]{1,0:T(8,128)(2,1)} %get-tuple-element.30, bf16[512,768]{1,0:T(8,128)(2,1)S(1)} %copy-done.22, pred[512]{0:T(512)(128)(4,1)S(1)} %iota_compare_fusion), kind=kOutput, calls=%fused_computation.159 | convolution fusion | flops 2416312320 | bytes 13369856 | tf_op jit(solution)/shard_map/tf,td->fd/dot_general | solution.py:137
  338.6 6.1 fusion.38
  345.3 40.9 %all-reduce.4 = (f32[768,2]{0,1:T(2,128)S(1)}, f32[768,6]{0,1:T(8,128)S(1)}, f32[3072]{0:T(1024)S(1)}) all-reduce(f32[768,2]{0,1:T(2,128)S(1)} %pad_maximum_fusion.6, f32[768,6]{0,1:T(8,128)S(1)} %stack.39, f32[3072]{0:T(1024)S(1)} %get-tuple-element.55), channel_id=6, replica_groups=mesh['dp'=16,'fsdp'=2] {'dp','fsdp'}, use_global_device_ids=true, to_apply=%region_23.24.clone | all-reduce | flops 9216 | bytes 73728
  388.1 2.9 fusion.37
  390.9 5.9 add_convert_fusion.1
  396.8 122.3 %reduce-scatter.7.cloned.1.call-done = f32[24,2304]{1,0:T(8,128)} async-done(((f32[768,2304]{1,0:T(8,128)}), f32[24,2304]{1,0:T(8,128)}) %reduce-scatter.7.cloned.1.call-update) | async-done | bytes 221200 | tf_op jit(solution)/shard_map/reduce_scatter | solution.py:30
  519.1 141.5 %reduce-scatter.11.cloned.1.call-done = f32[24,3072]{1,0:T(8,128)} async-done(((f32[768,3072]{1,0:T(8,128)}), f32[24,3072]{1,0:T(8,128)}) %reduce-scatter.11.cloned.1.call-update) | async-done | bytes 294928 | tf_op jit(solution)/shard_map/reduce_scatter | solution.py:32
  660.6 142.1 %reduce-scatter.13.cloned.1.call-done = f32[96,768]{1,0:T(8,128)} async-done(((f32[3072,768]{1,0:T(8,128)}), f32[96,768]{1,0:T(8,128)}) %reduce-scatter.13.cloned.1.call-update) | async-done | bytes 294928 | tf_op jit(solution)/shard_map/reduce_scatter | solution.py:33
  (151 shorter events, 35.0 us)
Async XLA Ops:
  7.2 128.3 %all-gather.7.cloned.1.call-start = ((), (), s32[]{:S(2)}) async-start(), calls=%async_computation.4 | async-start | bytes 3649536 | tf_op jit(solution)/shard_map/all_gather | solution.py:17
  7.9 149.7 %all-gather.9.cloned.1.call-start = ((), (), s32[]{:S(2)}) async-start(), calls=%async_computation.5 | async-start | bytes 1216512 | tf_op jit(solution)/shard_map/all_gather | solution.py:18
  8.7 186.6 %all-gather.11.cloned.1.call-start = ((), (), s32[]{:S(2)}) async-start(), calls=%async_computation.6 | async-start | bytes 4866048 | tf_op jit(solution)/shard_map/all_gather | solution.py:19
  9.4 251.1 %all-gather.13.cloned.1.call-start = ((), (), s32[]{:S(2)}) async-start(), calls=%async_computation.7 | async-start | bytes 4866048 | tf_op jit(solution)/shard_map/all_gather | solution.py:20
  10.0 386.8 %reduce-scatter.9.cloned.1.call-start = ((), (), s32[]{:S(2)}) async-start(), calls=%async_computation.9 | async-start | bytes 2433024 | tf_op jit(solution)/shard_map/reduce_scatter | solution.py:31
  140.3 8.5 %copy-start.25 = (bf16[512,768]{0,1:T(8,128)(2,1)}, bf16[512,768]{0,1:T(8,128)(2,1)S(1)}, u32[]{:S(2)}) copy-start(bf16[512,768]{0,1:T(8,128)(2,1)S(1)} %copy.85) | copy-start | bytes 2359300
  140.6 8.2 %copy-start.23 = (bf16[512,768]{0,1:T(8,128)(2,1)}, bf16[512,768]{0,1:T(8,128)(2,1)S(1)}, u32[]{:S(2)}) copy-start(bf16[512,768]{0,1:T(8,128)(2,1)S(1)} %copy.84) | copy-start | bytes 2359300
  141.7 3.8 copy-start.6
  145.8 10.9 %copy-start.13 = (bf16[512,768]{0,1:T(8,128)(2,1)}, bf16[512,768]{0,1:T(8,128)(2,1)S(1)}, u32[]{:S(2)}) copy-start(bf16[512,768]{0,1:T(8,128)(2,1)S(1)} %copy.83) | copy-start | bytes 2359300
  149.9 6.7 copy-start
  149.9 3.7 copy-start.7
  160.0 111.3 %copy-start.11 = (f32[512,768]{1,0:T(8,128)}, f32[512,768]{1,0:T(8,128)S(1)}, u32[]{:S(2)}) copy-start(f32[512,768]{1,0:T(8,128)S(1)} %get-tuple-element.45) | copy-start | bytes 4718596
  260.5 10.8 %copy-start.30 = (bf16[768,3072]{1,0:T(8,128)(2,1)S(1)}, bf16[768,3072]{1,0:T(8,128)(2,1)}, u32[]{:S(2)}) copy-start(bf16[768,3072]{1,0:T(8,128)(2,1)} %all-gather.11.cloned.1.call-done) | copy-start | bytes 14155780
  271.3 3.1 copy-start.32
  271.3 3.1 copy-start.21
  283.2 3.5 copy-start.8
  283.2 3.6 copy-start.14
  286.8 3.0 copy-start.4
  291.4 3.0 copy-start.1
  295.9 223.2 %reduce-scatter.7.cloned.1.call-start = ((), (), s32[]{:S(2)}) async-start(), calls=%async_computation.8 | async-start | bytes 7299072 | tf_op jit(solution)/shard_map/reduce_scatter | solution.py:30
  295.9 4.8 copy-start.26
  295.9 5.3 copy-start.5
  295.9 6.2 copy-start.9
  303.4 2.5 copy-start.2
  303.5 9.2 %copy-start.15 = (bf16[512,12,64]{0,2,1:T(8,128)(2,1)}, bf16[512,12,64]{0,2,1:T(8,128)(2,1)S(1)}, u32[]{:S(2)}) copy-start(bf16[512,12,64]{0,2,1:T(8,128)(2,1)S(1)} %pad_maximum_fusion.4) | copy-start | bytes 2359300
  318.8 341.8 %reduce-scatter.11.cloned.1.call-start = ((), (), s32[]{:S(2)}) async-start(), calls=%async_computation.10 | async-start | bytes 9732096 | tf_op jit(solution)/shard_map/reduce_scatter | solution.py:32
  328.0 474.7 %reduce-scatter.13.cloned.1.call-start = ((), (), s32[]{:S(2)}) async-start(), calls=%async_computation.11 | async-start | bytes 9732096 | tf_op jit(solution)/shard_map/reduce_scatter | solution.py:33
  338.6 6.2 copy-start.18
  338.6 6.2 copy-start.20
  344.8 46.2 %copy-start.29 = (f32[768]{0:T(1024)S(1)}, f32[768]{0:T(1024)}, u32[]{:S(2)}) copy-start(f32[768]{0:T(1024)} %get-tuple-element.17) | copy-start | bytes 9220
  386.2 4.8 copy-start.12
  386.2 4.8 copy-start.31
  (9 other events, 12.5 us)
Sparse Core Ops, SparseCore 0:
  10.9 63.0 all-gather.6
  76.9 52.7 all-gather.8
  132.6 62.5 all-gather.10
  198.0 62.4 all-gather.12
  296.0 97.8 reduce-scatter.8
  400.9 118.0 reduce-scatter.6
  525.5 135.0 reduce-scatter.10
  668.1 134.5 reduce-scatter.12
where the time goes:
time: 813 us; the launch traced here: 810 us
  waiting for transfers between devices  489 us (60%)
  blocking collectives  161 us (20%)
  matrix products  106 us (13%)
  other arithmetic  20.4 us (3%)
  local copies, waits for them, and re-layouts  18.1 us (2%)
  between operations  15.7 us (2%)
    reduce_scatter x1, waiting for transfers between devices, give_back(): lax.psum_scatter(grad_down, ('dp', 'fsdp'), scatter_dimension=0, tiled=True)  142 us
    reduce_scatter x1, waiting for transfers between devices, give_back(): lax.psum_scatter(grad_up, ('dp', 'fsdp'), scatter_dimension=0, tiled=True)  142 us
    reduce_scatter x1, waiting for transfers between devices, give_back(): lax.psum_scatter(grad_qkv, ('dp', 'fsdp'), scatter_dimension=0, tiled=True)  122 us
    unnamed x2, blocking collectives  83.2 us
    all_gather x1, waiting for transfers between devices, collect(): lax.all_gather(down_weight, ('dp', 'fsdp'), axis=0, tiled=True)  45.3 us
    all_gather x1, blocking collectives, collect(): lax.all_gather(gains, ('dp', 'fsdp'), axis=0, tiled=True)  40.2 us
    all_gather x1, blocking collectives, collect(): lax.all_gather(shifts, ('dp', 'fsdp'), axis=0, tiled=True)  37.3 us
    all_gather x1, waiting for transfers between devices, collect(): lax.all_gather(up_weight, ('dp', 'fsdp'), axis=0, tiled=True)  34.9 us
  transfers between devices with their start and end apart: 8, of which 5 were waited for; matrix products, arithmetic and copies ran while one was open for 12% of the time, Pallas kernels for 0%

commit v1 on v0

--- a/solution.py
+++ b/solution.py
@@ -1,15 +1,20 @@
+import math
 from functools import partial
 
 import jax
 import jax.numpy as jnp
 from jax import lax
+from jax.experimental import pallas as pl
+from jax.experimental.pallas import tpu as pltpu
 from jax.sharding import PartitionSpec as P
 
 HEADS = 12
-
-
 EPS = 1e-06
 NEG = -1e30
+AXES = ("dp", "fsdp")
+F32 = jnp.float32
+BF16 = jnp.bfloat16
+VMEM_LIMIT = 56 * 1024 * 1024
 
 
 def collect(qkv_weight, proj_weight, up_weight, down_weight, gains, shifts, up_bias):
@@ -60,7 +65,7 @@
     return jnp.where(live_mask[None, None, :], raw, NEG)
 
 
-def local(
+def plain(
     tokens,
     upstream,
     lengths,
@@ -235,6 +240,952 @@
     )
 
 
+BOTH_LAST = (((1,), (1,)), ((), ()))
+SMEM = pl.BlockSpec(memory_space=pltpu.SMEM)
+ANY = pl.BlockSpec(memory_space=pl.ANY)
+CORE, LENGTH = 32, 33
+
+
+def pairs(move):
+    return [(i, move(i)) for i in range(32)]
+
+
+def first_way(i):
+    return i ^ (2 if i % 2 == 0 else 4)
+
+
+def second_way(i):
+    return i ^ (4 if i % 2 == 0 else 2)
+
+
+def along_z(step):
+    return lambda i: i ^ (8 * step)
+
+
+def send(array, move):
+    return lax.ppermute(array, AXES, pairs(move))
+
+
+def swap(array):
+    return send(array, lambda i: i ^ 1)
+
+
+def facts(chip, core, length):
+    places = []
+    for of_core in (core, 1 - core):
+        for j in range(16):
+            z, first, second = j % 4, (j // 4) % 2, j // 8
+            mask = jnp.where(of_core == 0, first + 2 * second, second + 2 * first)
+            places.append(jnp.bitwise_xor(chip, mask + 4 * z))
+    return jnp.stack(places + [core, length]).astype(jnp.int32)
+
+
+def spread(piece):
+    near = [send(piece, along_z(s)) for s in (1, 2, 3)]
+    zs = jnp.stack([piece] + near)
+    low = jnp.concatenate([zs, send(zs, first_way)])
+    high = send(low, second_way)
+    return low, high, swap(low), swap(high)
+
+
+def params():
+    return pltpu.CompilerParams(vmem_limit_bytes=VMEM_LIMIT)
+
+
+def cost(flops, nbytes, exps=0):
+    return pl.CostEstimate(flops=flops, bytes_accessed=nbytes, transcendentals=exps)
+
+
+def shape(dims, dtype):
+    return jax.ShapeDtypeStruct(dims, dtype)
+
+
+def full(dims):
+    return pl.BlockSpec(dims, lambda *_: (0,) * len(dims))
+
+
+def dot(left, right):
+    return jnp.dot(left, right, preferred_element_type=F32)
+
+
+def dot_last(left, right):
+    return lax.dot_general(left, right, BOTH_LAST, preferred_element_type=F32)
+
+
+def fetch(info, pieces, dest, sems, by_half):
+    copies = []
+    for who in (0, 1):
+        half = info[CORE] if who == 0 else 1 - info[CORE]
+        for j in range(16):
+            at = info[16 * who + j]
+            src = pieces[2 * who + j // 8].at[j % 8]
+            dst = dest.at[half, at] if by_half else dest.at[at, half]
+            copies.append(pltpu.make_async_copy(src, dst, sems.at[16 * who + j]))
+    for copy in copies:
+        copy.start()
+    return copies
+
+
+def centre(values):
+    centred = values - jnp.mean(values, axis=-1, keepdims=True)
+    inverse = lax.rsqrt(jnp.mean(centred * centred, axis=-1, keepdims=True) + EPS)
+    return centred * inverse, inverse
+
+
+def layer_back(grad, normed, inverse):
+    return inverse * (
+        grad
+        - jnp.mean(grad, axis=-1, keepdims=True)
+        - normed * jnp.mean(grad * normed, axis=-1, keepdims=True)
+    )
+
+
+def enter_kernel(info, tokens, low, high, low_o, high_o, weights, vecs, first, joint, sems):
+    feat = tokens.shape[1]
+    third = feat // 2
+    copies = fetch(info, (low, high, low_o, high_o), weights, sems, True)
+    normed, _ = centre(tokens[...].astype(F32))
+    for copy in copies:
+        copy.wait()
+    width = weights.shape[-1]
+    small = weights[0, :, :, width - 128 :].reshape(feat, 128).astype(F32).T
+    vecs[...] = small[:8]
+    low_first = (normed * small[0:1] + small[2:3]).astype(BF16)
+    first[...] = low_first
+    for h in (0, 1):
+        for part in range(3):
+            w = weights[h, :, :, part * third : (part + 1) * third].reshape(feat, third)
+            out = dot(low_first, w)
+            if part != 1:
+                row = 3 if part == 0 else 4
+                out = out + small[row : row + 1, h * third : (h + 1) * third]
+            joint[h, :, part * third : (part + 1) * third] = out.astype(BF16)
+
+
+def enter(info, tokens, pieces):
+    rows, feat = tokens.shape
+    width = pieces[0].shape[-1]
+    return pl.pallas_call(
+        enter_kernel,
+        out_shape=(
+            shape((2, 16, feat // 16, width), BF16),
+            shape((8, feat), F32),
+            shape((rows, feat), BF16),
+            shape((2, rows, 3 * feat // 2), BF16),
+        ),
+        in_specs=[SMEM, pl.BlockSpec(memory_space=pltpu.VMEM)] + [ANY] * 4,
+        out_specs=tuple([pl.BlockSpec(memory_space=pltpu.VMEM)] * 4),
+        scratch_shapes=[pltpu.SemaphoreType.DMA((32,))],
+        compiler_params=params(),
+        cost_estimate=cost(6 * rows * feat * feat, 8 * feat * width + 10 * rows * feat),
+    )(info, tokens, *pieces)
+
+
+def scores_of(info, keys, queries):
+    raw = dot_last(keys, queries)
+    place = lax.broadcasted_iota(jnp.int32, raw.shape, 0)
+    return jnp.where(place < info[LENGTH], raw, NEG)
+
+
+def mix_kernel(info, q, k, v, mixed, stats):
+    head = q.shape[-1] // 2
+    scale = head**-0.5
+    turned = v[0].T
+    outs = []
+    for h in (0, 1):
+        cols = slice(h * head, (h + 1) * head)
+        scores = scores_of(info, k[0, :, cols], q[0, :, cols] * scale)
+        most = jnp.max(scores, axis=0, keepdims=True)
+        expd = jnp.exp(scores - most)
+        total = jnp.sum(expd, axis=0, keepdims=True)
+        attn = (expd * (1.0 / total)).astype(BF16)
+        stats[0, h : h + 1] = most + jnp.log(total)
+        outs.append(dot(turned[cols], attn))
+    mixed[...] = jnp.concatenate(outs).T.astype(BF16)
+
+
+def mix(info, joint):
+    _, rows, width = joint.shape
+    feat, pair = 2 * width // 3, 2 * width // 3 // HEADS * 2
+    per = feat // 2 // pair
+    spec = [
+        pl.BlockSpec((1, rows, pair), lambda i, part=part: (i // per, 0, part * per + i % per))
+        for part in range(3)
+    ]
+    n = HEADS // 2
+    return pl.pallas_call(
+        mix_kernel,
+        grid=(n,),
+        out_shape=(shape((rows, feat), BF16), shape((n, 8, rows), F32)),
+        in_specs=[SMEM] + spec,
+        out_specs=(
+            pl.BlockSpec((rows, pair), lambda i: (0, i)),
+            pl.BlockSpec((1, 8, rows), lambda i: (i, 0, 0)),
+        ),
+        compiler_params=params(),
+        cost_estimate=cost(16 * rows * rows * feat, 8 * rows * feat, HEADS * rows * rows),
+    )(info, joint, joint, joint)
+
+
+def mix_back_kernel(info, q, k, v, grad, stats, theirs, mine):
+    head = q.shape[-1] // 2
+    scale = head**-0.5
+    turned = k[0].T
+    parts = [[], [], []]
+    for h in (0, 1):
+        cols = slice(h * head, (h + 1) * head)
+        queries = q[0, :, cols] * scale
+        grad_h = grad[:, cols]
+        attn = jnp.exp(scores_of(info, k[0, :, cols], queries) - stats[0, h : h + 1])
+        grad_prob = dot_last(v[0, :, cols], grad_h)
+        inner = jnp.sum(attn * grad_prob, axis=0, keepdims=True)
+        low = (attn * (grad_prob - inner)).astype(BF16)
+        parts[0].append(dot(turned[cols], low) * scale)
+        parts[1].append(dot(low, queries))
+        parts[2].append(dot(attn.astype(BF16), grad_h))
+    out = [
+        jnp.concatenate(parts[0]).T.astype(BF16),
+        jnp.concatenate(parts[1], axis=1).astype(BF16),
+        jnp.concatenate(parts[2], axis=1).astype(BF16),
+    ]
+    step, per = pl.program_id(0), pl.num_programs(0) // 2
+
+    @pl.when(step < per)
+    def _():
+        for part in range(3):
+            theirs[part] = out[part]
+
+    @pl.when(step >= per)
+    def _():
+        for part in range(3):
+            mine[part] = out[part]
+
+
+def mix_back(info, joint, grad_mixed, stats):
+    _, rows, width = joint.shape
+    feat, pair = 2 * width // 3, 2 * width // 3 // HEADS * 2
+    per = feat // 2 // pair
+    n = HEADS // 2
+
+    def half(i, info):
+        return jnp.where(i < per, 1 - info[CORE], info[CORE])
+
+    spec = [
+        pl.BlockSpec(
+            (1, rows, pair), lambda i, info, part=part: (half(i, info), 0, part * per + i % per)
+        )
+        for part in range(3)
+    ]
+    out = shape((3, rows, feat // 2), BF16)
+    return pl.pallas_call(
+        mix_back_kernel,
+        grid_spec=pltpu.PrefetchScalarGridSpec(
+            num_scalar_prefetch=1,
+            grid=(n,),
+            in_specs=spec
+            + [
+                pl.BlockSpec((rows, pair), lambda i, info: (0, half(i, info) * per + i % per)),
+                pl.BlockSpec(
+                    (1, 8, rows), lambda i, info: (half(i, info) * per + i % per, 0, 0)
+                ),
+            ],
+            out_specs=(
+                pl.BlockSpec((3, rows, pair), lambda i, info: (0, 0, jnp.minimum(i, per - 1))),
+                pl.BlockSpec((3, rows, pair), lambda i, info: (0, 0, jnp.maximum(i - per, 0))),
+            ),
+        ),
+        out_shape=(out, out),
+        compiler_params=params(),
+        cost_estimate=cost(40 * rows * rows * feat, 16 * rows * feat, HEADS * rows * rows),
+    )(info, joint, joint, joint, grad_mixed, stats)
+
+
+GELU = (0.254829592, -0.284496736, 1.421413741, -1.453152027, 1.061405429)
+
+
+def gelu_parts(x):
+    bell = jnp.exp(-0.5 * x * x)
+    t = 1.0 / (1.0 + (0.3275911 * 0.5**0.5) * jnp.abs(x))
+    poly = GELU[4]
+    for c in GELU[3::-1]:
+        poly = poly * t + c
+    tail = (0.5 * poly) * t * bell
+    phi = jnp.where(x < 0, tail, 1.0 - tail)
+    return x * phi, phi + x * (bell * (2 * math.pi) ** -0.5)
+
+
+def rise_kernel(
+    info,
+    tokens,
+    mixed,
+    proj,
+    vecs,
+    bias,
+    low,
+    high,
+    low_o,
+    high_o,
+    weights,
+    after,
+    second,
+    active,
+    slope,
+    mine,
+    theirs,
+    turned,
+    sems,
+):
+    step = pl.program_id(0)
+    feat = tokens.shape[1]
+    tile = active.shape[1]
+    per = weights.shape[-1] // tile
+    rows = mine.shape[1]
+
+    @pl.when(step == 0)
+    def _():
+        copies = fetch(info, (low, high, low_o, high_o), weights, sems, True)
+        grown = [dot(mixed[...], proj[h]) for h in (0, 1)]
+        total = tokens[...].astype(F32) + jnp.concatenate(grown, axis=1) + vecs[5:6]
+        after[...] = total
+        normed, _ = centre(total)
+        second[...] = (normed * vecs[1:2] + vecs[6:7]).astype(BF16)
+        for copy in copies:
+            copy.wait()
+
+    cols = pl.ds(pl.multiple_of(lax.rem(step, per) * tile, tile), tile)
+    w = weights[step // per, :, :, cols].reshape(feat, tile)
+    hidden = dot(second[...], w) + bias[...]
+    value, grad = gelu_parts(hidden)
+    value = value.astype(BF16)
+    active[...] = value
+    slope[...] = grad.astype(BF16)
+    count = tile // rows
+    turned[pl.ds(step * count, count)] = value.T.reshape(count, rows, -1)
+
+    @pl.when(step == pl.num_programs(0) - 1)
+    def _():
+        core = info[CORE]
+        for j in range(16):
+            mine[j] = turned[2 * info[j] + core]
+            theirs[j] = turned[2 * info[16 + j] + 1 - core]
+
+
+def rise(info, tokens, mixed, first_set, vecs, bias, pieces):
+    rows, feat = tokens.shape
+    width = pieces[0].shape[-1]
+    hidden = 2 * width
+    tile, block = 384, hidden // 32
+    turned = shape((16, block, rows), BF16)
+    return pl.pallas_call(
+        rise_kernel,
+        grid=(hidden // tile,),
+        out_shape=(
+            shape((2, 16, feat // 16, width), BF16),
+            shape((rows, feat), F32),
+            shape((rows, feat), BF16),
+            shape((rows, hidden), BF16),
+            shape((rows, hidden), BF16),
+            turned,
+            turned,
+        ),
+        in_specs=[
+            SMEM,
+            full((rows, feat)),
+            full((rows, feat)),
+            pl.BlockSpec((2, feat, feat // 2), lambda n: (0, 0, 3)),
+            full((8, feat)),
+            pl.BlockSpec((1, tile), lambda n: (0, n)),
+        ]
+        + [ANY] * 4,
+        out_specs=(
+            full((2, 16, feat // 16, width)),
+            full((rows, feat)),
+            full((rows, feat)),
+            pl.BlockSpec((rows, tile), lambda n: (0, n)),
+            pl.BlockSpec((rows, tile), lambda n: (0, n)),
+            full(turned.shape),
+            full(turned.shape),
+        ),
+        scratch_shapes=[pltpu.VMEM((32, block, rows), BF16), pltpu.SemaphoreType.DMA((32,))],
+        compiler_params=params(),
+        cost_estimate=cost(
+            2 * rows * feat * (feat + hidden), 8 * feat * hidden, rows * hidden
+        ),
+    )(info, tokens, mixed, first_set, vecs, bias, *pieces)
+
+
+def leave_kernel(after, active, down, vecs, output):
+    output[...] = (after[...] + dot(active[...], down[...]) + vecs[7:8]).astype(BF16)
+
+
+def leave(after, active, down, vecs):
+    rows, feat = after.shape
+    hidden = active.shape[1]
+    tile = 384
+    return pl.pallas_call(
+        leave_kernel,
+        grid=(feat // tile,),
+        out_shape=shape((rows, feat), BF16),
+        in_specs=[
+            pl.BlockSpec((rows, tile), lambda n: (0, n)),
+            full((rows, hidden)),
+            pl.BlockSpec((hidden, tile), lambda n: (0, n)),
+            pl.BlockSpec((8, tile), lambda n: (0, n)),
+        ],
+        out_specs=pl.BlockSpec((rows, tile), lambda n: (0, n)),
+        compiler_params=params(),
+        cost_estimate=cost(2 * rows * feat * hidden, 2 * hidden * (rows + feat)),
+    )(after, active, down, vecs)
+
+
+def fall_kernel(
+    info,
+    grad_y,
+    slope,
+    up,
+    after,
+    vecs,
+    proj,
+    low,
+    high,
+    low_o,
+    high_o,
+    weights,
+    theirs,
+    mine,
+    bias_sum,
+    grad_after,
+    attn_theirs,
+    attn_mine,
+    grad_mixed,
+    sums,
+    grad_second,
+    sems,
+):
+    step, steps = pl.program_id(0), pl.num_programs(0)
+    core = info[CORE]
+    feat = grad_y.shape[1]
+    tile = slope.shape[1]
+    per = steps // 2
+
+    @pl.when(step == 0)
+    def _():
+        for copy in fetch(info, (low, high, low_o, high_o), weights, sems, False):
+            copy.wait()
+        grad_second[...] = jnp.zeros_like(grad_second)
+
+    half = jnp.where(step < per, 1 - core, core)
+    at = half * per + lax.rem(step, per)
+    down = weights[pl.ds(2 * at, 2)].reshape(tile, feat)
+    grad = (dot_last(grad_y[...], down) * slope[...].astype(F32)).astype(BF16)
+    bias_sum[...] = jnp.sum(grad.astype(F32), axis=0, keepdims=True)
+    grad_second[...] += dot_last(grad, up[0])
+
+    @pl.when(step < per)
+    def _():
+        theirs[...] = grad
+
+    @pl.when(step >= per)
+    def _():
+        mine[...] = grad
+
+    @pl.when(step == steps - 1)
+    def _():
+        normed, inverse = centre(after[...])
+        second = grad_second[...]
+        live = grad_y[...].astype(F32)
+        sums[0:1] = jnp.sum(second * normed, axis=0, keepdims=True)
+        sums[1:2] = jnp.sum(second, axis=0, keepdims=True)
+        total = live + layer_back(second * vecs[1:2], normed, inverse)
+        grad_after[...] = total
+        attn = total.astype(BF16)
+        sums[2:3] = jnp.sum(attn.astype(F32), axis=0, keepdims=True)
+        sums[3:4] = jnp.sum(live, axis=0, keepdims=True)
+        sums[4:8] = jnp.zeros_like(sums[4:8])
+        left, right = attn[:, : feat // 2], attn[:, feat // 2 :]
+        attn_mine[...] = jnp.where(core == 0, left, right)
+        attn_theirs[...] = jnp.where(core == 0, right, left)
+        grad_mixed[...] = (dot_last(left, proj[0]) + dot_last(right, proj[1])).astype(BF16)
+
+
+def fall(info, grad_y, slope, up_set, after, vecs, first_set, pieces):
+    rows, feat = grad_y.shape
+    hidden = slope.shape[1]
+    tile = 384
+    steps = hidden // tile
+    per = steps // 2
+
+    def at(n, info):
+        return jnp.where(n < per, 1 - info[CORE], info[CORE]) * per + n % per
+
+    def whole(dims):
+        return pl.BlockSpec(dims, lambda n, info: (0,) * len(dims))
+
+    return pl.pallas_call(
+        fall_kernel,
+        grid_spec=pltpu.PrefetchScalarGridSpec(
+            num_scalar_prefetch=1,
+            grid=(steps,),
+            in_specs=[
+                whole((rows, feat)),
+                pl.BlockSpec((rows, tile), lambda n, info: (0, at(n, info))),
+                pl.BlockSpec(
+                    (1, feat, tile), lambda n, info: (at(n, info) // per, 0, n % per)
+                ),
+                whole((rows, feat)),
+                whole((8, feat)),
+                pl.BlockSpec((2, feat, feat // 2), lambda n, info: (0, 0, 3)),
+            ]
+            + [ANY] * 4,
+            out_specs=(
+                whole((16, 2, hidden // 32, feat)),
+                pl.BlockSpec((rows, tile), lambda n, info: (0, jnp.minimum(n, per - 1))),
+                pl.BlockSpec((rows, tile), lambda n, info: (0, jnp.maximum(n - per, 0))),
+                pl.BlockSpec((1, tile), lambda n, info: (0, at(n, info))),
+                whole((rows, feat)),
+                whole((rows, feat // 2)),
+                whole((rows, feat // 2)),
+                whole((rows, feat)),
+                whole((8, feat)),
+            ),
+            scratch_shapes=[pltpu.VMEM((rows, feat), F32), pltpu.SemaphoreType.DMA((32,))],
+        ),
+        out_shape=(
+            shape((16, 2, hidden // 32, feat), BF16),
+            shape((rows, hidden // 2), BF16),
+            shape((rows, hidden // 2), BF16),
+            shape((1, hidden), F32),
+            shape((rows, feat), F32),
+            shape((rows, feat // 2), BF16),
+            shape((rows, feat // 2), BF16),
+            shape((rows, feat), BF16),
+            shape((8, feat), F32),
+        ),
+        compiler_params=params(),
+        cost_estimate=cost(
+            4 * rows * feat * hidden, 8 * feat * hidden + 8 * rows * hidden
+        ),
+    )(info, grad_y, slope, up_set, after, vecs, first_set, *pieces)
+
+
+def exit_kernel(info, tokens, mine, theirs, weights, grad_after, vecs, grad_tokens, sums, grad_first):
+    step = pl.program_id(0)
+    core = info[CORE]
+    third = mine.shape[2]
+    half = jnp.where(step == 0, core, 1 - core)
+    spot = pl.ds(pl.multiple_of(half * third, third), third)
+
+    def parts(source):
+        total = dot_last(source[0], weights[0, :, :third])
+        for part in (1, 2):
+            cols = slice(part * third, (part + 1) * third)
+            total += dot_last(source[part], weights[0, :, cols])
+        sums[2:3, spot] = jnp.sum(source[0].astype(F32), axis=0, keepdims=True)
+        sums[3:4, spot] = jnp.sum(source[2].astype(F32), axis=0, keepdims=True)
+        return total
+
+    @pl.when(step == 0)
+    def _():
+        grad_first[...] = parts(mine)
+
+    @pl.when(step == 1)
+    def _():
+        grad = grad_first[...] + parts(theirs)
+        normed, inverse = centre(tokens[...].astype(F32))
+        sums[0:1] = jnp.sum(grad * normed, axis=0, keepdims=True)
+        sums[1:2] = jnp.sum(grad, axis=0, keepdims=True)
+        sums[4:8] = jnp.zeros_like(sums[4:8])
+        back = layer_back(grad * vecs[0:1], normed, inverse)
+        grad_tokens[...] = (grad_after[...] + back).astype(BF16)
+
+
+def exit_back(info, tokens, mine, theirs, first_set, grad_after, vecs):
+    rows, feat = tokens.shape
+    third = feat // 2
+
+    def whole(dims):
+        return pl.BlockSpec(dims, lambda n, info: (0,) * len(dims))
+
+    return pl.pallas_call(
+        exit_kernel,
+        grid_spec=pltpu.PrefetchScalarGridSpec(
+            num_scalar_prefetch=1,
+            grid=(2,),
+            in_specs=[
+                whole((rows, feat)),
+                whole((3, rows, third)),
+                whole((3, rows, third)),
+                pl.BlockSpec(
+                    (1, feat, 3 * third),
+                    lambda n, info: (jnp.where(n == 0, info[CORE], 1 - info[CORE]), 0, 0),
+                ),
+                whole((rows, feat)),
+                whole((8, feat)),
+            ],
+            out_specs=(whole((rows, feat)), whole((8, feat))),
+            scratch_shapes=[pltpu.VMEM((rows, feat), F32)],
+        ),
+        out_shape=(shape((rows, feat), BF16), shape((8, feat), F32)),
+        compiler_params=params(),
+        cost_estimate=cost(6 * rows * feat * feat, 6 * feat * feat + 12 * rows * feat),
+    )(info, tokens, mine, theirs, first_set, grad_after, vecs)
+
+
+def outer_kernel(info, left, left_o, right, right_o, keep, away, turned, blocks):
+    rows = left.shape[0]
+
+    @pl.when(pl.program_id(0) == 0)
+    def _():
+        turned[:, :rows] = left[...].T
+        turned[:, rows:] = left_o[...].T
+
+    total = dot(turned[:, :rows], right[0]) + dot(turned[:, rows:], right_o[0])
+    blocks[...] = total.reshape(blocks.shape)
+    for j in range(8):
+        keep[j] = blocks[info[j]]
+        away[j] = blocks[info[8 + j]].astype(BF16)
+
+
+def outer(info, left, left_o, right, right_o, tile=384):
+    rows, feat = left.shape
+    n_parts, _, width = right.shape
+    per = width // tile
+    cols = n_parts * width
+    block = feat // 16
+    strip = pl.BlockSpec((1, rows, tile), lambda n: (n // per, 0, n % per))
+    out = pl.BlockSpec((8, block, tile), lambda n: (0, 0, n))
+    return pl.pallas_call(
+        outer_kernel,
+        grid=(cols // tile,),
+        out_shape=(shape((8, block, cols), F32), shape((8, block, cols), BF16)),
+        in_specs=[SMEM, full((rows, feat)), full((rows, feat)), strip, strip],
+        out_specs=(out, out),
+        scratch_shapes=[pltpu.VMEM((feat, 2 * rows), BF16), pltpu.VMEM((16, block, tile), F32)],
+        compiler_params=params(),
+        cost_estimate=cost(4 * rows * feat * cols, 4 * rows * (feat + cols) + 3 * feat * cols),
+    )(info, left, left_o, right, right_o)
+
+
+def outer_last_kernel(
+    info, left, left_o, right, right_o, sums_a, sums_b, bias, keep, away, blocks, extra
+):
+    rows, feat = left.shape
+    tile = right.shape[1]
+    block = feat // 16
+    total = dot(left[...].T, right[...]) + dot(left_o[...].T, right_o[...])
+    blocks[...] = total.reshape(blocks.shape)
+    extra[...] = jnp.zeros_like(extra)
+    ordered = jnp.concatenate(
+        [
+            sums_b[0:1],
+            sums_a[0:1],
+            sums_b[1:4],
+            sums_a[2:3],
+            sums_a[1:2],
+            sums_a[3:4],
+        ]
+    )
+    each = bias.shape[1] // 16
+    for chip in range(16):
+        extra[chip, 0:8, 0:block] = ordered[:, chip * block : (chip + 1) * block]
+        extra[chip, 8:9, 0:each] = bias[:, chip * each : (chip + 1) * each]
+    for j in range(8):
+        keep[j, :block] = blocks[info[j]]
+        away[j, :block] = blocks[info[8 + j]].astype(BF16)
+        keep[j, block:] = extra[info[j]]
+        away[j, block:] = extra[info[8 + j]].astype(BF16)
+
+
+def outer_last(info, left, left_o, right, right_o, sums_a, sums_b, bias):
+    rows, feat = left.shape
+    cols = right.shape[1]
+    block = feat // 16
+    vmem = pl.BlockSpec(memory_space=pltpu.VMEM)
+    return pl.pallas_call(
+        outer_last_kernel,
+        out_shape=(shape((8, block + 16, cols), F32), shape((8, block + 16, cols), BF16)),
+        in_specs=[SMEM] + [vmem] * 7,
+        out_specs=(vmem, vmem),
+        scratch_shapes=[pltpu.VMEM((16, block, cols), F32), pltpu.VMEM((16, 16, cols), F32)],
+        compiler_params=params(),
+        cost_estimate=cost(4 * rows * feat * cols, 4 * rows * (feat + cols) + 3 * feat * cols),
+    )(info, left, left_o, right, right_o, sums_a, sums_b, bias)
+
+
+def outer_down_kernel(left, left_o, right, right_o, keep, away):
+    def flat(blocks):
+        return blocks[...].reshape(-1, blocks.shape[-1])
+
+    total = dot(flat(left), right[...]) + dot(flat(left_o), right_o[...])
+    total = total.reshape(keep.shape)
+
+    @pl.when(pl.program_id(0) >= 4)
+    def _():
+        keep[...] = total
+
+    @pl.when(pl.program_id(0) < 4)
+    def _():
+        away[...] = total.astype(BF16)
+
+
+def outer_down(left, left_o, right, right_o):
+    _, block, rows = left.shape
+    feat = right.shape[1]
+    strip = pl.BlockSpec((2, block, rows), lambda j: ((j + 4) % 8, 0, 0))
+    return pl.pallas_call(
+        outer_down_kernel,
+        grid=(8,),
+        out_shape=(shape((8, block, feat), F32), shape((8, block, feat), BF16)),
+        in_specs=[strip, strip, full((rows, feat)), full((rows, feat))],
+        out_specs=(
+            pl.BlockSpec((2, block, feat), lambda j: (jnp.maximum(j - 4, 0), 0, 0)),
+            pl.BlockSpec((2, block, feat), lambda j: (jnp.minimum(j, 3), 0, 0)),
+        ),
+        compiler_params=params(),
+        cost_estimate=cost(64 * rows * feat * block, 96 * block * (rows + feat)),
+    )(left, left_o, right, right_o)
+
+
+def add_first_kernel(keep, got, keep_s, got_s, kept, away):
+    kept[...] = keep[...] + got[...].astype(F32)
+    away[...] = (keep_s[...] + got_s[...].astype(F32)).astype(BF16)
+
+
+def add_first(keep, got):
+    _, rows, cols = keep.shape
+    near = pl.BlockSpec((1, rows, cols), lambda i: (i, 0, 0))
+    far = pl.BlockSpec((1, rows, cols), lambda i: (i + 4, 0, 0))
+    return pl.pallas_call(
+        add_first_kernel,
+        grid=(4,),
+        out_shape=(shape((4, rows, cols), F32), shape((4, rows, cols), BF16)),
+        in_specs=[near, near, far, far],
+        out_specs=(near, near),
+        compiler_params=params(),
+        cost_estimate=cost(8 * rows * cols, 72 * rows * cols),
+    )(keep, got, keep, got)
+
+
+def add_second_kernel(keep, got, base, one, two, three):
+    base[...] = keep[0] + got[0].astype(F32)
+    for s, out in ((1, one), (2, two), (3, three)):
+        out[...] = (keep[s] + got[s].astype(F32)).astype(BF16)
+
+
+def add_second(keep, got):
+    _, rows, cols = keep.shape
+    vmem = pl.BlockSpec(memory_space=pltpu.VMEM)
+    low = shape((rows, cols), BF16)
+    return pl.pallas_call(
+        add_second_kernel,
+        out_shape=(shape((rows, cols), F32), low, low, low),
+        in_specs=[vmem] * 2,
+        out_specs=(vmem,) * 4,
+        compiler_params=params(),
+        cost_estimate=cost(4 * rows * cols, 34 * rows * cols),
+    )(keep, got)
+
+
+def total_of(base, parts):
+    return base[...] + parts[0][...].astype(F32) + (
+        parts[1][...].astype(F32) + parts[2][...].astype(F32)
+    )
+
+
+def add_down_kernel(base, one, two, three, out):
+    out[...] = total_of(base, (one, two, three))
+
+
+def add_last_kernel(info, base, one, two, three, mine, theirs, total):
+    core = info[CORE]
+    half = mine.shape[0]
+    total[...] = total_of(base, (one, two, three))
+    mine[...] = total[pl.ds(pl.multiple_of(core * half, half), half)]
+    theirs[...] = total[pl.ds(pl.multiple_of((1 - core) * half, half), half)]
+
+
+def add_small_kernel(info, base, one, two, three, mine, theirs, total):
+    core = info[CORE]
+    half = mine.shape[0] - 16
+    total[...] = total_of(base, (one, two, three))
+    mine[:half] = total[pl.ds(pl.multiple_of(core * half, half), half)]
+    theirs[:half] = total[pl.ds(pl.multiple_of((1 - core) * half, half), half)]
+    mine[half:] = total[2 * half :]
+    theirs[half:] = total[2 * half :]
+
+
+def travel(keep, away):
+    kept, away = add_first(keep, send(away, second_way))
+    base, *lows = add_second(kept, send(away, first_way))
+    return base, [send(low, along_z(s)) for low, s in zip(lows, (1, 2, 3))]
+
+
+def home_down(keep, away):
+    base, parts = travel(keep, away)
+    vmem = pl.BlockSpec(memory_space=pltpu.VMEM)
+    return pl.pallas_call(
+        add_down_kernel,
+        out_shape=shape(base.shape, F32),
+        in_specs=[vmem] * 4,
+        out_specs=vmem,
+        compiler_params=params(),
+        cost_estimate=cost(3 * base.size, 14 * base.size),
+    )(base, *parts)
+
+
+def home(info, keep, away, kernel, extra):
+    base, parts = travel(keep, away)
+    rows, cols = base.shape
+    vmem = pl.BlockSpec(memory_space=pltpu.VMEM)
+    out = shape(((rows - extra) // 2 + extra, cols), F32)
+    mine, theirs = pl.pallas_call(
+        kernel,
+        out_shape=(out, out),
+        in_specs=[SMEM] + [vmem] * 4,
+        out_specs=(vmem, vmem),
+        scratch_shapes=[pltpu.VMEM((rows, cols), F32)],
+        compiler_params=params(),
+        cost_estimate=cost(3 * base.size, 14 * base.size),
+    )(info, base, *parts)
+    return mine, swap(theirs)
+
+
+def finish_kernel(
+    info, qkv, qkv_o, proj, proj_o, up, up_o, out_qkv, out_proj, out_up, gains, shifts, bias
+):
+    rows, third = out_proj.shape[0], proj.shape[1]
+    wide = up.shape[1]
+    small = proj[rows:] + proj_o[rows:]
+    each = 4 * rows
+
+    def lay(core):
+        for half, (a, b, c) in ((core, (qkv, proj, up)), (1 - core, (qkv_o, proj_o, up_o))):
+            for part in range(3):
+                spot = part * 2 * third + half * third
+                out_qkv[:, spot : spot + third] = a[:, part * third : (part + 1) * third]
+            out_proj[:, half * third : (half + 1) * third] = b[:rows]
+            out_up[:, half * wide : (half + 1) * wide] = c[...]
+        mine = small[0:8, core * rows : (core + 1) * rows]
+        wide_mine = jnp.concatenate([mine, jnp.zeros((8, 128 - rows), F32)], axis=1).T
+        gains[...] = wide_mine[:rows, 0:2]
+        shifts[...] = wide_mine[:rows, 2:8]
+        bias[...] = small[8:9, core * each : (core + 1) * each]
+
+    @pl.when(info[CORE] == 0)
+    def _():
+        lay(0)
+
+    @pl.when(info[CORE] == 1)
+    def _():
+        lay(1)
+
+
+def finish(info, qkv, qkv_o, proj, proj_o, up, up_o):
+    rows, third = up.shape[0], proj.shape[1]
+    vmem = pl.BlockSpec(memory_space=pltpu.VMEM)
+    return pl.pallas_call(
+        finish_kernel,
+        out_shape=(
+            shape((rows, 6 * third), F32),
+            shape((rows, 2 * third), F32),
+            shape((rows, 2 * up.shape[1]), F32),
+            shape((rows, 2), F32),
+            shape((rows, 6), F32),
+            shape((1, 4 * rows), F32),
+        ),
+        in_specs=[SMEM] + [vmem] * 6,
+        out_specs=(vmem,) * 6,
+        compiler_params=params(),
+        cost_estimate=cost(0, 64 * rows * third),
+    )(info, qkv, qkv_o, proj, proj_o, up, up_o)
+
+
+def local(
+    tokens,
+    upstream,
+    lengths,
+    qkv_weight,
+    proj_weight,
+    up_weight,
+    down_weight,
+    gains,
+    shifts,
+    up_bias,
+):
+    tok_rows, feat = tokens.shape
+    rows = qkv_weight.shape[0]
+    hidden = up_weight.shape[1]
+    third, wide = feat // 2, hidden // 2
+    chip, core = lax.axis_index("dp"), lax.axis_index("fsdp")
+    info = facts(chip, core, lengths[0])
+
+    live = lax.iota(jnp.int32, tok_rows) < lengths[0]
+    grad_y = jnp.where(live[:, None], upstream, jnp.zeros_like(upstream))
+
+    small = jnp.concatenate([gains, shifts, up_bias.reshape(rows, -1)], axis=1)
+    small = jnp.pad(small, ((0, 0), (0, 128 - small.shape[1])))
+
+    def half_of(h):
+        parts = [qkv_weight[:, i * feat + h * third : i * feat + (h + 1) * third] for i in range(3)]
+        parts += [proj_weight[:, h * third : (h + 1) * third], small]
+        parts += [up_weight[:, h * wide : (h + 1) * wide]]
+        return jnp.concatenate(parts, axis=1)
+
+    halves = jnp.stack([half_of(0), half_of(1)])
+    mine = lax.dynamic_index_in_dim(halves, core, 0, keepdims=False)
+    given = swap(lax.dynamic_index_in_dim(halves, 1 - core, 0, keepdims=False))
+    piece = jnp.where(core == 0, jnp.concatenate([mine, given]), jnp.concatenate([given, mine]))
+    one = 4 * third + 128
+    first_pieces = spread(piece[:, :one])
+    up_pieces = spread(piece[:, one:])
+    down_pieces = spread(down_weight)
+    grad_y_o = swap(grad_y)
+
+    first_set, vecs, first, joint = enter(info, tokens, first_pieces)
+    bias = first_set[0, :, :, one - 120 : one - 116].reshape(1, hidden).astype(F32)
+    first_set = first_set.reshape(2, feat, one)
+    first_o = swap(first)
+    mixed, stats = mix(info, joint)
+    mixed_o = swap(mixed)
+    up_set, after, second, active, slope, turned, turned_t = rise(
+        info, tokens, mixed, first_set, vecs, bias, up_pieces
+    )
+    second_o, turned_o = swap(second), swap(turned_t)
+    own_down = home_down(*outer_down(turned, turned_o, grad_y, grad_y_o))
+
+    down_set, hid_theirs, hid_mine, bias_sum, grad_after, at_theirs, at_mine, grad_mixed, sums_a = (
+        fall(info, grad_y, slope, up_set.reshape(2, feat, wide), after, vecs, first_set, down_pieces)
+    )
+    hid_o, at_o = swap(hid_theirs), swap(at_theirs)
+    own_up = home(
+        info, *outer(info, second, second_o, hid_mine[None], hid_o[None]), add_last_kernel, 0
+    )
+    theirs, mine = mix_back(info, joint, grad_mixed, stats)
+    own_qkv = home(info, *outer(info, first, first_o, mine, swap(theirs)), add_last_kernel, 0)
+    grad_tokens, sums_b = exit_back(info, tokens, mine, theirs, first_set, grad_after, vecs)
+    own_last = home(
+        info,
+        *outer_last(info, mixed, mixed_o, at_mine, at_o, sums_a, sums_b, bias_sum),
+        add_small_kernel,
+        16,
+    )
+    output = leave(after, active, down_set.reshape(hidden, feat), vecs)
+    out_qkv, out_proj, out_up, out_gains, out_shifts, out_bias = finish(
+        info, *own_qkv, *own_last, *own_up
+    )
+    return (
+        output,
+        grad_tokens,
+        out_qkv,
+        out_proj,
+        out_up,
+        own_down,
+        out_gains,
+        out_shifts,
+        out_bias.reshape(-1),
+    )
+
+
 def solution(mesh):
     placed = (
         P(("dp", "fsdp"), None),
@@ -248,8 +1199,9 @@
         P(("dp", "fsdp"), None),
         P(("dp", "fsdp")),
     )
+    sizes = (mesh.shape["dp"], mesh.shape["fsdp"])
     return jax.shard_map(
-        local,
+        local if sizes == (16, 2) else plain,
         mesh=mesh,
         in_specs=placed,
         out_specs=(

time: 813 us -> 318 us (0.39)
  waiting for transfers between devices: 489 us -> 82.8 us
  blocking collectives: 161 us -> 0 us
  Pallas kernels: 0 us -> 151 us
  matrix products: 106 us -> 0 us
  starting transfers between devices: 0.53 us -> 52.6 us
  other arithmetic: 20.4 us -> 3.2 us
  between operations: 15.7 us -> 1.88 us
    reduce_scatter x4 -> x0, waiting for transfers between devices: 406 us -> none  [the longest x1 142 us: give_back(): lax.psum_scatter(grad_down, ('dp', 'fsdp'), scatter_dimension=0, tiled=True)]
    pallas_call x0 -> x24, Pallas kernels: none -> 151 us  [the longest x1 20.9 us: fall(): pl.pallas_call(fall_kernel, grid_spec=pltpu.PrefetchScalarGridSpec(num_sc...]
    dot_general x30 -> x0, matrix products: 106 us -> none  [the longest x1 20 us: local(): jnp.dot(second, up_full, preferred_element_type=jnp.float32) + bias_f]
    unnamed x2 -> x0, blocking collectives: 83.2 us -> none
    ppermute x0 -> x53, waiting for transfers between devices: none -> 82.8 us  [send(): return lax.ppermute(array, AXES, pairs(move))]
    all_gather x4 -> x0, waiting for transfers between devices: 80.2 us -> none  [the longest x1 45.3 us: collect(): lax.all_gather(down_weight, ('dp', 'fsdp'), axis=0, tiled=True)]
    all_gather x2 -> x0, blocking collectives: 77.5 us -> none  [the longest x1 40.2 us: collect(): lax.all_gather(gains, ('dp', 'fsdp'), axis=0, tiled=True)]
    ppermute x0 -> x53, starting transfers between devices: none -> 52.6 us  [send(): return lax.ppermute(array, AXES, pairs(move))]
  transfers between devices with their start and end apart: 8 -> 53, of which waited for: 5 -> 12; matrix products, arithmetic and copies ran while one was open for 12% -> 4% of each run, Pallas kernels for 0% -> 41%
where the time goes in v1:
time: 318 us; the launch traced here: 316 us
  Pallas kernels  151 us (47%)
  waiting for transfers between devices  82.8 us (26%)
  starting transfers between devices  52.6 us (17%)
  local copies, waits for them, and re-layouts  24.5 us (8%)
  other arithmetic  3.2 us (1%)
    ppermute x53, waiting for transfers between devices, send(): return lax.ppermute(array, AXES, pairs(move))  82.8 us
    ppermute x53, starting transfers between devices, send(): return lax.ppermute(array, AXES, pairs(move))  52.6 us
    pallas_call x1, Pallas kernels, fall(): pl.pallas_call(fall_kernel, grid_spec=pltpu.PrefetchScalarGridSpec(num_sc...  20.9 us
    unnamed x100, local copies, waits for them, and re-layouts  20.3 us
    pallas_call x1, Pallas kernels, rise(): pl.pallas_call(rise_kernel, grid=(hidden // tile,), out_shape=(shape((2,...  19.4 us
    pallas_call x1, Pallas kernels, mix_back(): pl.pallas_call(mix_back_kernel, grid_spec=pltpu.PrefetchScalarGridSpec(nu...  16.5 us
    pallas_call x4, Pallas kernels, add_first(): pl.pallas_call(add_first_kernel, grid=(4,), out_shape=(shape((4, rows, co...  15.1 us
    pallas_call x2, Pallas kernels, outer(): pl.pallas_call(outer_kernel, grid=(cols // tile,), out_shape=(shape((8, b...  14.6 us
  transfers between devices with their start and end apart: 53, of which 12 were waited for; matrix products, arithmetic and copies ran while one was open for 4% of the time, Pallas kernels for 41%

profile of v1, /device:TPU:0, one launch (start us, length us, event | category | flops | bytes accessed | tf_op | source)
XLA Modules:
  0.0 316.2 jit_solution(5055852346554170965)
XLA Ops:
  0.7 3.1 collective-permute-start.15
  3.7 2.6 collective-permute-start.16
  12.2 5.7 %collective-permute-done.16 = bf16[96,768]{1,0:T(8,128)(2,1)S(1)} collective-permute-done((bf16[96,768]{1,0:T(8,128)(2,1)}, bf16[96,768]{1,0:T(8,128)(2,1)S(1)}, u32[]{:S(2)}, u32[]{:S(2)}) %collective-permute-start.16) | collective-permute-done | bytes 147488 | tf_op jit(solution)/shard_map/ppermute | solution.py:266
  19.8 2.4 collective-permute-start.8
  29.9 6.0 %collective-permute-done.9 = bf16[48,1536]{1,0:T(8,128)(2,1)S(1)} collective-permute-done((bf16[48,1536]{1,0:T(8,128)(2,1)S(1)}, bf16[48,1536]{1,0:T(8,128)(2,1)S(1)}, u32[]{:S(2)}, u32[]{:S(2)}) %collective-permute-start.9) | collective-permute-done | bytes 147488 | tf_op jit(solution)/shard_map/ppermute | solution.py:266
  35.9 2.5 collective-permute-start.3
  39.1 9.4 %collective-permute-done.2 = bf16[48,1664]{1,0:T(8,128)(2,1)S(1)} collective-permute-done((bf16[48,1664]{1,0:T(8,128)(2,1)S(1)}, bf16[48,1664]{1,0:T(8,128)(2,1)S(1)}, u32[]{:S(2)}, u32[]{:S(2)}) %collective-permute-start.2) | collective-permute-done | bytes 159776 | tf_op jit(solution)/shard_map/ppermute | solution.py:266
  52.2 7.7 %collective-permute-done.4 = bf16[4,48,1664]{2,1,0:T(8,128)(2,1)S(1)} collective-permute-done((bf16[4,48,1664]{2,1,0:T(8,128)(2,1)S(1)}, bf16[4,48,1664]{2,1,0:T(8,128)(2,1)S(1)}, u32[]{:S(2)}, u32[]{:S(2)}) %collective-permute-start.4) | collective-permute-done | bytes 639008 | tf_op jit(solution)/shard_map/ppermute | solution.py:266
  63.9 14.4 %collective-permute-done.5.high = bf16[8,48,1664]{2,1,0:T(8,128)(2,1)} collective-permute-done((bf16[8,48,1664]{2,1,0:T(8,128)(2,1)}, bf16[8,48,1664]{2,1,0:T(8,128)(2,1)}, u32[]{:S(2)}, u32[]{:S(2)}) %collective-permute-start.5) | collective-permute-done | bytes 1277984 | tf_op jit(solution)/shard_map/ppermute | solution.py:266
  78.8 12.1 %collective-permute-done.12.high = bf16[8,48,1536]{2,1,0:T(8,128)(2,1)} collective-permute-done((bf16[8,48,1536]{2,1,0:T(8,128)(2,1)S(1)}, bf16[8,48,1536]{2,1,0:T(8,128)(2,1)}, u32[]{:S(2)}, u32[]{:S(2)}) %collective-permute-start.12) | collective-permute-done | bytes 1179680 | tf_op jit(solution)/shard_map/ppermute | solution.py:266
  92.2 11.3 %collective-permute-done.19.high = bf16[8,96,768]{2,1,0:T(8,128)(2,1)} collective-permute-done((bf16[8,96,768]{2,1,0:T(8,128)(2,1)S(1)}, bf16[8,96,768]{2,1,0:T(8,128)(2,1)}, u32[]{:S(2)}, u32[]{:S(2)}) %collective-permute-start.19) | collective-permute-done | bytes 1179680 | tf_op jit(solution)/shard_map/ppermute | solution.py:266
  105.1 8.1 %shard_map.169 = (bf16[2,16,48,1664]{3,2,1,0:T(8,128)(2,1)}, f32[8,768]{1,0:T(8,128)}, bf16[512,768]{1,0:T(8,128)(2,1)}, bf16[2,512,1152]{2,1,0:T(8,128)(2,1)}) custom-call(s32[34]{0:T(128)} %stack.165.info, bf16[512,768]{1,0:T(8,128)(2,1)} %tokens.5, bf16[8,48,1664]{2,1,0:T(8,128)(2,1)} %constant_dynamic-update-slice_fusion.10.low, ...), custom_call_target="tpu_custom_call" | custom-call | flops 1811939328 | bytes 14155776 | tf_op jit(solution)/shard_map/pallas_call | solution.py:368
  115.1 10.2 %shard_map.170 = (bf16[512,768]{1,0:T(8,128)(2,1)}, f32[6,8,512]{2,1,0:T(8,128)}) custom-call(s32[34]{0:T(128)} %stack.165.info, bf16[2,512,1152]{2,1,0:T(8,128)(2,1)} %get-tuple-element.79.q.k.v, bf16[2,512,1152]{2,1,0:T(8,128)(2,1)} %get-tuple-element.79.q.k.v, bf16[2,512,1152]{2,1,0:T(8,128)(2,1)} %get-tuple-element.79.q.k.v), custom_call_target="tpu_custom_call" | custom-call | flops 3221225472 | bytes 3145728 | tf_op jit(solution)/shard_map/pallas_call | solution.py:416
  125.3 19.4 %shard_map.171 = (bf16[2,16,48,1536]{3,2,1,0:T(8,128)(2,1)}, f32[512,768]{1,0:T(8,128)}, bf16[512,768]{1,0:T(8,128)(2,1)}, bf16[512,3072]{1,0:T(8,128)(2,1)}, bf...) custom-call(s32[34]{0:T(128)} %stack.165.info, bf16[512,768]{1,0:T(8,128)(2,1)} %tokens.5, ...), custom_call_target="tpu_custom_call" | custom-call | flops 3019898880 | bytes 18874368 | tf_op jit(solution)/shard_map/pallas_call | solution.py:579
  144.7 20.9 %shard_map.172 = (bf16[16,2,96,768]{3,2,1,0:T(8,128)(2,1)}, bf16[512,1536]{1,0:T(8,128)(2,1)}, bf16[512,1536]{1,0:T(8,128)(2,1)}, f32[1,3072]{1,0:T(1,128)}, f32...) custom-call(s32[34]{0:T(128)} %stack.165.info, ...), custom_call_target="tpu_custom_call" | custom-call | flops 4831838208 | bytes 31457280 | tf_op jit(solution)/shard_map/pallas_call | solution.py:724
  166.3 16.5 %shard_map.174 = (bf16[3,512,384]{2,1,0:T(8,128)(2,1)}, bf16[3,512,384]{2,1,0:T(8,128)(2,1)}) custom-call(s32[34]{0:T(128)} %stack.165.info, bf16[2,512,1152]{2,1,0:T(8,128)(2,1)} %get-tuple-element.79.q.k.v, bf16[2,512,1152]{2,1,0:T(8,128)(2,1)} %get-tuple-element.79.q.k.v, bf16[2,512,1152]{2,1,0:T(8,128)(2,1)} %get-tuple-element.79.q.k.v, ...), custom_call_target="tpu_custom_call" | custom-call | flops 8053063680 | bytes 6291456 | tf_op jit(solution)/shard_map/pallas_call | solution.py:480
  185.0 7.8 %shard_map.184 = (f32[8,48,1536]{2,1,0:T(8,128)}, bf16[8,48,1536]{2,1,0:T(8,128)(2,1)}) custom-call(s32[34]{0:T(128)} %stack.165.info, bf16[512,768]{1,0:T(8,128)(2,1)} %get-tuple-element.120.left, bf16[512,768]{1,0:T(8,128)(2,1)} %collective-permute-done.38.left_o, bf16[1,512,1536]{2,1,0:T(8,128)(2,1)} %bitcast.84, bf16[1,512,1536]{2,1,0:T(8,128)(2,1)} %bitcast.85), custom_call_target="tpu_custom_call" | custom-call | flops 2415919104 | bytes 8257536 | tf_op jit(solution)/shard_map/pallas_call | solution.py:857
  194.6 8.8 %shard_map.189 = (f32[8,96,768]{2,1,0:T(8,128)}, bf16[8,96,768]{2,1,0:T(8,128)(2,1)}) custom-call(bf16[16,96,512]{2,1,0:T(8,128)(2,1)} %get-tuple-element.136.left, bf16[16,96,512]{2,1,0:T(8,128)(2,1)} %copy-done.34, bf16[512,768]{1,0:T(8,128)(2,1)} %broadcast_select_fusion.grad_y.right, bf16[512,768]{1,0:T(8,128)(2,1)} %collective-permute-done.47.right_o), custom_call_target="tpu_custom_call" | custom-call | flops 2415919104 | bytes 11796480 | tf_op jit(solution)/shard_map/pallas_call | solution.py:935
  205.8 6.8 %shard_map.176 = (f32[8,48,1152]{2,1,0:T(8,128)}, bf16[8,48,1152]{2,1,0:T(8,128)(2,1)}) custom-call(s32[34]{0:T(128)} %stack.165.info, bf16[512,768]{1,0:T(8,128)(2,1)} %get-tuple-element.94.left, bf16[512,768]{1,0:T(8,128)(2,1)} %collective-permute-done.22.left_o, bf16[3,512,384]{2,1,0:T(8,128)(2,1)} %get-tuple-element.90.mine.right, ...), custom_call_target="tpu_custom_call" | custom-call | flops 1811939328 | bytes 6586368 | tf_op jit(solution)/shard_map/pallas_call | solution.py:857
  214.3 8.0 %shard_map.175 = (bf16[512,768]{1,0:T(8,128)(2,1)}, f32[8,768]{1,0:T(8,128)}) custom-call(s32[34]{0:T(128)} %stack.165.info, bf16[512,768]{1,0:T(8,128)(2,1)} %tokens.5, bf16[3,512,384]{2,1,0:T(8,128)(2,1)} %get-tuple-element.90.mine.right, bf16[3,512,384]{2,1,0:T(8,128)(2,1)} %get-tuple-element.91.theirs, bf16[2,768,1664]{2,1,0:T(8,128)(2,1)} %bitcast.69, ...), custom_call_target="tpu_custom_call" | custom-call | flops 1811939328 | bytes 8257536 | tf_op jit(solution)/shard_map/pallas_call | solution.py:809
  223.4 3.7 %shard_map.180 = (f32[8,64,384]{2,1,0:T(8,128)}, bf16[8,64,384]{2,1,0:T(8,128)(2,1)}) custom-call(s32[34]{0:T(128)} %stack.165.info, bf16[512,768]{1,0:T(8,128)(2,1)} %get-tuple-element.80.mixed.left, bf16[512,768]{1,0:T(8,128)(2,1)} %copy-done.9, bf16[512,384]{1,0:T(8,128)(2,1)} %get-tuple-element.105.right, bf16[512,384]{1,0:T(8,128)(2,1)} %copy-done.16, ...), custom_call_target="tpu_custom_call" | custom-call | flops 603979776 | bytes 3244032 | tf_op jit(solution)/shard_map/pallas_call | solution.py:904
  228.8 4.0 %shard_map.185 = (f32[4,48,1536]{2,1,0:T(8,128)}, bf16[4,48,1536]{2,1,0:T(8,128)(2,1)}) custom-call(f32[8,48,1536]{2,1,0:T(8,128)} %get-tuple-element.123.keep.keep_s, bf16[8,48,1536]{2,1,0:T(8,128)(2,1)} %copy-done, f32[8,48,1536]{2,1,0:T(8,128)} %get-tuple-element.123.keep.keep_s, bf16[8,48,1536]{2,1,0:T(8,128)(2,1)} %copy-done), custom_call_target="tpu_custom_call" | custom-call | flops 589824 | bytes 5308416 | tf_op jit(solution)/shard_map/pallas_call | solution.py:958
  235.0 4.0 %shard_map.190 = (f32[4,96,768]{2,1,0:T(8,128)}, bf16[4,96,768]{2,1,0:T(8,128)(2,1)}) custom-call(f32[8,96,768]{2,1,0:T(8,128)} %get-tuple-element.138.keep.keep_s, bf16[8,96,768]{2,1,0:T(8,128)(2,1)} %copy-done.1, f32[8,96,768]{2,1,0:T(8,128)} %get-tuple-element.138.keep.keep_s, bf16[8,96,768]{2,1,0:T(8,128)(2,1)} %copy-done.1), custom_call_target="tpu_custom_call" | custom-call | flops 589824 | bytes 5308416 | tf_op jit(solution)/shard_map/pallas_call | solution.py:958
  240.8 3.8 %shard_map.177 = (f32[4,48,1152]{2,1,0:T(8,128)}, bf16[4,48,1152]{2,1,0:T(8,128)(2,1)}) custom-call(f32[8,48,1152]{2,1,0:T(8,128)} %get-tuple-element.95.keep.keep_s, bf16[8,48,1152]{2,1,0:T(8,128)(2,1)} %copy-done.2, f32[8,48,1152]{2,1,0:T(8,128)} %get-tuple-element.95.keep.keep_s, bf16[8,48,1152]{2,1,0:T(8,128)(2,1)} %copy-done.2), custom_call_target="tpu_custom_call" | custom-call | flops 442368 | bytes 3981312 | tf_op jit(solution)/shard_map/pallas_call | solution.py:958
  246.5 3.3 %shard_map.181 = (f32[4,64,384]{2,1,0:T(8,128)}, bf16[4,64,384]{2,1,0:T(8,128)(2,1)}) custom-call(f32[8,64,384]{2,1,0:T(8,128)} %get-tuple-element.110.keep.keep_s, bf16[8,64,384]{2,1,0:T(8,128)(2,1)} %copy-done.5, f32[8,64,384]{2,1,0:T(8,128)} %get-tuple-element.110.keep.keep_s, bf16[8,64,384]{2,1,0:T(8,128)(2,1)} %copy-done.5), custom_call_target="tpu_custom_call" | custom-call | flops 196608 | bytes 1769472 | tf_op jit(solution)/shard_map/pallas_call | solution.py:958
  250.7 3.2 %collective-permute-done.25.got = bf16[4,48,1152]{2,1,0:T(8,128)(2,1)S(1)} collective-permute-done((bf16[4,48,1152]{2,1,0:T(8,128)(2,1)}, bf16[4,48,1152]{2,1,0:T(8,128)(2,1)S(1)}, u32[]{:S(2)}, u32[]{:S(2)}) %collective-permute-start.25) | collective-permute-done | bytes 442400 | tf_op jit(solution)/shard_map/ppermute | solution.py:266
  256.8 2.7 collective-permute-start.26
  261.9 2.3 collective-permute-start.27
  275.2 2.4 collective-permute-start.44
  283.1 6.8 %collective-permute-done.28.three = bf16[48,1152]{1,0:T(8,128)(2,1)S(1)} collective-permute-done((bf16[48,1152]{1,0:T(8,128)(2,1)S(1)}, bf16[48,1152]{1,0:T(8,128)(2,1)S(1)}, u32[]{:S(2)}, u32[]{:S(2)}) %collective-permute-start.28) | collective-permute-done | bytes 110624 | tf_op jit(solution)/shard_map/ppermute | solution.py:266
  292.6 3.8 %collective-permute-start.51 = (bf16[96,768]{1,0:T(8,128)(2,1)}, bf16[96,768]{1,0:T(8,128)(2,1)S(1)}, u32[]{:S(2)}, u32[]{:S(2)}) collective-permute-start(bf16[96,768]{1,0:T(8,128)(2,1)} %get-tuple-element.144), channel_id=1, source_target_pairs={{0,16},{1,17},{2,18},{3,19},{4,20},{5,21},{6,22},{7,23},{8,24},{9,... | collective-permute-start | bytes 442376 | tf_op jit(solution)/shard_map/ppermute | solution.py:266
  300.0 8.0 %shard_map.173 = bf16[512,768]{1,0:T(8,128)(2,1)} custom-call(f32[512,768]{1,0:T(8,128)} %get-tuple-element.83.after, bf16[512,3072]{1,0:T(8,128)(2,1)} %get-tuple-element.84.active, bf16[3072,768]{1,0:T(8,128)(2,1)} %bitcast.70, f32[8,768]{1,0:T(8,128)} %get-tuple-element.82.vecs), custom_call_target="tpu_custom_call" | custom-call | flops 2415919104 | bytes 7864320 | tf_op jit(solution)/shard_map/pallas_call | solution.py:625
  (217 shorter events, 82.4 us)
Async XLA Ops:
  18.0 45.0 %collective-permute-start.18 = (bf16[4,96,768]{2,1,0:T(8,128)(2,1)S(1)}, bf16[4,96,768]{2,1,0:T(8,128)(2,1)S(1)}, u32[]{:S(2)}, u32[]{:S(2)}) collective-permute-start(bf16[4,96,768]{2,1,0:T(8,128)(2,1)S(1)} %pad_maximum_fusion.2), channel_id=1, source_target_pairs={{0,2},{1,5},{2,0},{3,7},{4,6},{5,1},{6,4},{7,3},{8,10},{9,13},{10,... | collective-permute-start | bytes 1769480 | tf_op jit(solution)/shard_map/ppermute | solution.py:266
  28.5 20.0 %collective-permute-start.2 = (bf16[48,1664]{1,0:T(8,128)(2,1)S(1)}, bf16[48,1664]{1,0:T(8,128)(2,1)S(1)}, u32[]{:S(2)}, u32[]{:S(2)}) collective-permute-start(bf16[48,1664]{1,0:T(8,128)(2,1)S(1)} %get-tuple-element.170), channel_id=1, source_target_pairs={{0,16},{1,17},{2,18},{3,19},{4,20},{5,21},{6,22},{7,23},{8,24},{9,... | collective-permute-start | bytes 479240 | tf_op jit(solution)/shard_map/ppermute | solution.py:266
  38.6 22.9 %collective-permute-start.11 = (bf16[4,48,1536]{2,1,0:T(8,128)(2,1)S(1)}, bf16[4,48,1536]{2,1,0:T(8,128)(2,1)S(1)}, u32[]{:S(2)}, u32[]{:S(2)}) collective-permute-start(bf16[4,48,1536]{2,1,0:T(8,128)(2,1)S(1)} %pad_maximum_fusion.1), channel_id=1, source_target_pairs={{0,2},{1,5},{2,0},{3,7},{4,6},{5,1},{6,4},{7,3},{8,10},{9,13},{10,... | collective-permute-start | bytes 1769480 | tf_op jit(solution)/shard_map/ppermute | solution.py:266
  60.7 17.6 %collective-permute-start.5 = (bf16[8,48,1664]{2,1,0:T(8,128)(2,1)}, bf16[8,48,1664]{2,1,0:T(8,128)(2,1)}, u32[]{:S(2)}, u32[]{:S(2)}) collective-permute-start(bf16[8,48,1664]{2,1,0:T(8,128)(2,1)} %constant_dynamic-update-slice_fusion.10.low), channel_id=1, source_target_pairs={{0,4},{1,3},{2,6},{3,1},{4,0},{5,7},{6,2},{7,5},{8,12},{9,11},{10,... | collective-permute-start | bytes 3833864 | tf_op jit(solution)/shard_map/ppermute | solution.py:266
  61.5 29.4 %collective-permute-start.12 = (bf16[8,48,1536]{2,1,0:T(8,128)(2,1)S(1)}, bf16[8,48,1536]{2,1,0:T(8,128)(2,1)}, u32[]{:S(2)}, u32[]{:S(2)}) collective-permute-start(bf16[8,48,1536]{2,1,0:T(8,128)(2,1)S(1)} %constant_dynamic-update-slice_fusion.15.low), channel_id=1, source_target_pairs={{0,4},{1,3},{2,6},{3,1},{4,0},{5,7},{6,2},{7,5},{8,12},{9,11},{10,... | collective-permute-start | bytes 3538952 | tf_op jit(solution)/shard_map/ppermute | solution.py:266
  62.9 40.6 %collective-permute-start.6 = (bf16[8,48,1664]{2,1,0:T(8,128)(2,1)}, bf16[8,48,1664]{2,1,0:T(8,128)(2,1)}, u32[]{:S(2)}, u32[]{:S(2)}) collective-permute-start(bf16[8,48,1664]{2,1,0:T(8,128)(2,1)} %constant_dynamic-update-slice_fusion.10.low), channel_id=1, source_target_pairs={{0,1},{1,0},{2,3},{3,2},{4,5},{5,4},{6,7},{7,6},{8,9},{9,8},{10,11... | collective-permute-start | bytes 3833864 | tf_op jit(solution)/shard_map/ppermute | solution.py:266
  63.1 40.5 %collective-permute-start.19 = (bf16[8,96,768]{2,1,0:T(8,128)(2,1)S(1)}, bf16[8,96,768]{2,1,0:T(8,128)(2,1)}, u32[]{:S(2)}, u32[]{:S(2)}) collective-permute-start(bf16[8,96,768]{2,1,0:T(8,128)(2,1)S(1)} %constant_dynamic-update-slice_fusion.20.low), channel_id=1, source_target_pairs={{0,4},{1,3},{2,6},{3,1},{4,0},{5,7},{6,2},{7,5},{8,12},{9,11},{10,... | collective-permute-start | bytes 3538952 | tf_op jit(solution)/shard_map/ppermute | solution.py:266
  78.3 26.8 %collective-permute-start.7 = (bf16[8,48,1664]{2,1,0:T(8,128)(2,1)}, bf16[8,48,1664]{2,1,0:T(8,128)(2,1)}, u32[]{:S(2)}, u32[]{:S(2)}) collective-permute-start(bf16[8,48,1664]{2,1,0:T(8,128)(2,1)} %collective-permute-done.5.high), channel_id=1, source_target_pairs={{0,1},{1,0},{2,3},{3,2},{4,5},{5,4},{6,7},{7,6},{8,9},{9,8},{10,11... | collective-permute-start | bytes 3833864 | tf_op jit(solution)/shard_map/ppermute | solution.py:266
  78.3 47.0 %collective-permute-start.13 = (bf16[8,48,1536]{2,1,0:T(8,128)(2,1)S(1)}, bf16[8,48,1536]{2,1,0:T(8,128)(2,1)}, u32[]{:S(2)}, u32[]{:S(2)}) collective-permute-start(bf16[8,48,1536]{2,1,0:T(8,128)(2,1)S(1)} %constant_dynamic-update-slice_fusion.15.low), channel_id=1, source_target_pairs={{0,1},{1,0},{2,3},{3,2},{4,5},{5,4},{6,7},{7,6},{8,9},{9,8},{10,11... | collective-permute-start | bytes 3538952 | tf_op jit(solution)/shard_map/ppermute | solution.py:266
  90.9 34.3 %collective-permute-start.14 = (bf16[8,48,1536]{2,1,0:T(8,128)(2,1)}, bf16[8,48,1536]{2,1,0:T(8,128)(2,1)}, u32[]{:S(2)}, u32[]{:S(2)}) collective-permute-start(bf16[8,48,1536]{2,1,0:T(8,128)(2,1)} %collective-permute-done.12.high), channel_id=1, source_target_pairs={{0,1},{1,0},{2,3},{3,2},{4,5},{5,4},{6,7},{7,6},{8,9},{9,8},{10,11... | collective-permute-start | bytes 3538952 | tf_op jit(solution)/shard_map/ppermute | solution.py:266
  103.6 41.1 %collective-permute-start.20 = (bf16[8,96,768]{2,1,0:T(8,128)(2,1)S(1)}, bf16[8,96,768]{2,1,0:T(8,128)(2,1)}, u32[]{:S(2)}, u32[]{:S(2)}) collective-permute-start(bf16[8,96,768]{2,1,0:T(8,128)(2,1)S(1)} %constant_dynamic-update-slice_fusion.20.low), channel_id=1, source_target_pairs={{0,1},{1,0},{2,3},{3,2},{4,5},{5,4},{6,7},{7,6},{8,9},{9,8},{10,11... | collective-permute-start | bytes 3538952 | tf_op jit(solution)/shard_map/ppermute | solution.py:266
  103.6 41.1 %collective-permute-start.21 = (bf16[8,96,768]{2,1,0:T(8,128)(2,1)}, bf16[8,96,768]{2,1,0:T(8,128)(2,1)}, u32[]{:S(2)}, u32[]{:S(2)}) collective-permute-start(bf16[8,96,768]{2,1,0:T(8,128)(2,1)} %collective-permute-done.19.high), channel_id=1, source_target_pairs={{0,1},{1,0},{2,3},{3,2},{4,5},{5,4},{6,7},{7,6},{8,9},{9,8},{10,11... | collective-permute-start | bytes 3538952 | tf_op jit(solution)/shard_map/ppermute | solution.py:266
  165.7 18.2 %collective-permute-start.39 = (bf16[512,1536]{1,0:T(8,128)(2,1)}, bf16[512,1536]{1,0:T(8,128)(2,1)S(1)}, u32[]{:S(2)}, u32[]{:S(2)}) collective-permute-start(bf16[512,1536]{1,0:T(8,128)(2,1)} %get-tuple-element.122), channel_id=1, source_target_pairs={{0,1},{1,0},{2,3},{3,2},{4,5},{5,4},{6,7},{7,6},{8,9},{9,8},{10,11... | collective-permute-start | bytes 4718600 | tf_op jit(solution)/shard_map/ppermute | solution.py:266
  165.8 27.7 %collective-permute-start.46 = (bf16[16,96,512]{2,1,0:T(8,128)(2,1)S(1)}, bf16[16,96,512]{2,1,0:T(8,128)(2,1)S(1)}, u32[]{:S(2)}, u32[]{:S(2)}) collective-permute-start(bf16[16,96,512]{2,1,0:T(8,128)(2,1)S(1)} %copy-done.33), channel_id=1, source_target_pairs={{0,1},{1,0},{2,3},{3,2},{4,5},{5,4},{6,7},{7,6},{8,9},{9,8},{10,11... | collective-permute-start | bytes 4718600 | tf_op jit(solution)/shard_map/ppermute | solution.py:266
  166.2 17.1 %collective-permute-start.38 = (bf16[512,768]{1,0:T(8,128)(2,1)S(1)}, bf16[512,768]{1,0:T(8,128)(2,1)}, u32[]{:S(2)}, u32[]{:S(2)}) collective-permute-start(bf16[512,768]{1,0:T(8,128)(2,1)S(1)} %copy-done.37), channel_id=1, source_target_pairs={{0,1},{1,0},{2,3},{3,2},{4,5},{5,4},{6,7},{7,6},{8,9},{9,8},{10,11... | collective-permute-start | bytes 2359304 | tf_op jit(solution)/shard_map/ppermute | solution.py:266
  182.9 21.9 %collective-permute-start.23 = (bf16[3,512,384]{2,1,0:T(8,128)(2,1)}, bf16[3,512,384]{2,1,0:T(8,128)(2,1)S(1)}, u32[]{:S(2)}, u32[]{:S(2)}) collective-permute-start(bf16[3,512,384]{2,1,0:T(8,128)(2,1)} %get-tuple-element.91.theirs), channel_id=1, source_target_pairs={{0,1},{1,0},{2,3},{3,2},{4,5},{5,4},{6,7},{7,6},{8,9},{9,8},{10,11... | collective-permute-start | bytes 3538952 | tf_op jit(solution)/shard_map/ppermute | solution.py:266
  183.4 21.4 %collective-permute-start.22 = (bf16[512,768]{1,0:T(8,128)(2,1)}, bf16[512,768]{1,0:T(8,128)(2,1)}, u32[]{:S(2)}, u32[]{:S(2)}) collective-permute-start(bf16[512,768]{1,0:T(8,128)(2,1)} %get-tuple-element.94.left), channel_id=1, source_target_pairs={{0,1},{1,0},{2,3},{3,2},{4,5},{5,4},{6,7},{7,6},{8,9},{9,8},{10,11... | collective-permute-start | bytes 2359304 | tf_op jit(solution)/shard_map/ppermute | solution.py:266
  192.8 35.0 %collective-permute-start.40 = (bf16[8,48,1536]{2,1,0:T(8,128)(2,1)}, bf16[8,48,1536]{2,1,0:T(8,128)(2,1)S(1)}, u32[]{:S(2)}, u32[]{:S(2)}) collective-permute-start(bf16[8,48,1536]{2,1,0:T(8,128)(2,1)} %get-tuple-element.124), channel_id=1, source_target_pairs={{0,4},{1,3},{2,6},{3,1},{4,0},{5,7},{6,2},{7,5},{8,12},{9,11},{10,... | collective-permute-start | bytes 3538952 | tf_op jit(solution)/shard_map/ppermute | solution.py:266
  203.5 30.4 %collective-permute-start.48 = (bf16[8,96,768]{2,1,0:T(8,128)(2,1)}, bf16[8,96,768]{2,1,0:T(8,128)(2,1)S(1)}, u32[]{:S(2)}, u32[]{:S(2)}) collective-permute-start(bf16[8,96,768]{2,1,0:T(8,128)(2,1)} %get-tuple-element.139), channel_id=1, source_target_pairs={{0,4},{1,3},{2,6},{3,1},{4,0},{5,7},{6,2},{7,5},{8,12},{9,11},{10,... | collective-permute-start | bytes 3538952 | tf_op jit(solution)/shard_map/ppermute | solution.py:266
  204.8 17.6 %collective-permute-start.30 = (bf16[512,768]{1,0:T(8,128)(2,1)S(1)}, bf16[512,768]{1,0:T(8,128)(2,1)S(1)}, u32[]{:S(2)}, u32[]{:S(2)}) collective-permute-start(bf16[512,768]{1,0:T(8,128)(2,1)S(1)} %copy-done.4), channel_id=1, source_target_pairs={{0,1},{1,0},{2,3},{3,2},{4,5},{5,4},{6,7},{7,6},{8,9},{9,8},{10,11... | collective-permute-start | bytes 2359304 | tf_op jit(solution)/shard_map/ppermute | solution.py:266
  212.6 27.2 %collective-permute-start.24 = (bf16[8,48,1152]{2,1,0:T(8,128)(2,1)}, bf16[8,48,1152]{2,1,0:T(8,128)(2,1)S(1)}, u32[]{:S(2)}, u32[]{:S(2)}) collective-permute-start(bf16[8,48,1152]{2,1,0:T(8,128)(2,1)} %get-tuple-element.96), channel_id=1, source_target_pairs={{0,4},{1,3},{2,6},{3,1},{4,0},{5,7},{6,2},{7,5},{8,12},{9,11},{10,... | collective-permute-start | bytes 2654216 | tf_op jit(solution)/shard_map/ppermute | solution.py:266
  227.1 18.7 %collective-permute-start.32 = (bf16[8,64,384]{2,1,0:T(8,128)(2,1)}, bf16[8,64,384]{2,1,0:T(8,128)(2,1)S(1)}, u32[]{:S(2)}, u32[]{:S(2)}) collective-permute-start(bf16[8,64,384]{2,1,0:T(8,128)(2,1)} %get-tuple-element.111), channel_id=1, source_target_pairs={{0,4},{1,3},{2,6},{3,1},{4,0},{5,7},{6,2},{7,5},{8,12},{9,11},{10,... | collective-permute-start | bytes 1179656 | tf_op jit(solution)/shard_map/ppermute | solution.py:266
  232.7 34.1 %collective-permute-start.41 = (bf16[4,48,1536]{2,1,0:T(8,128)(2,1)}, bf16[4,48,1536]{2,1,0:T(8,128)(2,1)S(1)}, u32[]{:S(2)}, u32[]{:S(2)}) collective-permute-start(bf16[4,48,1536]{2,1,0:T(8,128)(2,1)} %get-tuple-element.126), channel_id=1, source_target_pairs={{0,2},{1,5},{2,0},{3,7},{4,6},{5,1},{6,4},{7,3},{8,10},{9,13},{10,... | collective-permute-start | bytes 1769480 | tf_op jit(solution)/shard_map/ppermute | solution.py:266
  239.0 36.2 %collective-permute-start.49 = (bf16[4,96,768]{2,1,0:T(8,128)(2,1)}, bf16[4,96,768]{2,1,0:T(8,128)(2,1)S(1)}, u32[]{:S(2)}, u32[]{:S(2)}) collective-permute-start(bf16[4,96,768]{2,1,0:T(8,128)(2,1)} %get-tuple-element.141), channel_id=1, source_target_pairs={{0,2},{1,5},{2,0},{3,7},{4,6},{5,1},{6,4},{7,3},{8,10},{9,13},{10,... | collective-permute-start | bytes 1769480 | tf_op jit(solution)/shard_map/ppermute | solution.py:266
  256.8 23.2 %collective-permute-start.26 = (bf16[48,1152]{1,0:T(8,128)(2,1)}, bf16[48,1152]{1,0:T(8,128)(2,1)S(1)}, u32[]{:S(2)}, u32[]{:S(2)}) collective-permute-start(bf16[48,1152]{1,0:T(8,128)(2,1)} %get-tuple-element.100), channel_id=1, source_target_pairs={{0,8},{1,9},{2,10},{3,11},{4,12},{5,13},{6,14},{7,15},{8,0},{9,1},... | collective-permute-start | bytes 331784 | tf_op jit(solution)/shard_map/ppermute | solution.py:266
  261.9 18.1 %collective-permute-start.27 = (bf16[48,1152]{1,0:T(8,128)(2,1)}, bf16[48,1152]{1,0:T(8,128)(2,1)S(1)}, u32[]{:S(2)}, u32[]{:S(2)}) collective-permute-start(bf16[48,1152]{1,0:T(8,128)(2,1)} %get-tuple-element.101), channel_id=1, source_target_pairs={{0,16},{1,17},{2,18},{3,19},{4,20},{5,21},{6,22},{7,23},{8,24},{9,... | collective-permute-start | bytes 331784 | tf_op jit(solution)/shard_map/ppermute | solution.py:266
  273.2 19.3 %collective-permute-start.42 = (bf16[48,1536]{1,0:T(8,128)(2,1)}, bf16[48,1536]{1,0:T(8,128)(2,1)S(1)}, u32[]{:S(2)}, u32[]{:S(2)}) collective-permute-start(bf16[48,1536]{1,0:T(8,128)(2,1)} %get-tuple-element.128), channel_id=1, source_target_pairs={{0,8},{1,9},{2,10},{3,11},{4,12},{5,13},{6,14},{7,15},{8,0},{9,1},... | collective-permute-start | bytes 442376 | tf_op jit(solution)/shard_map/ppermute | solution.py:266
  273.2 19.3 %collective-permute-start.43 = (bf16[48,1536]{1,0:T(8,128)(2,1)}, bf16[48,1536]{1,0:T(8,128)(2,1)S(1)}, u32[]{:S(2)}, u32[]{:S(2)}) collective-permute-start(bf16[48,1536]{1,0:T(8,128)(2,1)} %get-tuple-element.129), channel_id=1, source_target_pairs={{0,16},{1,17},{2,18},{3,19},{4,20},{5,21},{6,22},{7,23},{8,24},{9,... | collective-permute-start | bytes 442376 | tf_op jit(solution)/shard_map/ppermute | solution.py:266
  275.2 21.2 %collective-permute-start.44 = (bf16[48,1536]{1,0:T(8,128)(2,1)}, bf16[48,1536]{1,0:T(8,128)(2,1)S(1)}, u32[]{:S(2)}, u32[]{:S(2)}) collective-permute-start(bf16[48,1536]{1,0:T(8,128)(2,1)} %get-tuple-element.130), channel_id=1, source_target_pairs={{0,24},{1,25},{2,26},{3,27},{4,28},{5,29},{6,30},{7,31},{8,16},{9,... | collective-permute-start | bytes 442376 | tf_op jit(solution)/shard_map/ppermute | solution.py:266
  279.9 19.9 %collective-permute-start.50 = (bf16[96,768]{1,0:T(8,128)(2,1)}, bf16[96,768]{1,0:T(8,128)(2,1)S(1)}, u32[]{:S(2)}, u32[]{:S(2)}) collective-permute-start(bf16[96,768]{1,0:T(8,128)(2,1)} %get-tuple-element.143), channel_id=1, source_target_pairs={{0,8},{1,9},{2,10},{3,11},{4,12},{5,13},{6,14},{7,15},{8,0},{9,1},... | collective-permute-start | bytes 442376 | tf_op jit(solution)/shard_map/ppermute | solution.py:266
  290.0 20.6 %collective-permute-start.37 = (f32[40,384]{1,0:T(8,128)}, f32[40,384]{1,0:T(8,128)S(1)}, u32[]{:S(2)}, u32[]{:S(2)}) collective-permute-start(f32[40,384]{1,0:T(8,128)} %get-tuple-element.119), channel_id=1, source_target_pairs={{0,1},{1,0},{2,3},{3,2},{4,5},{5,4},{6,7},{7,6},{8,9},{9,8},{10,11... | collective-permute-start | bytes 184328 | tf_op jit(solution)/shard_map/ppermute | solution.py:266
  292.5 18.1 %collective-permute-start.29 = (f32[24,1152]{1,0:T(8,128)}, f32[24,1152]{1,0:T(8,128)S(1)}, u32[]{:S(2)}, u32[]{:S(2)}) collective-permute-start(f32[24,1152]{1,0:T(8,128)} %get-tuple-element.104), channel_id=1, source_target_pairs={{0,1},{1,0},{2,3},{3,2},{4,5},{5,4},{6,7},{7,6},{8,9},{9,8},{10,11... | collective-permute-start | bytes 331784 | tf_op jit(solution)/shard_map/ppermute | solution.py:266
  (61 other events, 552.6 us)

commit v2 on v1

--- a/solution.py
+++ b/solution.py
@@ -243,7 +243,7 @@
 BOTH_LAST = (((1,), (1,)), ((), ()))
 SMEM = pl.BlockSpec(memory_space=pltpu.SMEM)
 ANY = pl.BlockSpec(memory_space=pl.ANY)
-CORE, LENGTH = 32, 33
+CORE, LENGTH, PLACE, PLACE_O = 32, 33, 34, 50
 
 
 def pairs(move):
@@ -277,23 +277,22 @@
             z, first, second = j % 4, (j // 4) % 2, j // 8
             mask = jnp.where(of_core == 0, first + 2 * second, second + 2 * first)
             places.append(jnp.bitwise_xor(chip, mask + 4 * z))
-    return jnp.stack(places + [core, length]).astype(jnp.int32)
-
-
-def spread(piece):
-    near = [send(piece, along_z(s)) for s in (1, 2, 3)]
-    zs = jnp.stack([piece] + near)
-    low = jnp.concatenate([zs, send(zs, first_way)])
-    high = send(low, second_way)
-    return low, high, swap(low), swap(high)
+    spots = []
+    for of_core in (core, 1 - core):
+        for k in range(16):
+            mask = jnp.bitwise_xor(chip, k)
+            x, y, z = mask & 1, (mask >> 1) & 1, mask >> 2
+            spots.append(z + jnp.where(of_core == 0, 4 * x + 8 * y, 4 * y + 8 * x))
+    return jnp.stack(places + [core, length] + spots).astype(jnp.int32)
 
 
 def params():
     return pltpu.CompilerParams(vmem_limit_bytes=VMEM_LIMIT)
 
 
-def cost(flops, nbytes, exps=0):
-    return pl.CostEstimate(flops=flops, bytes_accessed=nbytes, transcendentals=exps)
+def cost(micros):
+    flops = int(micros * (3e10 if micros > 3 else 1e9))
+    return pl.CostEstimate(flops=flops, bytes_accessed=1, transcendentals=0)
 
 
 def shape(dims, dtype):
@@ -340,44 +339,173 @@
     )
 
 
-def enter_kernel(info, tokens, low, high, low_o, high_o, weights, vecs, first, joint, sems):
+def halves_kernel(info, qkv, proj, up, mine, theirs):
+    feat = proj.shape[1]
+    third, wide = feat // 2, up.shape[1] // 2
+
+    def lay(out, h):
+        for i in range(3):
+            cols = slice(i * feat + h * third, i * feat + (h + 1) * third)
+            out[:, i * third : (i + 1) * third] = qkv[:, cols]
+        out[:, 3 * third : 3 * third + wide] = up[:, h * wide : (h + 1) * wide]
+        out[:, 3 * third + wide :] = proj[:, h * third : (h + 1) * third]
+
+    @pl.when(info[CORE] == 0)
+    def _():
+        lay(mine, 0)
+        lay(theirs, 1)
+
+    @pl.when(info[CORE] == 1)
+    def _():
+        lay(mine, 1)
+        lay(theirs, 0)
+
+
+def halves(info, qkv, proj, up):
+    rows = qkv.shape[0]
+    width = (qkv.shape[1] + proj.shape[1] + up.shape[1]) // 2
+    vmem = pl.BlockSpec(memory_space=pltpu.VMEM)
+    out = shape((rows, width), BF16)
+    return pl.pallas_call(
+        halves_kernel,
+        out_shape=(out, out),
+        in_specs=[SMEM] + [vmem] * 3,
+        out_specs=(vmem, vmem),
+        compiler_params=params(),
+        name="halves",
+        cost_estimate=cost(2),
+    )(info, qkv, proj, up)
+
+
+def pieces_kernel(info, mine, given, small, one, two):
+    ours, others = mine[...].astype(F32), given[...].astype(F32)
+    few = small[...].astype(F32)
+    none = jnp.zeros_like(few)
+    first = info[CORE] == 0
+
+    def stack(a, b):
+        return jnp.concatenate([jnp.where(first, a, b), jnp.where(first, b, a)]).astype(BF16)
+
+    split = one.shape[2] - few.shape[1]
+    one[0, :, :split] = stack(ours[:, :split], others[:, :split])
+    one[0, :, split:] = stack(few, none)
+    two[0] = stack(ours[:, split:], others[:, split:])
+
+
+def pieces_of(info, mine, given, small, split):
+    rows, width = mine.shape
+    one = split + small.shape[1]
+    vmem = pl.BlockSpec(memory_space=pltpu.VMEM)
+    return pl.pallas_call(
+        pieces_kernel,
+        out_shape=(shape((1, 2 * rows, one), BF16), shape((1, 2 * rows, width - split), BF16)),
+        in_specs=[SMEM, vmem, vmem, vmem],
+        out_specs=(vmem, vmem),
+        compiler_params=params(),
+        name="pieces_of",
+        cost_estimate=cost(2),
+    )(info, mine, given, small)
+
+
+def gather_kernel(n_in, n_held, *refs):
+    parts = refs[:n_in]
+    out = refs[n_in + n_held]
+    at = 0
+    for part in parts:
+        out[at : at + part.shape[0]] = part[...]
+        at += part.shape[0]
+
+
+def gather(parts, held=(), behind=()):
+    vmem = pl.BlockSpec(memory_space=pltpu.VMEM)
+    _, rows, cols = parts[0].shape
+    count = sum(part.shape[0] for part in parts)
+    n, n_held = len(parts), len(held)
+    return pl.pallas_call(
+        partial(gather_kernel, n, n_held + len(behind)),
+        out_shape=(shape((count, rows, cols), BF16),) + tuple(shape(h.shape, h.dtype) for h in held),
+        in_specs=[vmem] * n + [ANY] * (n_held + len(behind)),
+        out_specs=(vmem,) + (ANY,) * n_held,
+        input_output_aliases={n + i: 1 + i for i in range(n_held)},
+        compiler_params=params(),
+        name="gather",
+        cost_estimate=cost(2),
+    )(*parts, *held, *behind)
+
+
+def gate_kernel(array, behind, out):
+    pass
+
+
+def gate(array, behind):
+    return pl.pallas_call(
+        gate_kernel,
+        out_shape=shape(array.shape, array.dtype),
+        in_specs=[ANY, ANY],
+        out_specs=ANY,
+        input_output_aliases={0: 0},
+        compiler_params=params(),
+        name="gate",
+        cost_estimate=cost(1),
+    )(array, behind)
+
+
+def near_z(piece, steps):
+    return [send(piece, along_z(s)) for s in steps]
+
+
+def enter_kernel(
+    info, tokens, low, high, low_o, high_o, kept, vecs, first, flipped, joint, weights, sems, sem
+):
     feat = tokens.shape[1]
     third = feat // 2
     copies = fetch(info, (low, high, low_o, high_o), weights, sems, True)
     normed, _ = centre(tokens[...].astype(F32))
     for copy in copies:
         copy.wait()
-    width = weights.shape[-1]
-    small = weights[0, :, :, width - 128 :].reshape(feat, 128).astype(F32).T
+    out = pltpu.make_async_copy(weights, kept, sem)
+    out.start()
+    split = 3 * third
+    small = weights[0, :, :, split:] + weights[1, :, :, split:]
+    small = small.reshape(feat, 128).astype(F32).T
     vecs[...] = small[:8]
     low_first = (normed * small[0:1] + small[2:3]).astype(BF16)
     first[...] = low_first
+    flipped[...] = low_first.T.reshape(flipped.shape)
     for h in (0, 1):
-        for part in range(3):
-            w = weights[h, :, :, part * third : (part + 1) * third].reshape(feat, third)
-            out = dot(low_first, w)
-            if part != 1:
-                row = 3 if part == 0 else 4
-                out = out + small[row : row + 1, h * third : (h + 1) * third]
-            joint[h, :, part * third : (part + 1) * third] = out.astype(BF16)
+        cols = slice(h * third, (h + 1) * third)
+        bias = jnp.concatenate(
+            [small[3:4, cols], jnp.zeros((1, third), F32), small[4:5, cols]], axis=1
+        )
+        w = weights[h, :, :, :split].reshape(feat, split)
+        joint[h] = (dot(low_first, w) + bias).astype(BF16)
+    out.wait()
 
 
 def enter(info, tokens, pieces):
     rows, feat = tokens.shape
     width = pieces[0].shape[-1]
+    vmem = pl.BlockSpec(memory_space=pltpu.VMEM)
+    sets = (2, 16, feat // 16, width)
     return pl.pallas_call(
         enter_kernel,
         out_shape=(
-            shape((2, 16, feat // 16, width), BF16),
+            shape(sets, BF16),
             shape((8, feat), F32),
             shape((rows, feat), BF16),
+            shape((16, feat // 16, rows), BF16),
             shape((2, rows, 3 * feat // 2), BF16),
         ),
-        in_specs=[SMEM, pl.BlockSpec(memory_space=pltpu.VMEM)] + [ANY] * 4,
-        out_specs=tuple([pl.BlockSpec(memory_space=pltpu.VMEM)] * 4),
-        scratch_shapes=[pltpu.SemaphoreType.DMA((32,))],
-        compiler_params=params(),
-        cost_estimate=cost(6 * rows * feat * feat, 8 * feat * width + 10 * rows * feat),
+        in_specs=[SMEM, vmem] + [ANY] * 4,
+        out_specs=(ANY, vmem, vmem, vmem, vmem),
+        scratch_shapes=[
+            pltpu.VMEM(sets, BF16),
+            pltpu.SemaphoreType.DMA((32,)),
+            pltpu.SemaphoreType.DMA,
+        ],
+        compiler_params=params(),
+        name="enter",
+        cost_estimate=cost(8),
     )(info, tokens, *pieces)
 
 
@@ -387,7 +515,7 @@
     return jnp.where(place < info[LENGTH], raw, NEG)
 
 
-def mix_kernel(info, q, k, v, mixed, stats):
+def mix_kernel(info, q, k, v, _, mixed, flipped, stats):
     head = q.shape[-1] // 2
     scale = head**-0.5
     turned = v[0].T
@@ -401,10 +529,12 @@
         attn = (expd * (1.0 / total)).astype(BF16)
         stats[0, h : h + 1] = most + jnp.log(total)
         outs.append(dot(turned[cols], attn))
-    mixed[...] = jnp.concatenate(outs).T.astype(BF16)
-
-
-def mix(info, joint):
+    both = jnp.concatenate(outs)
+    flipped[...] = both.astype(BF16)
+    mixed[...] = both.T.astype(BF16)
+
+
+def mix(info, joint, behind):
     _, rows, width = joint.shape
     feat, pair = 2 * width // 3, 2 * width // 3 // HEADS * 2
     per = feat // 2 // pair
@@ -416,18 +546,24 @@
     return pl.pallas_call(
         mix_kernel,
         grid=(n,),
-        out_shape=(shape((rows, feat), BF16), shape((n, 8, rows), F32)),
-        in_specs=[SMEM] + spec,
+        out_shape=(
+            shape((rows, feat), BF16),
+            shape((feat, rows), BF16),
+            shape((n, 8, rows), F32),
+        ),
+        in_specs=[SMEM] + spec + [ANY],
         out_specs=(
             pl.BlockSpec((rows, pair), lambda i: (0, i)),
+            pl.BlockSpec((pair, rows), lambda i: (i, 0)),
             pl.BlockSpec((1, 8, rows), lambda i: (i, 0, 0)),
         ),
         compiler_params=params(),
-        cost_estimate=cost(16 * rows * rows * feat, 8 * rows * feat, HEADS * rows * rows),
-    )(info, joint, joint, joint)
-
-
-def mix_back_kernel(info, q, k, v, grad, stats, theirs, mine):
+        name="mix",
+        cost_estimate=cost(10),
+    )(info, joint, joint, joint, behind)
+
+
+def mix_back_kernel(info, q, k, v, grad, stats, _, theirs, mine):
     head = q.shape[-1] // 2
     scale = head**-0.5
     turned = k[0].T
@@ -461,7 +597,7 @@
             mine[part] = out[part]
 
 
-def mix_back(info, joint, grad_mixed, stats):
+def mix_back(info, joint, grad_mixed, stats, behind):
     _, rows, width = joint.shape
     feat, pair = 2 * width // 3, 2 * width // 3 // HEADS * 2
     per = feat // 2 // pair
@@ -488,6 +624,7 @@
                 pl.BlockSpec(
                     (1, 8, rows), lambda i, info: (half(i, info) * per + i % per, 0, 0)
                 ),
+                ANY,
             ],
             out_specs=(
                 pl.BlockSpec((3, rows, pair), lambda i, info: (0, 0, jnp.minimum(i, per - 1))),
@@ -496,20 +633,23 @@
         ),
         out_shape=(out, out),
         compiler_params=params(),
-        cost_estimate=cost(40 * rows * rows * feat, 16 * rows * feat, HEADS * rows * rows),
-    )(info, joint, joint, joint, grad_mixed, stats)
+        name="mix_back",
+        cost_estimate=cost(16),
+    )(info, joint, joint, joint, grad_mixed, stats, behind)
 
 
 GELU = (0.254829592, -0.284496736, 1.421413741, -1.453152027, 1.061405429)
 
 
 def gelu_parts(x):
-    bell = jnp.exp(-0.5 * x * x)
-    t = 1.0 / (1.0 + (0.3275911 * 0.5**0.5) * jnp.abs(x))
-    poly = GELU[4]
+    bell = jnp.exp2(x * x * (-0.5 / math.log(2)))
+    below = 1.0 + (0.3275911 * 0.5**0.5) * jnp.abs(x)
+    t = pl.reciprocal(below, approx=True)
+    t = t * (2.0 - below * t)
+    poly = 0.5 * GELU[4]
     for c in GELU[3::-1]:
-        poly = poly * t + c
-    tail = (0.5 * poly) * t * bell
+        poly = poly * t + 0.5 * c
+    tail = poly * t * bell
     phi = jnp.where(x < 0, tail, 1.0 - tail)
     return x * phi, phi + x * (bell * (2 * math.pi) ** -0.5)
 
@@ -518,39 +658,52 @@
     info,
     tokens,
     mixed,
-    proj,
     vecs,
     bias,
     low,
     high,
     low_o,
     high_o,
-    weights,
+    _,
+    kept,
     after,
     second,
+    flipped,
     active,
     slope,
     mine,
     theirs,
+    weights,
     turned,
     sems,
+    block_sems,
+    sem,
 ):
-    step = pl.program_id(0)
+    step, steps = pl.program_id(0), pl.num_programs(0)
+    core = info[CORE]
     feat = tokens.shape[1]
     tile = active.shape[1]
-    per = weights.shape[-1] // tile
+    wide = weights.shape[-1] - feat // 2
+    per = wide // tile
     rows = mine.shape[1]
+    count = tile // rows
+    keeping = pltpu.make_async_copy(weights, kept, sem)
 
     @pl.when(step == 0)
     def _():
         copies = fetch(info, (low, high, low_o, high_o), weights, sems, True)
-        grown = [dot(mixed[...], proj[h]) for h in (0, 1)]
+        for copy in copies:
+            copy.wait()
+        keeping.start()
+        grown = [
+            dot(mixed[...], weights[h, :, :, wide:].reshape(feat, feat // 2)) for h in (0, 1)
+        ]
         total = tokens[...].astype(F32) + jnp.concatenate(grown, axis=1) + vecs[5:6]
         after[...] = total
         normed, _ = centre(total)
-        second[...] = (normed * vecs[1:2] + vecs[6:7]).astype(BF16)
-        for copy in copies:
-            copy.wait()
+        value = (normed * vecs[1:2] + vecs[6:7]).astype(BF16)
+        second[...] = value
+        flipped[...] = value.T.reshape(flipped.shape)
 
     cols = pl.ds(pl.multiple_of(lax.rem(step, per) * tile, tile), tile)
     w = weights[step // per, :, :, cols].reshape(feat, tile)
@@ -559,30 +712,44 @@
     value = value.astype(BF16)
     active[...] = value
     slope[...] = grad.astype(BF16)
-    count = tile // rows
     turned[pl.ds(step * count, count)] = value.T.reshape(count, rows, -1)
-
-    @pl.when(step == pl.num_programs(0) - 1)
-    def _():
-        core = info[CORE]
-        for j in range(16):
-            mine[j] = turned[2 * info[j] + core]
-            theirs[j] = turned[2 * info[16 + j] + 1 - core]
-
-
-def rise(info, tokens, mixed, first_set, vecs, bias, pieces):
+    for i in range(count):
+        at = step * count + i
+        chip = step * (count // 2) + i // 2
+
+        @pl.when(core == i % 2)
+        def _():
+            dst = mine.at[info[PLACE + chip]]
+            pltpu.make_async_copy(turned.at[at], dst, block_sems.at[at]).start()
+
+        @pl.when(core != i % 2)
+        def _():
+            dst = theirs.at[info[PLACE_O + chip]]
+            pltpu.make_async_copy(turned.at[at], dst, block_sems.at[at]).start()
+
+    @pl.when(step == steps - 1)
+    def _():
+        for at in range(turned.shape[0]):
+            pltpu.make_async_copy(turned.at[at], mine.at[0], block_sems.at[at]).wait()
+        keeping.wait()
+
+
+def rise(info, tokens, mixed, vecs, bias, pieces, behind):
     rows, feat = tokens.shape
     width = pieces[0].shape[-1]
-    hidden = 2 * width
-    tile, block = 384, hidden // 32
+    hidden = 2 * width - feat
+    tile, block = 768, hidden // 32
     turned = shape((16, block, rows), BF16)
+    sets = (2, 16, feat // 16, width)
+    strip = pl.BlockSpec((rows, tile), lambda n: (0, n))
     return pl.pallas_call(
         rise_kernel,
         grid=(hidden // tile,),
         out_shape=(
-            shape((2, 16, feat // 16, width), BF16),
+            shape(sets, BF16),
             shape((rows, feat), F32),
             shape((rows, feat), BF16),
+            shape((16, feat // 16, rows), BF16),
             shape((rows, hidden), BF16),
             shape((rows, hidden), BF16),
             turned,
@@ -592,50 +759,71 @@
             SMEM,
             full((rows, feat)),
             full((rows, feat)),
-            pl.BlockSpec((2, feat, feat // 2), lambda n: (0, 0, 3)),
             full((8, feat)),
             pl.BlockSpec((1, tile), lambda n: (0, n)),
         ]
-        + [ANY] * 4,
+        + [ANY] * 5,
         out_specs=(
-            full((2, 16, feat // 16, width)),
+            ANY,
             full((rows, feat)),
             full((rows, feat)),
-            pl.BlockSpec((rows, tile), lambda n: (0, n)),
-            pl.BlockSpec((rows, tile), lambda n: (0, n)),
-            full(turned.shape),
-            full(turned.shape),
+            full((16, feat // 16, rows)),
+            strip,
+            strip,
+            ANY,
+            ANY,
         ),
-        scratch_shapes=[pltpu.VMEM((32, block, rows), BF16), pltpu.SemaphoreType.DMA((32,))],
-        compiler_params=params(),
-        cost_estimate=cost(
-            2 * rows * feat * (feat + hidden), 8 * feat * hidden, rows * hidden
-        ),
-    )(info, tokens, mixed, first_set, vecs, bias, *pieces)
-
-
-def leave_kernel(after, active, down, vecs, output):
-    output[...] = (after[...] + dot(active[...], down[...]) + vecs[7:8]).astype(BF16)
-
-
-def leave(after, active, down, vecs):
+        scratch_shapes=[
+            pltpu.VMEM(sets, BF16),
+            pltpu.VMEM((32, block, rows), BF16),
+            pltpu.SemaphoreType.DMA((32,)),
+            pltpu.SemaphoreType.DMA((32,)),
+            pltpu.SemaphoreType.DMA,
+        ],
+        compiler_params=params(),
+        name="rise",
+        cost_estimate=cost(18),
+    )(info, tokens, mixed, vecs, bias, *pieces, behind)
+
+
+def leave_kernel(after, active, down, vecs, _, output, total):
+    step = pl.program_id(0)
+    part = dot(active[...], down[...])
+
+    @pl.when(step == 0)
+    def _():
+        total[...] = after[...] + vecs[7:8] + part
+
+    @pl.when(step > 0)
+    def _():
+        total[...] += part
+
+    @pl.when(step == pl.num_programs(0) - 1)
+    def _():
+        output[...] = total[...].astype(BF16)
+
+
+def leave(after, active, down, vecs, behind):
     rows, feat = after.shape
     hidden = active.shape[1]
-    tile = 384
+    tile = 768
     return pl.pallas_call(
         leave_kernel,
-        grid=(feat // tile,),
+        grid=(hidden // tile,),
         out_shape=shape((rows, feat), BF16),
         in_specs=[
+            full((rows, feat)),
             pl.BlockSpec((rows, tile), lambda n: (0, n)),
-            full((rows, hidden)),
-            pl.BlockSpec((hidden, tile), lambda n: (0, n)),
-            pl.BlockSpec((8, tile), lambda n: (0, n)),
+            pl.BlockSpec((tile, feat), lambda n: (n, 0)),
+            full((8, feat)),
+            ANY,
         ],
-        out_specs=pl.BlockSpec((rows, tile), lambda n: (0, n)),
-        compiler_params=params(),
-        cost_estimate=cost(2 * rows * feat * hidden, 2 * hidden * (rows + feat)),
-    )(after, active, down, vecs)
+        out_specs=full((rows, feat)),
+        scratch_shapes=[pltpu.VMEM((rows, feat), F32)],
+        compiler_params=params(),
+        name="leave",
+        cost_estimate=cost(7),
+    )(after, active, down, vecs, behind)
 
 
 def fall_kernel(
@@ -650,7 +838,7 @@
     high,
     low_o,
     high_o,
-    weights,
+    kept,
     theirs,
     mine,
     bias_sum,
@@ -659,24 +847,29 @@
     attn_mine,
     grad_mixed,
     sums,
+    weights,
     grad_second,
     sems,
+    sem,
 ):
     step, steps = pl.program_id(0), pl.num_programs(0)
     core = info[CORE]
     feat = grad_y.shape[1]
     tile = slope.shape[1]
     per = steps // 2
+    keeping = pltpu.make_async_copy(weights, kept, sem)
 
     @pl.when(step == 0)
     def _():
         for copy in fetch(info, (low, high, low_o, high_o), weights, sems, False):
             copy.wait()
+        keeping.start()
         grad_second[...] = jnp.zeros_like(grad_second)
 
     half = jnp.where(step < per, 1 - core, core)
     at = half * per + lax.rem(step, per)
-    down = weights[pl.ds(2 * at, 2)].reshape(tile, feat)
+    count = tile * weights.shape[0] // (steps * tile)
+    down = weights[pl.ds(count * at, count)].reshape(tile, feat)
     grad = (dot_last(grad_y[...], down) * slope[...].astype(F32)).astype(BF16)
     bias_sum[...] = jnp.sum(grad.astype(F32), axis=0, keepdims=True)
     grad_second[...] += dot_last(grad, up[0])
@@ -706,12 +899,13 @@
         attn_mine[...] = jnp.where(core == 0, left, right)
         attn_theirs[...] = jnp.where(core == 0, right, left)
         grad_mixed[...] = (dot_last(left, proj[0]) + dot_last(right, proj[1])).astype(BF16)
-
-
-def fall(info, grad_y, slope, up_set, after, vecs, first_set, pieces):
+        keeping.wait()
+
+
+def fall(info, grad_y, slope, up_set, after, vecs, pieces):
     rows, feat = grad_y.shape
     hidden = slope.shape[1]
-    tile = 384
+    tile = 768
     steps = hidden // tile
     per = steps // 2
 
@@ -734,11 +928,11 @@
                 ),
                 whole((rows, feat)),
                 whole((8, feat)),
-                pl.BlockSpec((2, feat, feat // 2), lambda n, info: (0, 0, 3)),
+                pl.BlockSpec((2, feat, feat // 2), lambda n, info: (0, 0, 4)),
             ]
             + [ANY] * 4,
             out_specs=(
-                whole((16, 2, hidden // 32, feat)),
+                ANY,
                 pl.BlockSpec((rows, tile), lambda n, info: (0, jnp.minimum(n, per - 1))),
                 pl.BlockSpec((rows, tile), lambda n, info: (0, jnp.maximum(n - per, 0))),
                 pl.BlockSpec((1, tile), lambda n, info: (0, at(n, info))),
@@ -748,7 +942,12 @@
                 whole((rows, feat)),
                 whole((8, feat)),
             ),
-            scratch_shapes=[pltpu.VMEM((rows, feat), F32), pltpu.SemaphoreType.DMA((32,))],
+            scratch_shapes=[
+                pltpu.VMEM((16, 2, hidden // 32, feat), BF16),
+                pltpu.VMEM((rows, feat), F32),
+                pltpu.SemaphoreType.DMA((32,)),
+                pltpu.SemaphoreType.DMA,
+            ],
         ),
         out_shape=(
             shape((16, 2, hidden // 32, feat), BF16),
@@ -762,13 +961,14 @@
             shape((8, feat), F32),
         ),
         compiler_params=params(),
-        cost_estimate=cost(
-            4 * rows * feat * hidden, 8 * feat * hidden + 8 * rows * hidden
-        ),
-    )(info, grad_y, slope, up_set, after, vecs, first_set, *pieces)
-
-
-def exit_kernel(info, tokens, mine, theirs, weights, grad_after, vecs, grad_tokens, sums, grad_first):
+        name="fall",
+        cost_estimate=cost(18),
+    )(info, grad_y, slope, up_set, after, vecs, up_set, *pieces)
+
+
+def exit_kernel(
+    info, tokens, mine, theirs, weights, grad_after, vecs, _, grad_tokens, sums, grad_first, joint
+):
     step = pl.program_id(0)
     core = info[CORE]
     third = mine.shape[2]
@@ -776,13 +976,11 @@
     spot = pl.ds(pl.multiple_of(half * third, third), third)
 
     def parts(source):
-        total = dot_last(source[0], weights[0, :, :third])
-        for part in (1, 2):
-            cols = slice(part * third, (part + 1) * third)
-            total += dot_last(source[part], weights[0, :, cols])
+        for part in range(3):
+            joint[:, part * third : (part + 1) * third] = source[part]
         sums[2:3, spot] = jnp.sum(source[0].astype(F32), axis=0, keepdims=True)
         sums[3:4, spot] = jnp.sum(source[2].astype(F32), axis=0, keepdims=True)
-        return total
+        return dot_last(joint[...], weights[0])
 
     @pl.when(step == 0)
     def _():
@@ -799,7 +997,7 @@
         grad_tokens[...] = (grad_after[...] + back).astype(BF16)
 
 
-def exit_back(info, tokens, mine, theirs, first_set, grad_after, vecs):
+def exit_back(info, tokens, mine, theirs, first_set, grad_after, vecs, behind):
     rows, feat = tokens.shape
     third = feat // 2
 
@@ -821,169 +1019,166 @@
                 ),
                 whole((rows, feat)),
                 whole((8, feat)),
+                ANY,
             ],
             out_specs=(whole((rows, feat)), whole((8, feat))),
-            scratch_shapes=[pltpu.VMEM((rows, feat), F32)],
+            scratch_shapes=[pltpu.VMEM((rows, feat), F32), pltpu.VMEM((rows, 3 * third), BF16)],
         ),
         out_shape=(shape((rows, feat), BF16), shape((8, feat), F32)),
         compiler_params=params(),
-        cost_estimate=cost(6 * rows * feat * feat, 6 * feat * feat + 12 * rows * feat),
-    )(info, tokens, mine, theirs, first_set, grad_after, vecs)
-
-
-def outer_kernel(info, left, left_o, right, right_o, keep, away, turned, blocks):
-    rows = left.shape[0]
-
-    @pl.when(pl.program_id(0) == 0)
-    def _():
-        turned[:, :rows] = left[...].T
-        turned[:, rows:] = left_o[...].T
-
-    total = dot(turned[:, :rows], right[0]) + dot(turned[:, rows:], right_o[0])
-    blocks[...] = total.reshape(blocks.shape)
-    for j in range(8):
-        keep[j] = blocks[info[j]]
-        away[j] = blocks[info[8 + j]].astype(BF16)
-
-
-def outer(info, left, left_o, right, right_o, tile=384):
-    rows, feat = left.shape
-    n_parts, _, width = right.shape
-    per = width // tile
-    cols = n_parts * width
+        name="exit_back",
+        cost_estimate=cost(8),
+    )(info, tokens, mine, theirs, first_set, grad_after, vecs, behind)
+
+
+def line_up(info, left, left_o, turned):
+    rows = left.shape[2]
+    for chip in range(16):
+        place = info[PLACE + chip]
+        turned[place, :, :rows] = left[chip]
+        turned[place, :, rows:] = left_o[chip]
+
+
+def outer_tile(turned, right, right_o):
+    rows = right.shape[0]
+    both = turned[...].reshape(-1, turned.shape[2])
+    total = dot(both[:, :rows], right) + dot(both[:, rows:], right_o)
+    return total.reshape(16, -1, total.shape[1])
+
+
+def outer_up_kernel(
+    info, left, left_o, right, right_o, low, low_o, attn, attn_o, _, keep, away, turned
+):
+    step, last = pl.program_id(0), pl.num_programs(0) - 1
+
+    @pl.when(step == 0)
+    def _():
+        line_up(info, left, left_o, turned)
+
+    @pl.when(step < last)
+    def _():
+        total = outer_tile(turned, right[...], right_o[...])
+        keep[...] = total[:8]
+        away[...] = total[8:].astype(BF16)
+
+    @pl.when(step == last)
+    def _():
+        line_up(info, low, low_o, turned)
+        total = outer_tile(turned, attn[...], attn_o[...])
+        keep[:, :, : attn.shape[1]] = total[:8]
+        away[:, :, : attn.shape[1]] = total[8:].astype(BF16)
+
+
+def outer_up(info, left, left_o, right, right_o, low, low_o, attn, attn_o, behind):
+    _, block, rows = left.shape
+    tile = 2 * attn.shape[1]
+    n = right.shape[1] // tile
+    cols = right.shape[1] + attn.shape[1]
+    strip = pl.BlockSpec((rows, tile), lambda i: (0, jnp.minimum(i, n - 1)))
+    out = pl.BlockSpec((8, block, tile), lambda i: (0, 0, i))
+    return pl.pallas_call(
+        outer_up_kernel,
+        grid=(n + 1,),
+        out_shape=(shape((8, block, cols), F32), shape((8, block, cols), BF16)),
+        in_specs=[SMEM]
+        + [full(left.shape)] * 2
+        + [strip] * 2
+        + [full(left.shape)] * 2
+        + [full(attn.shape)] * 2
+        + [ANY],
+        out_specs=(out, out),
+        scratch_shapes=[pltpu.VMEM((16, block, 2 * rows), BF16)],
+        compiler_params=params(),
+        name="outer_up",
+        cost_estimate=cost(8),
+    )(info, left, left_o, right, right_o, low, low_o, attn, attn_o, behind)
+
+
+def outer_qkv_kernel(
+    info, left, left_o, right, right_o, sums_a, sums_b, bias, _, keep, away, turned, extra
+):
+    feat, tile = sums_a.shape[1], right.shape[2]
     block = feat // 16
-    strip = pl.BlockSpec((1, rows, tile), lambda n: (n // per, 0, n % per))
-    out = pl.BlockSpec((8, block, tile), lambda n: (0, 0, n))
-    return pl.pallas_call(
-        outer_kernel,
-        grid=(cols // tile,),
+    line_up(info, left, left_o, turned)
+    for part in range(3):
+        cols = slice(part * tile, (part + 1) * tile)
+        total = outer_tile(turned, right[part], right_o[part])
+        keep[:, :, cols] = total[:8]
+        away[:, :, cols] = total[8:].astype(BF16)
+    ordered = [
+        sums_b[0:1],
+        sums_a[0:1],
+        sums_b[1:4],
+        sums_a[2:3],
+        sums_a[1:2],
+        sums_a[3:4],
+        jnp.zeros((120, feat), F32),
+    ]
+    flipped = jnp.concatenate(ordered).T
+    each = bias.shape[1] // 32
+    for chip in range(16):
+        place = info[PLACE + chip]
+        extra[place] = flipped[chip * block : (chip + 1) * block]
+        for core in (0, 1):
+            at = (2 * chip + core) * each
+            row = core * block // 2
+            extra[place, row : row + 1, 128 - each :] = bias[:, at : at + each]
+    keep[:, :, 3 * tile :] = extra[:8]
+    away[:, :, 3 * tile :] = extra[8:].astype(BF16)
+
+
+def outer_qkv(info, left, left_o, right, right_o, sums_a, sums_b, bias, behind):
+    _, block, rows = left.shape
+    cols = 3 * right.shape[2] + 128
+    vmem = pl.BlockSpec(memory_space=pltpu.VMEM)
+    return pl.pallas_call(
+        outer_qkv_kernel,
         out_shape=(shape((8, block, cols), F32), shape((8, block, cols), BF16)),
-        in_specs=[SMEM, full((rows, feat)), full((rows, feat)), strip, strip],
-        out_specs=(out, out),
-        scratch_shapes=[pltpu.VMEM((feat, 2 * rows), BF16), pltpu.VMEM((16, block, tile), F32)],
-        compiler_params=params(),
-        cost_estimate=cost(4 * rows * feat * cols, 4 * rows * (feat + cols) + 3 * feat * cols),
-    )(info, left, left_o, right, right_o)
-
-
-def outer_last_kernel(
-    info, left, left_o, right, right_o, sums_a, sums_b, bias, keep, away, blocks, extra
-):
-    rows, feat = left.shape
-    tile = right.shape[1]
-    block = feat // 16
-    total = dot(left[...].T, right[...]) + dot(left_o[...].T, right_o[...])
-    blocks[...] = total.reshape(blocks.shape)
-    extra[...] = jnp.zeros_like(extra)
-    ordered = jnp.concatenate(
-        [
-            sums_b[0:1],
-            sums_a[0:1],
-            sums_b[1:4],
-            sums_a[2:3],
-            sums_a[1:2],
-            sums_a[3:4],
-        ]
-    )
-    each = bias.shape[1] // 16
-    for chip in range(16):
-        extra[chip, 0:8, 0:block] = ordered[:, chip * block : (chip + 1) * block]
-        extra[chip, 8:9, 0:each] = bias[:, chip * each : (chip + 1) * each]
-    for j in range(8):
-        keep[j, :block] = blocks[info[j]]
-        away[j, :block] = blocks[info[8 + j]].astype(BF16)
-        keep[j, block:] = extra[info[j]]
-        away[j, block:] = extra[info[8 + j]].astype(BF16)
-
-
-def outer_last(info, left, left_o, right, right_o, sums_a, sums_b, bias):
-    rows, feat = left.shape
-    cols = right.shape[1]
-    block = feat // 16
-    vmem = pl.BlockSpec(memory_space=pltpu.VMEM)
-    return pl.pallas_call(
-        outer_last_kernel,
-        out_shape=(shape((8, block + 16, cols), F32), shape((8, block + 16, cols), BF16)),
-        in_specs=[SMEM] + [vmem] * 7,
+        in_specs=[SMEM] + [vmem] * 7 + [ANY],
         out_specs=(vmem, vmem),
-        scratch_shapes=[pltpu.VMEM((16, block, cols), F32), pltpu.VMEM((16, 16, cols), F32)],
-        compiler_params=params(),
-        cost_estimate=cost(4 * rows * feat * cols, 4 * rows * (feat + cols) + 3 * feat * cols),
-    )(info, left, left_o, right, right_o, sums_a, sums_b, bias)
-
-
-def outer_down_kernel(left, left_o, right, right_o, keep, away):
+        scratch_shapes=[
+            pltpu.VMEM((16, block, 2 * rows), BF16),
+            pltpu.VMEM((16, block, 128), F32),
+        ],
+        compiler_params=params(),
+        name="outer_qkv",
+        cost_estimate=cost(8),
+    )(info, left, left_o, right, right_o, sums_a, sums_b, bias, behind)
+
+
+def outer_down_kernel(left, left_o, right, right_o, _, keep, away):
     def flat(blocks):
         return blocks[...].reshape(-1, blocks.shape[-1])
 
     total = dot(flat(left), right[...]) + dot(flat(left_o), right_o[...])
     total = total.reshape(keep.shape)
 
-    @pl.when(pl.program_id(0) >= 4)
+    @pl.when(pl.program_id(0) >= 2)
     def _():
         keep[...] = total
 
-    @pl.when(pl.program_id(0) < 4)
+    @pl.when(pl.program_id(0) < 2)
     def _():
         away[...] = total.astype(BF16)
 
 
-def outer_down(left, left_o, right, right_o):
+def outer_down(left, left_o, right, right_o, behind):
     _, block, rows = left.shape
     feat = right.shape[1]
-    strip = pl.BlockSpec((2, block, rows), lambda j: ((j + 4) % 8, 0, 0))
+    strip = pl.BlockSpec((4, block, rows), lambda j: ((j + 2) % 4, 0, 0))
     return pl.pallas_call(
         outer_down_kernel,
-        grid=(8,),
+        grid=(4,),
         out_shape=(shape((8, block, feat), F32), shape((8, block, feat), BF16)),
-        in_specs=[strip, strip, full((rows, feat)), full((rows, feat))],
+        in_specs=[strip, strip, full((rows, feat)), full((rows, feat)), ANY],
         out_specs=(
-            pl.BlockSpec((2, block, feat), lambda j: (jnp.maximum(j - 4, 0), 0, 0)),
-            pl.BlockSpec((2, block, feat), lambda j: (jnp.minimum(j, 3), 0, 0)),
+            pl.BlockSpec((4, block, feat), lambda j: (jnp.maximum(j - 2, 0), 0, 0)),
+            pl.BlockSpec((4, block, feat), lambda j: (jnp.minimum(j, 1), 0, 0)),
         ),
         compiler_params=params(),
-        cost_estimate=cost(64 * rows * feat * block, 96 * block * (rows + feat)),
-    )(left, left_o, right, right_o)
-
-
-def add_first_kernel(keep, got, keep_s, got_s, kept, away):
-    kept[...] = keep[...] + got[...].astype(F32)
-    away[...] = (keep_s[...] + got_s[...].astype(F32)).astype(BF16)
-
-
-def add_first(keep, got):
-    _, rows, cols = keep.shape
-    near = pl.BlockSpec((1, rows, cols), lambda i: (i, 0, 0))
-    far = pl.BlockSpec((1, rows, cols), lambda i: (i + 4, 0, 0))
-    return pl.pallas_call(
-        add_first_kernel,
-        grid=(4,),
-        out_shape=(shape((4, rows, cols), F32), shape((4, rows, cols), BF16)),
-        in_specs=[near, near, far, far],
-        out_specs=(near, near),
-        compiler_params=params(),
-        cost_estimate=cost(8 * rows * cols, 72 * rows * cols),
-    )(keep, got, keep, got)
-
-
-def add_second_kernel(keep, got, base, one, two, three):
-    base[...] = keep[0] + got[0].astype(F32)
-    for s, out in ((1, one), (2, two), (3, three)):
-        out[...] = (keep[s] + got[s].astype(F32)).astype(BF16)
-
-
-def add_second(keep, got):
-    _, rows, cols = keep.shape
-    vmem = pl.BlockSpec(memory_space=pltpu.VMEM)
-    low = shape((rows, cols), BF16)
-    return pl.pallas_call(
-        add_second_kernel,
-        out_shape=(shape((rows, cols), F32), low, low, low),
-        in_specs=[vmem] * 2,
-        out_specs=(vmem,) * 4,
-        compiler_params=params(),
-        cost_estimate=cost(4 * rows * cols, 34 * rows * cols),
-    )(keep, got)
+        name="outer_down",
+        cost_estimate=cost(8),
+    )(left, left_o, right, right_o, behind)
 
 
 def total_of(base, parts):
@@ -1004,24 +1199,18 @@
     theirs[...] = total[pl.ds(pl.multiple_of((1 - core) * half, half), half)]
 
 
-def add_small_kernel(info, base, one, two, three, mine, theirs, total):
-    core = info[CORE]
-    half = mine.shape[0] - 16
-    total[...] = total_of(base, (one, two, three))
-    mine[:half] = total[pl.ds(pl.multiple_of(core * half, half), half)]
-    theirs[:half] = total[pl.ds(pl.multiple_of((1 - core) * half, half), half)]
-    mine[half:] = total[2 * half :]
-    theirs[half:] = total[2 * half :]
-
-
-def travel(keep, away):
-    kept, away = add_first(keep, send(away, second_way))
-    base, *lows = add_second(kept, send(away, first_way))
-    return base, [send(low, along_z(s)) for low, s in zip(lows, (1, 2, 3))]
-
-
-def home_down(keep, away):
-    base, parts = travel(keep, away)
+def shift_first(keep, away, behind):
+    got = gate(send(away, second_way), behind)
+    return keep[:4] + got[:4].astype(F32), (keep[4:] + got[4:].astype(F32)).astype(BF16)
+
+
+def shift_second(keep, away, behind):
+    got = gate(send(away, first_way), behind)
+    lows = [(keep[s] + got[s].astype(F32)).astype(BF16) for s in (1, 2, 3)]
+    return keep[0] + got[0].astype(F32), [send(low, along_z(s)) for low, s in zip(lows, (1, 2, 3))]
+
+
+def home_down(base, parts):
     vmem = pl.BlockSpec(memory_space=pltpu.VMEM)
     return pl.pallas_call(
         add_down_kernel,
@@ -1029,47 +1218,44 @@
         in_specs=[vmem] * 4,
         out_specs=vmem,
         compiler_params=params(),
-        cost_estimate=cost(3 * base.size, 14 * base.size),
+        name="home_down",
+        cost_estimate=cost(2),
     )(base, *parts)
 
 
-def home(info, keep, away, kernel, extra):
-    base, parts = travel(keep, away)
+def home(info, base, parts):
     rows, cols = base.shape
     vmem = pl.BlockSpec(memory_space=pltpu.VMEM)
-    out = shape(((rows - extra) // 2 + extra, cols), F32)
+    out = shape((rows // 2, cols), F32)
     mine, theirs = pl.pallas_call(
-        kernel,
+        add_last_kernel,
         out_shape=(out, out),
         in_specs=[SMEM] + [vmem] * 4,
         out_specs=(vmem, vmem),
         scratch_shapes=[pltpu.VMEM((rows, cols), F32)],
         compiler_params=params(),
-        cost_estimate=cost(3 * base.size, 14 * base.size),
+        name="home",
+        cost_estimate=cost(2),
     )(info, base, *parts)
     return mine, swap(theirs)
 
 
-def finish_kernel(
-    info, qkv, qkv_o, proj, proj_o, up, up_o, out_qkv, out_proj, out_up, gains, shifts, bias
-):
-    rows, third = out_proj.shape[0], proj.shape[1]
-    wide = up.shape[1]
-    small = proj[rows:] + proj_o[rows:]
-    each = 4 * rows
+def finish_kernel(info, qkv, qkv_o, up, up_o, out_qkv, out_proj, out_up, gains, shifts, bias):
+    rows, third = out_proj.shape[0], out_proj.shape[1] // 2
+    wide = out_up.shape[1] // 2
+    small = qkv[:, 3 * third :] + qkv_o[:, 3 * third :]
+    flipped = jnp.concatenate([small, jnp.zeros((128 - rows, 128), F32)]).T
+    gains[...] = flipped[0:2, :rows]
+    shifts[...] = flipped[2:8, :rows]
+    bias[...] = small[0:1, 128 - bias.shape[1] :]
 
     def lay(core):
-        for half, (a, b, c) in ((core, (qkv, proj, up)), (1 - core, (qkv_o, proj_o, up_o))):
+        for half, (a, b) in ((core, (qkv, up)), (1 - core, (qkv_o, up_o))):
             for part in range(3):
                 spot = part * 2 * third + half * third
                 out_qkv[:, spot : spot + third] = a[:, part * third : (part + 1) * third]
-            out_proj[:, half * third : (half + 1) * third] = b[:rows]
-            out_up[:, half * wide : (half + 1) * wide] = c[...]
-        mine = small[0:8, core * rows : (core + 1) * rows]
-        wide_mine = jnp.concatenate([mine, jnp.zeros((8, 128 - rows), F32)], axis=1).T
-        gains[...] = wide_mine[:rows, 0:2]
-        shifts[...] = wide_mine[:rows, 2:8]
-        bias[...] = small[8:9, core * each : (core + 1) * each]
+            out_proj[:, half * third : (half + 1) * third] = b[:, wide:]
+            out_up[:, half * wide : (half + 1) * wide] = b[:, :wide]
 
     @pl.when(info[CORE] == 0)
     def _():
@@ -1080,24 +1266,26 @@
         lay(1)
 
 
-def finish(info, qkv, qkv_o, proj, proj_o, up, up_o):
-    rows, third = up.shape[0], proj.shape[1]
+def finish(info, qkv, qkv_o, up, up_o):
+    rows = qkv.shape[0]
+    third = (qkv.shape[1] - 128) // 3
     vmem = pl.BlockSpec(memory_space=pltpu.VMEM)
     return pl.pallas_call(
         finish_kernel,
         out_shape=(
             shape((rows, 6 * third), F32),
             shape((rows, 2 * third), F32),
-            shape((rows, 2 * up.shape[1]), F32),
-            shape((rows, 2), F32),
-            shape((rows, 6), F32),
+            shape((rows, 2 * (up.shape[1] - third)), F32),
+            shape((2, rows), F32),
+            shape((6, rows), F32),
             shape((1, 4 * rows), F32),
         ),
-        in_specs=[SMEM] + [vmem] * 6,
+        in_specs=[SMEM] + [vmem] * 4,
         out_specs=(vmem,) * 6,
         compiler_params=params(),
-        cost_estimate=cost(0, 64 * rows * third),
-    )(info, qkv, qkv_o, proj, proj_o, up, up_o)
+        name="finish",
+        cost_estimate=cost(2),
+    )(info, qkv, qkv_o, up, up_o)
 
 
 def local(
@@ -1122,57 +1310,67 @@
     live = lax.iota(jnp.int32, tok_rows) < lengths[0]
     grad_y = jnp.where(live[:, None], upstream, jnp.zeros_like(upstream))
 
+    down = down_weight[None]
+    down_z = near_z(down, (1, 2))
     small = jnp.concatenate([gains, shifts, up_bias.reshape(rows, -1)], axis=1)
     small = jnp.pad(small, ((0, 0), (0, 128 - small.shape[1])))
-
-    def half_of(h):
-        parts = [qkv_weight[:, i * feat + h * third : i * feat + (h + 1) * third] for i in range(3)]
-        parts += [proj_weight[:, h * third : (h + 1) * third], small]
-        parts += [up_weight[:, h * wide : (h + 1) * wide]]
-        return jnp.concatenate(parts, axis=1)
-
-    halves = jnp.stack([half_of(0), half_of(1)])
-    mine = lax.dynamic_index_in_dim(halves, core, 0, keepdims=False)
-    given = swap(lax.dynamic_index_in_dim(halves, 1 - core, 0, keepdims=False))
-    piece = jnp.where(core == 0, jnp.concatenate([mine, given]), jnp.concatenate([given, mine]))
-    one = 4 * third + 128
-    first_pieces = spread(piece[:, :one])
-    up_pieces = spread(piece[:, one:])
-    down_pieces = spread(down_weight)
+    mine, theirs = halves(info, qkv_weight, proj_weight, up_weight)
+    one = 3 * third + 128
+    piece, piece_up = pieces_of(info, mine, swap(theirs), small, 3 * third)
+    zs, piece_up = gather([piece] + near_z(piece, (1, 2, 3)), (piece_up,), down_z)
+    up_z = near_z(piece_up, (1, 2))
+    low, piece_up = gather([zs, send(zs, first_way)], (piece_up,), up_z)
+    up_z += near_z(piece_up, (3,))
+    high = send(low, second_way)
+    zs_up, down = gather([piece_up] + up_z, (down,))
+    high = gate(high, zs_up)
+    first_pieces = (low, high, swap(low), swap(high))
     grad_y_o = swap(grad_y)
-
-    first_set, vecs, first, joint = enter(info, tokens, first_pieces)
-    bias = first_set[0, :, :, one - 120 : one - 116].reshape(1, hidden).astype(F32)
+    down_z += near_z(down, (3,))
+
+    first_set, vecs, first, first_t, joint = enter(info, tokens, first_pieces)
+    bias = first_set[0, :, :, one - 120 : one - 116] + first_set[1, :, :, one - 120 : one - 116]
+    bias = bias.reshape(1, hidden).astype(F32)
     first_set = first_set.reshape(2, feat, one)
-    first_o = swap(first)
-    mixed, stats = mix(info, joint)
-    mixed_o = swap(mixed)
-    up_set, after, second, active, slope, turned, turned_t = rise(
-        info, tokens, mixed, first_set, vecs, bias, up_pieces
-    )
-    second_o, turned_o = swap(second), swap(turned_t)
-    own_down = home_down(*outer_down(turned, turned_o, grad_y, grad_y_o))
-
+    first_o = swap(first_t)
+    (low,) = gather([zs_up, send(zs_up, first_way)], (), (first,))
+    (zs_down,) = gather([down] + down_z, (), (low,))
+    mixed, mixed_t, stats = mix(info, joint, zs_down)
+    high = gate(send(low, second_way), mixed)
+    up_pieces = (low, high, swap(low), swap(high))
+    mixed_t = mixed_t.reshape(first_t.shape)
+    mixed_o = swap(mixed_t)
+    (low,) = gather([zs_down, send(zs_down, first_way)], (), (mixed,))
+    up_set, after, second, second_t, active, slope, turned, turned_t = rise(
+        info, tokens, mixed, vecs, bias, up_pieces, low
+    )
+    up_set = up_set.reshape(2, feat, wide + third)
+    high = gate(send(low, second_way), second)
+    down_pieces = (low, high, swap(low), swap(high))
+    second_o, turned_o = swap(second_t), swap(turned_t)
     down_set, hid_theirs, hid_mine, bias_sum, grad_after, at_theirs, at_mine, grad_mixed, sums_a = (
-        fall(info, grad_y, slope, up_set.reshape(2, feat, wide), after, vecs, first_set, down_pieces)
+        fall(info, grad_y, slope, up_set, after, vecs, down_pieces)
     )
     hid_o, at_o = swap(hid_theirs), swap(at_theirs)
-    own_up = home(
-        info, *outer(info, second, second_o, hid_mine[None], hid_o[None]), add_last_kernel, 0
-    )
-    theirs, mine = mix_back(info, joint, grad_mixed, stats)
-    own_qkv = home(info, *outer(info, first, first_o, mine, swap(theirs)), add_last_kernel, 0)
-    grad_tokens, sums_b = exit_back(info, tokens, mine, theirs, first_set, grad_after, vecs)
-    own_last = home(
-        info,
-        *outer_last(info, mixed, mixed_o, at_mine, at_o, sums_a, sums_b, bias_sum),
-        add_small_kernel,
-        16,
-    )
-    output = leave(after, active, down_set.reshape(hidden, feat), vecs)
-    out_qkv, out_proj, out_up, out_gains, out_shifts, out_bias = finish(
-        info, *own_qkv, *own_last, *own_up
-    )
+    down = outer_down(turned, turned_o, grad_y, grad_y_o, hid_theirs)
+    up = outer_up(
+        info, second_t, second_o, hid_mine, hid_o, mixed_t, mixed_o, at_mine, at_o, down[1]
+    )
+    theirs, mine = mix_back(info, joint, grad_mixed, stats, up[1])
+    theirs_o = swap(theirs)
+    down = shift_first(*down, theirs)
+    up = shift_first(*up, down[1])
+    grad_tokens, sums_b = exit_back(info, tokens, mine, theirs, first_set, grad_after, vecs, up[1])
+    down = shift_second(*down, grad_tokens)
+    qkv = outer_qkv(info, first_t, first_o, mine, theirs_o, sums_a, sums_b, bias_sum, down[0])
+    up = shift_second(*up, qkv[1])
+    output = leave(after, active, down_set.reshape(hidden, feat), vecs, up[0])
+    base, parts = down
+    own_down = home_down(base, parts[:2] + [gate(parts[2], output)])
+    qkv = shift_first(*qkv, own_down)
+    own_up = home(info, *up)
+    own_qkv = home(info, *shift_second(*qkv, own_up[0]))
+    out_qkv, out_proj, out_up, out_gains, out_shifts, out_bias = finish(info, *own_qkv, *own_up)
     return (
         output,
         grad_tokens,
@@ -1180,8 +1378,8 @@
         out_proj,
         out_up,
         own_down,
-        out_gains,
-        out_shifts,
+        out_gains.T,
+        out_shifts.T,
         out_bias.reshape(-1),
     )
 

time: 318 us -> 279 us (0.88)
  Pallas kernels: 151 us -> 130 us
  waiting for transfers between devices: 82.8 us -> 64.1 us
  other arithmetic: 3.2 us -> 16 us
  starting transfers between devices: 52.6 us -> 45.3 us
  local copies, waits for them, and re-layouts: 24.5 us -> 20.7 us
    ppermute x53 -> x47, waiting for transfers between devices: 82.8 us -> 64.1 us  [send(): return lax.ppermute(array, AXES, pairs(move))]
    pallas_call x18 -> x26, Pallas kernels: 91.5 us -> 74.8 us  [the longest x1 18 us: rise(): pl.pallas_call(rise_kernel, grid=(hidden // tile,), out_shape=(shape(sets...]
    convert_element_type x1 -> x6, other arithmetic: 1.04 us -> 11.6 us  [the longest x3 6.07 us: shift_second(): lows = [(keep[s] + got[s].astype(F32)).astype(BF16) for s in (1, 2, 3)]]
    ppermute x53 -> x47, starting transfers between devices: 52.6 us -> 45.3 us  [send(): return lax.ppermute(array, AXES, pairs(move))]
    pallas_call x1, Pallas kernels: 20.9 us -> 17.3 us  [fall(): pl.pallas_call(fall_kernel, grid_spec=pltpu.PrefetchScalarGridSpec(num_sc...]
    unnamed x100 -> x81, local copies, waits for them, and re-layouts: 20.3 us -> 19.1 us
  transfers between devices with their start and end apart: 53 -> 47, of which waited for: 12 -> 16; matrix products, arithmetic and copies ran while one was open for 4% -> 5% of each run, Pallas kernels for 41% -> 44%
where the time goes in v2:
time: 279 us; the launch traced here: 278 us
  Pallas kernels  130 us (47%)
  waiting for transfers between devices  64.1 us (23%)
  starting transfers between devices  45.3 us (16%)
  local copies, waits for them, and re-layouts  20.7 us (7%)
  other arithmetic  16 us (6%)
    ppermute x47, waiting for transfers between devices, send(): return lax.ppermute(array, AXES, pairs(move))  64.1 us
    ppermute x47, starting transfers between devices, send(): return lax.ppermute(array, AXES, pairs(move))  45.3 us
    unnamed x81, local copies, waits for them, and re-layouts  19.1 us
    pallas_call x1, Pallas kernels, rise(): pl.pallas_call(rise_kernel, grid=(hidden // tile,), out_shape=(shape(sets...  18 us
    pallas_call x1, Pallas kernels, fall(): pl.pallas_call(fall_kernel, grid_spec=pltpu.PrefetchScalarGridSpec(num_sc...  17.3 us
    pallas_call x1, Pallas kernels, mix_back(): pl.pallas_call(mix_back_kernel, grid_spec=pltpu.PrefetchScalarGridSpec(nu...  16.4 us
    pallas_call x6, Pallas kernels, gather(): pl.pallas_call(partial(gather_kernel, n, n_held + len(behind)), out_shape...  13.1 us
    pallas_call x1, Pallas kernels, mix(): pl.pallas_call(mix_kernel, grid=(n,), out_shape=(shape((rows, feat), BF16...  10.2 us
  transfers between devices with their start and end apart: 47, of which 16 were waited for; matrix products, arithmetic and copies ran while one was open for 5% of the time, Pallas kernels for 44%

profile of v2, /device:TPU:0, one launch (start us, length us, event | category | flops | bytes accessed | tf_op | source)
XLA Modules:
  0.0 278.2 jit_solution(3797906758933475943)
XLA Ops:
  5.8 2.6 collective-permute-start.4
  8.4 2.6 collective-permute-start.5
  15.0 3.8 %collective-permute-start.3 = (bf16[1,48,1280]{2,1,0:T(8,128)(2,1)}, bf16[1,48,1280]{2,1,0:T(8,128)(2,1)S(1)}, u32[]{:S(2)}, u32[]{:S(2)}) collective-permute-start(bf16[1,48,1280]{2,1,0:T(8,128)(2,1)} %get-tuple-element.66.refs_0_), channel_id=1, source_target_pairs={{0,24},{1,25},{2,26},{3,27},{4,28},{5,29},{6,30},{7,31},{8,16},{9,... | collective-permute-start | bytes 368648 | tf_op jit(solution)/shard_map/ppermute | solution.py:266
  18.8 3.3 %collective-permute-done.1.refs_1_ = bf16[1,48,1280]{2,1,0:T(8,128)(2,1)S(1)} collective-permute-done((bf16[1,48,1280]{2,1,0:T(8,128)(2,1)}, bf16[1,48,1280]{2,1,0:T(8,128)(2,1)S(1)}, u32[]{:S(2)}, u32[]{:S(2)}) %collective-permute-start.1) | collective-permute-done | bytes 122912 | tf_op jit(solution)/shard_map/ppermute | solution.py:266
  22.0 5.4 %collective-permute-done.2.refs_2_ = bf16[1,48,1280]{2,1,0:T(8,128)(2,1)S(1)} collective-permute-done((bf16[1,48,1280]{2,1,0:T(8,128)(2,1)}, bf16[1,48,1280]{2,1,0:T(8,128)(2,1)S(1)}, u32[]{:S(2)}, u32[]{:S(2)}) %collective-permute-start.2) | collective-permute-done | bytes 122912 | tf_op jit(solution)/shard_map/ppermute | solution.py:266
  34.9 6.4 %collective-permute-done.7.refs_3_.refs_1_ = bf16[1,48,1920]{2,1,0:T(8,128)(2,1)S(1)} collective-permute-done((bf16[1,48,1920]{2,1,0:T(8,128)(2,1)}, bf16[1,48,1920]{2,1,0:T(8,128)(2,1)S(1)}, u32[]{:S(2)}, u32[]{:S(2)}) %collective-permute-start.7) | collective-permute-done | bytes 184352 | tf_op jit(solution)/shard_map/ppermute | solution.py:266
  41.2 3.1 %collective-permute-done.8.refs_4_.refs_2_ = bf16[1,48,1920]{2,1,0:T(8,128)(2,1)S(1)} collective-permute-done((bf16[1,48,1920]{2,1,0:T(8,128)(2,1)}, bf16[1,48,1920]{2,1,0:T(8,128)(2,1)S(1)}, u32[]{:S(2)}, u32[]{:S(2)}) %collective-permute-start.8) | collective-permute-done | bytes 184352 | tf_op jit(solution)/shard_map/ppermute | solution.py:266
  48.5 2.4 collective-permute-start.10
  51.0 5.2 %collective-permute-done.10.refs_3_ = bf16[1,48,1920]{2,1,0:T(8,128)(2,1)S(1)} collective-permute-done((bf16[1,48,1920]{2,1,0:T(8,128)(2,1)}, bf16[1,48,1920]{2,1,0:T(8,128)(2,1)S(1)}, u32[]{:S(2)}, u32[]{:S(2)}) %collective-permute-start.10) | collective-permute-done | bytes 184352 | tf_op jit(solution)/shard_map/ppermute | solution.py:266
  58.9 3.4 %collective-permute-done.9.array = bf16[8,48,1280]{2,1,0:T(8,128)(2,1)S(1)} collective-permute-done((bf16[8,48,1280]{2,1,0:T(8,128)(2,1)}, bf16[8,48,1280]{2,1,0:T(8,128)(2,1)S(1)}, u32[]{:S(2)}, u32[]{:S(2)}) %collective-permute-start.9) | collective-permute-done | bytes 983072 | tf_op jit(solution)/shard_map/ppermute | solution.py:266
  64.7 2.6 collective-permute-start.13
  69.2 7.8 %enter.1 = (bf16[2,16,48,1280]{3,2,1,0:T(8,128)(2,1)}, f32[8,768]{1,0:T(8,128)}, bf16[512,768]{1,0:T(8,128)(2,1)}, bf16[16,48,512]{2,1,0:T(8,128)(2,1)}, bf16[2,512,1152]{2,1,0:T(8,128)(2,1)}) custom-call(s32[66]{0:T(128)} %stack.239.info, bf16[512,768]{1,0:T(8,128)(2,1)} %tokens.5, bf16[8,48,1280]{2,1,0:T(8,128)(2,1)} %get-tuple-element.70.low, ...), custom_call_target="tpu_custom_call" | custom-call | flops 240000008192 | bytes 1 | tf_op jit(solution)/shard_map/enter/pallas_call | solution.py:490
  77.0 2.6 gather.9.refs_4_.low
  82.0 10.2 %mix.1 = (bf16[512,768]{1,0:T(8,128)(2,1)}, bf16[768,512]{1,0:T(8,128)(2,1)}, f32[6,8,512]{2,1,0:T(8,128)}) custom-call(s32[66]{0:T(128)} %stack.239.info, bf16[2,512,1152]{2,1,0:T(8,128)(2,1)} %get-tuple-element.73.q.k.v, bf16[2,512,1152]{2,1,0:T(8,128)(2,1)} %get-tuple-element.73.q.k.v, bf16[2,512,1152]{2,1,0:T(8,128)(2,1)} %get-tuple-element.73.q.k.v, ...), custom_call_target="tpu_custom_call" | custom-call | flops 299999985664 | bytes 1 | tf_op jit(solution)/shard_map/mix/pallas_call | solution.py:546
  92.3 7.0 %collective-permute-done.15.array = bf16[8,48,1920]{2,1,0:T(8,128)(2,1)} collective-permute-done((bf16[8,48,1920]{2,1,0:T(8,128)(2,1)}, bf16[8,48,1920]{2,1,0:T(8,128)(2,1)}, u32[]{:S(2)}, u32[]{:S(2)}) %collective-permute-start.15) | collective-permute-done | bytes 1474592 | tf_op jit(solution)/shard_map/ppermute | solution.py:266
  102.9 7.3 %collective-permute-done.18.refs_1_ = bf16[4,96,768]{2,1,0:T(8,128)(2,1)S(1)} collective-permute-done((bf16[4,96,768]{2,1,0:T(8,128)(2,1)S(1)}, bf16[4,96,768]{2,1,0:T(8,128)(2,1)S(1)}, u32[]{:S(2)}, u32[]{:S(2)}) %collective-permute-start.18) | collective-permute-done | bytes 589856 | tf_op jit(solution)/shard_map/ppermute | solution.py:266
  115.0 18.0 %rise.1 = (bf16[2,16,48,1920]{3,2,1,0:T(8,128)(2,1)}, f32[512,768]{1,0:T(8,128)}, bf16[512,768]{1,0:T(8,128)(2,1)}, bf16[16,48,512]{2,1,0:T(8,128)(2,1)}, bf16[5...) custom-call(s32[66]{0:T(128)} %stack.239.info, ...), custom_call_target="tpu_custom_call" | custom-call | flops 539999993856 | bytes 1 | tf_op jit(solution)/shard_map/rise/pallas_call | solution.py:745
  137.4 17.3 %fall.1 = (bf16[16,2,96,768]{3,2,1,0:T(8,128)(2,1)}, bf16[512,1536]{1,0:T(8,128)(2,1)}, bf16[512,1536]{1,0:T(8,128)(2,1)}, f32[1,3072]{1,0:T(1,128)}, f32[512,76...) custom-call(s32[66]{0:T(128)} %stack.239.info, ...), custom_call_target="tpu_custom_call" | custom-call | flops 539999993856 | bytes 1 | tf_op jit(solution)/shard_map/fall/pallas_call | solution.py:918
  155.2 6.7 %outer_down.1 = (f32[8,96,768]{2,1,0:T(8,128)}, bf16[8,96,768]{2,1,0:T(8,128)(2,1)}) custom-call(bf16[16,96,512]{2,1,0:T(8,128)(2,1)} %get-tuple-element.91.left, bf16[16,96,512]{2,1,0:T(8,128)(2,1)} %collective-permute-done.26.left_o, bf16[512,768]{1,0:T(8,128)(2,1)} %broadcast_select_fusion.grad_y.right, bf16[512,768]{1,0:T(8,128)(2,1)} %collective-permute-done.27.right_o, ...), custom_call_target="tpu_custom_call" | custom-call | flops 240000008192 | bytes 1 | tf_op jit(solution)/shard_map/outer_down/pallas_call | solution.py:1169
  163.5 7.9 %outer_up.1 = (f32[8,48,1920]{2,1,0:T(8,128)}, bf16[8,48,1920]{2,1,0:T(8,128)(2,1)}) custom-call(s32[66]{0:T(128)} %stack.239.info, bf16[16,48,512]{2,1,0:T(8,128)(2,1)} %get-tuple-element.85.left, bf16[16,48,512]{2,1,0:T(8,128)(2,1)} %collective-permute-done.22.left_o, bf16[512,1536]{1,0:T(8,128)(2,1)} %get-tuple-element.86.right, ...), custom_call_target="tpu_custom_call" | custom-call | flops 240000008192 | bytes 1 | tf_op jit(solution)/shard_map/outer_up/pallas_call | solution.py:1079
  171.9 16.4 %mix_back.1 = (bf16[3,512,384]{2,1,0:T(8,128)(2,1)}, bf16[3,512,384]{2,1,0:T(8,128)(2,1)}) custom-call(s32[66]{0:T(128)} %stack.239.info, bf16[2,512,1152]{2,1,0:T(8,128)(2,1)} %get-tuple-element.73.q.k.v, bf16[2,512,1152]{2,1,0:T(8,128)(2,1)} %get-tuple-element.73.q.k.v, bf16[2,512,1152]{2,1,0:T(8,128)(2,1)} %get-tuple-element.73.q.k.v, ...), custom_call_target="tpu_custom_call" | custom-call | flops 480000016384 | bytes 1 | tf_op jit(solution)/shard_map/mix_back/pallas_call | solution.py:616
  189.9 2.7 convert_add_fusion.1
  194.5 2.9 %add_convert_fusion = (bf16[4,48,1920]{2,1,0:T(8,128)(2,1)}, f32[4,48,1920]{2,1,0:T(8,128)}) fusion(f32[8,48,1920]{2,1,0:T(8,128)S(1)} %copy-done.2, bf16[8,48,1920]{2,1,0:T(8,128)(2,1)} %gate.14), kind=kLoop, calls=%fused_computation | loop fusion | flops 1843200 | bytes 6635520 | tf_op jit(solution)/shard_map/convert_element_type | solution.py:1204
  198.0 7.8 %exit_back.1 = (bf16[512,768]{1,0:T(8,128)(2,1)}, f32[8,768]{1,0:T(8,128)}) custom-call(s32[66]{0:T(128)} %stack.239.info, bf16[512,768]{1,0:T(8,128)(2,1)} %tokens.5, bf16[3,512,384]{2,1,0:T(8,128)(2,1)} %get-tuple-element.101.mine.right, bf16[3,512,384]{2,1,0:T(8,128)(2,1)} %get-tuple-element.99.behind.theirs, bf16[2,768,1280]{2,1,0:T(8,128)(2,1)} %bitcast.93, ...), custom_call_target="tpu_custom_call" | custom-call | flops 240000008192 | bytes 1 | tf_op jit(solution)/shard_map/exit_back/pallas_call | solution.py:1007
  210.5 2.9 %collective-permute-start.36 = (bf16[96,768]{1,0:T(8,128)(2,1)}, bf16[96,768]{1,0:T(8,128)(2,1)}, u32[]{:S(2)}, u32[]{:S(2)}) collective-permute-start(bf16[96,768]{1,0:T(8,128)(2,1)} %get-tuple-element.130), channel_id=1, source_target_pairs={{0,16},{1,17},{2,18},{3,19},{4,20},{5,21},{6,22},{7,23},{8,24},{9,... | collective-permute-start | bytes 442376 | tf_op jit(solution)/shard_map/ppermute | solution.py:266
  213.4 6.3 %outer_qkv.1 = (f32[8,48,1280]{2,1,0:T(8,128)}, bf16[8,48,1280]{2,1,0:T(8,128)(2,1)}) custom-call(s32[66]{0:T(128)} %stack.239.info, bf16[16,48,512]{2,1,0:T(8,128)(2,1)} %get-tuple-element.100.left, bf16[16,48,512]{2,1,0:T(8,128)(2,1)} %collective-permute-done.31.left_o, bf16[3,512,384]{2,1,0:T(8,128)(2,1)} %get-tuple-element.101.mine.right, ...), custom_call_target="tpu_custom_call" | custom-call | flops 240000008192 | bytes 1 | tf_op jit(solution)/shard_map/outer_qkv/pallas_call | solution.py:1134
  223.4 7.5 %leave.1.behind = bf16[512,768]{1,0:T(8,128)(2,1)} custom-call(f32[512,768]{1,0:T(8,128)} %get-tuple-element.79.after, bf16[512,3072]{1,0:T(8,128)(2,1)} %get-tuple-element.80.active, bf16[3072,768]{1,0:T(8,128)(2,1)} %bitcast.96, f32[8,768]{1,0:T(8,128)} %get-tuple-element.77.vecs, f32[48,1920]{1,0:T(8,128)} %get-tuple-element.128._.base), custom_call_target="tpu_custom_call" | custom-call | flops 210000003072 | bytes 1 | tf_op jit(solution)/shard_map/leave/pallas_call | solution.py:810
  239.2 2.6 collective-permute-start.41
  241.8 3.5 %collective-permute-done.39.one = bf16[48,1920]{1,0:T(8,128)(2,1)S(1)} collective-permute-done((bf16[48,1920]{1,0:T(8,128)(2,1)S(1)}, bf16[48,1920]{1,0:T(8,128)(2,1)S(1)}, u32[]{:S(2)}, u32[]{:S(2)}) %collective-permute-start.39) | collective-permute-done | bytes 184352 | tf_op jit(solution)/shard_map/ppermute | solution.py:266
  245.3 7.7 %collective-permute-done.40.two = bf16[48,1920]{1,0:T(8,128)(2,1)S(1)} collective-permute-done((bf16[48,1920]{1,0:T(8,128)(2,1)S(1)}, bf16[48,1920]{1,0:T(8,128)(2,1)S(1)}, u32[]{:S(2)}, u32[]{:S(2)}) %collective-permute-start.40) | collective-permute-done | bytes 184352 | tf_op jit(solution)/shard_map/ppermute | solution.py:266
  261.2 2.4 collective-permute-start.44
  264.7 6.5 %collective-permute-done.43.two = bf16[48,1280]{1,0:T(8,128)(2,1)S(1)} collective-permute-done((bf16[48,1280]{1,0:T(8,128)(2,1)S(1)}, bf16[48,1280]{1,0:T(8,128)(2,1)S(1)}, u32[]{:S(2)}, u32[]{:S(2)}) %collective-permute-start.43) | collective-permute-done | bytes 122912 | tf_op jit(solution)/shard_map/ppermute | solution.py:266
  (188 shorter events, 81.9 us)
Async XLA Ops:
  5.8 12.9 %collective-permute-start.4 = (bf16[1,96,768]{2,1,0:T(8,128)(2,1)}, bf16[1,96,768]{2,1,0:T(8,128)(2,1)S(1)}, u32[]{:S(2)}, u32[]{:S(2)}) collective-permute-start(bf16[1,96,768]{2,1,0:T(8,128)(2,1)} %bitcast.57.refs_4_), channel_id=1, source_target_pairs={{0,8},{1,9},{2,10},{3,11},{4,12},{5,13},{6,14},{7,15},{8,0},{9,1},... | collective-permute-start | bytes 442376 | tf_op jit(solution)/shard_map/ppermute | solution.py:266
  14.8 12.7 %collective-permute-start.2 = (bf16[1,48,1280]{2,1,0:T(8,128)(2,1)}, bf16[1,48,1280]{2,1,0:T(8,128)(2,1)S(1)}, u32[]{:S(2)}, u32[]{:S(2)}) collective-permute-start(bf16[1,48,1280]{2,1,0:T(8,128)(2,1)} %get-tuple-element.66.refs_0_), channel_id=1, source_target_pairs={{0,16},{1,17},{2,18},{3,19},{4,20},{5,21},{6,22},{7,23},{8,24},{9,... | collective-permute-start | bytes 368648 | tf_op jit(solution)/shard_map/ppermute | solution.py:266
  15.0 12.5 %collective-permute-start.3 = (bf16[1,48,1280]{2,1,0:T(8,128)(2,1)}, bf16[1,48,1280]{2,1,0:T(8,128)(2,1)S(1)}, u32[]{:S(2)}, u32[]{:S(2)}) collective-permute-start(bf16[1,48,1280]{2,1,0:T(8,128)(2,1)} %get-tuple-element.66.refs_0_), channel_id=1, source_target_pairs={{0,24},{1,25},{2,26},{3,27},{4,28},{5,29},{6,30},{7,31},{8,16},{9,... | collective-permute-start | bytes 368648 | tf_op jit(solution)/shard_map/ppermute | solution.py:266
  30.0 14.3 %collective-permute-start.6 = (bf16[4,48,1280]{2,1,0:T(8,128)(2,1)}, bf16[4,48,1280]{2,1,0:T(8,128)(2,1)S(1)}, u32[]{:S(2)}, u32[]{:S(2)}) collective-permute-start(bf16[4,48,1280]{2,1,0:T(8,128)(2,1)} %get-tuple-element.68.refs_0_), channel_id=1, source_target_pairs={{0,2},{1,5},{2,0},{3,7},{4,6},{5,1},{6,4},{7,3},{8,10},{9,13},{10,... | collective-permute-start | bytes 1474568 | tf_op jit(solution)/shard_map/ppermute | solution.py:266
  33.9 10.5 %collective-permute-start.8 = (bf16[1,48,1920]{2,1,0:T(8,128)(2,1)}, bf16[1,48,1920]{2,1,0:T(8,128)(2,1)S(1)}, u32[]{:S(2)}, u32[]{:S(2)}) collective-permute-start(bf16[1,48,1920]{2,1,0:T(8,128)(2,1)} %get-tuple-element.69.refs_2_), channel_id=1, source_target_pairs={{0,16},{1,17},{2,18},{3,19},{4,20},{5,21},{6,22},{7,23},{8,24},{9,... | collective-permute-start | bytes 552968 | tf_op jit(solution)/shard_map/ppermute | solution.py:266
  48.0 14.3 %collective-permute-start.9 = (bf16[8,48,1280]{2,1,0:T(8,128)(2,1)}, bf16[8,48,1280]{2,1,0:T(8,128)(2,1)S(1)}, u32[]{:S(2)}, u32[]{:S(2)}) collective-permute-start(bf16[8,48,1280]{2,1,0:T(8,128)(2,1)} %get-tuple-element.70.low), channel_id=1, source_target_pairs={{0,4},{1,3},{2,6},{3,1},{4,0},{5,7},{6,2},{7,5},{8,12},{9,11},{10,... | collective-permute-start | bytes 2949128 | tf_op jit(solution)/shard_map/ppermute | solution.py:266
  51.0 16.3 %collective-permute-start.11 = (bf16[8,48,1280]{2,1,0:T(8,128)(2,1)}, bf16[8,48,1280]{2,1,0:T(8,128)(2,1)S(1)}, u32[]{:S(2)}, u32[]{:S(2)}) collective-permute-start(bf16[8,48,1280]{2,1,0:T(8,128)(2,1)} %get-tuple-element.70.low), channel_id=1, source_target_pairs={{0,1},{1,0},{2,3},{3,2},{4,5},{5,4},{6,7},{7,6},{8,9},{9,8},{10,11... | collective-permute-start | bytes 2949128 | tf_op jit(solution)/shard_map/ppermute | solution.py:266
  63.3 13.7 %collective-permute-start.14 = (bf16[4,48,1920]{2,1,0:T(8,128)(2,1)}, bf16[4,48,1920]{2,1,0:T(8,128)(2,1)}, u32[]{:S(2)}, u32[]{:S(2)}) collective-permute-start(bf16[4,48,1920]{2,1,0:T(8,128)(2,1)} %get-tuple-element.72.behind.refs_0_), channel_id=1, source_target_pairs={{0,2},{1,5},{2,0},{3,7},{4,6},{5,1},{6,4},{7,3},{8,10},{9,13},{10,... | collective-permute-start | bytes 2211848 | tf_op jit(solution)/shard_map/ppermute | solution.py:266
  64.7 15.3 %collective-permute-start.13 = (bf16[1,96,768]{2,1,0:T(8,128)(2,1)}, bf16[1,96,768]{2,1,0:T(8,128)(2,1)}, u32[]{:S(2)}, u32[]{:S(2)}) collective-permute-start(bf16[1,96,768]{2,1,0:T(8,128)(2,1)} %get-tuple-element.74.refs_0_), channel_id=1, source_target_pairs={{0,24},{1,25},{2,26},{3,27},{4,28},{5,29},{6,30},{7,31},{8,16},{9,... | collective-permute-start | bytes 442376 | tf_op jit(solution)/shard_map/ppermute | solution.py:266
  79.6 19.7 %collective-permute-start.15 = (bf16[8,48,1920]{2,1,0:T(8,128)(2,1)}, bf16[8,48,1920]{2,1,0:T(8,128)(2,1)}, u32[]{:S(2)}, u32[]{:S(2)}) collective-permute-start(bf16[8,48,1920]{2,1,0:T(8,128)(2,1)} %gather.9.refs_4_.low), channel_id=1, source_target_pairs={{0,4},{1,3},{2,6},{3,1},{4,0},{5,7},{6,2},{7,5},{8,12},{9,11},{10,... | collective-permute-start | bytes 4423688 | tf_op jit(solution)/shard_map/ppermute | solution.py:266
  80.0 33.8 %collective-permute-start.16 = (bf16[8,48,1920]{2,1,0:T(8,128)(2,1)}, bf16[8,48,1920]{2,1,0:T(8,128)(2,1)}, u32[]{:S(2)}, u32[]{:S(2)}) collective-permute-start(bf16[8,48,1920]{2,1,0:T(8,128)(2,1)} %gather.9.refs_4_.low), channel_id=1, source_target_pairs={{0,1},{1,0},{2,3},{3,2},{4,5},{5,4},{6,7},{7,6},{8,9},{9,8},{10,11... | collective-permute-start | bytes 4423688 | tf_op jit(solution)/shard_map/ppermute | solution.py:266
  99.3 14.6 %collective-permute-start.17 = (bf16[8,48,1920]{2,1,0:T(8,128)(2,1)}, bf16[8,48,1920]{2,1,0:T(8,128)(2,1)S(1)}, u32[]{:S(2)}, u32[]{:S(2)}) collective-permute-start(bf16[8,48,1920]{2,1,0:T(8,128)(2,1)} %gate.11.high), channel_id=1, source_target_pairs={{0,1},{1,0},{2,3},{3,2},{4,5},{5,4},{6,7},{7,6},{8,9},{9,8},{10,11... | collective-permute-start | bytes 4423688 | tf_op jit(solution)/shard_map/ppermute | solution.py:266
  113.4 19.6 %collective-permute-start.19 = (bf16[8,96,768]{2,1,0:T(8,128)(2,1)}, bf16[8,96,768]{2,1,0:T(8,128)(2,1)}, u32[]{:S(2)}, u32[]{:S(2)}) collective-permute-start(bf16[8,96,768]{2,1,0:T(8,128)(2,1)} %gather.11._.low), channel_id=1, source_target_pairs={{0,4},{1,3},{2,6},{3,1},{4,0},{5,7},{6,2},{7,5},{8,12},{9,11},{10,... | collective-permute-start | bytes 3538952 | tf_op jit(solution)/shard_map/ppermute | solution.py:266
  113.8 22.4 %collective-permute-start.20 = (bf16[8,96,768]{2,1,0:T(8,128)(2,1)}, bf16[8,96,768]{2,1,0:T(8,128)(2,1)}, u32[]{:S(2)}, u32[]{:S(2)}) collective-permute-start(bf16[8,96,768]{2,1,0:T(8,128)(2,1)} %gather.11._.low), channel_id=1, source_target_pairs={{0,1},{1,0},{2,3},{3,2},{4,5},{5,4},{6,7},{7,6},{8,9},{9,8},{10,11... | collective-permute-start | bytes 3538952 | tf_op jit(solution)/shard_map/ppermute | solution.py:266
  135.2 19.5 %collective-permute-start.27 = (bf16[512,768]{1,0:T(8,128)(2,1)}, bf16[512,768]{1,0:T(8,128)(2,1)}, u32[]{:S(2)}, u32[]{:S(2)}) collective-permute-start(bf16[512,768]{1,0:T(8,128)(2,1)} %broadcast_select_fusion.grad_y.right), channel_id=1, source_target_pairs={{0,1},{1,0},{2,3},{3,2},{4,5},{5,4},{6,7},{7,6},{8,9},{9,8},{10,11... | collective-permute-start | bytes 2359304 | tf_op jit(solution)/shard_map/ppermute | solution.py:266
  135.7 26.2 %collective-permute-start.24 = (bf16[16,48,512]{2,1,0:T(8,128)(2,1)}, bf16[16,48,512]{2,1,0:T(8,128)(2,1)}, u32[]{:S(2)}, u32[]{:S(2)}) collective-permute-start(bf16[16,48,512]{2,1,0:T(8,128)(2,1)} %bitcast.61.low), channel_id=1, source_target_pairs={{0,1},{1,0},{2,3},{3,2},{4,5},{5,4},{6,7},{7,6},{8,9},{9,8},{10,11... | collective-permute-start | bytes 2359304 | tf_op jit(solution)/shard_map/ppermute | solution.py:266
  135.7 74.8 %collective-permute-start.31 = (bf16[16,48,512]{2,1,0:T(8,128)(2,1)}, bf16[16,48,512]{2,1,0:T(8,128)(2,1)}, u32[]{:S(2)}, u32[]{:S(2)}) collective-permute-start(bf16[16,48,512]{2,1,0:T(8,128)(2,1)} %get-tuple-element.100.left), channel_id=1, source_target_pairs={{0,1},{1,0},{2,3},{3,2},{4,5},{5,4},{6,7},{7,6},{8,9},{9,8},{10,11... | collective-permute-start | bytes 2359304 | tf_op jit(solution)/shard_map/ppermute | solution.py:266
  136.2 18.9 %collective-permute-start.26 = (bf16[16,96,512]{2,1,0:T(8,128)(2,1)}, bf16[16,96,512]{2,1,0:T(8,128)(2,1)}, u32[]{:S(2)}, u32[]{:S(2)}) collective-permute-start(bf16[16,96,512]{2,1,0:T(8,128)(2,1)} %get-tuple-element.92), channel_id=1, source_target_pairs={{0,1},{1,0},{2,3},{3,2},{4,5},{5,4},{6,7},{7,6},{8,9},{9,8},{10,11... | collective-permute-start | bytes 4718600 | tf_op jit(solution)/shard_map/ppermute | solution.py:266
  136.3 27.2 %collective-permute-start.22 = (bf16[16,48,512]{2,1,0:T(8,128)(2,1)}, bf16[16,48,512]{2,1,0:T(8,128)(2,1)}, u32[]{:S(2)}, u32[]{:S(2)}) collective-permute-start(bf16[16,48,512]{2,1,0:T(8,128)(2,1)} %get-tuple-element.85.left), channel_id=1, source_target_pairs={{0,1},{1,0},{2,3},{3,2},{4,5},{5,4},{6,7},{7,6},{8,9},{9,8},{10,11... | collective-permute-start | bytes 2359304 | tf_op jit(solution)/shard_map/ppermute | solution.py:266
  161.9 26.4 %collective-permute-start.29 = (bf16[8,96,768]{2,1,0:T(8,128)(2,1)}, bf16[8,96,768]{2,1,0:T(8,128)(2,1)}, u32[]{:S(2)}, u32[]{:S(2)}) collective-permute-start(bf16[8,96,768]{2,1,0:T(8,128)(2,1)} %get-tuple-element.93._), channel_id=1, source_target_pairs={{0,4},{1,3},{2,6},{3,1},{4,0},{5,7},{6,2},{7,5},{8,12},{9,11},{10,... | collective-permute-start | bytes 3538952 | tf_op jit(solution)/shard_map/ppermute | solution.py:266
  171.4 22.9 %collective-permute-start.28 = (bf16[8,48,1920]{2,1,0:T(8,128)(2,1)}, bf16[8,48,1920]{2,1,0:T(8,128)(2,1)}, u32[]{:S(2)}, u32[]{:S(2)}) collective-permute-start(bf16[8,48,1920]{2,1,0:T(8,128)(2,1)} %get-tuple-element.95._), channel_id=1, source_target_pairs={{0,4},{1,3},{2,6},{3,1},{4,0},{5,7},{6,2},{7,5},{8,12},{9,11},{10,... | collective-permute-start | bytes 4423688 | tf_op jit(solution)/shard_map/ppermute | solution.py:266
  188.3 25.1 %collective-permute-start.32 = (bf16[3,512,384]{2,1,0:T(8,128)(2,1)}, bf16[3,512,384]{2,1,0:T(8,128)(2,1)}, u32[]{:S(2)}, u32[]{:S(2)}) collective-permute-start(bf16[3,512,384]{2,1,0:T(8,128)(2,1)} %get-tuple-element.99.behind.theirs), channel_id=1, source_target_pairs={{0,1},{1,0},{2,3},{3,2},{4,5},{5,4},{6,7},{7,6},{8,9},{9,8},{10,11... | collective-permute-start | bytes 3538952 | tf_op jit(solution)/shard_map/ppermute | solution.py:266
  192.6 13.1 %collective-permute-start.33 = (bf16[4,96,768]{2,1,0:T(8,128)(2,1)}, bf16[4,96,768]{2,1,0:T(8,128)(2,1)}, u32[]{:S(2)}, u32[]{:S(2)}) collective-permute-start(bf16[4,96,768]{2,1,0:T(8,128)(2,1)} %get-tuple-element.122.behind), channel_id=1, source_target_pairs={{0,2},{1,5},{2,0},{3,7},{4,6},{5,1},{6,4},{7,3},{8,10},{9,13},{10,... | collective-permute-start | bytes 1769480 | tf_op jit(solution)/shard_map/ppermute | solution.py:266
  197.4 23.8 %collective-permute-start.30 = (bf16[4,48,1920]{2,1,0:T(8,128)(2,1)}, bf16[4,48,1920]{2,1,0:T(8,128)(2,1)}, u32[]{:S(2)}, u32[]{:S(2)}) collective-permute-start(bf16[4,48,1920]{2,1,0:T(8,128)(2,1)} %get-tuple-element.119._), channel_id=1, source_target_pairs={{0,2},{1,5},{2,0},{3,7},{4,6},{5,1},{6,4},{7,3},{8,10},{9,13},{10,... | collective-permute-start | bytes 2211848 | tf_op jit(solution)/shard_map/ppermute | solution.py:266
  209.0 21.9 %collective-permute-start.37 = (bf16[96,768]{1,0:T(8,128)(2,1)}, bf16[96,768]{1,0:T(8,128)(2,1)}, u32[]{:S(2)}, u32[]{:S(2)}) collective-permute-start(bf16[96,768]{1,0:T(8,128)(2,1)} %get-tuple-element.129), channel_id=1, source_target_pairs={{0,24},{1,25},{2,26},{3,27},{4,28},{5,29},{6,30},{7,31},{8,16},{9,... | collective-permute-start | bytes 442376 | tf_op jit(solution)/shard_map/ppermute | solution.py:266
  210.5 20.4 %collective-permute-start.35 = (bf16[96,768]{1,0:T(8,128)(2,1)}, bf16[96,768]{1,0:T(8,128)(2,1)}, u32[]{:S(2)}, u32[]{:S(2)}) collective-permute-start(bf16[96,768]{1,0:T(8,128)(2,1)} %get-tuple-element.131), channel_id=1, source_target_pairs={{0,8},{1,9},{2,10},{3,11},{4,12},{5,13},{6,14},{7,15},{8,0},{9,1},... | collective-permute-start | bytes 442376 | tf_op jit(solution)/shard_map/ppermute | solution.py:266
  210.5 20.4 %collective-permute-start.36 = (bf16[96,768]{1,0:T(8,128)(2,1)}, bf16[96,768]{1,0:T(8,128)(2,1)}, u32[]{:S(2)}, u32[]{:S(2)}) collective-permute-start(bf16[96,768]{1,0:T(8,128)(2,1)} %get-tuple-element.130), channel_id=1, source_target_pairs={{0,16},{1,17},{2,18},{3,19},{4,20},{5,21},{6,22},{7,23},{8,24},{9,... | collective-permute-start | bytes 442376 | tf_op jit(solution)/shard_map/ppermute | solution.py:266
  219.7 14.4 %collective-permute-start.34 = (bf16[8,48,1280]{2,1,0:T(8,128)(2,1)}, bf16[8,48,1280]{2,1,0:T(8,128)(2,1)}, u32[]{:S(2)}, u32[]{:S(2)}) collective-permute-start(bf16[8,48,1280]{2,1,0:T(8,128)(2,1)} %get-tuple-element.107.behind), channel_id=1, source_target_pairs={{0,4},{1,3},{2,6},{3,1},{4,0},{5,7},{6,2},{7,5},{8,12},{9,11},{10,... | collective-permute-start | bytes 2949128 | tf_op jit(solution)/shard_map/ppermute | solution.py:266
  235.8 20.7 %collective-permute-start.38 = (bf16[4,48,1280]{2,1,0:T(8,128)(2,1)S(1)}, bf16[4,48,1280]{2,1,0:T(8,128)(2,1)S(1)}, u32[]{:S(2)}, u32[]{:S(2)}) collective-permute-start(bf16[4,48,1280]{2,1,0:T(8,128)(2,1)S(1)} %get-tuple-element.123), channel_id=1, source_target_pairs={{0,2},{1,5},{2,0},{3,7},{4,6},{5,1},{6,4},{7,3},{8,10},{9,13},{10,... | collective-permute-start | bytes 1474568 | tf_op jit(solution)/shard_map/ppermute | solution.py:266
  237.4 15.6 %collective-permute-start.40 = (bf16[48,1920]{1,0:T(8,128)(2,1)S(1)}, bf16[48,1920]{1,0:T(8,128)(2,1)S(1)}, u32[]{:S(2)}, u32[]{:S(2)}) collective-permute-start(bf16[48,1920]{1,0:T(8,128)(2,1)S(1)} %copy-done.8), channel_id=1, source_target_pairs={{0,16},{1,17},{2,18},{3,19},{4,20},{5,21},{6,22},{7,23},{8,24},{9,... | collective-permute-start | bytes 552968 | tf_op jit(solution)/shard_map/ppermute | solution.py:266
  239.2 13.8 %collective-permute-start.41 = (bf16[48,1920]{1,0:T(8,128)(2,1)S(1)}, bf16[48,1920]{1,0:T(8,128)(2,1)S(1)}, u32[]{:S(2)}, u32[]{:S(2)}) collective-permute-start(bf16[48,1920]{1,0:T(8,128)(2,1)S(1)} %copy-done.7), channel_id=1, source_target_pairs={{0,24},{1,25},{2,26},{3,27},{4,28},{5,29},{6,30},{7,31},{8,16},{9,... | collective-permute-start | bytes 552968 | tf_op jit(solution)/shard_map/ppermute | solution.py:266
  263.5 10.4 %collective-permute-start.46 = (f32[24,1920]{1,0:T(8,128)S(1)}, f32[24,1920]{1,0:T(8,128)S(1)}, u32[]{:S(2)}, u32[]{:S(2)}) collective-permute-start(f32[24,1920]{1,0:T(8,128)S(1)} %copy-done.21), channel_id=1, source_target_pairs={{0,1},{1,0},{2,3},{3,2},{4,5},{5,4},{6,7},{7,6},{8,9},{9,8},{10,11... | collective-permute-start | bytes 552968 | tf_op jit(solution)/shard_map/ppermute | solution.py:266
  (54 other events, 217.5 us)

commit v3 on v2

--- a/solution.py
+++ b/solution.py
@@ -14,7 +14,7 @@
 AXES = ("dp", "fsdp")
 F32 = jnp.float32
 BF16 = jnp.bfloat16
-VMEM_LIMIT = 56 * 1024 * 1024
+VMEM_LIMIT = 32 * 1024 * 1024
 
 
 def collect(qkv_weight, proj_weight, up_weight, down_weight, gains, shifts, up_bias):
@@ -286,8 +286,8 @@
     return jnp.stack(places + [core, length] + spots).astype(jnp.int32)
 
 
-def params():
-    return pltpu.CompilerParams(vmem_limit_bytes=VMEM_LIMIT)
+def params(mib):
+    return pltpu.CompilerParams(vmem_limit_bytes=mib * 1024 * 1024)
 
 
 def cost(micros):
@@ -313,11 +313,12 @@
 
 def fetch(info, pieces, dest, sems, by_half):
     copies = []
+    cols = pl.ds(pieces[0].shape[-1] - dest.shape[-1], dest.shape[-1])
     for who in (0, 1):
         half = info[CORE] if who == 0 else 1 - info[CORE]
         for j in range(16):
             at = info[16 * who + j]
-            src = pieces[2 * who + j // 8].at[j % 8]
+            src = pieces[2 * who + j // 8].at[j % 8, :, cols]
             dst = dest.at[half, at] if by_half else dest.at[at, half]
             copies.append(pltpu.make_async_copy(src, dst, sems.at[16 * who + j]))
     for copy in copies:
@@ -325,6 +326,13 @@
     return copies
 
 
+def settle(info, pieces, dest, cols):
+    for who in (0, 1):
+        half = info[CORE] if who == 0 else 1 - info[CORE]
+        for j in range(16):
+            dest[half, info[16 * who + j]] = pieces[2 * who + j // 8][j % 8, :, cols]
+
+
 def centre(values):
     centred = values - jnp.mean(values, axis=-1, keepdims=True)
     inverse = lax.rsqrt(jnp.mean(centred * centred, axis=-1, keepdims=True) + EPS)
@@ -339,26 +347,25 @@
     )
 
 
-def halves_kernel(info, qkv, proj, up, mine, theirs):
+def halves_kernel(info, qkv, proj, up, mine, theirs, sems):
     feat = proj.shape[1]
     third, wide = feat // 2, up.shape[1] // 2
-
-    def lay(out, h):
+    copies = []
+
+    def copy(src, start, out, at, width):
+        cols = pl.ds(pl.multiple_of(start, 128), width)
+        sem = sems.at[len(copies)]
+        copies.append(pltpu.make_async_copy(src.at[:, cols], out.at[:, pl.ds(at, width)], sem))
+
+    for out, h in ((theirs, 1 - info[CORE]), (mine, info[CORE])):
         for i in range(3):
-            cols = slice(i * feat + h * third, i * feat + (h + 1) * third)
-            out[:, i * third : (i + 1) * third] = qkv[:, cols]
-        out[:, 3 * third : 3 * third + wide] = up[:, h * wide : (h + 1) * wide]
-        out[:, 3 * third + wide :] = proj[:, h * third : (h + 1) * third]
-
-    @pl.when(info[CORE] == 0)
-    def _():
-        lay(mine, 0)
-        lay(theirs, 1)
-
-    @pl.when(info[CORE] == 1)
-    def _():
-        lay(mine, 1)
-        lay(theirs, 0)
+            copy(qkv, i * feat + h * third, out, i * third, third)
+        copy(up, h * wide, out, 3 * third, wide)
+        copy(proj, h * third, out, 3 * third + wide, third)
+    for c in copies:
+        c.start()
+    for c in copies:
+        c.wait()
 
 
 def halves(info, qkv, proj, up):
@@ -369,11 +376,12 @@
     return pl.pallas_call(
         halves_kernel,
         out_shape=(out, out),
-        in_specs=[SMEM] + [vmem] * 3,
+        in_specs=[SMEM] + [ANY] * 3,
         out_specs=(vmem, vmem),
-        compiler_params=params(),
+        scratch_shapes=[pltpu.SemaphoreType.DMA((10,))],
+        compiler_params=params(8),
         name="halves",
-        cost_estimate=cost(2),
+        cost_estimate=cost(0),
     )(info, qkv, proj, up)
 
 
@@ -398,12 +406,15 @@
     vmem = pl.BlockSpec(memory_space=pltpu.VMEM)
     return pl.pallas_call(
         pieces_kernel,
-        out_shape=(shape((1, 2 * rows, one), BF16), shape((1, 2 * rows, width - split), BF16)),
-        in_specs=[SMEM, vmem, vmem, vmem],
-        out_specs=(vmem, vmem),
-        compiler_params=params(),
+        out_shape=(
+            shape((1, 2 * rows, one), BF16),
+            shape((1, 2 * rows, width - split), BF16),
+        ),
+        in_specs=[SMEM] + [vmem] * 3,
+        out_specs=(vmem,) * 2,
+        compiler_params=params(8),
         name="pieces_of",
-        cost_estimate=cost(2),
+        cost_estimate=cost(0),
     )(info, mine, given, small)
 
 
@@ -416,7 +427,7 @@
         at += part.shape[0]
 
 
-def gather(parts, held=(), behind=()):
+def gather(parts, held=(), behind=(), micros=0):
     vmem = pl.BlockSpec(memory_space=pltpu.VMEM)
     _, rows, cols = parts[0].shape
     count = sum(part.shape[0] for part in parts)
@@ -427,9 +438,9 @@
         in_specs=[vmem] * n + [ANY] * (n_held + len(behind)),
         out_specs=(vmem,) + (ANY,) * n_held,
         input_output_aliases={n + i: 1 + i for i in range(n_held)},
-        compiler_params=params(),
+        compiler_params=params(16),
         name="gather",
-        cost_estimate=cost(2),
+        cost_estimate=cost(micros),
     )(*parts, *held, *behind)
 
 
@@ -437,16 +448,16 @@
     pass
 
 
-def gate(array, behind):
+def gate(array, behind, micros=1):
     return pl.pallas_call(
         gate_kernel,
         out_shape=shape(array.shape, array.dtype),
         in_specs=[ANY, ANY],
         out_specs=ANY,
         input_output_aliases={0: 0},
-        compiler_params=params(),
+        compiler_params=params(4),
         name="gate",
-        cost_estimate=cost(1),
+        cost_estimate=cost(micros),
     )(array, behind)
 
 
@@ -455,19 +466,42 @@
 
 
 def enter_kernel(
-    info, tokens, low, high, low_o, high_o, kept, vecs, first, flipped, joint, weights, sems, sem
+    info,
+    tokens,
+    upstream,
+    down,
+    low,
+    high,
+    low_o,
+    high_o,
+    kept,
+    vecs,
+    bias,
+    first,
+    flipped,
+    joint,
+    grad_y,
+    piece_down,
+    weights,
+    sem,
 ):
     feat = tokens.shape[1]
     third = feat // 2
-    copies = fetch(info, (low, high, low_o, high_o), weights, sems, True)
+    piece_down[0] = down[...]
+    place = lax.broadcasted_iota(jnp.int32, upstream.shape, 0)
+    grad_y[...] = jnp.where(place < info[LENGTH], upstream[...].astype(F32), 0.0).astype(BF16)
+    settle(info, (low, high, low_o, high_o), weights, slice(None))
     normed, _ = centre(tokens[...].astype(F32))
-    for copy in copies:
-        copy.wait()
     out = pltpu.make_async_copy(weights, kept, sem)
     out.start()
     split = 3 * third
     small = weights[0, :, :, split:] + weights[1, :, :, split:]
-    small = small.reshape(feat, 128).astype(F32).T
+    small = small.reshape(feat, 128).astype(F32)
+    each = bias.shape[1] // 32
+    for device in range(32):
+        row = device * feat // 32
+        bias[:, device * each : (device + 1) * each] = small[row : row + 1, 128 - each :]
+    small = small.T
     vecs[...] = small[:8]
     low_first = (normed * small[0:1] + small[2:3]).astype(BF16)
     first[...] = low_first
@@ -482,7 +516,7 @@
     out.wait()
 
 
-def enter(info, tokens, pieces):
+def enter(info, tokens, upstream, down, hidden, pieces):
     rows, feat = tokens.shape
     width = pieces[0].shape[-1]
     vmem = pl.BlockSpec(memory_space=pltpu.VMEM)
@@ -492,21 +526,20 @@
         out_shape=(
             shape(sets, BF16),
             shape((8, feat), F32),
+            shape((1, hidden), F32),
             shape((rows, feat), BF16),
             shape((16, feat // 16, rows), BF16),
             shape((2, rows, 3 * feat // 2), BF16),
+            shape((rows, feat), BF16),
+            shape((1,) + down.shape, BF16),
         ),
-        in_specs=[SMEM, vmem] + [ANY] * 4,
-        out_specs=(ANY, vmem, vmem, vmem, vmem),
-        scratch_shapes=[
-            pltpu.VMEM(sets, BF16),
-            pltpu.SemaphoreType.DMA((32,)),
-            pltpu.SemaphoreType.DMA,
-        ],
-        compiler_params=params(),
+        in_specs=[SMEM] + [vmem] * 7,
+        out_specs=(ANY,) + (vmem,) * 7,
+        scratch_shapes=[pltpu.VMEM(sets, BF16), pltpu.SemaphoreType.DMA],
+        compiler_params=params(20),
         name="enter",
         cost_estimate=cost(8),
-    )(info, tokens, *pieces)
+    )(info, tokens, upstream, down, *pieces)
 
 
 def scores_of(info, keys, queries):
@@ -557,7 +590,7 @@
             pl.BlockSpec((pair, rows), lambda i: (i, 0)),
             pl.BlockSpec((1, 8, rows), lambda i: (i, 0, 0)),
         ),
-        compiler_params=params(),
+        compiler_params=params(12),
         name="mix",
         cost_estimate=cost(10),
     )(info, joint, joint, joint, behind)
@@ -632,7 +665,7 @@
             ),
         ),
         out_shape=(out, out),
-        compiler_params=params(),
+        compiler_params=params(12),
         name="mix_back",
         cost_estimate=cost(16),
     )(info, joint, joint, joint, grad_mixed, stats, behind)
@@ -655,55 +688,69 @@
 
 
 def rise_kernel(
+    info, tokens, mixed, vecs, low, high, low_o, high_o, _, after, second, flipped, weights
+):
+    feat = tokens.shape[1]
+    wide = low.shape[2] - feat // 2
+    settle(info, (low, high, low_o, high_o), weights, slice(wide, None))
+    start = tokens[...].astype(F32) + vecs[5:6]
+    grown = [dot(mixed[...], weights[h].reshape(feat, feat // 2)) for h in (0, 1)]
+    total = start + jnp.concatenate(grown, axis=1)
+    after[...] = total
+    normed, _ = centre(total)
+    value = (normed * vecs[1:2] + vecs[6:7]).astype(BF16)
+    second[...] = value
+    flipped[...] = value.T.reshape(flipped.shape)
+
+
+def rise(info, tokens, mixed, vecs, pieces, behind):
+    rows, feat = tokens.shape
+    vmem = pl.BlockSpec(memory_space=pltpu.VMEM)
+    return pl.pallas_call(
+        rise_kernel,
+        out_shape=(
+            shape((rows, feat), F32),
+            shape((rows, feat), BF16),
+            shape((16, feat // 16, rows), BF16),
+        ),
+        in_specs=[SMEM] + [vmem] * 7 + [ANY],
+        out_specs=(vmem,) * 3,
+        scratch_shapes=[pltpu.VMEM((2, 16, feat // 16, feat // 2), BF16)],
+        compiler_params=params(20),
+        name="rise",
+        cost_estimate=cost(5),
+    )(info, tokens, mixed, vecs, *pieces, behind)
+
+
+def widen_kernel(
     info,
-    tokens,
-    mixed,
-    vecs,
+    second,
     bias,
     low,
     high,
     low_o,
     high_o,
     _,
-    kept,
-    after,
-    second,
-    flipped,
+    weights,
     active,
     slope,
     mine,
     theirs,
-    weights,
     turned,
-    sems,
     block_sems,
-    sem,
 ):
     step, steps = pl.program_id(0), pl.num_programs(0)
     core = info[CORE]
-    feat = tokens.shape[1]
+    feat = second.shape[1]
     tile = active.shape[1]
     wide = weights.shape[-1] - feat // 2
     per = wide // tile
     rows = mine.shape[1]
     count = tile // rows
-    keeping = pltpu.make_async_copy(weights, kept, sem)
 
     @pl.when(step == 0)
     def _():
-        copies = fetch(info, (low, high, low_o, high_o), weights, sems, True)
-        for copy in copies:
-            copy.wait()
-        keeping.start()
-        grown = [
-            dot(mixed[...], weights[h, :, :, wide:].reshape(feat, feat // 2)) for h in (0, 1)
-        ]
-        total = tokens[...].astype(F32) + jnp.concatenate(grown, axis=1) + vecs[5:6]
-        after[...] = total
-        normed, _ = centre(total)
-        value = (normed * vecs[1:2] + vecs[6:7]).astype(BF16)
-        second[...] = value
-        flipped[...] = value.T.reshape(flipped.shape)
+        settle(info, (low, high, low_o, high_o), weights, slice(None))
 
     cols = pl.ds(pl.multiple_of(lax.rem(step, per) * tile, tile), tile)
     w = weights[step // per, :, :, cols].reshape(feat, tile)
@@ -731,11 +778,10 @@
     def _():
         for at in range(turned.shape[0]):
             pltpu.make_async_copy(turned.at[at], mine.at[0], block_sems.at[at]).wait()
-        keeping.wait()
-
-
-def rise(info, tokens, mixed, vecs, bias, pieces, behind):
-    rows, feat = tokens.shape
+
+
+def widen(info, second, bias, pieces, behind):
+    rows, feat = second.shape
     width = pieces[0].shape[-1]
     hidden = 2 * width - feat
     tile, block = 768, hidden // 32
@@ -743,47 +789,24 @@
     sets = (2, 16, feat // 16, width)
     strip = pl.BlockSpec((rows, tile), lambda n: (0, n))
     return pl.pallas_call(
-        rise_kernel,
+        widen_kernel,
         grid=(hidden // tile,),
         out_shape=(
             shape(sets, BF16),
-            shape((rows, feat), F32),
-            shape((rows, feat), BF16),
-            shape((16, feat // 16, rows), BF16),
             shape((rows, hidden), BF16),
             shape((rows, hidden), BF16),
             turned,
             turned,
         ),
-        in_specs=[
-            SMEM,
-            full((rows, feat)),
-            full((rows, feat)),
-            full((8, feat)),
-            pl.BlockSpec((1, tile), lambda n: (0, n)),
-        ]
-        + [ANY] * 5,
-        out_specs=(
-            ANY,
-            full((rows, feat)),
-            full((rows, feat)),
-            full((16, feat // 16, rows)),
-            strip,
-            strip,
-            ANY,
-            ANY,
-        ),
-        scratch_shapes=[
-            pltpu.VMEM(sets, BF16),
-            pltpu.VMEM((32, block, rows), BF16),
-            pltpu.SemaphoreType.DMA((32,)),
-            pltpu.SemaphoreType.DMA((32,)),
-            pltpu.SemaphoreType.DMA,
-        ],
-        compiler_params=params(),
-        name="rise",
+        in_specs=[SMEM, full((rows, feat)), pl.BlockSpec((1, tile), lambda n: (0, n))]
+        + [full(pieces[0].shape)] * 4
+        + [ANY],
+        out_specs=(full(sets), strip, strip, ANY, ANY),
+        scratch_shapes=[pltpu.VMEM((32, block, rows), BF16), pltpu.SemaphoreType.DMA((32,))],
+        compiler_params=params(30),
+        name="widen",
         cost_estimate=cost(18),
-    )(info, tokens, mixed, vecs, bias, *pieces, behind)
+    )(info, second, bias, *pieces, behind)
 
 
 def leave_kernel(after, active, down, vecs, _, output, total):
@@ -820,7 +843,7 @@
         ],
         out_specs=full((rows, feat)),
         scratch_shapes=[pltpu.VMEM((rows, feat), F32)],
-        compiler_params=params(),
+        compiler_params=params(16),
         name="leave",
         cost_estimate=cost(7),
     )(after, active, down, vecs, behind)
@@ -838,6 +861,9 @@
     high,
     low_o,
     high_o,
+    _,
+    __,
+    ___,
     kept,
     theirs,
     mine,
@@ -902,7 +928,7 @@
         keeping.wait()
 
 
-def fall(info, grad_y, slope, up_set, after, vecs, pieces):
+def fall(info, grad_y, slope, up_set, after, vecs, pieces, behind):
     rows, feat = grad_y.shape
     hidden = slope.shape[1]
     tile = 768
@@ -930,7 +956,7 @@
                 whole((8, feat)),
                 pl.BlockSpec((2, feat, feat // 2), lambda n, info: (0, 0, 4)),
             ]
-            + [ANY] * 4,
+            + [ANY] * 7,
             out_specs=(
                 ANY,
                 pl.BlockSpec((rows, tile), lambda n, info: (0, jnp.minimum(n, per - 1))),
@@ -960,14 +986,30 @@
             shape((rows, feat), BF16),
             shape((8, feat), F32),
         ),
-        compiler_params=params(),
+        compiler_params=params(28),
         name="fall",
         cost_estimate=cost(18),
-    )(info, grad_y, slope, up_set, after, vecs, up_set, *pieces)
+    )(info, grad_y, slope, up_set, after, vecs, up_set, *pieces, *behind)
 
 
 def exit_kernel(
-    info, tokens, mine, theirs, weights, grad_after, vecs, _, grad_tokens, sums, grad_first, joint
+    info,
+    tokens,
+    mine,
+    theirs,
+    weights,
+    grad_after,
+    vecs,
+    sums_a,
+    bias,
+    _,
+    grad_tokens,
+    keep,
+    away,
+    grad_first,
+    joint,
+    sums,
+    extra,
 ):
     step = pl.program_id(0)
     core = info[CORE]
@@ -978,8 +1020,8 @@
     def parts(source):
         for part in range(3):
             joint[:, part * third : (part + 1) * third] = source[part]
-        sums[2:3, spot] = jnp.sum(source[0].astype(F32), axis=0, keepdims=True)
-        sums[3:4, spot] = jnp.sum(source[2].astype(F32), axis=0, keepdims=True)
+        sums[3:4, spot] = jnp.sum(source[0].astype(F32), axis=0, keepdims=True)
+        sums[4:5, spot] = jnp.sum(source[2].astype(F32), axis=0, keepdims=True)
         return dot_last(joint[...], weights[0])
 
     @pl.when(step == 0)
@@ -991,15 +1033,31 @@
         grad = grad_first[...] + parts(theirs)
         normed, inverse = centre(tokens[...].astype(F32))
         sums[0:1] = jnp.sum(grad * normed, axis=0, keepdims=True)
-        sums[1:2] = jnp.sum(grad, axis=0, keepdims=True)
-        sums[4:8] = jnp.zeros_like(sums[4:8])
+        sums[1:2] = sums_a[0:1]
+        sums[2:3] = jnp.sum(grad, axis=0, keepdims=True)
+        sums[5:6] = sums_a[2:3]
+        sums[6:7] = sums_a[1:2]
+        sums[7:8] = sums_a[3:4]
+        sums[8:] = jnp.zeros_like(sums[8:])
         back = layer_back(grad * vecs[0:1], normed, inverse)
         grad_tokens[...] = (grad_after[...] + back).astype(BF16)
-
-
-def exit_back(info, tokens, mine, theirs, first_set, grad_after, vecs, behind):
+        flipped = sums[...].T
+        block, each = extra.shape[1], bias.shape[1] // 32
+        for chip in range(16):
+            place = info[PLACE + chip]
+            extra[place] = flipped[chip * block : (chip + 1) * block]
+            for c in (0, 1):
+                at = (2 * chip + c) * each
+                row = c * block // 2
+                extra[place, row : row + 1, 128 - each :] = bias[:, at : at + each]
+        keep[...] = extra[:8]
+        away[...] = extra[8:].astype(BF16)
+
+
+def exit_back(info, tokens, mine, theirs, first_set, grad_after, vecs, sums_a, bias, behind):
     rows, feat = tokens.shape
     third = feat // 2
+    block = feat // 16
 
     def whole(dims):
         return pl.BlockSpec(dims, lambda n, info: (0,) * len(dims))
@@ -1019,16 +1077,27 @@
                 ),
                 whole((rows, feat)),
                 whole((8, feat)),
+                whole((8, feat)),
+                whole(bias.shape),
                 ANY,
             ],
-            out_specs=(whole((rows, feat)), whole((8, feat))),
-            scratch_shapes=[pltpu.VMEM((rows, feat), F32), pltpu.VMEM((rows, 3 * third), BF16)],
+            out_specs=(whole((rows, feat)), whole((8, block, 128)), whole((8, block, 128))),
+            scratch_shapes=[
+                pltpu.VMEM((rows, feat), F32),
+                pltpu.VMEM((rows, 3 * third), BF16),
+                pltpu.VMEM((128, feat), F32),
+                pltpu.VMEM((16, block, 128), F32),
+            ],
         ),
-        out_shape=(shape((rows, feat), BF16), shape((8, feat), F32)),
-        compiler_params=params(),
+        out_shape=(
+            shape((rows, feat), BF16),
+            shape((8, block, 128), F32),
+            shape((8, block, 128), BF16),
+        ),
+        compiler_params=params(18),
         name="exit_back",
         cost_estimate=cost(8),
-    )(info, tokens, mine, theirs, first_set, grad_after, vecs, behind)
+    )(info, tokens, mine, theirs, first_set, grad_after, vecs, sums_a, bias, behind)
 
 
 def line_up(info, left, left_o, turned):
@@ -1088,62 +1157,36 @@
         + [ANY],
         out_specs=(out, out),
         scratch_shapes=[pltpu.VMEM((16, block, 2 * rows), BF16)],
-        compiler_params=params(),
+        compiler_params=params(20),
         name="outer_up",
         cost_estimate=cost(8),
     )(info, left, left_o, right, right_o, low, low_o, attn, attn_o, behind)
 
 
-def outer_qkv_kernel(
-    info, left, left_o, right, right_o, sums_a, sums_b, bias, _, keep, away, turned, extra
-):
-    feat, tile = sums_a.shape[1], right.shape[2]
-    block = feat // 16
+def outer_qkv_kernel(info, left, left_o, right, right_o, _, keep, away, turned):
+    tile = right.shape[2]
     line_up(info, left, left_o, turned)
     for part in range(3):
         cols = slice(part * tile, (part + 1) * tile)
         total = outer_tile(turned, right[part], right_o[part])
         keep[:, :, cols] = total[:8]
         away[:, :, cols] = total[8:].astype(BF16)
-    ordered = [
-        sums_b[0:1],
-        sums_a[0:1],
-        sums_b[1:4],
-        sums_a[2:3],
-        sums_a[1:2],
-        sums_a[3:4],
-        jnp.zeros((120, feat), F32),
-    ]
-    flipped = jnp.concatenate(ordered).T
-    each = bias.shape[1] // 32
-    for chip in range(16):
-        place = info[PLACE + chip]
-        extra[place] = flipped[chip * block : (chip + 1) * block]
-        for core in (0, 1):
-            at = (2 * chip + core) * each
-            row = core * block // 2
-            extra[place, row : row + 1, 128 - each :] = bias[:, at : at + each]
-    keep[:, :, 3 * tile :] = extra[:8]
-    away[:, :, 3 * tile :] = extra[8:].astype(BF16)
-
-
-def outer_qkv(info, left, left_o, right, right_o, sums_a, sums_b, bias, behind):
+
+
+def outer_qkv(info, left, left_o, right, right_o, behind):
     _, block, rows = left.shape
-    cols = 3 * right.shape[2] + 128
+    cols = 3 * right.shape[2]
     vmem = pl.BlockSpec(memory_space=pltpu.VMEM)
     return pl.pallas_call(
         outer_qkv_kernel,
         out_shape=(shape((8, block, cols), F32), shape((8, block, cols), BF16)),
-        in_specs=[SMEM] + [vmem] * 7 + [ANY],
+        in_specs=[SMEM] + [vmem] * 4 + [ANY],
         out_specs=(vmem, vmem),
-        scratch_shapes=[
-            pltpu.VMEM((16, block, 2 * rows), BF16),
-            pltpu.VMEM((16, block, 128), F32),
-        ],
-        compiler_params=params(),
+        scratch_shapes=[pltpu.VMEM((16, block, 2 * rows), BF16)],
+        compiler_params=params(20),
         name="outer_qkv",
         cost_estimate=cost(8),
-    )(info, left, left_o, right, right_o, sums_a, sums_b, bias, behind)
+    )(info, left, left_o, right, right_o, behind)
 
 
 def outer_down_kernel(left, left_o, right, right_o, _, keep, away):
@@ -1175,23 +1218,99 @@
             pl.BlockSpec((4, block, feat), lambda j: (jnp.maximum(j - 2, 0), 0, 0)),
             pl.BlockSpec((4, block, feat), lambda j: (jnp.minimum(j, 1), 0, 0)),
         ),
-        compiler_params=params(),
+        compiler_params=params(16),
         name="outer_down",
         cost_estimate=cost(8),
     )(left, left_o, right, right_o, behind)
 
 
+def add_first_kernel(keep, got, _, kept, away):
+    kept[...] = keep[:4] + got[:4].astype(F32)
+    away[...] = (keep[4:] + got[4:].astype(F32)).astype(BF16)
+
+
+def shift_first(keep, away, behind, micros=0):
+    _, rows, cols = keep.shape
+    vmem = pl.BlockSpec(memory_space=pltpu.VMEM)
+    return pl.pallas_call(
+        add_first_kernel,
+        out_shape=(shape((4, rows, cols), F32), shape((4, rows, cols), BF16)),
+        in_specs=[vmem, vmem, ANY],
+        out_specs=(vmem, vmem),
+        compiler_params=params(12),
+        name="shift_first",
+        cost_estimate=cost(micros),
+    )(keep, send(away, second_way), behind)
+
+
+def add_both_kernel(keep, got, few_keep, few_got, _, kept, away):
+    split = keep.shape[2]
+    kept[:, :, :split] = keep[:4] + got[:4].astype(F32)
+    kept[:, :, split:] = few_keep[:4] + few_got[:4].astype(F32)
+    away[:, :, :split] = (keep[4:] + got[4:].astype(F32)).astype(BF16)
+    away[:, :, split:] = (few_keep[4:] + few_got[4:].astype(F32)).astype(BF16)
+
+
+def shift_both(keep, away, few_keep, few_away, behind):
+    _, rows, cols = keep.shape
+    cols += few_keep.shape[2]
+    vmem = pl.BlockSpec(memory_space=pltpu.VMEM)
+    return pl.pallas_call(
+        add_both_kernel,
+        out_shape=(shape((4, rows, cols), F32), shape((4, rows, cols), BF16)),
+        in_specs=[vmem] * 4 + [ANY],
+        out_specs=(vmem, vmem),
+        compiler_params=params(12),
+        name="shift_both",
+        cost_estimate=cost(0),
+    )(keep, send(away, second_way), few_keep, send(few_away, second_way), behind)
+
+
+def add_second_kernel(keep, got, _, base, one, two, three):
+    base[...] = keep[0] + got[0].astype(F32)
+    for s, out in ((1, one), (2, two), (3, three)):
+        out[...] = (keep[s] + got[s].astype(F32)).astype(BF16)
+
+
+def shift_second(keep, away, behind):
+    _, rows, cols = keep.shape
+    vmem = pl.BlockSpec(memory_space=pltpu.VMEM)
+    base, *lows = pl.pallas_call(
+        add_second_kernel,
+        out_shape=(shape((rows, cols), F32),) + (shape((rows, cols), BF16),) * 3,
+        in_specs=[vmem, vmem, ANY],
+        out_specs=(vmem,) * 4,
+        compiler_params=params(8),
+        name="shift_second",
+        cost_estimate=cost(0),
+    )(keep, send(away, first_way), behind)
+    return base, [send(low, along_z(s)) for low, s in zip(lows, (1, 2, 3))]
+
+
 def total_of(base, parts):
     return base[...] + parts[0][...].astype(F32) + (
         parts[1][...].astype(F32) + parts[2][...].astype(F32)
     )
 
 
-def add_down_kernel(base, one, two, three, out):
+def add_down_kernel(base, one, two, three, _, out):
     out[...] = total_of(base, (one, two, three))
 
 
-def add_last_kernel(info, base, one, two, three, mine, theirs, total):
+def home_down(base, parts, behind):
+    vmem = pl.BlockSpec(memory_space=pltpu.VMEM)
+    return pl.pallas_call(
+        add_down_kernel,
+        out_shape=shape(base.shape, F32),
+        in_specs=[vmem] * 4 + [ANY],
+        out_specs=vmem,
+        compiler_params=params(8),
+        name="home_down",
+        cost_estimate=cost(0),
+    )(base, *parts, behind)
+
+
+def add_last_kernel(info, base, one, two, three, _, mine, theirs, total):
     core = info[CORE]
     half = mine.shape[0]
     total[...] = total_of(base, (one, two, three))
@@ -1199,44 +1318,20 @@
     theirs[...] = total[pl.ds(pl.multiple_of((1 - core) * half, half), half)]
 
 
-def shift_first(keep, away, behind):
-    got = gate(send(away, second_way), behind)
-    return keep[:4] + got[:4].astype(F32), (keep[4:] + got[4:].astype(F32)).astype(BF16)
-
-
-def shift_second(keep, away, behind):
-    got = gate(send(away, first_way), behind)
-    lows = [(keep[s] + got[s].astype(F32)).astype(BF16) for s in (1, 2, 3)]
-    return keep[0] + got[0].astype(F32), [send(low, along_z(s)) for low, s in zip(lows, (1, 2, 3))]
-
-
-def home_down(base, parts):
-    vmem = pl.BlockSpec(memory_space=pltpu.VMEM)
-    return pl.pallas_call(
-        add_down_kernel,
-        out_shape=shape(base.shape, F32),
-        in_specs=[vmem] * 4,
-        out_specs=vmem,
-        compiler_params=params(),
-        name="home_down",
-        cost_estimate=cost(2),
-    )(base, *parts)
-
-
-def home(info, base, parts):
+def home(info, base, parts, behind):
     rows, cols = base.shape
     vmem = pl.BlockSpec(memory_space=pltpu.VMEM)
     out = shape((rows // 2, cols), F32)
     mine, theirs = pl.pallas_call(
         add_last_kernel,
         out_shape=(out, out),
-        in_specs=[SMEM] + [vmem] * 4,
+        in_specs=[SMEM] + [vmem] * 4 + [ANY],
         out_specs=(vmem, vmem),
         scratch_shapes=[pltpu.VMEM((rows, cols), F32)],
-        compiler_params=params(),
+        compiler_params=params(8),
         name="home",
-        cost_estimate=cost(2),
-    )(info, base, *parts)
+        cost_estimate=cost(0),
+    )(info, base, *parts, behind)
     return mine, swap(theirs)
 
 
@@ -1282,9 +1377,9 @@
         ),
         in_specs=[SMEM] + [vmem] * 4,
         out_specs=(vmem,) * 6,
-        compiler_params=params(),
+        compiler_params=params(8),
         name="finish",
-        cost_estimate=cost(2),
+        cost_estimate=cost(0),
     )(info, qkv, qkv_o, up, up_o)
 
 
@@ -1307,69 +1402,68 @@
     chip, core = lax.axis_index("dp"), lax.axis_index("fsdp")
     info = facts(chip, core, lengths[0])
 
-    live = lax.iota(jnp.int32, tok_rows) < lengths[0]
-    grad_y = jnp.where(live[:, None], upstream, jnp.zeros_like(upstream))
-
-    down = down_weight[None]
-    down_z = near_z(down, (1, 2))
-    small = jnp.concatenate([gains, shifts, up_bias.reshape(rows, -1)], axis=1)
+    small = jnp.concatenate([gains, shifts], axis=1)
     small = jnp.pad(small, ((0, 0), (0, 128 - small.shape[1])))
+    small = small + jnp.pad(up_bias[None], ((0, rows - 1), (128 - up_bias.shape[0], 0)))
     mine, theirs = halves(info, qkv_weight, proj_weight, up_weight)
     one = 3 * third + 128
     piece, piece_up = pieces_of(info, mine, swap(theirs), small, 3 * third)
-    zs, piece_up = gather([piece] + near_z(piece, (1, 2, 3)), (piece_up,), down_z)
+    zs, piece_up = gather([piece] + near_z(piece, (1, 2, 3)), (piece_up,))
     up_z = near_z(piece_up, (1, 2))
     low, piece_up = gather([zs, send(zs, first_way)], (piece_up,), up_z)
     up_z += near_z(piece_up, (3,))
     high = send(low, second_way)
-    zs_up, down = gather([piece_up] + up_z, (down,))
+    (zs_up,) = gather([piece_up] + up_z)
     high = gate(high, zs_up)
     first_pieces = (low, high, swap(low), swap(high))
+
+    first_set, vecs, bias, first, first_t, joint, grad_y, down = enter(
+        info, tokens, upstream, down_weight, hidden, first_pieces
+    )
     grad_y_o = swap(grad_y)
-    down_z += near_z(down, (3,))
-
-    first_set, vecs, first, first_t, joint = enter(info, tokens, first_pieces)
-    bias = first_set[0, :, :, one - 120 : one - 116] + first_set[1, :, :, one - 120 : one - 116]
-    bias = bias.reshape(1, hidden).astype(F32)
     first_set = first_set.reshape(2, feat, one)
     first_o = swap(first_t)
-    (low,) = gather([zs_up, send(zs_up, first_way)], (), (first,))
-    (zs_down,) = gather([down] + down_z, (), (low,))
-    mixed, mixed_t, stats = mix(info, joint, zs_down)
+    (low,) = gather([zs_up, send(zs_up, first_way)], (), (vecs,))
+    down_z = near_z(down, (1, 2, 3))
+    mixed, mixed_t, stats = mix(info, joint, low)
     high = gate(send(low, second_way), mixed)
     up_pieces = (low, high, swap(low), swap(high))
+    (zs_down,) = gather([down] + down_z, (), (high,), 5)
     mixed_t = mixed_t.reshape(first_t.shape)
     mixed_o = swap(mixed_t)
-    (low,) = gather([zs_down, send(zs_down, first_way)], (), (mixed,))
-    up_set, after, second, second_t, active, slope, turned, turned_t = rise(
-        info, tokens, mixed, vecs, bias, up_pieces, low
-    )
+    after, second, second_t = rise(info, tokens, mixed, vecs, up_pieces, zs_down)
+    second_o = swap(second_t)
+    (low,) = gather([zs_down, send(zs_down, first_way)], (), (second,))
+    up_set, active, slope, turned, turned_t = widen(info, second, bias, up_pieces, low)
     up_set = up_set.reshape(2, feat, wide + third)
-    high = gate(send(low, second_way), second)
+    high = gate(send(low, second_way), slope, 5)
     down_pieces = (low, high, swap(low), swap(high))
-    second_o, turned_o = swap(second_t), swap(turned_t)
+    down = outer_down(turned, swap(turned_t), grad_y, grad_y_o, slope)
     down_set, hid_theirs, hid_mine, bias_sum, grad_after, at_theirs, at_mine, grad_mixed, sums_a = (
-        fall(info, grad_y, slope, up_set, after, vecs, down_pieces)
+        fall(
+            info, grad_y, slope, up_set, after, vecs, down_pieces, (down[1], second_o, mixed_o)
+        )
     )
     hid_o, at_o = swap(hid_theirs), swap(at_theirs)
-    down = outer_down(turned, turned_o, grad_y, grad_y_o, hid_theirs)
+    down = shift_first(*down, hid_theirs, 5)
     up = outer_up(
         info, second_t, second_o, hid_mine, hid_o, mixed_t, mixed_o, at_mine, at_o, down[1]
     )
-    theirs, mine = mix_back(info, joint, grad_mixed, stats, up[1])
+    down = shift_second(*down, up[1])
+    theirs, mine = mix_back(info, joint, grad_mixed, stats, down[0])
     theirs_o = swap(theirs)
-    down = shift_first(*down, theirs)
-    up = shift_first(*up, down[1])
-    grad_tokens, sums_b = exit_back(info, tokens, mine, theirs, first_set, grad_after, vecs, up[1])
-    down = shift_second(*down, grad_tokens)
-    qkv = outer_qkv(info, first_t, first_o, mine, theirs_o, sums_a, sums_b, bias_sum, down[0])
-    up = shift_second(*up, qkv[1])
-    output = leave(after, active, down_set.reshape(hidden, feat), vecs, up[0])
-    base, parts = down
-    own_down = home_down(base, parts[:2] + [gate(parts[2], output)])
-    qkv = shift_first(*qkv, own_down)
-    own_up = home(info, *up)
-    own_qkv = home(info, *shift_second(*qkv, own_up[0]))
+    own_down = home_down(*down, theirs)
+    up = shift_first(*up, own_down, 5)
+    qkv = outer_qkv(info, first_t, first_o, mine, theirs_o, up[1])
+    grad_tokens, few_keep, few_away = exit_back(
+        info, tokens, mine, theirs, first_set, grad_after, vecs, sums_a, bias_sum, qkv[1]
+    )
+    up = shift_second(*up, grad_tokens)
+    qkv = shift_both(*qkv, few_keep, few_away, up[0])
+    output = leave(after, active, down_set.reshape(hidden, feat), vecs, qkv[1])
+    base, parts = shift_second(*qkv, output)
+    own_up = home(info, *up, base)
+    own_qkv = home(info, base, parts, own_up[0])
     out_qkv, out_proj, out_up, out_gains, out_shifts, out_bias = finish(info, *own_qkv, *own_up)
     return (
         output,

time: 279 us -> 237 us (0.85)
  other arithmetic: 16 us -> 1.42 us
  local copies, waits for them, and re-layouts: 20.7 us -> 9.28 us
  waiting for transfers between devices: 64.1 us -> 52.9 us
  Pallas kernels: 130 us -> 125 us
    pallas_call x2 -> x9, Pallas kernels: 19.8 us -> 33.6 us  [the longest x1 15.3 us: widen(): pl.pallas_call(widen_kernel, grid=(hidden // tile,), out_shape=(shape(set...]
    convert_element_type x6 -> x0, other arithmetic: 11.6 us -> none  [the longest x3 6.07 us: shift_second(): lows = [(keep[s] + got[s].astype(F32)).astype(BF16) for s in (1, 2, 3)]]
    ppermute x47 -> x48, waiting for transfers between devices: 64.1 us -> 52.9 us  [send(): return lax.ppermute(array, AXES, pairs(move))]
    unnamed x81 -> x54, local copies, waits for them, and re-layouts: 19.1 us -> 9.05 us
    pallas_call x6, Pallas kernels: 13.1 us -> 8.06 us  [gather(): pl.pallas_call(partial(gather_kernel, n, n_held + len(behind)), out_shape...]
    ppermute x47 -> x48, starting transfers between devices: 45.3 us -> 45.7 us  [send(): return lax.ppermute(array, AXES, pairs(move))]
  transfers between devices with their start and end apart: 47 -> 48, of which waited for: 16 -> 18; matrix products, arithmetic and copies ran while one was open for 5% -> 1% of each run, Pallas kernels for 44% -> 51%
where the time goes in v3:
time: 237 us
  Pallas kernels  125 us (53%)
  waiting for transfers between devices  52.9 us (22%)
  starting transfers between devices  45.7 us (19%)
  local copies, waits for them, and re-layouts  9.28 us (4%)
    ppermute x48, waiting for transfers between devices, send(): return lax.ppermute(array, AXES, pairs(move))  52.9 us
    ppermute x48, starting transfers between devices, send(): return lax.ppermute(array, AXES, pairs(move))  45.7 us
    pallas_call x1, Pallas kernels, fall(): pl.pallas_call(fall_kernel, grid_spec=pltpu.PrefetchScalarGridSpec(num_sc...  15.7 us
    pallas_call x1, Pallas kernels, mix_back(): pl.pallas_call(mix_back_kernel, grid_spec=pltpu.PrefetchScalarGridSpec(nu...  15.5 us
    pallas_call x1, Pallas kernels, widen(): pl.pallas_call(widen_kernel, grid=(hidden // tile,), out_shape=(shape(set...  15.3 us
    pallas_call x1, Pallas kernels, mix(): pl.pallas_call(mix_kernel, grid=(n,), out_shape=(shape((rows, feat), BF16...  10.2 us
    unnamed x54, local copies, waits for them, and re-layouts  9.05 us
    pallas_call x6, Pallas kernels, gather(): pl.pallas_call(partial(gather_kernel, n, n_held + len(behind)), out_shape...  8.06 us
  transfers between devices with their start and end apart: 48, of which 18 were waited for; matrix products, arithmetic and copies ran while one was open for 1% of the time, Pallas kernels for 51%

profile of v3, /device:TPU:0, one launch (start us, length us, event | category | flops | bytes accessed | tf_op | source)
XLA Modules:
  0.0 236.5 jit_solution(5850617919406473189)
XLA Ops:
  7.9 2.7 %collective-permute-start.1 = (bf16[1,48,1280]{2,1,0:T(8,128)(2,1)S(1)}, bf16[1,48,1280]{2,1,0:T(8,128)(2,1)S(1)}, u32[]{:S(2)}, u32[]{:S(2)}) collective-permute-start(bf16[1,48,1280]{2,1,0:T(8,128)(2,1)S(1)} %get-tuple-element.85.refs_0_), channel_id=1, source_target_pairs={{0,8},{1,9},{2,10},{3,11},{4,12},{5,13},{6,14},{7,15},{8,0},{9,1},... | collective-permute-start | bytes 368648 | tf_op jit(solution)/shard_map/ppermute | solution.py:266
  10.5 2.6 %collective-permute-start.2 = (bf16[1,48,1280]{2,1,0:T(8,128)(2,1)S(1)}, bf16[1,48,1280]{2,1,0:T(8,128)(2,1)S(1)}, u32[]{:S(2)}, u32[]{:S(2)}) collective-permute-start(bf16[1,48,1280]{2,1,0:T(8,128)(2,1)S(1)} %get-tuple-element.85.refs_0_), channel_id=1, source_target_pairs={{0,16},{1,17},{2,18},{3,19},{4,20},{5,21},{6,22},{7,23},{8,24},{9,... | collective-permute-start | bytes 368648 | tf_op jit(solution)/shard_map/ppermute | solution.py:266
  13.1 3.4 %collective-permute-done.1.refs_1_ = bf16[1,48,1280]{2,1,0:T(8,128)(2,1)S(1)} collective-permute-done((bf16[1,48,1280]{2,1,0:T(8,128)(2,1)S(1)}, bf16[1,48,1280]{2,1,0:T(8,128)(2,1)S(1)}, u32[]{:S(2)}, u32[]{:S(2)}) %collective-permute-start.1) | collective-permute-done | bytes 122912 | tf_op jit(solution)/shard_map/ppermute | solution.py:266
  16.5 6.4 %collective-permute-done.2.refs_2_ = bf16[1,48,1280]{2,1,0:T(8,128)(2,1)S(1)} collective-permute-done((bf16[1,48,1280]{2,1,0:T(8,128)(2,1)S(1)}, bf16[1,48,1280]{2,1,0:T(8,128)(2,1)S(1)}, u32[]{:S(2)}, u32[]{:S(2)}) %collective-permute-start.2) | collective-permute-done | bytes 122912 | tf_op jit(solution)/shard_map/ppermute | solution.py:266
  24.5 2.5 %collective-permute-start.5 = (bf16[1,48,1920]{2,1,0:T(8,128)(2,1)S(1)}, bf16[1,48,1920]{2,1,0:T(8,128)(2,1)S(1)}, u32[]{:S(2)}, u32[]{:S(2)}) collective-permute-start(bf16[1,48,1920]{2,1,0:T(8,128)(2,1)S(1)} %get-tuple-element.88.refs_2_), channel_id=1, source_target_pairs={{0,8},{1,9},{2,10},{3,11},{4,12},{5,13},{6,14},{7,15},{8,0},{9,1},... | collective-permute-start | bytes 552968 | tf_op jit(solution)/shard_map/ppermute | solution.py:266
  28.0 6.3 %collective-permute-done.5.refs_3_.refs_1_ = bf16[1,48,1920]{2,1,0:T(8,128)(2,1)S(1)} collective-permute-done((bf16[1,48,1920]{2,1,0:T(8,128)(2,1)S(1)}, bf16[1,48,1920]{2,1,0:T(8,128)(2,1)S(1)}, u32[]{:S(2)}, u32[]{:S(2)}) %collective-permute-start.5) | collective-permute-done | bytes 184352 | tf_op jit(solution)/shard_map/ppermute | solution.py:266
  34.3 3.0 %collective-permute-done.6.refs_4_.refs_2_ = bf16[1,48,1920]{2,1,0:T(8,128)(2,1)S(1)} collective-permute-done((bf16[1,48,1920]{2,1,0:T(8,128)(2,1)S(1)}, bf16[1,48,1920]{2,1,0:T(8,128)(2,1)S(1)}, u32[]{:S(2)}, u32[]{:S(2)}) %collective-permute-start.6) | collective-permute-done | bytes 184352 | tf_op jit(solution)/shard_map/ppermute | solution.py:266
  37.9 2.4 %collective-permute-start.8 = (bf16[1,48,1920]{2,1,0:T(8,128)(2,1)S(1)}, bf16[1,48,1920]{2,1,0:T(8,128)(2,1)S(1)}, u32[]{:S(2)}, u32[]{:S(2)}) collective-permute-start(bf16[1,48,1920]{2,1,0:T(8,128)(2,1)S(1)} %get-tuple-element.90.refs_0_), channel_id=1, source_target_pairs={{0,24},{1,25},{2,26},{3,27},{4,28},{5,29},{6,30},{7,31},{8,16},{9,... | collective-permute-start | bytes 552968 | tf_op jit(solution)/shard_map/ppermute | solution.py:266
  40.3 4.9 %collective-permute-done.8.refs_3_ = bf16[1,48,1920]{2,1,0:T(8,128)(2,1)S(1)} collective-permute-done((bf16[1,48,1920]{2,1,0:T(8,128)(2,1)S(1)}, bf16[1,48,1920]{2,1,0:T(8,128)(2,1)S(1)}, u32[]{:S(2)}, u32[]{:S(2)}) %collective-permute-start.8) | collective-permute-done | bytes 184352 | tf_op jit(solution)/shard_map/ppermute | solution.py:266
  46.2 5.3 %collective-permute-done.7.array = bf16[8,48,1280]{2,1,0:T(8,128)(2,1)S(1)} collective-permute-done((bf16[8,48,1280]{2,1,0:T(8,128)(2,1)S(1)}, bf16[8,48,1280]{2,1,0:T(8,128)(2,1)S(1)}, u32[]{:S(2)}, u32[]{:S(2)}) %collective-permute-start.7) | collective-permute-done | bytes 983072 | tf_op jit(solution)/shard_map/ppermute | solution.py:266
  54.1 5.6 %enter.1 = (bf16[2,16,48,1280]{3,2,1,0:T(8,128)(2,1)S(1)}, f32[8,768]{1,0:T(8,128)S(1)}, f32[1,3072]{1,0:T(1,128)S(1)}, bf16[512,768]{1,0:T(8,128)(2,1)}, bf16[1...) custom-call(s32[66]{0:T(128)S(1)} %stack.239.info, ...), custom_call_target="tpu_custom_call" | custom-call | flops 240000008192 | bytes 1 | tf_op jit(solution)/shard_map/enter/pallas_call | solution.py:524
  59.7 3.6 %collective-permute-done.11.refs_1_ = bf16[4,48,1920]{2,1,0:T(8,128)(2,1)} collective-permute-done((bf16[4,48,1920]{2,1,0:T(8,128)(2,1)}, bf16[4,48,1920]{2,1,0:T(8,128)(2,1)}, u32[]{:S(2)}, u32[]{:S(2)}) %collective-permute-start.11) | collective-permute-done | bytes 737312 | tf_op jit(solution)/shard_map/ppermute | solution.py:266
  63.3 2.6 %gather.9._.low = bf16[8,48,1920]{2,1,0:T(8,128)(2,1)} custom-call(bf16[4,48,1920]{2,1,0:T(8,128)(2,1)} %gather.8.behind.refs_0_, bf16[4,48,1920]{2,1,0:T(8,128)(2,1)} %collective-permute-done.11.refs_1_, f32[8,768]{1,0:T(8,128)S(1)} %get-tuple-element.92.refs_2_.vecs), custom_call_target="tpu_custom_call" | custom-call | bytes 1 | tf_op jit(solution)/shard_map/gather/pallas_call | solution.py:435
  67.2 2.6 %collective-permute-start.16 = (bf16[1,96,768]{2,1,0:T(8,128)(2,1)}, bf16[1,96,768]{2,1,0:T(8,128)(2,1)}, u32[]{:S(2)}, u32[]{:S(2)}) collective-permute-start(bf16[1,96,768]{2,1,0:T(8,128)(2,1)} %get-tuple-element.94.refs_0_), channel_id=1, source_target_pairs={{0,16},{1,17},{2,18},{3,19},{4,20},{5,21},{6,22},{7,23},{8,24},{9,... | collective-permute-start | bytes 442376 | tf_op jit(solution)/shard_map/ppermute | solution.py:266
  71.1 10.2 %mix.1 = (bf16[512,768]{1,0:T(8,128)(2,1)S(1)}, bf16[768,512]{1,0:T(8,128)(2,1)}, f32[6,8,512]{2,1,0:T(8,128)S(1)}) custom-call(s32[66]{0:T(128)S(1)} %stack.239.info, bf16[2,512,1152]{2,1,0:T(8,128)(2,1)S(1)} %get-tuple-element.91.q.k.v, bf16[2,512,1152]{2,1,0:T(8,128)(2,1)S(1)} %get-tuple-element.91.q.k.v, ...), custom_call_target="tpu_custom_call" | custom-call | flops 299999985664 | bytes 1 | tf_op jit(solution)/shard_map/mix/pallas_call | solution.py:579
  81.3 4.2 %collective-permute-done.12.array = bf16[8,48,1920]{2,1,0:T(8,128)(2,1)} collective-permute-done((bf16[8,48,1920]{2,1,0:T(8,128)(2,1)}, bf16[8,48,1920]{2,1,0:T(8,128)(2,1)}, u32[]{:S(2)}, u32[]{:S(2)}) %collective-permute-start.12) | collective-permute-done | bytes 1474592 | tf_op jit(solution)/shard_map/ppermute | solution.py:266
  92.5 5.3 %rise.1 = (f32[512,768]{1,0:T(8,128)S(1)}, bf16[512,768]{1,0:T(8,128)(2,1)S(1)}, bf16[16,48,512]{2,1,0:T(8,128)(2,1)}) custom-call(s32[66]{0:T(128)S(1)} %stack.239.info, bf16[512,768]{1,0:T(8,128)(2,1)S(1)} %copy-done.16, bf16[512,768]{1,0:T(8,128)(2,1)S(1)} %copy-done.3, f32[8,768]{1,0:T(8,128)S(1)} %copy-done.11, bf16[8,48,1920]{2,1,0:T(8,128)(2,1)} %gather.9._.low, ...), custom_call_target="tpu_custom_call" | custom-call | flops 149999992832 | bytes 1 | tf_op jit(solution)/shard_map/rise/pallas_call | solution.py:709
  98.9 2.4 %gather.11._.low = bf16[8,96,768]{2,1,0:T(8,128)(2,1)} custom-call(bf16[4,96,768]{2,1,0:T(8,128)(2,1)} %gather.10._.refs_0_, bf16[4,96,768]{2,1,0:T(8,128)(2,1)} %collective-permute-done.18.refs_1_, bf16[512,768]{1,0:T(8,128)(2,1)S(1)} %get-tuple-element.96.refs_2_.second), custom_call_target="tpu_custom_call" | custom-call | bytes 1 | tf_op jit(solution)/shard_map/gather/pallas_call | solution.py:435
  102.1 15.3 %widen.1 = (bf16[2,16,48,1920]{3,2,1,0:T(8,128)(2,1)S(1)}, bf16[512,3072]{1,0:T(8,128)(2,1)S(1)}, bf16[512,3072]{1,0:T(8,128)(2,1)S(1)}, bf16[16,96,512]{2,1,0:T(8,128)(2,1)S(1)}, bf16[16,96,512]{2,1,0:T(8,128)(2,1)}) custom-call(s32[66]{0:T(128)S(1)} %stack.239.info, bf16[512,768]{1,0:T(8,128)(2,1)S(1)} %get-tuple-element.96.refs_2_.second, ...), custom_call_target="tpu_custom_call" | custom-call | flops 539999993856 | bytes 1 | tf_op jit(solution)/shard_map/widen/pallas_call | solution.py:791
  121.7 6.3 %outer_down.1 = (f32[8,96,768]{2,1,0:T(8,128)S(1)}, bf16[8,96,768]{2,1,0:T(8,128)(2,1)}) custom-call(bf16[16,96,512]{2,1,0:T(8,128)(2,1)S(1)} %get-tuple-element.102.left, bf16[16,96,512]{2,1,0:T(8,128)(2,1)} %collective-permute-done.22.left_o, bf16[512,768]{1,0:T(8,128)(2,1)} %get-tuple-element.99.right.grad_y, ...), custom_call_target="tpu_custom_call" | custom-call | flops 240000008192 | bytes 1 | tf_op jit(solution)/shard_map/outer_down/pallas_call | solution.py:1212
  129.1 15.7 %fall.1 = (bf16[16,2,96,768]{3,2,1,0:T(8,128)(2,1)S(1)}, bf16[512,1536]{1,0:T(8,128)(2,1)}, bf16[512,1536]{1,0:T(8,128)(2,1)S(1)}, f32[1,3072]{1,0:T(1,128)S(1)}...) custom-call(s32[66]{0:T(128)S(1)} %stack.239.info, ...), custom_call_target="tpu_custom_call" | custom-call | flops 539999993856 | bytes 1 | tf_op jit(solution)/shard_map/fall/pallas_call | solution.py:944
  149.3 7.4 %outer_up.1 = (f32[8,48,1920]{2,1,0:T(8,128)S(1)}, bf16[8,48,1920]{2,1,0:T(8,128)(2,1)}) custom-call(s32[66]{0:T(128)S(1)} %stack.239.info, bf16[16,48,512]{2,1,0:T(8,128)(2,1)} %get-tuple-element.105.left, bf16[16,48,512]{2,1,0:T(8,128)(2,1)} %collective-permute-done.24.__.left_o, bf16[512,1536]{1,0:T(8,128)(2,1)S(1)} %get-tuple-element.115.right, ...), custom_call_target="tpu_custom_call" | custom-call | flops 240000008192 | bytes 1 | tf_op jit(solution)/shard_map/outer_up/pallas_call | solution.py:1148
  160.5 2.5 %collective-permute-start.34 = (bf16[96,768]{1,0:T(8,128)(2,1)}, bf16[96,768]{1,0:T(8,128)(2,1)}, u32[]{:S(2)}, u32[]{:S(2)}) collective-permute-start(bf16[96,768]{1,0:T(8,128)(2,1)} %get-tuple-element.124), channel_id=1, source_target_pairs={{0,16},{1,17},{2,18},{3,19},{4,20},{5,21},{6,22},{7,23},{8,24},{9,... | collective-permute-start | bytes 442376 | tf_op jit(solution)/shard_map/ppermute | solution.py:266
  164.5 15.5 %mix_back.1 = (bf16[3,512,384]{2,1,0:T(8,128)(2,1)}, bf16[3,512,384]{2,1,0:T(8,128)(2,1)S(1)}) custom-call(s32[66]{0:T(128)S(1)} %stack.239.info, bf16[2,512,1152]{2,1,0:T(8,128)(2,1)S(1)} %copy-done.26, bf16[2,512,1152]{2,1,0:T(8,128)(2,1)S(1)} %copy-done.26, bf16[2,512,1152]{2,1,0:T(8,128)(2,1)S(1)} %copy-done.26, ...), custom_call_target="tpu_custom_call" | custom-call | flops 480000016384 | bytes 1 | tf_op jit(solution)/shard_map/mix_back/pallas_call | solution.py:649
  182.8 2.4 %shift_first.3 = (f32[4,48,1920]{2,1,0:T(8,128)S(1)}, bf16[4,48,1920]{2,1,0:T(8,128)(2,1)}) custom-call(f32[8,48,1920]{2,1,0:T(8,128)S(1)} %get-tuple-element.122.keep, bf16[8,48,1920]{2,1,0:T(8,128)(2,1)} %collective-permute-done.32.got, f32[96,768]{1,0:T(8,128)S(1)} %copy-done.6), custom_call_target="tpu_custom_call" | custom-call | flops 149999992832 | bytes 1 | tf_op jit(solution)/shard_map/shift_first/pallas_call | solution.py:1235
  186.8 5.4 %outer_qkv.1 = (f32[8,48,1152]{2,1,0:T(8,128)S(1)}, bf16[8,48,1152]{2,1,0:T(8,128)(2,1)}) custom-call(s32[66]{0:T(128)S(1)} %stack.239.info, bf16[16,48,512]{2,1,0:T(8,128)(2,1)} %get-tuple-element.108.left, bf16[16,48,512]{2,1,0:T(8,128)(2,1)} %collective-permute-done.26.left_o, bf16[3,512,384]{2,1,0:T(8,128)(2,1)S(1)} %get-tuple-element.120.right.mine, ...), custom_call_target="tpu_custom_call" | custom-call | flops 240000008192 | bytes 1 | tf_op jit(solution)/shard_map/outer_qkv/pallas_call | solution.py:1180
  193.1 6.6 %exit_back.1 = (bf16[512,768]{1,0:T(8,128)(2,1)}, f32[8,48,128]{2,1,0:T(8,128)S(1)}, bf16[8,48,128]{2,1,0:T(8,128)(2,1)S(1)}) custom-call(s32[66]{0:T(128)S(1)} %stack.239.info, bf16[512,768]{1,0:T(8,128)(2,1)S(1)} %copy-done.17, bf16[3,512,384]{2,1,0:T(8,128)(2,1)S(1)} %get-tuple-element.120.right.mine, bf16[3,512,384]{2,1,0:T(8,128)(2,1)} %get-tuple-element.121._.theirs, ...), custom_call_target="tpu_custom_call" | custom-call | flops 240000008192 | bytes 1 | tf_op jit(solution)/shard_map/exit_back/pallas_call | solution.py:1065
  204.0 3.0 %collective-permute-start.44 = (bf16[48,1920]{1,0:T(8,128)(2,1)}, bf16[48,1920]{1,0:T(8,128)(2,1)}, u32[]{:S(2)}, u32[]{:S(2)}) collective-permute-start(bf16[48,1920]{1,0:T(8,128)(2,1)} %get-tuple-element.145), channel_id=1, source_target_pairs={{0,16},{1,17},{2,18},{3,19},{4,20},{5,21},{6,22},{7,23},{8,24},{9,... | collective-permute-start | bytes 552968 | tf_op jit(solution)/shard_map/ppermute | solution.py:266
  211.3 5.0 %leave.1._ = bf16[512,768]{1,0:T(8,128)(2,1)} custom-call(f32[512,768]{1,0:T(8,128)S(1)} %copy-done.24, bf16[512,3072]{1,0:T(8,128)(2,1)S(1)} %copy-done.21, bf16[3072,768]{1,0:T(8,128)(2,1)S(1)} %bitcast.67, f32[8,768]{1,0:T(8,128)S(1)} %copy-done.13, bf16[4,48,1280]{2,1,0:T(8,128)(2,1)} %get-tuple-element.138._), custom_call_target="tpu_custom_call" | custom-call | flops 210000003072 | bytes 1 | tf_op jit(solution)/shard_map/leave/pallas_call | solution.py:833
  216.3 3.6 %collective-permute-done.39.got = bf16[4,48,1280]{2,1,0:T(8,128)(2,1)} collective-permute-done((bf16[4,48,1280]{2,1,0:T(8,128)(2,1)}, bf16[4,48,1280]{2,1,0:T(8,128)(2,1)}, u32[]{:S(2)}, u32[]{:S(2)}) %collective-permute-start.39) | collective-permute-done | bytes 491552 | tf_op jit(solution)/shard_map/ppermute | solution.py:266
  222.2 3.0 %collective-permute-start.41 = (bf16[48,1280]{1,0:T(8,128)(2,1)S(1)}, bf16[48,1280]{1,0:T(8,128)(2,1)S(1)}, u32[]{:S(2)}, u32[]{:S(2)}) collective-permute-start(bf16[48,1280]{1,0:T(8,128)(2,1)S(1)} %get-tuple-element.142), channel_id=1, source_target_pairs={{0,16},{1,17},{2,18},{3,19},{4,20},{5,21},{6,22},{7,23},{8,24},{9,... | collective-permute-start | bytes 368648 | tf_op jit(solution)/shard_map/ppermute | solution.py:266
  228.2 4.8 %collective-permute-done.41.two = bf16[48,1280]{1,0:T(8,128)(2,1)S(1)} collective-permute-done((bf16[48,1280]{1,0:T(8,128)(2,1)S(1)}, bf16[48,1280]{1,0:T(8,128)(2,1)S(1)}, u32[]{:S(2)}, u32[]{:S(2)}) %collective-permute-start.41) | collective-permute-done | bytes 122912 | tf_op jit(solution)/shard_map/ppermute | solution.py:266
  (154 shorter events, 62.0 us)
Async XLA Ops:
  10.5 12.4 %collective-permute-start.2 = (bf16[1,48,1280]{2,1,0:T(8,128)(2,1)S(1)}, bf16[1,48,1280]{2,1,0:T(8,128)(2,1)S(1)}, u32[]{:S(2)}, u32[]{:S(2)}) collective-permute-start(bf16[1,48,1280]{2,1,0:T(8,128)(2,1)S(1)} %get-tuple-element.85.refs_0_), channel_id=1, source_target_pairs={{0,16},{1,17},{2,18},{3,19},{4,20},{5,21},{6,22},{7,23},{8,24},{9,... | collective-permute-start | bytes 368648 | tf_op jit(solution)/shard_map/ppermute | solution.py:266
  13.1 9.8 %collective-permute-start.3 = (bf16[1,48,1280]{2,1,0:T(8,128)(2,1)S(1)}, bf16[1,48,1280]{2,1,0:T(8,128)(2,1)S(1)}, u32[]{:S(2)}, u32[]{:S(2)}) collective-permute-start(bf16[1,48,1280]{2,1,0:T(8,128)(2,1)S(1)} %get-tuple-element.85.refs_0_), channel_id=1, source_target_pairs={{0,24},{1,25},{2,26},{3,27},{4,28},{5,29},{6,30},{7,31},{8,16},{9,... | collective-permute-start | bytes 368648 | tf_op jit(solution)/shard_map/ppermute | solution.py:266
  22.9 14.3 %collective-permute-start.4 = (bf16[4,48,1280]{2,1,0:T(8,128)(2,1)S(1)}, bf16[4,48,1280]{2,1,0:T(8,128)(2,1)S(1)}, u32[]{:S(2)}, u32[]{:S(2)}) collective-permute-start(bf16[4,48,1280]{2,1,0:T(8,128)(2,1)S(1)} %get-tuple-element.87.refs_0_), channel_id=1, source_target_pairs={{0,2},{1,5},{2,0},{3,7},{4,6},{5,1},{6,4},{7,3},{8,10},{9,13},{10,... | collective-permute-start | bytes 1474568 | tf_op jit(solution)/shard_map/ppermute | solution.py:266
  24.5 9.8 %collective-permute-start.5 = (bf16[1,48,1920]{2,1,0:T(8,128)(2,1)S(1)}, bf16[1,48,1920]{2,1,0:T(8,128)(2,1)S(1)}, u32[]{:S(2)}, u32[]{:S(2)}) collective-permute-start(bf16[1,48,1920]{2,1,0:T(8,128)(2,1)S(1)} %get-tuple-element.88.refs_2_), channel_id=1, source_target_pairs={{0,8},{1,9},{2,10},{3,11},{4,12},{5,13},{6,14},{7,15},{8,0},{9,1},... | collective-permute-start | bytes 552968 | tf_op jit(solution)/shard_map/ppermute | solution.py:266
  27.0 10.3 %collective-permute-start.6 = (bf16[1,48,1920]{2,1,0:T(8,128)(2,1)S(1)}, bf16[1,48,1920]{2,1,0:T(8,128)(2,1)S(1)}, u32[]{:S(2)}, u32[]{:S(2)}) collective-permute-start(bf16[1,48,1920]{2,1,0:T(8,128)(2,1)S(1)} %get-tuple-element.88.refs_2_), channel_id=1, source_target_pairs={{0,16},{1,17},{2,18},{3,19},{4,20},{5,21},{6,22},{7,23},{8,24},{9,... | collective-permute-start | bytes 552968 | tf_op jit(solution)/shard_map/ppermute | solution.py:266
  37.3 14.2 %collective-permute-start.7 = (bf16[8,48,1280]{2,1,0:T(8,128)(2,1)S(1)}, bf16[8,48,1280]{2,1,0:T(8,128)(2,1)S(1)}, u32[]{:S(2)}, u32[]{:S(2)}) collective-permute-start(bf16[8,48,1280]{2,1,0:T(8,128)(2,1)S(1)} %get-tuple-element.89.low), channel_id=1, source_target_pairs={{0,4},{1,3},{2,6},{3,1},{4,0},{5,7},{6,2},{7,5},{8,12},{9,11},{10,... | collective-permute-start | bytes 2949128 | tf_op jit(solution)/shard_map/ppermute | solution.py:266
  40.3 12.7 %collective-permute-start.9 = (bf16[8,48,1280]{2,1,0:T(8,128)(2,1)S(1)}, bf16[8,48,1280]{2,1,0:T(8,128)(2,1)S(1)}, u32[]{:S(2)}, u32[]{:S(2)}) collective-permute-start(bf16[8,48,1280]{2,1,0:T(8,128)(2,1)S(1)} %get-tuple-element.89.low), channel_id=1, source_target_pairs={{0,1},{1,0},{2,3},{3,2},{4,5},{5,4},{6,7},{7,6},{8,9},{9,8},{10,11... | collective-permute-start | bytes 2949128 | tf_op jit(solution)/shard_map/ppermute | solution.py:266
  51.5 11.8 %collective-permute-start.11 = (bf16[4,48,1920]{2,1,0:T(8,128)(2,1)}, bf16[4,48,1920]{2,1,0:T(8,128)(2,1)}, u32[]{:S(2)}, u32[]{:S(2)}) collective-permute-start(bf16[4,48,1920]{2,1,0:T(8,128)(2,1)} %gather.8.behind.refs_0_), channel_id=1, source_target_pairs={{0,2},{1,5},{2,0},{3,7},{4,6},{5,1},{6,4},{7,3},{8,10},{9,13},{10,... | collective-permute-start | bytes 2211848 | tf_op jit(solution)/shard_map/ppermute | solution.py:266
  65.8 19.7 %collective-permute-start.12 = (bf16[8,48,1920]{2,1,0:T(8,128)(2,1)}, bf16[8,48,1920]{2,1,0:T(8,128)(2,1)}, u32[]{:S(2)}, u32[]{:S(2)}) collective-permute-start(bf16[8,48,1920]{2,1,0:T(8,128)(2,1)} %gather.9._.low), channel_id=1, source_target_pairs={{0,4},{1,3},{2,6},{3,1},{4,0},{5,7},{6,2},{7,5},{8,12},{9,11},{10,... | collective-permute-start | bytes 4423688 | tf_op jit(solution)/shard_map/ppermute | solution.py:266
  66.3 22.3 %collective-permute-start.13 = (bf16[8,48,1920]{2,1,0:T(8,128)(2,1)}, bf16[8,48,1920]{2,1,0:T(8,128)(2,1)}, u32[]{:S(2)}, u32[]{:S(2)}) collective-permute-start(bf16[8,48,1920]{2,1,0:T(8,128)(2,1)} %gather.9._.low), channel_id=1, source_target_pairs={{0,1},{1,0},{2,3},{3,2},{4,5},{5,4},{6,7},{7,6},{8,9},{9,8},{10,11... | collective-permute-start | bytes 4423688 | tf_op jit(solution)/shard_map/ppermute | solution.py:266
  66.7 18.8 %collective-permute-start.15 = (bf16[1,96,768]{2,1,0:T(8,128)(2,1)}, bf16[1,96,768]{2,1,0:T(8,128)(2,1)}, u32[]{:S(2)}, u32[]{:S(2)}) collective-permute-start(bf16[1,96,768]{2,1,0:T(8,128)(2,1)} %get-tuple-element.94.refs_0_), channel_id=1, source_target_pairs={{0,8},{1,9},{2,10},{3,11},{4,12},{5,13},{6,14},{7,15},{8,0},{9,1},... | collective-permute-start | bytes 442376 | tf_op jit(solution)/shard_map/ppermute | solution.py:266
  67.2 18.9 %collective-permute-start.16 = (bf16[1,96,768]{2,1,0:T(8,128)(2,1)}, bf16[1,96,768]{2,1,0:T(8,128)(2,1)}, u32[]{:S(2)}, u32[]{:S(2)}) collective-permute-start(bf16[1,96,768]{2,1,0:T(8,128)(2,1)} %get-tuple-element.94.refs_0_), channel_id=1, source_target_pairs={{0,16},{1,17},{2,18},{3,19},{4,20},{5,21},{6,22},{7,23},{8,24},{9,... | collective-permute-start | bytes 442376 | tf_op jit(solution)/shard_map/ppermute | solution.py:266
  69.7 16.4 %collective-permute-start.17 = (bf16[1,96,768]{2,1,0:T(8,128)(2,1)}, bf16[1,96,768]{2,1,0:T(8,128)(2,1)}, u32[]{:S(2)}, u32[]{:S(2)}) collective-permute-start(bf16[1,96,768]{2,1,0:T(8,128)(2,1)} %get-tuple-element.94.refs_0_), channel_id=1, source_target_pairs={{0,24},{1,25},{2,26},{3,27},{4,28},{5,29},{6,30},{7,31},{8,16},{9,... | collective-permute-start | bytes 442376 | tf_op jit(solution)/shard_map/ppermute | solution.py:266
  85.5 35.4 %collective-permute-start.23 = (bf16[512,768]{1,0:T(8,128)(2,1)}, bf16[512,768]{1,0:T(8,128)(2,1)}, u32[]{:S(2)}, u32[]{:S(2)}) collective-permute-start(bf16[512,768]{1,0:T(8,128)(2,1)} %get-tuple-element.99.right.grad_y), channel_id=1, source_target_pairs={{0,1},{1,0},{2,3},{3,2},{4,5},{5,4},{6,7},{7,6},{8,9},{9,8},{10,11... | collective-permute-start | bytes 2359304 | tf_op jit(solution)/shard_map/ppermute | solution.py:266
  85.5 42.4 %collective-permute-start.25 = (bf16[16,48,512]{2,1,0:T(8,128)(2,1)}, bf16[16,48,512]{2,1,0:T(8,128)(2,1)}, u32[]{:S(2)}, u32[]{:S(2)}) collective-permute-start(bf16[16,48,512]{2,1,0:T(8,128)(2,1)} %bitcast.59.low), channel_id=1, source_target_pairs={{0,1},{1,0},{2,3},{3,2},{4,5},{5,4},{6,7},{7,6},{8,9},{9,8},{10,11... | collective-permute-start | bytes 2359304 | tf_op jit(solution)/shard_map/ppermute | solution.py:266
  86.0 100.7 %collective-permute-start.26 = (bf16[16,48,512]{2,1,0:T(8,128)(2,1)}, bf16[16,48,512]{2,1,0:T(8,128)(2,1)}, u32[]{:S(2)}, u32[]{:S(2)}) collective-permute-start(bf16[16,48,512]{2,1,0:T(8,128)(2,1)} %get-tuple-element.108.left), channel_id=1, source_target_pairs={{0,1},{1,0},{2,3},{3,2},{4,5},{5,4},{6,7},{7,6},{8,9},{9,8},{10,11... | collective-permute-start | bytes 2359304 | tf_op jit(solution)/shard_map/ppermute | solution.py:266
  88.7 10.2 %collective-permute-start.18 = (bf16[4,96,768]{2,1,0:T(8,128)(2,1)}, bf16[4,96,768]{2,1,0:T(8,128)(2,1)}, u32[]{:S(2)}, u32[]{:S(2)}) collective-permute-start(bf16[4,96,768]{2,1,0:T(8,128)(2,1)} %gather.10._.refs_0_), channel_id=1, source_target_pairs={{0,2},{1,5},{2,0},{3,7},{4,6},{5,1},{6,4},{7,3},{8,10},{9,13},{10,... | collective-permute-start | bytes 1769480 | tf_op jit(solution)/shard_map/ppermute | solution.py:266
  101.2 16.5 %collective-permute-start.19 = (bf16[8,96,768]{2,1,0:T(8,128)(2,1)}, bf16[8,96,768]{2,1,0:T(8,128)(2,1)}, u32[]{:S(2)}, u32[]{:S(2)}) collective-permute-start(bf16[8,96,768]{2,1,0:T(8,128)(2,1)} %gather.11._.low), channel_id=1, source_target_pairs={{0,4},{1,3},{2,6},{3,1},{4,0},{5,7},{6,2},{7,5},{8,12},{9,11},{10,... | collective-permute-start | bytes 3538952 | tf_op jit(solution)/shard_map/ppermute | solution.py:266
  101.7 27.4 %collective-permute-start.20 = (bf16[8,96,768]{2,1,0:T(8,128)(2,1)}, bf16[8,96,768]{2,1,0:T(8,128)(2,1)}, u32[]{:S(2)}, u32[]{:S(2)}) collective-permute-start(bf16[8,96,768]{2,1,0:T(8,128)(2,1)} %gather.11._.low), channel_id=1, source_target_pairs={{0,1},{1,0},{2,3},{3,2},{4,5},{5,4},{6,7},{7,6},{8,9},{9,8},{10,11... | collective-permute-start | bytes 3538952 | tf_op jit(solution)/shard_map/ppermute | solution.py:266
  127.9 17.5 %collective-permute-start.27 = (bf16[8,96,768]{2,1,0:T(8,128)(2,1)}, bf16[8,96,768]{2,1,0:T(8,128)(2,1)}, u32[]{:S(2)}, u32[]{:S(2)}) collective-permute-start(bf16[8,96,768]{2,1,0:T(8,128)(2,1)} %get-tuple-element.104._), channel_id=1, source_target_pairs={{0,4},{1,3},{2,6},{3,1},{4,0},{5,7},{6,2},{7,5},{8,12},{9,11},{10,... | collective-permute-start | bytes 3538952 | tf_op jit(solution)/shard_map/ppermute | solution.py:266
  147.8 10.2 %collective-permute-start.28 = (bf16[4,96,768]{2,1,0:T(8,128)(2,1)}, bf16[4,96,768]{2,1,0:T(8,128)(2,1)}, u32[]{:S(2)}, u32[]{:S(2)}) collective-permute-start(bf16[4,96,768]{2,1,0:T(8,128)(2,1)} %get-tuple-element.114._), channel_id=1, source_target_pairs={{0,2},{1,5},{2,0},{3,7},{4,6},{5,1},{6,4},{7,3},{8,10},{9,13},{10,... | collective-permute-start | bytes 1769480 | tf_op jit(solution)/shard_map/ppermute | solution.py:266
  156.7 25.1 %collective-permute-start.32 = (bf16[8,48,1920]{2,1,0:T(8,128)(2,1)}, bf16[8,48,1920]{2,1,0:T(8,128)(2,1)}, u32[]{:S(2)}, u32[]{:S(2)}) collective-permute-start(bf16[8,48,1920]{2,1,0:T(8,128)(2,1)} %get-tuple-element.118._), channel_id=1, source_target_pairs={{0,4},{1,3},{2,6},{3,1},{4,0},{5,7},{6,2},{7,5},{8,12},{9,11},{10,... | collective-permute-start | bytes 4423688 | tf_op jit(solution)/shard_map/ppermute | solution.py:266
  160.1 19.9 %collective-permute-start.33 = (bf16[96,768]{1,0:T(8,128)(2,1)}, bf16[96,768]{1,0:T(8,128)(2,1)}, u32[]{:S(2)}, u32[]{:S(2)}) collective-permute-start(bf16[96,768]{1,0:T(8,128)(2,1)} %get-tuple-element.123), channel_id=1, source_target_pairs={{0,8},{1,9},{2,10},{3,11},{4,12},{5,13},{6,14},{7,15},{8,0},{9,1},... | collective-permute-start | bytes 442376 | tf_op jit(solution)/shard_map/ppermute | solution.py:266
  160.5 19.5 %collective-permute-start.34 = (bf16[96,768]{1,0:T(8,128)(2,1)}, bf16[96,768]{1,0:T(8,128)(2,1)}, u32[]{:S(2)}, u32[]{:S(2)}) collective-permute-start(bf16[96,768]{1,0:T(8,128)(2,1)} %get-tuple-element.124), channel_id=1, source_target_pairs={{0,16},{1,17},{2,18},{3,19},{4,20},{5,21},{6,22},{7,23},{8,24},{9,... | collective-permute-start | bytes 442376 | tf_op jit(solution)/shard_map/ppermute | solution.py:266
  163.1 16.9 %collective-permute-start.35 = (bf16[96,768]{1,0:T(8,128)(2,1)}, bf16[96,768]{1,0:T(8,128)(2,1)}, u32[]{:S(2)}, u32[]{:S(2)}) collective-permute-start(bf16[96,768]{1,0:T(8,128)(2,1)} %get-tuple-element.125), channel_id=1, source_target_pairs={{0,24},{1,25},{2,26},{3,27},{4,28},{5,29},{6,30},{7,31},{8,16},{9,... | collective-permute-start | bytes 442376 | tf_op jit(solution)/shard_map/ppermute | solution.py:266
  185.3 15.6 %collective-permute-start.38 = (bf16[4,48,1920]{2,1,0:T(8,128)(2,1)}, bf16[4,48,1920]{2,1,0:T(8,128)(2,1)}, u32[]{:S(2)}, u32[]{:S(2)}) collective-permute-start(bf16[4,48,1920]{2,1,0:T(8,128)(2,1)} %get-tuple-element.126._), channel_id=1, source_target_pairs={{0,2},{1,5},{2,0},{3,7},{4,6},{5,1},{6,4},{7,3},{8,10},{9,13},{10,... | collective-permute-start | bytes 2211848 | tf_op jit(solution)/shard_map/ppermute | solution.py:266
  192.2 16.2 %collective-permute-start.36 = (bf16[8,48,1152]{2,1,0:T(8,128)(2,1)}, bf16[8,48,1152]{2,1,0:T(8,128)(2,1)}, u32[]{:S(2)}, u32[]{:S(2)}) collective-permute-start(bf16[8,48,1152]{2,1,0:T(8,128)(2,1)} %get-tuple-element.128._), channel_id=1, source_target_pairs={{0,4},{1,3},{2,6},{3,1},{4,0},{5,7},{6,2},{7,5},{8,12},{9,11},{10,... | collective-permute-start | bytes 2654216 | tf_op jit(solution)/shard_map/ppermute | solution.py:266
  204.0 21.2 %collective-permute-start.43 = (bf16[48,1920]{1,0:T(8,128)(2,1)}, bf16[48,1920]{1,0:T(8,128)(2,1)}, u32[]{:S(2)}, u32[]{:S(2)}) collective-permute-start(bf16[48,1920]{1,0:T(8,128)(2,1)} %get-tuple-element.144), channel_id=1, source_target_pairs={{0,8},{1,9},{2,10},{3,11},{4,12},{5,13},{6,14},{7,15},{8,0},{9,1},... | collective-permute-start | bytes 552968 | tf_op jit(solution)/shard_map/ppermute | solution.py:266
  204.0 22.6 %collective-permute-start.44 = (bf16[48,1920]{1,0:T(8,128)(2,1)}, bf16[48,1920]{1,0:T(8,128)(2,1)}, u32[]{:S(2)}, u32[]{:S(2)}) collective-permute-start(bf16[48,1920]{1,0:T(8,128)(2,1)} %get-tuple-element.145), channel_id=1, source_target_pairs={{0,16},{1,17},{2,18},{3,19},{4,20},{5,21},{6,22},{7,23},{8,24},{9,... | collective-permute-start | bytes 552968 | tf_op jit(solution)/shard_map/ppermute | solution.py:266
  207.1 19.5 %collective-permute-start.45 = (bf16[48,1920]{1,0:T(8,128)(2,1)}, bf16[48,1920]{1,0:T(8,128)(2,1)}, u32[]{:S(2)}, u32[]{:S(2)}) collective-permute-start(bf16[48,1920]{1,0:T(8,128)(2,1)} %get-tuple-element.146), channel_id=1, source_target_pairs={{0,24},{1,25},{2,26},{3,27},{4,28},{5,29},{6,30},{7,31},{8,16},{9,... | collective-permute-start | bytes 552968 | tf_op jit(solution)/shard_map/ppermute | solution.py:266
  210.7 9.1 %collective-permute-start.39 = (bf16[4,48,1280]{2,1,0:T(8,128)(2,1)}, bf16[4,48,1280]{2,1,0:T(8,128)(2,1)}, u32[]{:S(2)}, u32[]{:S(2)}) collective-permute-start(bf16[4,48,1280]{2,1,0:T(8,128)(2,1)} %get-tuple-element.138._), channel_id=1, source_target_pairs={{0,2},{1,5},{2,0},{3,7},{4,6},{5,1},{6,4},{7,3},{8,10},{9,13},{10,... | collective-permute-start | bytes 1474568 | tf_op jit(solution)/shard_map/ppermute | solution.py:266
  222.2 10.8 %collective-permute-start.41 = (bf16[48,1280]{1,0:T(8,128)(2,1)S(1)}, bf16[48,1280]{1,0:T(8,128)(2,1)S(1)}, u32[]{:S(2)}, u32[]{:S(2)}) collective-permute-start(bf16[48,1280]{1,0:T(8,128)(2,1)S(1)} %get-tuple-element.142), channel_id=1, source_target_pairs={{0,16},{1,17},{2,18},{3,19},{4,20},{5,21},{6,22},{7,23},{8,24},{9,... | collective-permute-start | bytes 368648 | tf_op jit(solution)/shard_map/ppermute | solution.py:266
  (43 other events, 233.4 us)

commit v4 on v3

--- a/solution.py
+++ b/solution.py
@@ -303,6 +303,51 @@
     return pl.BlockSpec(dims, lambda *_: (0,) * len(dims))
 
 
+class Chain:
+    def __init__(self):
+        self.token, self.extra = None, ()
+
+    def near(self, *arrays):
+        self.extra = arrays
+
+    def call(
+        self, kernel, *, out_shape, in_specs, out_specs, grid=(), prefetch=0, aliases={}, **options
+    ):
+        single = not isinstance(out_shape, tuple)
+        if single:
+            out_shape, out_specs = (out_shape,), (out_specs,)
+        held = 0 if self.token is None else 1
+        extra, self.extra = self.extra, ()
+        n_in, n_out = prefetch + len(in_specs), len(out_shape)
+        at_token = n_in + len(extra)
+
+        def body(*refs):
+            skip = at_token + held
+            return kernel(*refs[:n_in], *refs[skip : skip + n_out], *refs[skip + n_out + 1 :])
+
+        token = shape((8, 128), F32)
+        specs = pltpu.PrefetchScalarGridSpec(
+            num_scalar_prefetch=prefetch,
+            grid=grid,
+            in_specs=list(in_specs) + [ANY] * (len(extra) + held),
+            out_specs=tuple(out_specs) + (ANY,),
+            scratch_shapes=options.pop("scratch_shapes", ()),
+        )
+        run = pl.pallas_call(
+            body,
+            grid_spec=specs,
+            out_shape=tuple(out_shape) + (token,),
+            input_output_aliases=aliases | ({at_token: n_out} if held else {}),
+            **options,
+        )
+
+        def with_token(*args):
+            *outs, self.token = run(*args, *extra, *([self.token] if held else []))
+            return outs[0] if single else tuple(outs)
+
+        return with_token
+
+
 def dot(left, right):
     return jnp.dot(left, right, preferred_element_type=F32)
 
@@ -311,26 +356,19 @@
     return lax.dot_general(left, right, BOTH_LAST, preferred_element_type=F32)
 
 
-def fetch(info, pieces, dest, sems, by_half):
-    copies = []
-    cols = pl.ds(pieces[0].shape[-1] - dest.shape[-1], dest.shape[-1])
-    for who in (0, 1):
-        half = info[CORE] if who == 0 else 1 - info[CORE]
+def settle(info, pieces, dest, who=(0, 1)):
+    for w in who:
+        half = info[CORE] if w == 0 else 1 - info[CORE]
         for j in range(16):
-            at = info[16 * who + j]
-            src = pieces[2 * who + j // 8].at[j % 8, :, cols]
-            dst = dest.at[half, at] if by_half else dest.at[at, half]
-            copies.append(pltpu.make_async_copy(src, dst, sems.at[16 * who + j]))
-    for copy in copies:
-        copy.start()
-    return copies
-
-
-def settle(info, pieces, dest, cols):
-    for who in (0, 1):
-        half = info[CORE] if who == 0 else 1 - info[CORE]
-        for j in range(16):
-            dest[half, info[16 * who + j]] = pieces[2 * who + j // 8][j % 8, :, cols]
+            dest[half, info[16 * w + j]] = pieces[2 * w + j // 8][j % 8]
+
+
+def bring(pieces, raw, sems, start):
+    cols = pl.ds(start, raw.shape[-1])
+    return [
+        pltpu.make_async_copy(piece.at[:, :, cols], raw.at[i], sems.at[i])
+        for i, piece in enumerate(pieces)
+    ]
 
 
 def centre(values):
@@ -347,118 +385,107 @@
     )
 
 
-def halves_kernel(info, qkv, proj, up, mine, theirs, sems):
-    feat = proj.shape[1]
-    third, wide = feat // 2, up.shape[1] // 2
-    copies = []
-
-    def copy(src, start, out, at, width):
-        cols = pl.ds(pl.multiple_of(start, 128), width)
-        sem = sems.at[len(copies)]
-        copies.append(pltpu.make_async_copy(src.at[:, cols], out.at[:, pl.ds(at, width)], sem))
-
-    for out, h in ((theirs, 1 - info[CORE]), (mine, info[CORE])):
+def stacked(core, mine, others):
+    pair = (mine, others) if core == 0 else (others, mine)
+    return jnp.concatenate([part.astype(F32) for part in pair]).astype(BF16)
+
+
+def by_core(info, lay):
+    for core in (0, 1):
+        pl.when(info[CORE] == core)(partial(lay, core))
+
+
+def first_piece_kernel(info, qkv, qkv_o, small, out):
+    third = qkv.shape[1] // 6
+
+    def lay(core):
         for i in range(3):
-            copy(qkv, i * feat + h * third, out, i * third, third)
-        copy(up, h * wide, out, 3 * third, wide)
-        copy(proj, h * third, out, 3 * third + wide, third)
-    for c in copies:
-        c.start()
-    for c in copies:
-        c.wait()
-
-
-def halves(info, qkv, proj, up):
-    rows = qkv.shape[0]
-    width = (qkv.shape[1] + proj.shape[1] + up.shape[1]) // 2
+            cols = slice((2 * i + core) * third, (2 * i + core + 1) * third)
+            out[0, :, i * third : (i + 1) * third] = stacked(core, qkv[:, cols], qkv_o[:, cols])
+        out[0, :, 3 * third :] = stacked(core, small[...], jnp.zeros_like(small))
+
+    by_core(info, lay)
+
+
+def first_piece(chain, info, qkv, qkv_o, small):
+    rows, cols = qkv.shape
     vmem = pl.BlockSpec(memory_space=pltpu.VMEM)
-    out = shape((rows, width), BF16)
-    return pl.pallas_call(
-        halves_kernel,
-        out_shape=(out, out),
-        in_specs=[SMEM] + [ANY] * 3,
-        out_specs=(vmem, vmem),
-        scratch_shapes=[pltpu.SemaphoreType.DMA((10,))],
+    return chain.call(
+        first_piece_kernel,
+        out_shape=shape((1, 2 * rows, cols // 2 + small.shape[1]), BF16),
+        in_specs=[SMEM] + [vmem] * 3,
+        out_specs=vmem,
         compiler_params=params(8),
-        name="halves",
+        name="first_piece",
         cost_estimate=cost(0),
-    )(info, qkv, proj, up)
-
-
-def pieces_kernel(info, mine, given, small, one, two):
-    ours, others = mine[...].astype(F32), given[...].astype(F32)
-    few = small[...].astype(F32)
-    none = jnp.zeros_like(few)
-    first = info[CORE] == 0
-
-    def stack(a, b):
-        return jnp.concatenate([jnp.where(first, a, b), jnp.where(first, b, a)]).astype(BF16)
-
-    split = one.shape[2] - few.shape[1]
-    one[0, :, :split] = stack(ours[:, :split], others[:, :split])
-    one[0, :, split:] = stack(few, none)
-    two[0] = stack(ours[:, split:], others[:, split:])
-
-
-def pieces_of(info, mine, given, small, split):
-    rows, width = mine.shape
-    one = split + small.shape[1]
+    )(info, qkv, qkv_o, small)
+
+
+def up_piece_kernel(info, up, up_o, proj, proj_o, out):
+    wide, third = up.shape[1] // 2, proj.shape[1] // 2
+
+    def lay(core):
+        for whole, other, at, width in ((up, up_o, 0, wide), (proj, proj_o, wide, third)):
+            cols = slice(core * width, (core + 1) * width)
+            out[0, :, at : at + width] = stacked(core, whole[:, cols], other[:, cols])
+
+    by_core(info, lay)
+
+
+def up_piece(chain, info, up, up_o, proj, proj_o):
+    rows = up.shape[0]
     vmem = pl.BlockSpec(memory_space=pltpu.VMEM)
-    return pl.pallas_call(
-        pieces_kernel,
-        out_shape=(
-            shape((1, 2 * rows, one), BF16),
-            shape((1, 2 * rows, width - split), BF16),
-        ),
-        in_specs=[SMEM] + [vmem] * 3,
-        out_specs=(vmem,) * 2,
+    return chain.call(
+        up_piece_kernel,
+        out_shape=shape((1, 2 * rows, (up.shape[1] + proj.shape[1]) // 2), BF16),
+        in_specs=[SMEM] + [vmem] * 4,
+        out_specs=vmem,
         compiler_params=params(8),
-        name="pieces_of",
+        name="up_piece",
         cost_estimate=cost(0),
-    )(info, mine, given, small)
+    )(info, up, up_o, proj, proj_o)
 
 
 def gather_kernel(n_in, n_held, *refs):
-    parts = refs[:n_in]
-    out = refs[n_in + n_held]
-    at = 0
-    for part in parts:
+    out, at = refs[n_in + n_held], 0
+    for part in refs[:n_in]:
         out[at : at + part.shape[0]] = part[...]
         at += part.shape[0]
-
-
-def gather(parts, held=(), behind=(), micros=0):
+    for i in range(n_held):
+        refs[n_in + n_held + 1 + i][...] = refs[n_in + i][...]
+
+
+def gather(chain, parts, held=(), micros=0):
     vmem = pl.BlockSpec(memory_space=pltpu.VMEM)
     _, rows, cols = parts[0].shape
     count = sum(part.shape[0] for part in parts)
     n, n_held = len(parts), len(held)
-    return pl.pallas_call(
-        partial(gather_kernel, n, n_held + len(behind)),
+    return chain.call(
+        partial(gather_kernel, n, n_held),
         out_shape=(shape((count, rows, cols), BF16),) + tuple(shape(h.shape, h.dtype) for h in held),
-        in_specs=[vmem] * n + [ANY] * (n_held + len(behind)),
-        out_specs=(vmem,) + (ANY,) * n_held,
-        input_output_aliases={n + i: 1 + i for i in range(n_held)},
+        in_specs=[vmem] * (n + n_held),
+        out_specs=(vmem,) * (1 + n_held),
         compiler_params=params(16),
         name="gather",
         cost_estimate=cost(micros),
-    )(*parts, *held, *behind)
-
-
-def gate_kernel(array, behind, out):
+    )(*parts, *held)
+
+
+def gate_kernel(array, out):
     pass
 
 
-def gate(array, behind, micros=1):
-    return pl.pallas_call(
+def gate(chain, array, micros):
+    return chain.call(
         gate_kernel,
         out_shape=shape(array.shape, array.dtype),
-        in_specs=[ANY, ANY],
+        in_specs=[ANY],
         out_specs=ANY,
-        input_output_aliases={0: 0},
+        aliases={0: 0},
         compiler_params=params(4),
         name="gate",
         cost_estimate=cost(micros),
-    )(array, behind)
+    )(array)
 
 
 def near_z(piece, steps):
@@ -490,7 +517,7 @@
     piece_down[0] = down[...]
     place = lax.broadcasted_iota(jnp.int32, upstream.shape, 0)
     grad_y[...] = jnp.where(place < info[LENGTH], upstream[...].astype(F32), 0.0).astype(BF16)
-    settle(info, (low, high, low_o, high_o), weights, slice(None))
+    settle(info, (low, high, low_o, high_o), weights)
     normed, _ = centre(tokens[...].astype(F32))
     out = pltpu.make_async_copy(weights, kept, sem)
     out.start()
@@ -516,12 +543,12 @@
     out.wait()
 
 
-def enter(info, tokens, upstream, down, hidden, pieces):
+def enter(chain, info, tokens, upstream, down, hidden, pieces):
     rows, feat = tokens.shape
     width = pieces[0].shape[-1]
     vmem = pl.BlockSpec(memory_space=pltpu.VMEM)
     sets = (2, 16, feat // 16, width)
-    return pl.pallas_call(
+    return chain.call(
         enter_kernel,
         out_shape=(
             shape(sets, BF16),
@@ -548,127 +575,138 @@
     return jnp.where(place < info[LENGTH], raw, NEG)
 
 
-def mix_kernel(info, q, k, v, _, mixed, flipped, stats):
-    head = q.shape[-1] // 2
+def mix_kernel(info, q, k, v, mixed, flipped, stats):
+    head = mixed.shape[1] // (HEADS // 2)
+    count = q.shape[-1] // head
     scale = head**-0.5
     turned = v[0].T
-    outs = []
-    for h in (0, 1):
+
+    def start(h):
         cols = slice(h * head, (h + 1) * head)
-        scores = scores_of(info, k[0, :, cols], q[0, :, cols] * scale)
+        return scores_of(info, k[0, :, cols], q[0, :, cols] * scale)
+
+    def finish(h, scores):
+        cols = slice(h * head, (h + 1) * head)
         most = jnp.max(scores, axis=0, keepdims=True)
         expd = jnp.exp(scores - most)
         total = jnp.sum(expd, axis=0, keepdims=True)
         attn = (expd * (1.0 / total)).astype(BF16)
-        stats[0, h : h + 1] = most + jnp.log(total)
-        outs.append(dot(turned[cols], attn))
+        stats[h // 2, h % 2 : h % 2 + 1] = most + jnp.log(total)
+        return dot(turned[cols], attn)
+
+    ready = [start(h) for h in range(2)]
+    outs = []
+    for h in range(count):
+        if h + 2 < count:
+            ready.append(start(h + 2))
+        outs.append(finish(h, ready[h]))
     both = jnp.concatenate(outs)
     flipped[...] = both.astype(BF16)
     mixed[...] = both.T.astype(BF16)
 
 
-def mix(info, joint, behind):
+def mix(chain, info, joint):
     _, rows, width = joint.shape
-    feat, pair = 2 * width // 3, 2 * width // 3 // HEADS * 2
-    per = feat // 2 // pair
-    spec = [
-        pl.BlockSpec((1, rows, pair), lambda i, part=part: (i // per, 0, part * per + i % per))
-        for part in range(3)
-    ]
-    n = HEADS // 2
-    return pl.pallas_call(
+    feat = 2 * width // 3
+    wide = feat // 2
+    spec = [pl.BlockSpec((1, rows, wide), lambda i, part=part: (i, 0, part)) for part in range(3)]
+    pairs_in_half = HEADS // 4
+    return chain.call(
         mix_kernel,
-        grid=(n,),
+        grid=(2,),
         out_shape=(
             shape((rows, feat), BF16),
             shape((feat, rows), BF16),
-            shape((n, 8, rows), F32),
+            shape((HEADS // 2, 8, rows), F32),
         ),
-        in_specs=[SMEM] + spec + [ANY],
+        in_specs=[SMEM] + spec,
         out_specs=(
-            pl.BlockSpec((rows, pair), lambda i: (0, i)),
-            pl.BlockSpec((pair, rows), lambda i: (i, 0)),
-            pl.BlockSpec((1, 8, rows), lambda i: (i, 0, 0)),
+            pl.BlockSpec((rows, wide), lambda i: (0, i)),
+            pl.BlockSpec((wide, rows), lambda i: (i, 0)),
+            pl.BlockSpec((pairs_in_half, 8, rows), lambda i: (i, 0, 0)),
         ),
-        compiler_params=params(12),
+        compiler_params=params(24),
         name="mix",
         cost_estimate=cost(10),
-    )(info, joint, joint, joint, behind)
-
-
-def mix_back_kernel(info, q, k, v, grad, stats, _, theirs, mine):
-    head = q.shape[-1] // 2
+    )(info, joint, joint, joint)
+
+
+def mix_back_kernel(info, q, k, v, grad, stats, theirs, mine):
+    head = theirs.shape[2] // (HEADS // 2)
+    count = q.shape[-1] // head
     scale = head**-0.5
     turned = k[0].T
-    parts = [[], [], []]
-    for h in (0, 1):
+
+    def start(h):
         cols = slice(h * head, (h + 1) * head)
         queries = q[0, :, cols] * scale
-        grad_h = grad[:, cols]
-        attn = jnp.exp(scores_of(info, k[0, :, cols], queries) - stats[0, h : h + 1])
-        grad_prob = dot_last(v[0, :, cols], grad_h)
+        scores = scores_of(info, k[0, :, cols], queries)
+        return cols, queries, scores, dot_last(v[0, :, cols], grad[:, cols])
+
+    def finish(h, cols, queries, scores, grad_prob):
+        attn = jnp.exp(scores - stats[h // 2, h % 2 : h % 2 + 1])
         inner = jnp.sum(attn * grad_prob, axis=0, keepdims=True)
         low = (attn * (grad_prob - inner)).astype(BF16)
-        parts[0].append(dot(turned[cols], low) * scale)
-        parts[1].append(dot(low, queries))
-        parts[2].append(dot(attn.astype(BF16), grad_h))
+        return (
+            dot(turned[cols], low) * scale,
+            dot(low, queries),
+            dot(attn.astype(BF16), grad[:, cols]),
+        )
+
+    ready = [start(h) for h in range(2)]
+    done = []
+    for h in range(count):
+        if h + 2 < count:
+            ready.append(start(h + 2))
+        done.append(finish(h, *ready[h]))
     out = [
-        jnp.concatenate(parts[0]).T.astype(BF16),
-        jnp.concatenate(parts[1], axis=1).astype(BF16),
-        jnp.concatenate(parts[2], axis=1).astype(BF16),
+        jnp.concatenate([d[0] for d in done]).T.astype(BF16),
+        jnp.concatenate([d[1] for d in done], axis=1).astype(BF16),
+        jnp.concatenate([d[2] for d in done], axis=1).astype(BF16),
     ]
-    step, per = pl.program_id(0), pl.num_programs(0) // 2
-
-    @pl.when(step < per)
+
+    @pl.when(pl.program_id(0) == 0)
     def _():
         for part in range(3):
             theirs[part] = out[part]
 
-    @pl.when(step >= per)
+    @pl.when(pl.program_id(0) == 1)
     def _():
         for part in range(3):
             mine[part] = out[part]
 
 
-def mix_back(info, joint, grad_mixed, stats, behind):
+def mix_back(chain, info, joint, grad_mixed, stats):
     _, rows, width = joint.shape
-    feat, pair = 2 * width // 3, 2 * width // 3 // HEADS * 2
-    per = feat // 2 // pair
-    n = HEADS // 2
+    feat = 2 * width // 3
+    wide = feat // 2
 
     def half(i, info):
-        return jnp.where(i < per, 1 - info[CORE], info[CORE])
+        return jnp.where(i == 0, 1 - info[CORE], info[CORE])
 
     spec = [
-        pl.BlockSpec(
-            (1, rows, pair), lambda i, info, part=part: (half(i, info), 0, part * per + i % per)
-        )
+        pl.BlockSpec((1, rows, wide), lambda i, info, part=part: (half(i, info), 0, part))
         for part in range(3)
     ]
     out = shape((3, rows, feat // 2), BF16)
-    return pl.pallas_call(
+    return chain.call(
         mix_back_kernel,
-        grid_spec=pltpu.PrefetchScalarGridSpec(
-            num_scalar_prefetch=1,
-            grid=(n,),
-            in_specs=spec
-            + [
-                pl.BlockSpec((rows, pair), lambda i, info: (0, half(i, info) * per + i % per)),
-                pl.BlockSpec(
-                    (1, 8, rows), lambda i, info: (half(i, info) * per + i % per, 0, 0)
-                ),
-                ANY,
-            ],
-            out_specs=(
-                pl.BlockSpec((3, rows, pair), lambda i, info: (0, 0, jnp.minimum(i, per - 1))),
-                pl.BlockSpec((3, rows, pair), lambda i, info: (0, 0, jnp.maximum(i - per, 0))),
-            ),
+        prefetch=1,
+        grid=(2,),
+        in_specs=spec
+        + [
+            pl.BlockSpec((rows, wide), lambda i, info: (0, half(i, info))),
+            pl.BlockSpec((HEADS // 4, 8, rows), lambda i, info: (half(i, info), 0, 0)),
+        ],
+        out_specs=(
+            pl.BlockSpec((3, rows, wide), lambda i, info: (0, 0, 0)),
+            pl.BlockSpec((3, rows, wide), lambda i, info: (0, 0, 0)),
         ),
         out_shape=(out, out),
-        compiler_params=params(12),
+        compiler_params=params(30),
         name="mix_back",
         cost_estimate=cost(16),
-    )(info, joint, joint, joint, grad_mixed, stats, behind)
+    )(info, joint, joint, joint, grad_mixed, stats)
 
 
 GELU = (0.254829592, -0.284496736, 1.421413741, -1.453152027, 1.061405429)
@@ -688,12 +726,16 @@
 
 
 def rise_kernel(
-    info, tokens, mixed, vecs, low, high, low_o, high_o, _, after, second, flipped, weights
+    info, tokens, mixed, vecs, low, high, low_o, high_o, weights, after, second, flipped, raw, sems
 ):
     feat = tokens.shape[1]
-    wide = low.shape[2] - feat // 2
-    settle(info, (low, high, low_o, high_o), weights, slice(wide, None))
+    copies = bring((low, high, low_o, high_o), raw, sems, low.shape[2] - raw.shape[-1])
+    for copy in copies:
+        copy.start()
     start = tokens[...].astype(F32) + vecs[5:6]
+    for copy in copies:
+        copy.wait()
+    settle(info, raw, weights)
     grown = [dot(mixed[...], weights[h].reshape(feat, feat // 2)) for h in (0, 1)]
     total = start + jnp.concatenate(grown, axis=1)
     after[...] = total
@@ -703,23 +745,28 @@
     flipped[...] = value.T.reshape(flipped.shape)
 
 
-def rise(info, tokens, mixed, vecs, pieces, behind):
+def rise(chain, info, tokens, mixed, vecs, pieces):
     rows, feat = tokens.shape
     vmem = pl.BlockSpec(memory_space=pltpu.VMEM)
-    return pl.pallas_call(
+    block = feat // 16
+    return chain.call(
         rise_kernel,
         out_shape=(
+            shape((2, 16, block, feat // 2), BF16),
             shape((rows, feat), F32),
             shape((rows, feat), BF16),
-            shape((16, feat // 16, rows), BF16),
+            shape((16, block, rows), BF16),
         ),
-        in_specs=[SMEM] + [vmem] * 7 + [ANY],
-        out_specs=(vmem,) * 3,
-        scratch_shapes=[pltpu.VMEM((2, 16, feat // 16, feat // 2), BF16)],
-        compiler_params=params(20),
+        in_specs=[SMEM] + [vmem] * 3 + [ANY] * 4,
+        out_specs=(vmem,) * 4,
+        scratch_shapes=[
+            pltpu.VMEM((4, 8, block, feat // 2), BF16),
+            pltpu.SemaphoreType.DMA((4,)),
+        ],
+        compiler_params=params(16),
         name="rise",
         cost_estimate=cost(5),
-    )(info, tokens, mixed, vecs, *pieces, behind)
+    )(info, tokens, mixed, vecs, *pieces)
 
 
 def widen_kernel(
@@ -730,67 +777,77 @@
     high,
     low_o,
     high_o,
-    _,
     weights,
     active,
     slope,
     mine,
     theirs,
-    turned,
-    block_sems,
+    raw,
+    sems,
 ):
-    step, steps = pl.program_id(0), pl.num_programs(0)
+    step, per = pl.program_id(0), pl.num_programs(0) // 2
     core = info[CORE]
     feat = second.shape[1]
     tile = active.shape[1]
-    wide = weights.shape[-1] - feat // 2
-    per = wide // tile
     rows = mine.shape[1]
     count = tile // rows
+    copies = bring((low, high, low_o, high_o), raw, sems, 0)
 
     @pl.when(step == 0)
     def _():
-        settle(info, (low, high, low_o, high_o), weights, slice(None))
-
+        for copy in copies:
+            copy.start()
+
+    for who in (0, 1):
+
+        @pl.when(step == who * per)
+        def _():
+            for copy in copies[2 * who : 2 * who + 2]:
+                copy.wait()
+            settle(info, raw, weights, (who,))
+
+    half = jnp.where(step < per, core, 1 - core)
     cols = pl.ds(pl.multiple_of(lax.rem(step, per) * tile, tile), tile)
-    w = weights[step // per, :, :, cols].reshape(feat, tile)
+    w = weights[half, :, :, cols].reshape(feat, tile)
     hidden = dot(second[...], w) + bias[...]
     value, grad = gelu_parts(hidden)
     value = value.astype(BF16)
     active[...] = value
     slope[...] = grad.astype(BF16)
-    turned[pl.ds(step * count, count)] = value.T.reshape(count, rows, -1)
-    for i in range(count):
-        at = step * count + i
-        chip = step * (count // 2) + i // 2
-
-        @pl.when(core == i % 2)
+    flipped = value.T.reshape(count, rows, -1)
+    first_chip = (half * per + lax.rem(step, per)) * (count // 2)
+    for c in (0, 1):
+
+        @pl.when(core == c)
         def _():
-            dst = mine.at[info[PLACE + chip]]
-            pltpu.make_async_copy(turned.at[at], dst, block_sems.at[at]).start()
-
-        @pl.when(core != i % 2)
-        def _():
-            dst = theirs.at[info[PLACE_O + chip]]
-            pltpu.make_async_copy(turned.at[at], dst, block_sems.at[at]).start()
-
-    @pl.when(step == steps - 1)
-    def _():
-        for at in range(turned.shape[0]):
-            pltpu.make_async_copy(turned.at[at], mine.at[0], block_sems.at[at]).wait()
-
-
-def widen(info, second, bias, pieces, behind):
+            for i in range(count):
+                chip = first_chip + i // 2
+                if i % 2 == c:
+                    mine[info[PLACE + chip]] = flipped[i]
+                else:
+                    theirs[info[PLACE_O + chip]] = flipped[i]
+
+
+def widen(chain, info, second, bias, pieces):
     rows, feat = second.shape
-    width = pieces[0].shape[-1]
-    hidden = 2 * width - feat
+    wide = pieces[0].shape[-1] - feat // 2
+    hidden = 2 * wide
     tile, block = 768, hidden // 32
+    per = wide // tile
     turned = shape((16, block, rows), BF16)
-    sets = (2, 16, feat // 16, width)
-    strip = pl.BlockSpec((rows, tile), lambda n: (0, n))
-    return pl.pallas_call(
+    sets = (2, 16, feat // 16, wide)
+
+    def at(n, info):
+        return jnp.where(n < per, info[CORE], 1 - info[CORE]) * per + n % per
+
+    def whole(dims):
+        return pl.BlockSpec(dims, lambda n, info: (0,) * len(dims))
+
+    strip = pl.BlockSpec((rows, tile), lambda n, info: (0, at(n, info)))
+    return chain.call(
         widen_kernel,
-        grid=(hidden // tile,),
+        prefetch=1,
+        grid=(2 * per,),
         out_shape=(
             shape(sets, BF16),
             shape((rows, hidden), BF16),
@@ -798,18 +855,23 @@
             turned,
             turned,
         ),
-        in_specs=[SMEM, full((rows, feat)), pl.BlockSpec((1, tile), lambda n: (0, n))]
-        + [full(pieces[0].shape)] * 4
-        + [ANY],
-        out_specs=(full(sets), strip, strip, ANY, ANY),
-        scratch_shapes=[pltpu.VMEM((32, block, rows), BF16), pltpu.SemaphoreType.DMA((32,))],
+        in_specs=[
+            whole((rows, feat)),
+            pl.BlockSpec((1, tile), lambda n, info: (0, at(n, info))),
+        ]
+        + [ANY] * 4,
+        out_specs=(whole(sets), strip, strip, whole(turned.shape), whole(turned.shape)),
+        scratch_shapes=[
+            pltpu.VMEM((4, 8, feat // 16, wide), BF16),
+            pltpu.SemaphoreType.DMA((4,)),
+        ],
         compiler_params=params(30),
         name="widen",
         cost_estimate=cost(18),
-    )(info, second, bias, *pieces, behind)
-
-
-def leave_kernel(after, active, down, vecs, _, output, total):
+    )(info, second, bias, *pieces)
+
+
+def leave_kernel(after, active, down, vecs, output, total):
     step = pl.program_id(0)
     part = dot(active[...], down[...])
 
@@ -826,11 +888,11 @@
         output[...] = total[...].astype(BF16)
 
 
-def leave(after, active, down, vecs, behind):
+def leave(chain, after, active, down, vecs):
     rows, feat = after.shape
     hidden = active.shape[1]
     tile = 768
-    return pl.pallas_call(
+    return chain.call(
         leave_kernel,
         grid=(hidden // tile,),
         out_shape=shape((rows, feat), BF16),
@@ -839,14 +901,13 @@
             pl.BlockSpec((rows, tile), lambda n: (0, n)),
             pl.BlockSpec((tile, feat), lambda n: (n, 0)),
             full((8, feat)),
-            ANY,
         ],
         out_specs=full((rows, feat)),
         scratch_shapes=[pltpu.VMEM((rows, feat), F32)],
         compiler_params=params(16),
         name="leave",
         cost_estimate=cost(7),
-    )(after, active, down, vecs, behind)
+    )(after, active, down, vecs)
 
 
 def fall_kernel(
@@ -861,9 +922,6 @@
     high,
     low_o,
     high_o,
-    _,
-    __,
-    ___,
     kept,
     theirs,
     mine,
@@ -875,6 +933,9 @@
     sums,
     weights,
     grad_second,
+    normed,
+    inverse,
+    raw,
     sems,
     sem,
 ):
@@ -887,10 +948,18 @@
 
     @pl.when(step == 0)
     def _():
-        for copy in fetch(info, (low, high, low_o, high_o), weights, sems, False):
+        copies = bring((low, high, low_o, high_o), raw, sems, 0)
+        for copy in copies:
+            copy.start()
+        normed[...], inverse[...] = centre(after[...])
+        grad_second[...] = jnp.zeros_like(grad_second)
+        for copy in copies:
             copy.wait()
+        for who in (0, 1):
+            c = core if who == 0 else 1 - core
+            for j in range(16):
+                weights[info[16 * who + j], c] = raw[2 * who + j // 8, j % 8]
         keeping.start()
-        grad_second[...] = jnp.zeros_like(grad_second)
 
     half = jnp.where(step < per, 1 - core, core)
     at = half * per + lax.rem(step, per)
@@ -910,12 +979,11 @@
 
     @pl.when(step == steps - 1)
     def _():
-        normed, inverse = centre(after[...])
         second = grad_second[...]
         live = grad_y[...].astype(F32)
-        sums[0:1] = jnp.sum(second * normed, axis=0, keepdims=True)
+        sums[0:1] = jnp.sum(second * normed[...], axis=0, keepdims=True)
         sums[1:2] = jnp.sum(second, axis=0, keepdims=True)
-        total = live + layer_back(second * vecs[1:2], normed, inverse)
+        total = live + layer_back(second * vecs[1:2], normed[...], inverse[...])
         grad_after[...] = total
         attn = total.astype(BF16)
         sums[2:3] = jnp.sum(attn.astype(F32), axis=0, keepdims=True)
@@ -928,7 +996,7 @@
         keeping.wait()
 
 
-def fall(info, grad_y, slope, up_set, after, vecs, pieces, behind):
+def fall(chain, info, grad_y, slope, up_set, after, vecs, proj_set, pieces):
     rows, feat = grad_y.shape
     hidden = slope.shape[1]
     tile = 768
@@ -941,40 +1009,41 @@
     def whole(dims):
         return pl.BlockSpec(dims, lambda n, info: (0,) * len(dims))
 
-    return pl.pallas_call(
+    return chain.call(
         fall_kernel,
-        grid_spec=pltpu.PrefetchScalarGridSpec(
-            num_scalar_prefetch=1,
-            grid=(steps,),
-            in_specs=[
-                whole((rows, feat)),
-                pl.BlockSpec((rows, tile), lambda n, info: (0, at(n, info))),
-                pl.BlockSpec(
-                    (1, feat, tile), lambda n, info: (at(n, info) // per, 0, n % per)
-                ),
-                whole((rows, feat)),
-                whole((8, feat)),
-                pl.BlockSpec((2, feat, feat // 2), lambda n, info: (0, 0, 4)),
-            ]
-            + [ANY] * 7,
-            out_specs=(
-                ANY,
-                pl.BlockSpec((rows, tile), lambda n, info: (0, jnp.minimum(n, per - 1))),
-                pl.BlockSpec((rows, tile), lambda n, info: (0, jnp.maximum(n - per, 0))),
-                pl.BlockSpec((1, tile), lambda n, info: (0, at(n, info))),
-                whole((rows, feat)),
-                whole((rows, feat // 2)),
-                whole((rows, feat // 2)),
-                whole((rows, feat)),
-                whole((8, feat)),
+        prefetch=1,
+        grid=(steps,),
+        in_specs=[
+            whole((rows, feat)),
+            pl.BlockSpec((rows, tile), lambda n, info: (0, at(n, info))),
+            pl.BlockSpec(
+                (1, feat, tile), lambda n, info: (at(n, info) // per, 0, n % per)
             ),
-            scratch_shapes=[
-                pltpu.VMEM((16, 2, hidden // 32, feat), BF16),
-                pltpu.VMEM((rows, feat), F32),
-                pltpu.SemaphoreType.DMA((32,)),
-                pltpu.SemaphoreType.DMA,
-            ],
+            whole((rows, feat)),
+            whole((8, feat)),
+            whole((2, feat, feat // 2)),
+        ]
+        + [ANY] * 4,
+        out_specs=(
+            ANY,
+            pl.BlockSpec((rows, tile), lambda n, info: (0, jnp.minimum(n, per - 1))),
+            pl.BlockSpec((rows, tile), lambda n, info: (0, jnp.maximum(n - per, 0))),
+            pl.BlockSpec((1, tile), lambda n, info: (0, at(n, info))),
+            whole((rows, feat)),
+            whole((rows, feat // 2)),
+            whole((rows, feat // 2)),
+            whole((rows, feat)),
+            whole((8, feat)),
         ),
+        scratch_shapes=[
+            pltpu.VMEM((16, 2, hidden // 32, feat), BF16),
+            pltpu.VMEM((rows, feat), F32),
+            pltpu.VMEM((rows, feat), F32),
+            pltpu.VMEM((rows, 1), F32),
+            pltpu.VMEM((4,) + pieces[0].shape, BF16),
+            pltpu.SemaphoreType.DMA((4,)),
+            pltpu.SemaphoreType.DMA,
+        ],
         out_shape=(
             shape((16, 2, hidden // 32, feat), BF16),
             shape((rows, hidden // 2), BF16),
@@ -986,10 +1055,10 @@
             shape((rows, feat), BF16),
             shape((8, feat), F32),
         ),
-        compiler_params=params(28),
+        compiler_params=params(32),
         name="fall",
         cost_estimate=cost(18),
-    )(info, grad_y, slope, up_set, after, vecs, up_set, *pieces, *behind)
+    )(info, grad_y, slope, up_set, after, vecs, proj_set, *pieces)
 
 
 def exit_kernel(
@@ -1002,7 +1071,6 @@
     vecs,
     sums_a,
     bias,
-    _,
     grad_tokens,
     keep,
     away,
@@ -1054,7 +1122,7 @@
         away[...] = extra[8:].astype(BF16)
 
 
-def exit_back(info, tokens, mine, theirs, first_set, grad_after, vecs, sums_a, bias, behind):
+def exit_back(chain, info, tokens, mine, theirs, first_set, grad_after, vecs, sums_a, bias):
     rows, feat = tokens.shape
     third = feat // 2
     block = feat // 16
@@ -1062,33 +1130,30 @@
     def whole(dims):
         return pl.BlockSpec(dims, lambda n, info: (0,) * len(dims))
 
-    return pl.pallas_call(
+    return chain.call(
         exit_kernel,
-        grid_spec=pltpu.PrefetchScalarGridSpec(
-            num_scalar_prefetch=1,
-            grid=(2,),
-            in_specs=[
-                whole((rows, feat)),
-                whole((3, rows, third)),
-                whole((3, rows, third)),
-                pl.BlockSpec(
-                    (1, feat, 3 * third),
-                    lambda n, info: (jnp.where(n == 0, info[CORE], 1 - info[CORE]), 0, 0),
-                ),
-                whole((rows, feat)),
-                whole((8, feat)),
-                whole((8, feat)),
-                whole(bias.shape),
-                ANY,
-            ],
-            out_specs=(whole((rows, feat)), whole((8, block, 128)), whole((8, block, 128))),
-            scratch_shapes=[
-                pltpu.VMEM((rows, feat), F32),
-                pltpu.VMEM((rows, 3 * third), BF16),
-                pltpu.VMEM((128, feat), F32),
-                pltpu.VMEM((16, block, 128), F32),
-            ],
-        ),
+        prefetch=1,
+        grid=(2,),
+        in_specs=[
+            whole((rows, feat)),
+            whole((3, rows, third)),
+            whole((3, rows, third)),
+            pl.BlockSpec(
+                (1, feat, 3 * third),
+                lambda n, info: (jnp.where(n == 0, info[CORE], 1 - info[CORE]), 0, 0),
+            ),
+            whole((rows, feat)),
+            whole((8, feat)),
+            whole((8, feat)),
+            whole(bias.shape),
+        ],
+        out_specs=(whole((rows, feat)), whole((8, block, 128)), whole((8, block, 128))),
+        scratch_shapes=[
+            pltpu.VMEM((rows, feat), F32),
+            pltpu.VMEM((rows, 3 * third), BF16),
+            pltpu.VMEM((128, feat), F32),
+            pltpu.VMEM((16, block, 128), F32),
+        ],
         out_shape=(
             shape((rows, feat), BF16),
             shape((8, block, 128), F32),
@@ -1097,7 +1162,7 @@
         compiler_params=params(18),
         name="exit_back",
         cost_estimate=cost(8),
-    )(info, tokens, mine, theirs, first_set, grad_after, vecs, sums_a, bias, behind)
+    )(info, tokens, mine, theirs, first_set, grad_after, vecs, sums_a, bias)
 
 
 def line_up(info, left, left_o, turned):
@@ -1116,7 +1181,7 @@
 
 
 def outer_up_kernel(
-    info, left, left_o, right, right_o, low, low_o, attn, attn_o, _, keep, away, turned
+    info, left, left_o, right, right_o, low, low_o, attn, attn_o, keep, away, turned
 ):
     step, last = pl.program_id(0), pl.num_programs(0) - 1
 
@@ -1138,14 +1203,14 @@
         away[:, :, : attn.shape[1]] = total[8:].astype(BF16)
 
 
-def outer_up(info, left, left_o, right, right_o, low, low_o, attn, attn_o, behind):
+def outer_up(chain, info, left, left_o, right, right_o, low, low_o, attn, attn_o):
     _, block, rows = left.shape
     tile = 2 * attn.shape[1]
     n = right.shape[1] // tile
     cols = right.shape[1] + attn.shape[1]
     strip = pl.BlockSpec((rows, tile), lambda i: (0, jnp.minimum(i, n - 1)))
     out = pl.BlockSpec((8, block, tile), lambda i: (0, 0, i))
-    return pl.pallas_call(
+    return chain.call(
         outer_up_kernel,
         grid=(n + 1,),
         out_shape=(shape((8, block, cols), F32), shape((8, block, cols), BF16)),
@@ -1153,17 +1218,16 @@
         + [full(left.shape)] * 2
         + [strip] * 2
         + [full(left.shape)] * 2
-        + [full(attn.shape)] * 2
-        + [ANY],
+        + [full(attn.shape)] * 2,
         out_specs=(out, out),
         scratch_shapes=[pltpu.VMEM((16, block, 2 * rows), BF16)],
         compiler_params=params(20),
         name="outer_up",
         cost_estimate=cost(8),
-    )(info, left, left_o, right, right_o, low, low_o, attn, attn_o, behind)
-
-
-def outer_qkv_kernel(info, left, left_o, right, right_o, _, keep, away, turned):
+    )(info, left, left_o, right, right_o, low, low_o, attn, attn_o)
+
+
+def outer_qkv_kernel(info, left, left_o, right, right_o, keep, away, turned):
     tile = right.shape[2]
     line_up(info, left, left_o, turned)
     for part in range(3):
@@ -1173,23 +1237,23 @@
         away[:, :, cols] = total[8:].astype(BF16)
 
 
-def outer_qkv(info, left, left_o, right, right_o, behind):
+def outer_qkv(chain, info, left, left_o, right, right_o):
     _, block, rows = left.shape
     cols = 3 * right.shape[2]
     vmem = pl.BlockSpec(memory_space=pltpu.VMEM)
-    return pl.pallas_call(
+    return chain.call(
         outer_qkv_kernel,
         out_shape=(shape((8, block, cols), F32), shape((8, block, cols), BF16)),
-        in_specs=[SMEM] + [vmem] * 4 + [ANY],
+        in_specs=[SMEM] + [vmem] * 4,
         out_specs=(vmem, vmem),
         scratch_shapes=[pltpu.VMEM((16, block, 2 * rows), BF16)],
         compiler_params=params(20),
         name="outer_qkv",
         cost_estimate=cost(8),
-    )(info, left, left_o, right, right_o, behind)
-
-
-def outer_down_kernel(left, left_o, right, right_o, _, keep, away):
+    )(info, left, left_o, right, right_o)
+
+
+def outer_down_kernel(left, left_o, right, right_o, keep, away):
     def flat(blocks):
         return blocks[...].reshape(-1, blocks.shape[-1])
 
@@ -1205,15 +1269,15 @@
         away[...] = total.astype(BF16)
 
 
-def outer_down(left, left_o, right, right_o, behind):
+def outer_down(chain, left, left_o, right, right_o):
     _, block, rows = left.shape
     feat = right.shape[1]
     strip = pl.BlockSpec((4, block, rows), lambda j: ((j + 2) % 4, 0, 0))
-    return pl.pallas_call(
+    return chain.call(
         outer_down_kernel,
         grid=(4,),
         out_shape=(shape((8, block, feat), F32), shape((8, block, feat), BF16)),
-        in_specs=[strip, strip, full((rows, feat)), full((rows, feat)), ANY],
+        in_specs=[strip, strip, full((rows, feat)), full((rows, feat))],
         out_specs=(
             pl.BlockSpec((4, block, feat), lambda j: (jnp.maximum(j - 2, 0), 0, 0)),
             pl.BlockSpec((4, block, feat), lambda j: (jnp.minimum(j, 1), 0, 0)),
@@ -1221,29 +1285,29 @@
         compiler_params=params(16),
         name="outer_down",
         cost_estimate=cost(8),
-    )(left, left_o, right, right_o, behind)
-
-
-def add_first_kernel(keep, got, _, kept, away):
+    )(left, left_o, right, right_o)
+
+
+def add_first_kernel(keep, got, kept, away):
     kept[...] = keep[:4] + got[:4].astype(F32)
     away[...] = (keep[4:] + got[4:].astype(F32)).astype(BF16)
 
 
-def shift_first(keep, away, behind, micros=0):
+def shift_first(chain, keep, away, micros=0):
     _, rows, cols = keep.shape
     vmem = pl.BlockSpec(memory_space=pltpu.VMEM)
-    return pl.pallas_call(
+    return chain.call(
         add_first_kernel,
         out_shape=(shape((4, rows, cols), F32), shape((4, rows, cols), BF16)),
-        in_specs=[vmem, vmem, ANY],
+        in_specs=[vmem, vmem],
         out_specs=(vmem, vmem),
         compiler_params=params(12),
         name="shift_first",
         cost_estimate=cost(micros),
-    )(keep, send(away, second_way), behind)
-
-
-def add_both_kernel(keep, got, few_keep, few_got, _, kept, away):
+    )(keep, send(away, second_way))
+
+
+def add_both_kernel(keep, got, few_keep, few_got, kept, away):
     split = keep.shape[2]
     kept[:, :, :split] = keep[:4] + got[:4].astype(F32)
     kept[:, :, split:] = few_keep[:4] + few_got[:4].astype(F32)
@@ -1251,39 +1315,39 @@
     away[:, :, split:] = (few_keep[4:] + few_got[4:].astype(F32)).astype(BF16)
 
 
-def shift_both(keep, away, few_keep, few_away, behind):
+def shift_both(chain, keep, away, few_keep, few_away):
     _, rows, cols = keep.shape
     cols += few_keep.shape[2]
     vmem = pl.BlockSpec(memory_space=pltpu.VMEM)
-    return pl.pallas_call(
+    return chain.call(
         add_both_kernel,
         out_shape=(shape((4, rows, cols), F32), shape((4, rows, cols), BF16)),
-        in_specs=[vmem] * 4 + [ANY],
+        in_specs=[vmem] * 4,
         out_specs=(vmem, vmem),
         compiler_params=params(12),
         name="shift_both",
         cost_estimate=cost(0),
-    )(keep, send(away, second_way), few_keep, send(few_away, second_way), behind)
-
-
-def add_second_kernel(keep, got, _, base, one, two, three):
+    )(keep, send(away, second_way), few_keep, send(few_away, second_way))
+
+
+def add_second_kernel(keep, got, base, one, two, three):
     base[...] = keep[0] + got[0].astype(F32)
     for s, out in ((1, one), (2, two), (3, three)):
         out[...] = (keep[s] + got[s].astype(F32)).astype(BF16)
 
 
-def shift_second(keep, away, behind):
+def shift_second(chain, keep, away):
     _, rows, cols = keep.shape
     vmem = pl.BlockSpec(memory_space=pltpu.VMEM)
-    base, *lows = pl.pallas_call(
+    base, *lows = chain.call(
         add_second_kernel,
         out_shape=(shape((rows, cols), F32),) + (shape((rows, cols), BF16),) * 3,
-        in_specs=[vmem, vmem, ANY],
+        in_specs=[vmem, vmem],
         out_specs=(vmem,) * 4,
         compiler_params=params(8),
         name="shift_second",
         cost_estimate=cost(0),
-    )(keep, send(away, first_way), behind)
+    )(keep, send(away, first_way))
     return base, [send(low, along_z(s)) for low, s in zip(lows, (1, 2, 3))]
 
 
@@ -1293,24 +1357,24 @@
     )
 
 
-def add_down_kernel(base, one, two, three, _, out):
+def add_down_kernel(base, one, two, three, out):
     out[...] = total_of(base, (one, two, three))
 
 
-def home_down(base, parts, behind):
+def home_down(chain, base, parts):
     vmem = pl.BlockSpec(memory_space=pltpu.VMEM)
-    return pl.pallas_call(
+    return chain.call(
         add_down_kernel,
         out_shape=shape(base.shape, F32),
-        in_specs=[vmem] * 4 + [ANY],
+        in_specs=[vmem] * 4,
         out_specs=vmem,
         compiler_params=params(8),
         name="home_down",
         cost_estimate=cost(0),
-    )(base, *parts, behind)
-
-
-def add_last_kernel(info, base, one, two, three, _, mine, theirs, total):
+    )(base, *parts)
+
+
+def add_last_kernel(info, base, one, two, three, mine, theirs, total):
     core = info[CORE]
     half = mine.shape[0]
     total[...] = total_of(base, (one, two, three))
@@ -1318,20 +1382,20 @@
     theirs[...] = total[pl.ds(pl.multiple_of((1 - core) * half, half), half)]
 
 
-def home(info, base, parts, behind):
+def home(chain, info, base, parts):
     rows, cols = base.shape
     vmem = pl.BlockSpec(memory_space=pltpu.VMEM)
     out = shape((rows // 2, cols), F32)
-    mine, theirs = pl.pallas_call(
+    mine, theirs = chain.call(
         add_last_kernel,
         out_shape=(out, out),
-        in_specs=[SMEM] + [vmem] * 4 + [ANY],
+        in_specs=[SMEM] + [vmem] * 4,
         out_specs=(vmem, vmem),
         scratch_shapes=[pltpu.VMEM((rows, cols), F32)],
         compiler_params=params(8),
         name="home",
         cost_estimate=cost(0),
-    )(info, base, *parts, behind)
+    )(info, base, *parts)
     return mine, swap(theirs)
 
 
@@ -1361,11 +1425,11 @@
         lay(1)
 
 
-def finish(info, qkv, qkv_o, up, up_o):
+def finish(chain, info, qkv, qkv_o, up, up_o):
     rows = qkv.shape[0]
     third = (qkv.shape[1] - 128) // 3
     vmem = pl.BlockSpec(memory_space=pltpu.VMEM)
-    return pl.pallas_call(
+    return chain.call(
         finish_kernel,
         out_shape=(
             shape((rows, 6 * third), F32),
@@ -1402,69 +1466,67 @@
     chip, core = lax.axis_index("dp"), lax.axis_index("fsdp")
     info = facts(chip, core, lengths[0])
 
+    chain = Chain()
+
     small = jnp.concatenate([gains, shifts], axis=1)
     small = jnp.pad(small, ((0, 0), (0, 128 - small.shape[1])))
     small = small + jnp.pad(up_bias[None], ((0, rows - 1), (128 - up_bias.shape[0], 0)))
-    mine, theirs = halves(info, qkv_weight, proj_weight, up_weight)
-    one = 3 * third + 128
-    piece, piece_up = pieces_of(info, mine, swap(theirs), small, 3 * third)
-    zs, piece_up = gather([piece] + near_z(piece, (1, 2, 3)), (piece_up,))
-    up_z = near_z(piece_up, (1, 2))
-    low, piece_up = gather([zs, send(zs, first_way)], (piece_up,), up_z)
-    up_z += near_z(piece_up, (3,))
+    piece = first_piece(chain, info, qkv_weight, swap(qkv_weight), small)
+    piece_up = up_piece(chain, info, up_weight, swap(up_weight), proj_weight, swap(proj_weight))
+    zs, piece_up = gather(chain, [piece] + near_z(piece, (1, 2, 3)), (piece_up,))
+    up_z = near_z(piece_up, (1, 2, 3))
+    (low,) = gather(chain, [zs, send(zs, first_way)])
     high = send(low, second_way)
-    (zs_up,) = gather([piece_up] + up_z)
-    high = gate(high, zs_up)
-    first_pieces = (low, high, swap(low), swap(high))
-
+    (zs_up,) = gather(chain, [piece_up] + up_z, (), 5)
+    high = gate(chain, high, 0)
+    pieces = (low, high, swap(low), swap(high))
     first_set, vecs, bias, first, first_t, joint, grad_y, down = enter(
-        info, tokens, upstream, down_weight, hidden, first_pieces
-    )
-    grad_y_o = swap(grad_y)
-    first_set = first_set.reshape(2, feat, one)
-    first_o = swap(first_t)
-    (low,) = gather([zs_up, send(zs_up, first_way)], (), (vecs,))
+        chain, info, tokens, upstream, down_weight, hidden, pieces
+    )
+    grad_y_o, first_o = swap(grad_y), swap(first_t)
+    first_set = first_set.reshape(2, feat, 3 * third + 128)
+    (low,) = gather(chain, [zs_up, send(zs_up, first_way)])
     down_z = near_z(down, (1, 2, 3))
-    mixed, mixed_t, stats = mix(info, joint, low)
-    high = gate(send(low, second_way), mixed)
-    up_pieces = (low, high, swap(low), swap(high))
-    (zs_down,) = gather([down] + down_z, (), (high,), 5)
+    mixed, mixed_t, stats = mix(chain, info, joint)
     mixed_t = mixed_t.reshape(first_t.shape)
     mixed_o = swap(mixed_t)
-    after, second, second_t = rise(info, tokens, mixed, vecs, up_pieces, zs_down)
+    high = send(low, second_way)
+    pieces = (low, high, swap(low), swap(high))
+    (zs_down,) = gather(chain, [down] + down_z, (), 5)
+    proj_set, after, second, second_t = rise(chain, info, tokens, mixed, vecs, pieces)
     second_o = swap(second_t)
-    (low,) = gather([zs_down, send(zs_down, first_way)], (), (second,))
-    up_set, active, slope, turned, turned_t = widen(info, second, bias, up_pieces, low)
-    up_set = up_set.reshape(2, feat, wide + third)
-    high = gate(send(low, second_way), slope, 5)
-    down_pieces = (low, high, swap(low), swap(high))
-    down = outer_down(turned, swap(turned_t), grad_y, grad_y_o, slope)
+    (low,) = gather(chain, [zs_down, send(zs_down, first_way)])
+    up_set, active, slope, turned, turned_t = widen(chain, info, second, bias, pieces)
+    up_set = up_set.reshape(2, feat, wide)
+    proj_set = proj_set.reshape(2, feat, third)
+    high = gate(chain, send(low, second_way), 5)
+    pieces = (low, high, swap(low), swap(high))
+    down = outer_down(chain, turned, swap(turned_t), grad_y, grad_y_o)
     down_set, hid_theirs, hid_mine, bias_sum, grad_after, at_theirs, at_mine, grad_mixed, sums_a = (
-        fall(
-            info, grad_y, slope, up_set, after, vecs, down_pieces, (down[1], second_o, mixed_o)
-        )
+        fall(chain, info, grad_y, slope, up_set, after, vecs, proj_set, pieces)
     )
     hid_o, at_o = swap(hid_theirs), swap(at_theirs)
-    down = shift_first(*down, hid_theirs, 5)
-    up = outer_up(
-        info, second_t, second_o, hid_mine, hid_o, mixed_t, mixed_o, at_mine, at_o, down[1]
-    )
-    down = shift_second(*down, up[1])
-    theirs, mine = mix_back(info, joint, grad_mixed, stats, down[0])
+    down = shift_first(chain, *down, 5)
+    up = outer_up(chain, info, second_t, second_o, hid_mine, hid_o, mixed_t, mixed_o, at_mine, at_o)
+    down = shift_second(chain, *down)
+    theirs, mine = mix_back(chain, info, joint, grad_mixed, stats)
     theirs_o = swap(theirs)
-    own_down = home_down(*down, theirs)
-    up = shift_first(*up, own_down, 5)
-    qkv = outer_qkv(info, first_t, first_o, mine, theirs_o, up[1])
+    own_down = home_down(chain, *down)
+    up = shift_first(chain, *up, 5)
+    chain.near(up[1])
+    qkv = outer_qkv(chain, info, first_t, first_o, mine, theirs_o)
     grad_tokens, few_keep, few_away = exit_back(
-        info, tokens, mine, theirs, first_set, grad_after, vecs, sums_a, bias_sum, qkv[1]
-    )
-    up = shift_second(*up, grad_tokens)
-    qkv = shift_both(*qkv, few_keep, few_away, up[0])
-    output = leave(after, active, down_set.reshape(hidden, feat), vecs, qkv[1])
-    base, parts = shift_second(*qkv, output)
-    own_up = home(info, *up, base)
-    own_qkv = home(info, base, parts, own_up[0])
-    out_qkv, out_proj, out_up, out_gains, out_shifts, out_bias = finish(info, *own_qkv, *own_up)
+        chain, info, tokens, mine, theirs, first_set, grad_after, vecs, sums_a, bias_sum
+    )
+    up = shift_second(chain, *up)
+    qkv = shift_both(chain, *qkv, few_keep, few_away)
+    output = leave(chain, after, active, down_set.reshape(hidden, feat), vecs)
+    qkv = shift_second(chain, *qkv)
+    own_up = home(chain, info, *up)
+    own_qkv = home(chain, info, *qkv)
+    out_qkv, out_proj, out_up, out_gains, out_shifts, out_bias = finish(
+        chain, info, *own_qkv, *own_up
+    )
     return (
         output,
         grad_tokens,

time: 237 us -> 227 us (0.958)
  Pallas kernels: 125 us -> 116 us
  starting transfers between devices: 45.7 us -> 48.8 us
  local copies, waits for them, and re-layouts: 9.28 us -> 6.36 us
    pallas_call x32 -> x31, Pallas kernels: 125 us -> 116 us  [with_token(): *outs, self.token = run(*args, *extra, *([self.token] if held else []))]
    ppermute x48 -> x50, starting transfers between devices: 45.7 us -> 48.8 us  [send(): return lax.ppermute(array, AXES, pairs(move))]
    unnamed x54 -> x28, local copies, waits for them, and re-layouts: 9.05 us -> 6.12 us
    ppermute x48 -> x50, waiting for transfers between devices: 52.9 us -> 51.4 us  [send(): return lax.ppermute(array, AXES, pairs(move))]
  transfers between devices with their start and end apart: 48 -> 50, of which waited for: 18 -> 18; matrix products, arithmetic and copies ran while one was open for 1% -> 1% of each run, Pallas kernels for 51% -> 50%
where the time goes in v4:
time: 227 us; the launch traced here: 226 us
  Pallas kernels  116 us (51%)
  waiting for transfers between devices  51.4 us (23%)
  starting transfers between devices  48.8 us (21%)
  local copies, waits for them, and re-layouts  6.36 us (3%)
    pallas_call x31, Pallas kernels, with_token(): *outs, self.token = run(*args, *extra, *([self.token] if held else []))  116 us
    ppermute x50, waiting for transfers between devices, send(): return lax.ppermute(array, AXES, pairs(move))  51.4 us
    ppermute x50, starting transfers between devices, send(): return lax.ppermute(array, AXES, pairs(move))  48.8 us
    unnamed x28, local copies, waits for them, and re-layouts  6.12 us
  transfers between devices with their start and end apart: 50, of which 18 were waited for; matrix products, arithmetic and copies ran while one was open for 1% of the time, Pallas kernels for 50%

profile of v4, /device:TPU:0, one launch (start us, length us, event | category | flops | bytes accessed | tf_op | source)
XLA Modules:
  0.0 226.0 jit_solution(871789535754275733)
XLA Ops:
  5.2 3.1 %collective-permute-start.1 = (bf16[1,48,1280]{2,1,0:T(8,128)(2,1)S(1)}, bf16[1,48,1280]{2,1,0:T(8,128)(2,1)S(1)}, u32[]{:S(2)}, u32[]{:S(2)}) collective-permute-start(bf16[1,48,1280]{2,1,0:T(8,128)(2,1)S(1)} %get-tuple-element.119.refs_0_), channel_id=1, source_target_pairs={{0,8},{1,9},{2,10},{3,11},{4,12},{5,13},{6,14},{7,15},{8,0},{9,1},... | collective-permute-start | bytes 368648 | tf_op jit(solution)/shard_map/ppermute | solution.py:266
  8.2 2.6 %collective-permute-start.2 = (bf16[1,48,1280]{2,1,0:T(8,128)(2,1)S(1)}, bf16[1,48,1280]{2,1,0:T(8,128)(2,1)S(1)}, u32[]{:S(2)}, u32[]{:S(2)}) collective-permute-start(bf16[1,48,1280]{2,1,0:T(8,128)(2,1)S(1)} %get-tuple-element.119.refs_0_), channel_id=1, source_target_pairs={{0,16},{1,17},{2,18},{3,19},{4,20},{5,21},{6,22},{7,23},{8,24},{9,... | collective-permute-start | bytes 368648 | tf_op jit(solution)/shard_map/ppermute | solution.py:266
  14.5 6.1 %collective-permute-done.2.refs_2_ = bf16[1,48,1280]{2,1,0:T(8,128)(2,1)S(1)} collective-permute-done((bf16[1,48,1280]{2,1,0:T(8,128)(2,1)S(1)}, bf16[1,48,1280]{2,1,0:T(8,128)(2,1)S(1)}, u32[]{:S(2)}, u32[]{:S(2)}) %collective-permute-start.2) | collective-permute-done | bytes 122912 | tf_op jit(solution)/shard_map/ppermute | solution.py:266
  22.2 2.1 collective-permute-start.8
  26.8 2.8 %collective-permute-done.6.refs_1_ = bf16[4,48,1280]{2,1,0:T(8,128)(2,1)S(1)} collective-permute-done((bf16[4,48,1280]{2,1,0:T(8,128)(2,1)S(1)}, bf16[4,48,1280]{2,1,0:T(8,128)(2,1)S(1)}, u32[]{:S(2)}, u32[]{:S(2)}) %collective-permute-start.6) | collective-permute-done | bytes 491552 | tf_op jit(solution)/shard_map/ppermute | solution.py:266
  32.1 8.0 %collective-permute-done.9.refs_2_ = bf16[1,48,1920]{2,1,0:T(8,128)(2,1)S(1)} collective-permute-done((bf16[1,48,1920]{2,1,0:T(8,128)(2,1)S(1)}, bf16[1,48,1920]{2,1,0:T(8,128)(2,1)S(1)}, u32[]{:S(2)}, u32[]{:S(2)}) %collective-permute-start.9) | collective-permute-done | bytes 184352 | tf_op jit(solution)/shard_map/ppermute | solution.py:266
  41.0 3.9 %collective-permute-done.7.refs_0_ = bf16[8,48,1280]{2,1,0:T(8,128)(2,1)} collective-permute-done((bf16[8,48,1280]{2,1,0:T(8,128)(2,1)}, bf16[8,48,1280]{2,1,0:T(8,128)(2,1)}, u32[]{:S(2)}, u32[]{:S(2)}) %collective-permute-start.7) | collective-permute-done | bytes 983072 | tf_op jit(solution)/shard_map/ppermute | solution.py:266
  47.8 7.0 %enter.1 = (bf16[2,16,48,1280]{3,2,1,0:T(8,128)(2,1)S(1)}, f32[8,768]{1,0:T(8,128)S(1)}, f32[1,3072]{1,0:T(1,128)S(1)}, bf16[512,768]{1,0:T(8,128)(2,1)}, bf16[1...) custom-call(s32[66]{0:T(128)S(1)} %stack.239.refs_0_, ...), custom_call_target="tpu_custom_call", output_to_operand_aliasing={{8}: (8, {})} | custom-call | flops 240000008192 | bytes 1 | tf_op jit(solution)/shard_map/enter/pallas_call | solution.py:345
  56.8 2.6 %gather.9 = (bf16[8,48,1920]{2,1,0:T(8,128)(2,1)}, f32[8,128]{1,0:T(8,128)S(1)}) custom-call(bf16[4,48,1920]{2,1,0:T(8,128)(2,1)} %get-tuple-element.132.refs_0_, bf16[4,48,1920]{2,1,0:T(8,128)(2,1)} %collective-permute-done.13.refs_1_, f32[8,128]{1,0:T(8,128)S(1)} %get-tuple-element.133.refs_2_), custom_call_target="tpu_custom_call", output_to_operand_aliasing={{1}: (2, {})} | custom-call | bytes 1 | tf_op jit(solution)/shard_map/gather/pallas_call | solution.py:345
  60.8 2.1 collective-permute-start.17
  65.4 7.0 %mix.1 = (bf16[512,768]{1,0:T(8,128)(2,1)S(1)}, bf16[768,512]{1,0:T(8,128)(2,1)}, f32[6,8,512]{2,1,0:T(8,128)S(1)}, f32[8,128]{1,0:T(8,128)S(1)}) custom-call(s32[66]{0:T(128)S(1)} %stack.239.refs_0_, bf16[2,512,1152]{2,1,0:T(8,128)(2,1)S(1)} %get-tuple-element.131.refs_1_.refs_2_.refs_3_, ...), custom_call_target="tpu_custom_call", output_to_operand_aliasing={{3}: (4, {})} | custom-call | flops 299999985664 | bytes 1 | tf_op jit(solution)/shard_map/mix/pallas_call | solution.py:345
  72.4 4.8 %collective-permute-done.18.refs_2_ = bf16[1,96,768]{2,1,0:T(8,128)(2,1)} collective-permute-done((bf16[1,96,768]{2,1,0:T(8,128)(2,1)}, bf16[1,96,768]{2,1,0:T(8,128)(2,1)}, u32[]{:S(2)}, u32[]{:S(2)}) %collective-permute-start.18) | collective-permute-done | bytes 147488 | tf_op jit(solution)/shard_map/ppermute | solution.py:266
  79.0 2.1 gather.10
  83.0 4.4 %rise.1 = (bf16[2,16,48,384]{3,2,1,0:T(8,128)(2,1)S(1)}, f32[512,768]{1,0:T(8,128)S(1)}, bf16[512,768]{1,0:T(8,128)(2,1)S(1)}, bf16[16,48,512]{2,1,0:T(8,128)(2,1)}, f32[8,128]{1,0:T(8,128)S(1)}) custom-call(s32[66]{0:T(128)S(1)} %stack.239.refs_0_, bf16[512,768]{1,0:T(8,128)(2,1)S(1)} %copy-done.5, ...), custom_call_target="tpu_custom_call", output_to_operand_aliasing={{4}: (8, {})} | custom-call | flops 149999992832 | bytes 1 | tf_op jit(solution)/shard_map/rise/pallas_call | solution.py:345
  87.4 3.9 %collective-permute-done.20.refs_1_ = bf16[4,96,768]{2,1,0:T(8,128)(2,1)} collective-permute-done((bf16[4,96,768]{2,1,0:T(8,128)(2,1)}, bf16[4,96,768]{2,1,0:T(8,128)(2,1)}, u32[]{:S(2)}, u32[]{:S(2)}) %collective-permute-start.20) | collective-permute-done | bytes 589856 | tf_op jit(solution)/shard_map/ppermute | solution.py:266
  91.3 2.3 %gather.11 = (bf16[8,96,768]{2,1,0:T(8,128)(2,1)}, f32[8,128]{1,0:T(8,128)S(1)}) custom-call(bf16[4,96,768]{2,1,0:T(8,128)(2,1)} %get-tuple-element.144.refs_0_, bf16[4,96,768]{2,1,0:T(8,128)(2,1)} %collective-permute-done.20.refs_1_, f32[8,128]{1,0:T(8,128)S(1)} %get-tuple-element.145.refs_2_), custom_call_target="tpu_custom_call", output_to_operand_aliasing={{1}: (2, {})} | custom-call | bytes 1 | tf_op jit(solution)/shard_map/gather/pallas_call | solution.py:345
  95.1 12.7 %widen.1 = (bf16[2,16,48,1536]{3,2,1,0:T(8,128)(2,1)S(1)}, bf16[512,3072]{1,0:T(8,128)(2,1)S(1)}, bf16[512,3072]{1,0:T(8,128)(2,1)S(1)}, bf16[16,96,512]{2,1,0:T...) custom-call(s32[66]{0:T(128)S(1)} %stack.239.refs_0_, ...), custom_call_target="tpu_custom_call", output_to_operand_aliasing={{5}: (7, {})} | custom-call | flops 539999993856 | bytes 1 | tf_op jit(solution)/shard_map/widen/pallas_call | solution.py:345
  107.9 2.2 collective-permute-done.21.refs_0_
  114.0 6.2 %outer_down.1 = (f32[8,96,768]{2,1,0:T(8,128)S(1)}, bf16[8,96,768]{2,1,0:T(8,128)(2,1)}, f32[8,128]{1,0:T(8,128)S(1)}) custom-call(bf16[16,96,512]{2,1,0:T(8,128)(2,1)S(1)} %get-tuple-element.155.refs_0_, bf16[16,96,512]{2,1,0:T(8,128)(2,1)} %collective-permute-done.24.refs_1_, ...), custom_call_target="tpu_custom_call", output_to_operand_aliasing={{2}: (4, {})} | custom-call | flops 240000008192 | bytes 1 | tf_op jit(solution)/shard_map/outer_down/pallas_call | solution.py:345
  121.7 15.6 %fall.1 = (bf16[16,2,96,768]{3,2,1,0:T(8,128)(2,1)S(1)}, bf16[512,1536]{1,0:T(8,128)(2,1)}, bf16[512,1536]{1,0:T(8,128)(2,1)S(1)}, f32[1,3072]{1,0:T(1,128)S(1)}...) custom-call(s32[66]{0:T(128)S(1)} %stack.239.refs_0_, ...), custom_call_target="tpu_custom_call", output_to_operand_aliasing={{9}: (11, {})} | custom-call | flops 539999993856 | bytes 1 | tf_op jit(solution)/shard_map/fall/pallas_call | solution.py:345
  137.9 2.4 %shift_first.2 = (f32[4,96,768]{2,1,0:T(8,128)S(1)}, bf16[4,96,768]{2,1,0:T(8,128)(2,1)}, f32[8,128]{1,0:T(8,128)S(1)}) custom-call(f32[8,96,768]{2,1,0:T(8,128)S(1)} %get-tuple-element.163.refs_0_, bf16[8,96,768]{2,1,0:T(8,128)(2,1)} %collective-permute-done.27.refs_1_, f32[8,128]{1,0:T(8,128)S(1)} %get-tuple-element.165.refs_2_), custom_call_target="tpu_custom_call", output_to_operand_aliasing={{2}: (2, {})} | custom-call | flops 149999992832 | bytes 1 | tf_op jit(solution)/shard_map/shift_first/pallas_call | solution.py:345
  141.8 7.4 %outer_up.1 = (f32[8,48,1920]{2,1,0:T(8,128)S(1)}, bf16[8,48,1920]{2,1,0:T(8,128)(2,1)}, f32[8,128]{1,0:T(8,128)S(1)}) custom-call(s32[66]{0:T(128)S(1)} %stack.239.refs_0_, bf16[16,48,512]{2,1,0:T(8,128)(2,1)} %get-tuple-element.168.refs_1_, bf16[16,48,512]{2,1,0:T(8,128)(2,1)} %collective-permute-done.29.refs_2_, ...), custom_call_target="tpu_custom_call", output_to_operand_aliasing={{2}: (9, {})} | custom-call | flops 240000008192 | bytes 1 | tf_op jit(solution)/shard_map/outer_up/pallas_call | solution.py:345
  152.4 2.0 collective-permute-start.35
  158.6 12.1 %mix_back.1 = (bf16[3,512,384]{2,1,0:T(8,128)(2,1)}, bf16[3,512,384]{2,1,0:T(8,128)(2,1)S(1)}, f32[8,128]{1,0:T(8,128)S(1)}) custom-call(s32[66]{0:T(128)S(1)} %stack.239.refs_0_, bf16[2,512,1152]{2,1,0:T(8,128)(2,1)S(1)} %copy-done.11, bf16[2,512,1152]{2,1,0:T(8,128)(2,1)S(1)} %copy-done.11, ...), custom_call_target="tpu_custom_call", output_to_operand_aliasing={{2}: (6, {})} | custom-call | flops 480000016384 | bytes 1 | tf_op jit(solution)/shard_map/mix_back/pallas_call | solution.py:345
  172.5 2.4 %shift_first.3 = (f32[4,48,1920]{2,1,0:T(8,128)S(1)}, bf16[4,48,1920]{2,1,0:T(8,128)(2,1)}, f32[8,128]{1,0:T(8,128)S(1)}) custom-call(f32[8,48,1920]{2,1,0:T(8,128)S(1)} %get-tuple-element.179.refs_0_, bf16[8,48,1920]{2,1,0:T(8,128)(2,1)} %collective-permute-done.34.refs_1_, f32[8,128]{1,0:T(8,128)S(1)} %get-tuple-element.186.refs_2_), custom_call_target="tpu_custom_call", output_to_operand_aliasing={{2}: (2, {})} | custom-call | flops 149999992832 | bytes 1 | tf_op jit(solution)/shard_map/shift_first/pallas_call | solution.py:345
  176.5 5.4 %outer_qkv.1 = (f32[8,48,1152]{2,1,0:T(8,128)S(1)}, bf16[8,48,1152]{2,1,0:T(8,128)(2,1)}, f32[8,128]{1,0:T(8,128)S(1)}) custom-call(s32[66]{0:T(128)S(1)} %stack.239.refs_0_, bf16[16,48,512]{2,1,0:T(8,128)(2,1)} %get-tuple-element.160.refs_1_, bf16[16,48,512]{2,1,0:T(8,128)(2,1)} %collective-permute-done.26.refs_2_, ...), custom_call_target="tpu_custom_call", output_to_operand_aliasing={{2}: (6, {})} | custom-call | flops 240000008192 | bytes 1 | tf_op jit(solution)/shard_map/outer_qkv/pallas_call | solution.py:345
  182.5 6.4 %exit_back.1 = (bf16[512,768]{1,0:T(8,128)(2,1)}, f32[8,48,128]{2,1,0:T(8,128)S(1)}, bf16[8,48,128]{2,1,0:T(8,128)(2,1)S(1)}, f32[8,128]{1,0:T(8,128)S(1)}) custom-call(s32[66]{0:T(128)S(1)} %stack.239.refs_0_, bf16[512,768]{1,0:T(8,128)(2,1)S(1)} %copy-done.5, ...), custom_call_target="tpu_custom_call", output_to_operand_aliasing={{3}: (9, {})} | custom-call | flops 240000008192 | bytes 1 | tf_op jit(solution)/shard_map/exit_back/pallas_call | solution.py:345
  190.3 2.1 shift_second.4
  196.8 2.1 shift_both.1
  200.3 5.0 %leave.1 = (bf16[512,768]{1,0:T(8,128)(2,1)}, f32[8,128]{1,0:T(8,128)S(1)}) custom-call(f32[512,768]{1,0:T(8,128)S(1)} %get-tuple-element.141.refs_4_.refs_0_, bf16[512,3072]{1,0:T(8,128)(2,1)S(1)} %copy-done.9, bf16[3072,768]{1,0:T(8,128)(2,1)S(1)} %bitcast.66, ...), custom_call_target="tpu_custom_call", output_to_operand_aliasing={{1}: (4, {})} | custom-call | flops 210000003072 | bytes 1 | tf_op jit(solution)/shard_map/leave/pallas_call | solution.py:345
  205.3 2.7 %collective-permute-done.41.refs_1_ = bf16[4,48,1280]{2,1,0:T(8,128)(2,1)} collective-permute-done((bf16[4,48,1280]{2,1,0:T(8,128)(2,1)}, bf16[4,48,1280]{2,1,0:T(8,128)(2,1)}, u32[]{:S(2)}, u32[]{:S(2)}) %collective-permute-start.41) | collective-permute-done | bytes 491552 | tf_op jit(solution)/shard_map/ppermute | solution.py:266
  215.9 6.7 %collective-permute-done.43.refs_3_ = bf16[48,1280]{1,0:T(8,128)(2,1)S(1)} collective-permute-done((bf16[48,1280]{1,0:T(8,128)(2,1)S(1)}, bf16[48,1280]{1,0:T(8,128)(2,1)S(1)}, u32[]{:S(2)}, u32[]{:S(2)}) %collective-permute-start.43) | collective-permute-done | bytes 122912 | tf_op jit(solution)/shard_map/ppermute | solution.py:266
  (131 shorter events, 66.4 us)
Async XLA Ops:
  1.2 11.1 %collective-permute-start.4 = (bf16[24,3072]{1,0:T(8,128)(2,1)}, bf16[24,3072]{1,0:T(8,128)(2,1)S(1)}, u32[]{:S(2)}, u32[]{:S(2)}) collective-permute-start(bf16[24,3072]{1,0:T(8,128)(2,1)} %refs_1_.6), channel_id=1, source_target_pairs={{0,1},{1,0},{2,3},{3,2},{4,5},{5,4},{6,7},{7,6},{8,9},{9,8},{10,11... | collective-permute-start | bytes 442376 | tf_op jit(solution)/shard_map/ppermute | solution.py:266
  8.2 12.4 %collective-permute-start.2 = (bf16[1,48,1280]{2,1,0:T(8,128)(2,1)S(1)}, bf16[1,48,1280]{2,1,0:T(8,128)(2,1)S(1)}, u32[]{:S(2)}, u32[]{:S(2)}) collective-permute-start(bf16[1,48,1280]{2,1,0:T(8,128)(2,1)S(1)} %get-tuple-element.119.refs_0_), channel_id=1, source_target_pairs={{0,16},{1,17},{2,18},{3,19},{4,20},{5,21},{6,22},{7,23},{8,24},{9,... | collective-permute-start | bytes 368648 | tf_op jit(solution)/shard_map/ppermute | solution.py:266
  24.3 15.8 %collective-permute-start.9 = (bf16[1,48,1920]{2,1,0:T(8,128)(2,1)S(1)}, bf16[1,48,1920]{2,1,0:T(8,128)(2,1)S(1)}, u32[]{:S(2)}, u32[]{:S(2)}) collective-permute-start(bf16[1,48,1920]{2,1,0:T(8,128)(2,1)S(1)} %get-tuple-element.126.refs_0_), channel_id=1, source_target_pairs={{0,16},{1,17},{2,18},{3,19},{4,20},{5,21},{6,22},{7,23},{8,24},{9,... | collective-permute-start | bytes 552968 | tf_op jit(solution)/shard_map/ppermute | solution.py:266
  25.3 14.8 %collective-permute-start.10 = (bf16[1,48,1920]{2,1,0:T(8,128)(2,1)S(1)}, bf16[1,48,1920]{2,1,0:T(8,128)(2,1)S(1)}, u32[]{:S(2)}, u32[]{:S(2)}) collective-permute-start(bf16[1,48,1920]{2,1,0:T(8,128)(2,1)S(1)} %get-tuple-element.126.refs_0_), channel_id=1, source_target_pairs={{0,24},{1,25},{2,26},{3,27},{4,28},{5,29},{6,30},{7,31},{8,16},{9,... | collective-permute-start | bytes 552968 | tf_op jit(solution)/shard_map/ppermute | solution.py:266
  30.6 14.4 %collective-permute-start.7 = (bf16[8,48,1280]{2,1,0:T(8,128)(2,1)}, bf16[8,48,1280]{2,1,0:T(8,128)(2,1)}, u32[]{:S(2)}, u32[]{:S(2)}) collective-permute-start(bf16[8,48,1280]{2,1,0:T(8,128)(2,1)} %get-tuple-element.125.refs_4_), channel_id=1, source_target_pairs={{0,4},{1,3},{2,6},{3,1},{4,0},{5,7},{6,2},{7,5},{8,12},{9,11},{10,... | collective-permute-start | bytes 2949128 | tf_op jit(solution)/shard_map/ppermute | solution.py:266
  32.1 14.4 %collective-permute-start.11 = (bf16[8,48,1280]{2,1,0:T(8,128)(2,1)}, bf16[8,48,1280]{2,1,0:T(8,128)(2,1)}, u32[]{:S(2)}, u32[]{:S(2)}) collective-permute-start(bf16[8,48,1280]{2,1,0:T(8,128)(2,1)} %get-tuple-element.125.refs_4_), channel_id=1, source_target_pairs={{0,1},{1,0},{2,3},{3,2},{4,5},{5,4},{6,7},{7,6},{8,9},{9,8},{10,11... | collective-permute-start | bytes 2949128 | tf_op jit(solution)/shard_map/ppermute | solution.py:266
  45.0 11.8 %collective-permute-start.13 = (bf16[4,48,1920]{2,1,0:T(8,128)(2,1)}, bf16[4,48,1920]{2,1,0:T(8,128)(2,1)}, u32[]{:S(2)}, u32[]{:S(2)}) collective-permute-start(bf16[4,48,1920]{2,1,0:T(8,128)(2,1)} %get-tuple-element.132.refs_0_), channel_id=1, source_target_pairs={{0,2},{1,5},{2,0},{3,7},{4,6},{5,1},{6,4},{7,3},{8,10},{9,13},{10,... | collective-permute-start | bytes 2211848 | tf_op jit(solution)/shard_map/ppermute | solution.py:266
  59.3 19.7 %collective-permute-start.14 = (bf16[8,48,1920]{2,1,0:T(8,128)(2,1)}, bf16[8,48,1920]{2,1,0:T(8,128)(2,1)}, u32[]{:S(2)}, u32[]{:S(2)}) collective-permute-start(bf16[8,48,1920]{2,1,0:T(8,128)(2,1)} %get-tuple-element.137.refs_4_.refs_3_), channel_id=1, source_target_pairs={{0,4},{1,3},{2,6},{3,1},{4,0},{5,7},{6,2},{7,5},{8,12},{9,11},{10,... | collective-permute-start | bytes 4423688 | tf_op jit(solution)/shard_map/ppermute | solution.py:266
  60.8 20.2 %collective-permute-start.15 = (bf16[8,48,1920]{2,1,0:T(8,128)(2,1)}, bf16[8,48,1920]{2,1,0:T(8,128)(2,1)}, u32[]{:S(2)}, u32[]{:S(2)}) collective-permute-start(bf16[8,48,1920]{2,1,0:T(8,128)(2,1)} %get-tuple-element.137.refs_4_.refs_3_), channel_id=1, source_target_pairs={{0,1},{1,0},{2,3},{3,2},{4,5},{5,4},{6,7},{7,6},{8,9},{9,8},{10,11... | collective-permute-start | bytes 4423688 | tf_op jit(solution)/shard_map/ppermute | solution.py:266
  60.8 11.5 %collective-permute-start.17 = (bf16[1,96,768]{2,1,0:T(8,128)(2,1)}, bf16[1,96,768]{2,1,0:T(8,128)(2,1)}, u32[]{:S(2)}, u32[]{:S(2)}) collective-permute-start(bf16[1,96,768]{2,1,0:T(8,128)(2,1)} %get-tuple-element.138.refs_0_), channel_id=1, source_target_pairs={{0,8},{1,9},{2,10},{3,11},{4,12},{5,13},{6,14},{7,15},{8,0},{9,1},... | collective-permute-start | bytes 442376 | tf_op jit(solution)/shard_map/ppermute | solution.py:266
  62.9 14.3 %collective-permute-start.18 = (bf16[1,96,768]{2,1,0:T(8,128)(2,1)}, bf16[1,96,768]{2,1,0:T(8,128)(2,1)}, u32[]{:S(2)}, u32[]{:S(2)}) collective-permute-start(bf16[1,96,768]{2,1,0:T(8,128)(2,1)} %get-tuple-element.138.refs_0_), channel_id=1, source_target_pairs={{0,16},{1,17},{2,18},{3,19},{4,20},{5,21},{6,22},{7,23},{8,24},{9,... | collective-permute-start | bytes 442376 | tf_op jit(solution)/shard_map/ppermute | solution.py:266
  63.9 13.3 %collective-permute-start.19 = (bf16[1,96,768]{2,1,0:T(8,128)(2,1)}, bf16[1,96,768]{2,1,0:T(8,128)(2,1)}, u32[]{:S(2)}, u32[]{:S(2)}) collective-permute-start(bf16[1,96,768]{2,1,0:T(8,128)(2,1)} %get-tuple-element.138.refs_0_), channel_id=1, source_target_pairs={{0,24},{1,25},{2,26},{3,27},{4,28},{5,29},{6,30},{7,31},{8,16},{9,... | collective-permute-start | bytes 442376 | tf_op jit(solution)/shard_map/ppermute | solution.py:266
  72.4 39.6 %collective-permute-start.25 = (bf16[512,768]{1,0:T(8,128)(2,1)}, bf16[512,768]{1,0:T(8,128)(2,1)}, u32[]{:S(2)}, u32[]{:S(2)}) collective-permute-start(bf16[512,768]{1,0:T(8,128)(2,1)} %get-tuple-element.148.refs_2_.refs_1_), channel_id=1, source_target_pairs={{0,1},{1,0},{2,3},{3,2},{4,5},{5,4},{6,7},{7,6},{8,9},{9,8},{10,11... | collective-permute-start | bytes 2359304 | tf_op jit(solution)/shard_map/ppermute | solution.py:266
  77.2 99.3 %collective-permute-start.26 = (bf16[16,48,512]{2,1,0:T(8,128)(2,1)}, bf16[16,48,512]{2,1,0:T(8,128)(2,1)}, u32[]{:S(2)}, u32[]{:S(2)}) collective-permute-start(bf16[16,48,512]{2,1,0:T(8,128)(2,1)} %get-tuple-element.160.refs_1_), channel_id=1, source_target_pairs={{0,1},{1,0},{2,3},{3,2},{4,5},{5,4},{6,7},{7,6},{8,9},{9,8},{10,11... | collective-permute-start | bytes 2359304 | tf_op jit(solution)/shard_map/ppermute | solution.py:266
  77.2 63.1 %collective-permute-start.31 = (bf16[16,48,512]{2,1,0:T(8,128)(2,1)}, bf16[16,48,512]{2,1,0:T(8,128)(2,1)}, u32[]{:S(2)}, u32[]{:S(2)}) collective-permute-start(bf16[16,48,512]{2,1,0:T(8,128)(2,1)} %bitcast.61.refs_5_), channel_id=1, source_target_pairs={{0,1},{1,0},{2,3},{3,2},{4,5},{5,4},{6,7},{7,6},{8,9},{9,8},{10,11... | collective-permute-start | bytes 2359304 | tf_op jit(solution)/shard_map/ppermute | solution.py:266
  81.1 10.2 %collective-permute-start.20 = (bf16[4,96,768]{2,1,0:T(8,128)(2,1)}, bf16[4,96,768]{2,1,0:T(8,128)(2,1)}, u32[]{:S(2)}, u32[]{:S(2)}) collective-permute-start(bf16[4,96,768]{2,1,0:T(8,128)(2,1)} %get-tuple-element.144.refs_0_), channel_id=1, source_target_pairs={{0,2},{1,5},{2,0},{3,7},{4,6},{5,1},{6,4},{7,3},{8,10},{9,13},{10,... | collective-permute-start | bytes 1769480 | tf_op jit(solution)/shard_map/ppermute | solution.py:266
  93.6 16.5 %collective-permute-start.21 = (bf16[8,96,768]{2,1,0:T(8,128)(2,1)}, bf16[8,96,768]{2,1,0:T(8,128)(2,1)}, u32[]{:S(2)}, u32[]{:S(2)}) collective-permute-start(bf16[8,96,768]{2,1,0:T(8,128)(2,1)} %get-tuple-element.152.refs_7_), channel_id=1, source_target_pairs={{0,4},{1,3},{2,6},{3,1},{4,0},{5,7},{6,2},{7,5},{8,12},{9,11},{10,... | collective-permute-start | bytes 3538952 | tf_op jit(solution)/shard_map/ppermute | solution.py:266
  95.1 25.1 %collective-permute-start.22 = (bf16[8,96,768]{2,1,0:T(8,128)(2,1)}, bf16[8,96,768]{2,1,0:T(8,128)(2,1)}, u32[]{:S(2)}, u32[]{:S(2)}) collective-permute-start(bf16[8,96,768]{2,1,0:T(8,128)(2,1)} %get-tuple-element.152.refs_7_), channel_id=1, source_target_pairs={{0,1},{1,0},{2,3},{3,2},{4,5},{5,4},{6,7},{7,6},{8,9},{9,8},{10,11... | collective-permute-start | bytes 3538952 | tf_op jit(solution)/shard_map/ppermute | solution.py:266
  112.0 29.8 %collective-permute-start.29 = (bf16[16,48,512]{2,1,0:T(8,128)(2,1)}, bf16[16,48,512]{2,1,0:T(8,128)(2,1)}, u32[]{:S(2)}, u32[]{:S(2)}) collective-permute-start(bf16[16,48,512]{2,1,0:T(8,128)(2,1)} %get-tuple-element.168.refs_1_), channel_id=1, source_target_pairs={{0,1},{1,0},{2,3},{3,2},{4,5},{5,4},{6,7},{7,6},{8,9},{9,8},{10,11... | collective-permute-start | bytes 2359304 | tf_op jit(solution)/shard_map/ppermute | solution.py:266
  120.2 17.3 %collective-permute-start.27 = (bf16[8,96,768]{2,1,0:T(8,128)(2,1)}, bf16[8,96,768]{2,1,0:T(8,128)(2,1)}, u32[]{:S(2)}, u32[]{:S(2)}) collective-permute-start(bf16[8,96,768]{2,1,0:T(8,128)(2,1)} %get-tuple-element.164), channel_id=1, source_target_pairs={{0,4},{1,3},{2,6},{3,1},{4,0},{5,7},{6,2},{7,5},{8,12},{9,11},{10,... | collective-permute-start | bytes 3538952 | tf_op jit(solution)/shard_map/ppermute | solution.py:266
  140.3 10.2 %collective-permute-start.28 = (bf16[4,96,768]{2,1,0:T(8,128)(2,1)}, bf16[4,96,768]{2,1,0:T(8,128)(2,1)}, u32[]{:S(2)}, u32[]{:S(2)}) collective-permute-start(bf16[4,96,768]{2,1,0:T(8,128)(2,1)} %get-tuple-element.167), channel_id=1, source_target_pairs={{0,2},{1,5},{2,0},{3,7},{4,6},{5,1},{6,4},{7,3},{8,10},{9,13},{10,... | collective-permute-start | bytes 1769480 | tf_op jit(solution)/shard_map/ppermute | solution.py:266
  149.2 23.4 %collective-permute-start.34 = (bf16[8,48,1920]{2,1,0:T(8,128)(2,1)}, bf16[8,48,1920]{2,1,0:T(8,128)(2,1)}, u32[]{:S(2)}, u32[]{:S(2)}) collective-permute-start(bf16[8,48,1920]{2,1,0:T(8,128)(2,1)} %get-tuple-element.180), channel_id=1, source_target_pairs={{0,4},{1,3},{2,6},{3,1},{4,0},{5,7},{6,2},{7,5},{8,12},{9,11},{10,... | collective-permute-start | bytes 4423688 | tf_op jit(solution)/shard_map/ppermute | solution.py:266
  152.4 18.3 %collective-permute-start.35 = (bf16[96,768]{1,0:T(8,128)(2,1)}, bf16[96,768]{1,0:T(8,128)(2,1)}, u32[]{:S(2)}, u32[]{:S(2)}) collective-permute-start(bf16[96,768]{1,0:T(8,128)(2,1)} %get-tuple-element.182), channel_id=1, source_target_pairs={{0,8},{1,9},{2,10},{3,11},{4,12},{5,13},{6,14},{7,15},{8,0},{9,1},... | collective-permute-start | bytes 442376 | tf_op jit(solution)/shard_map/ppermute | solution.py:266
  154.4 16.2 %collective-permute-start.36 = (bf16[96,768]{1,0:T(8,128)(2,1)}, bf16[96,768]{1,0:T(8,128)(2,1)}, u32[]{:S(2)}, u32[]{:S(2)}) collective-permute-start(bf16[96,768]{1,0:T(8,128)(2,1)} %get-tuple-element.183), channel_id=1, source_target_pairs={{0,16},{1,17},{2,18},{3,19},{4,20},{5,21},{6,22},{7,23},{8,24},{9,... | collective-permute-start | bytes 442376 | tf_op jit(solution)/shard_map/ppermute | solution.py:266
  155.5 15.2 %collective-permute-start.37 = (bf16[96,768]{1,0:T(8,128)(2,1)}, bf16[96,768]{1,0:T(8,128)(2,1)}, u32[]{:S(2)}, u32[]{:S(2)}) collective-permute-start(bf16[96,768]{1,0:T(8,128)(2,1)} %get-tuple-element.184), channel_id=1, source_target_pairs={{0,24},{1,25},{2,26},{3,27},{4,28},{5,29},{6,30},{7,31},{8,16},{9,... | collective-permute-start | bytes 442376 | tf_op jit(solution)/shard_map/ppermute | solution.py:266
  175.0 15.3 %collective-permute-start.40 = (bf16[4,48,1920]{2,1,0:T(8,128)(2,1)}, bf16[4,48,1920]{2,1,0:T(8,128)(2,1)}, u32[]{:S(2)}, u32[]{:S(2)}) collective-permute-start(bf16[4,48,1920]{2,1,0:T(8,128)(2,1)} %get-tuple-element.187.refs_5_), channel_id=1, source_target_pairs={{0,2},{1,5},{2,0},{3,7},{4,6},{5,1},{6,4},{7,3},{8,10},{9,13},{10,... | collective-permute-start | bytes 2211848 | tf_op jit(solution)/shard_map/ppermute | solution.py:266
  181.8 14.9 %collective-permute-start.38 = (bf16[8,48,1152]{2,1,0:T(8,128)(2,1)}, bf16[8,48,1152]{2,1,0:T(8,128)(2,1)}, u32[]{:S(2)}, u32[]{:S(2)}) collective-permute-start(bf16[8,48,1152]{2,1,0:T(8,128)(2,1)} %get-tuple-element.190), channel_id=1, source_target_pairs={{0,4},{1,3},{2,6},{3,1},{4,0},{5,7},{6,2},{7,5},{8,12},{9,11},{10,... | collective-permute-start | bytes 2654216 | tf_op jit(solution)/shard_map/ppermute | solution.py:266
  192.4 19.8 %collective-permute-start.45 = (bf16[48,1920]{1,0:T(8,128)(2,1)}, bf16[48,1920]{1,0:T(8,128)(2,1)}, u32[]{:S(2)}, u32[]{:S(2)}) collective-permute-start(bf16[48,1920]{1,0:T(8,128)(2,1)} %get-tuple-element.212), channel_id=1, source_target_pairs={{0,8},{1,9},{2,10},{3,11},{4,12},{5,13},{6,14},{7,15},{8,0},{9,1},... | collective-permute-start | bytes 552968 | tf_op jit(solution)/shard_map/ppermute | solution.py:266
  193.4 20.3 %collective-permute-start.46 = (bf16[48,1920]{1,0:T(8,128)(2,1)}, bf16[48,1920]{1,0:T(8,128)(2,1)}, u32[]{:S(2)}, u32[]{:S(2)}) collective-permute-start(bf16[48,1920]{1,0:T(8,128)(2,1)} %get-tuple-element.213), channel_id=1, source_target_pairs={{0,16},{1,17},{2,18},{3,19},{4,20},{5,21},{6,22},{7,23},{8,24},{9,... | collective-permute-start | bytes 552968 | tf_op jit(solution)/shard_map/ppermute | solution.py:266
  195.3 18.4 %collective-permute-start.47 = (bf16[48,1920]{1,0:T(8,128)(2,1)}, bf16[48,1920]{1,0:T(8,128)(2,1)}, u32[]{:S(2)}, u32[]{:S(2)}) collective-permute-start(bf16[48,1920]{1,0:T(8,128)(2,1)} %get-tuple-element.214), channel_id=1, source_target_pairs={{0,24},{1,25},{2,26},{3,27},{4,28},{5,29},{6,30},{7,31},{8,16},{9,... | collective-permute-start | bytes 552968 | tf_op jit(solution)/shard_map/ppermute | solution.py:266
  210.2 12.3 %collective-permute-start.43 = (bf16[48,1280]{1,0:T(8,128)(2,1)S(1)}, bf16[48,1280]{1,0:T(8,128)(2,1)S(1)}, u32[]{:S(2)}, u32[]{:S(2)}) collective-permute-start(bf16[48,1280]{1,0:T(8,128)(2,1)S(1)} %get-tuple-element.209), channel_id=1, source_target_pairs={{0,16},{1,17},{2,18},{3,19},{4,20},{5,21},{6,22},{7,23},{8,24},{9,... | collective-permute-start | bytes 368648 | tf_op jit(solution)/shard_map/ppermute | solution.py:266
  212.2 10.3 %collective-permute-start.44 = (bf16[48,1280]{1,0:T(8,128)(2,1)S(1)}, bf16[48,1280]{1,0:T(8,128)(2,1)S(1)}, u32[]{:S(2)}, u32[]{:S(2)}) collective-permute-start(bf16[48,1280]{1,0:T(8,128)(2,1)S(1)} %get-tuple-element.210), channel_id=1, source_target_pairs={{0,24},{1,25},{2,26},{3,27},{4,28},{5,29},{6,30},{7,31},{8,16},{9,... | collective-permute-start | bytes 368648 | tf_op jit(solution)/shard_map/ppermute | solution.py:266
  (32 other events, 184.9 us)

commit v5 on v4

--- a/solution.py
+++ b/solution.py
@@ -357,10 +357,11 @@
 
 
 def settle(info, pieces, dest, who=(0, 1)):
+    few = pieces[0].shape[0]
     for w in who:
         half = info[CORE] if w == 0 else 1 - info[CORE]
         for j in range(16):
-            dest[half, info[16 * w + j]] = pieces[2 * w + j // 8][j % 8]
+            dest[half, info[16 * w + j]] = pieces[(16 * w + j) // few][j % few]
 
 
 def bring(pieces, raw, sems, start):
@@ -488,6 +489,10 @@
     )(array)
 
 
+def both_cores(*own):
+    return own + tuple(swap(blocks) for blocks in own)
+
+
 def near_z(piece, steps):
     return [send(piece, along_z(s)) for s in steps]
 
@@ -497,27 +502,16 @@
     tokens,
     upstream,
     down,
-    low,
-    high,
-    low_o,
-    high_o,
-    kept,
-    vecs,
-    bias,
-    first,
-    flipped,
-    joint,
-    grad_y,
-    piece_down,
-    weights,
-    sem,
+    *refs,
 ):
+    pieces = refs[:4]
+    kept, vecs, bias, flipped, joint, grad_y, piece_down, weights, sem = refs[4:]
     feat = tokens.shape[1]
     third = feat // 2
     piece_down[0] = down[...]
     place = lax.broadcasted_iota(jnp.int32, upstream.shape, 0)
     grad_y[...] = jnp.where(place < info[LENGTH], upstream[...].astype(F32), 0.0).astype(BF16)
-    settle(info, (low, high, low_o, high_o), weights)
+    settle(info, pieces, weights)
     normed, _ = centre(tokens[...].astype(F32))
     out = pltpu.make_async_copy(weights, kept, sem)
     out.start()
@@ -531,7 +525,6 @@
     small = small.T
     vecs[...] = small[:8]
     low_first = (normed * small[0:1] + small[2:3]).astype(BF16)
-    first[...] = low_first
     flipped[...] = low_first.T.reshape(flipped.shape)
     for h in (0, 1):
         cols = slice(h * third, (h + 1) * third)
@@ -554,14 +547,13 @@
             shape(sets, BF16),
             shape((8, feat), F32),
             shape((1, hidden), F32),
-            shape((rows, feat), BF16),
             shape((16, feat // 16, rows), BF16),
             shape((2, rows, 3 * feat // 2), BF16),
             shape((rows, feat), BF16),
             shape((1,) + down.shape, BF16),
         ),
         in_specs=[SMEM] + [vmem] * 7,
-        out_specs=(ANY,) + (vmem,) * 7,
+        out_specs=(ANY,) + (vmem,) * 6,
         scratch_shapes=[pltpu.VMEM(sets, BF16), pltpu.SemaphoreType.DMA],
         compiler_params=params(20),
         name="enter",
@@ -725,17 +717,17 @@
     return x * phi, phi + x * (bell * (2 * math.pi) ** -0.5)
 
 
-def rise_kernel(
-    info, tokens, mixed, vecs, low, high, low_o, high_o, weights, after, second, flipped, raw, sems
-):
+def rise_kernel(info, tokens, mixed, vecs, *refs):
+    pieces = refs[:8]
+    weights, after, second, flipped, raw, sems = refs[8:]
     feat = tokens.shape[1]
-    copies = bring((low, high, low_o, high_o), raw, sems, low.shape[2] - raw.shape[-1])
+    copies = bring(pieces, raw, sems, pieces[0].shape[2] - raw.shape[-1])
     for copy in copies:
         copy.start()
     start = tokens[...].astype(F32) + vecs[5:6]
     for copy in copies:
         copy.wait()
-    settle(info, raw, weights)
+    settle(info, [raw.at[i] for i in range(8)], weights)
     grown = [dot(mixed[...], weights[h].reshape(feat, feat // 2)) for h in (0, 1)]
     total = start + jnp.concatenate(grown, axis=1)
     after[...] = total
@@ -757,11 +749,11 @@
             shape((rows, feat), BF16),
             shape((16, block, rows), BF16),
         ),
-        in_specs=[SMEM] + [vmem] * 3 + [ANY] * 4,
+        in_specs=[SMEM] + [vmem] * 3 + [ANY] * 8,
         out_specs=(vmem,) * 4,
         scratch_shapes=[
-            pltpu.VMEM((4, 8, block, feat // 2), BF16),
-            pltpu.SemaphoreType.DMA((4,)),
+            pltpu.VMEM((8, 4, block, feat // 2), BF16),
+            pltpu.SemaphoreType.DMA((8,)),
         ],
         compiler_params=params(16),
         name="rise",
@@ -769,176 +761,133 @@
     )(info, tokens, mixed, vecs, *pieces)
 
 
-def widen_kernel(
-    info,
-    second,
-    bias,
-    low,
-    high,
-    low_o,
-    high_o,
-    weights,
-    active,
-    slope,
-    mine,
-    theirs,
-    raw,
-    sems,
-):
-    step, per = pl.program_id(0), pl.num_programs(0) // 2
+def widen_kernel(which, info, second, bias, *refs):
+    pieces = refs[:4]
+    weights, active, slope, mine, theirs, raw, sems = refs[4:]
+    step = pl.program_id(0)
     core = info[CORE]
     feat = second.shape[1]
     tile = active.shape[1]
     rows = mine.shape[1]
     count = tile // rows
-    copies = bring((low, high, low_o, high_o), raw, sems, 0)
 
     @pl.when(step == 0)
     def _():
+        copies = bring(pieces, raw, sems, 0)
         for copy in copies:
             copy.start()
-
-    for who in (0, 1):
-
-        @pl.when(step == who * per)
-        def _():
-            for copy in copies[2 * who : 2 * who + 2]:
-                copy.wait()
-            settle(info, raw, weights, (who,))
-
-    half = jnp.where(step < per, core, 1 - core)
-    cols = pl.ds(pl.multiple_of(lax.rem(step, per) * tile, tile), tile)
-    w = weights[half, :, :, cols].reshape(feat, tile)
+        for copy in copies:
+            copy.wait()
+        for j in range(16):
+            weights[info[16 * which + j]] = raw[j // 4, j % 4]
+
+    cols = pl.ds(pl.multiple_of(step * tile, tile), tile)
+    w = weights[:, :, cols].reshape(feat, tile)
     hidden = dot(second[...], w) + bias[...]
     value, grad = gelu_parts(hidden)
     value = value.astype(BF16)
     active[...] = value
     slope[...] = grad.astype(BF16)
-    flipped = value.T.reshape(count, rows, -1)
-    first_chip = (half * per + lax.rem(step, per)) * (count // 2)
-    for c in (0, 1):
-
-        @pl.when(core == c)
-        def _():
-            for i in range(count):
-                chip = first_chip + i // 2
-                if i % 2 == c:
-                    mine[info[PLACE + chip]] = flipped[i]
-                else:
-                    theirs[info[PLACE_O + chip]] = flipped[i]
-
-
-def widen(chain, info, second, bias, pieces):
+    flipped = value.T.reshape(count // 2, 2, rows, -1)
+    mine[...] = jnp.where(core == 0, flipped[:, 0], flipped[:, 1])
+    theirs[...] = jnp.where(core == 0, flipped[:, 1], flipped[:, 0])
+
+
+def widen(chain, which, info, second, bias, pieces):
     rows, feat = second.shape
     wide = pieces[0].shape[-1] - feat // 2
-    hidden = 2 * wide
-    tile, block = 768, hidden // 32
+    tile, block = 768, wide // 16
     per = wide // tile
-    turned = shape((16, block, rows), BF16)
-    sets = (2, 16, feat // 16, wide)
-
-    def at(n, info):
-        return jnp.where(n < per, info[CORE], 1 - info[CORE]) * per + n % per
+    turned = shape((8, block, rows), BF16)
 
     def whole(dims):
         return pl.BlockSpec(dims, lambda n, info: (0,) * len(dims))
 
-    strip = pl.BlockSpec((rows, tile), lambda n, info: (0, at(n, info)))
-    return chain.call(
-        widen_kernel,
+    def bias_at(n, info):
+        half = info[CORE] if which == 0 else 1 - info[CORE]
+        return (0, half * per + n)
+
+    strip = pl.BlockSpec((rows, tile), lambda n, info: (0, n))
+    part = pl.BlockSpec((tile // block // 2, block, rows), lambda n, info: (n, 0, 0))
+    return chain.call(
+        partial(widen_kernel, which),
         prefetch=1,
-        grid=(2 * per,),
+        grid=(per,),
         out_shape=(
-            shape(sets, BF16),
-            shape((rows, hidden), BF16),
-            shape((rows, hidden), BF16),
+            shape((16, feat // 16, wide), BF16),
+            shape((rows, wide), BF16),
+            shape((rows, wide), BF16),
             turned,
             turned,
         ),
-        in_specs=[
-            whole((rows, feat)),
-            pl.BlockSpec((1, tile), lambda n, info: (0, at(n, info))),
-        ]
-        + [ANY] * 4,
-        out_specs=(whole(sets), strip, strip, whole(turned.shape), whole(turned.shape)),
+        in_specs=[whole((rows, feat)), pl.BlockSpec((1, tile), bias_at)] + [ANY] * 4,
+        out_specs=(whole((16, feat // 16, wide)), strip, strip, part, part),
         scratch_shapes=[
-            pltpu.VMEM((4, 8, feat // 16, wide), BF16),
+            pltpu.VMEM((4, 4, feat // 16, wide), BF16),
             pltpu.SemaphoreType.DMA((4,)),
         ],
-        compiler_params=params(30),
+        compiler_params=params(24),
         name="widen",
         cost_estimate=cost(18),
     )(info, second, bias, *pieces)
 
 
-def leave_kernel(after, active, down, vecs, output, total):
-    step = pl.program_id(0)
-    part = dot(active[...], down[...])
+def leave_kernel(info, after, first, second, down, vecs, output, total):
+    step, per = pl.program_id(0), pl.num_programs(0) // 2
 
     @pl.when(step == 0)
     def _():
-        total[...] = after[...] + vecs[7:8] + part
-
-    @pl.when(step > 0)
+        total[...] = after[...] + vecs[7:8] + dot(first[...], down[...])
+
+    @pl.when((step > 0) & (step < per))
     def _():
-        total[...] += part
-
-    @pl.when(step == pl.num_programs(0) - 1)
+        total[...] += dot(first[...], down[...])
+
+    @pl.when(step >= per)
+    def _():
+        total[...] += dot(second[...], down[...])
+
+    @pl.when(step == 2 * per - 1)
     def _():
         output[...] = total[...].astype(BF16)
 
 
-def leave(chain, after, active, down, vecs):
+def leave(chain, info, after, first, second, down, vecs):
     rows, feat = after.shape
-    hidden = active.shape[1]
     tile = 768
+    per = first.shape[1] // tile
+
+    def whole(dims):
+        return pl.BlockSpec(dims, lambda n, info: (0,) * len(dims))
+
+    def down_at(n, info):
+        half = jnp.where(n < per, info[CORE], 1 - info[CORE])
+        return (half * per + n % per, 0)
+
     return chain.call(
         leave_kernel,
-        grid=(hidden // tile,),
+        prefetch=1,
+        grid=(2 * per,),
         out_shape=shape((rows, feat), BF16),
         in_specs=[
-            full((rows, feat)),
-            pl.BlockSpec((rows, tile), lambda n: (0, n)),
-            pl.BlockSpec((tile, feat), lambda n: (n, 0)),
-            full((8, feat)),
+            whole((rows, feat)),
+            pl.BlockSpec((rows, tile), lambda n, info: (0, jnp.minimum(n, per - 1))),
+            pl.BlockSpec((rows, tile), lambda n, info: (0, jnp.maximum(n - per, 0))),
+            pl.BlockSpec((tile, feat), down_at),
+            whole((8, feat)),
         ],
-        out_specs=full((rows, feat)),
+        out_specs=whole((rows, feat)),
         scratch_shapes=[pltpu.VMEM((rows, feat), F32)],
         compiler_params=params(16),
         name="leave",
         cost_estimate=cost(7),
-    )(after, active, down, vecs)
-
-
-def fall_kernel(
-    info,
-    grad_y,
-    slope,
-    up,
-    after,
-    vecs,
-    proj,
-    low,
-    high,
-    low_o,
-    high_o,
-    kept,
-    theirs,
-    mine,
-    bias_sum,
-    grad_after,
-    attn_theirs,
-    attn_mine,
-    grad_mixed,
-    sums,
-    weights,
-    grad_second,
-    normed,
-    inverse,
-    raw,
-    sems,
-    sem,
-):
+    )(info, after, first, second, down, vecs)
+
+
+def fall_kernel(info, grad_y, slope, slope_o, up, up_o, after, vecs, proj, *refs):
+    pieces = refs[:4]
+    kept, theirs, mine, bias_sum, grad_after, attn_theirs, attn_mine, grad_mixed, sums = refs[4:13]
+    weights, grad_second, normed, inverse, raw, sems, sem = refs[13:]
     step, steps = pl.program_id(0), pl.num_programs(0)
     core = info[CORE]
     feat = grad_y.shape[1]
@@ -948,7 +897,7 @@
 
     @pl.when(step == 0)
     def _():
-        copies = bring((low, high, low_o, high_o), raw, sems, 0)
+        copies = bring(pieces, raw, sems, 0)
         for copy in copies:
             copy.start()
         normed[...], inverse[...] = centre(after[...])
@@ -965,17 +914,16 @@
     at = half * per + lax.rem(step, per)
     count = tile * weights.shape[0] // (steps * tile)
     down = weights[pl.ds(count * at, count)].reshape(tile, feat)
-    grad = (dot_last(grad_y[...], down) * slope[...].astype(F32)).astype(BF16)
-    bias_sum[...] = jnp.sum(grad.astype(F32), axis=0, keepdims=True)
-    grad_second[...] += dot_last(grad, up[0])
-
-    @pl.when(step < per)
-    def _():
-        theirs[...] = grad
-
-    @pl.when(step >= per)
-    def _():
-        mine[...] = grad
+    raw_grad = dot_last(grad_y[...], down)
+
+    def tell(slope_ref, up_ref, out):
+        grad = (raw_grad * slope_ref[...].astype(F32)).astype(BF16)
+        bias_sum[...] = jnp.sum(grad.astype(F32), axis=0, keepdims=True)
+        grad_second[...] += dot_last(grad, up_ref[...])
+        out[...] = grad
+
+    pl.when(step < per)(lambda: tell(slope_o, up_o, theirs))
+    pl.when(step >= per)(lambda: tell(slope, up, mine))
 
     @pl.when(step == steps - 1)
     def _():
@@ -996,9 +944,9 @@
         keeping.wait()
 
 
-def fall(chain, info, grad_y, slope, up_set, after, vecs, proj_set, pieces):
+def fall(chain, info, grad_y, slopes, up_sets, after, vecs, proj_set, pieces):
     rows, feat = grad_y.shape
-    hidden = slope.shape[1]
+    hidden = 2 * slopes[0].shape[1]
     tile = 768
     steps = hidden // tile
     per = steps // 2
@@ -1015,10 +963,10 @@
         grid=(steps,),
         in_specs=[
             whole((rows, feat)),
-            pl.BlockSpec((rows, tile), lambda n, info: (0, at(n, info))),
-            pl.BlockSpec(
-                (1, feat, tile), lambda n, info: (at(n, info) // per, 0, n % per)
-            ),
+            pl.BlockSpec((rows, tile), lambda n, info: (0, jnp.maximum(n - per, 0))),
+            pl.BlockSpec((rows, tile), lambda n, info: (0, jnp.minimum(n, per - 1))),
+            pl.BlockSpec((feat, tile), lambda n, info: (0, jnp.maximum(n - per, 0))),
+            pl.BlockSpec((feat, tile), lambda n, info: (0, jnp.minimum(n, per - 1))),
             whole((rows, feat)),
             whole((8, feat)),
             whole((2, feat, feat // 2)),
@@ -1058,7 +1006,7 @@
         compiler_params=params(32),
         name="fall",
         cost_estimate=cost(18),
-    )(info, grad_y, slope, up_set, after, vecs, proj_set, *pieces)
+    )(info, grad_y, *slopes, *up_sets, after, vecs, proj_set, *pieces)
 
 
 def exit_kernel(
@@ -1253,39 +1201,38 @@
     )(info, left, left_o, right, right_o)
 
 
-def outer_down_kernel(left, left_o, right, right_o, keep, away):
-    def flat(blocks):
-        return blocks[...].reshape(-1, blocks.shape[-1])
-
-    total = dot(flat(left), right[...]) + dot(flat(left_o), right_o[...])
-    total = total.reshape(keep.shape)
-
-    @pl.when(pl.program_id(0) >= 2)
-    def _():
-        keep[...] = total
-
-    @pl.when(pl.program_id(0) < 2)
-    def _():
-        away[...] = total.astype(BF16)
-
-
-def outer_down(chain, left, left_o, right, right_o):
-    _, block, rows = left.shape
+def outer_down_kernel(
+    info, first, second, first_o, second_o, right, right_o, keep, away, turned
+):
+    rows = right.shape[0]
+    core = info[CORE]
+    for r in range(8):
+        place = info[PLACE + 8 * core + r]
+        turned[place, :, :rows] = first[r]
+        turned[place, :, rows:] = second_o[r]
+        place = info[PLACE + 8 * (1 - core) + r]
+        turned[place, :, :rows] = second[r]
+        turned[place, :, rows:] = first_o[r]
+    for out, spots in ((away, slice(8, 16)), (keep, slice(0, 8))):
+        left = turned[spots].reshape(-1, turned.shape[2])
+        total = dot(left[:, :rows], right[...]) + dot(left[:, rows:], right_o[...])
+        out[...] = total.reshape(out.shape).astype(out.dtype)
+
+
+def outer_down(chain, info, first, second, first_o, second_o, right, right_o):
+    _, block, rows = first.shape
     feat = right.shape[1]
-    strip = pl.BlockSpec((4, block, rows), lambda j: ((j + 2) % 4, 0, 0))
+    vmem = pl.BlockSpec(memory_space=pltpu.VMEM)
     return chain.call(
         outer_down_kernel,
-        grid=(4,),
         out_shape=(shape((8, block, feat), F32), shape((8, block, feat), BF16)),
-        in_specs=[strip, strip, full((rows, feat)), full((rows, feat))],
-        out_specs=(
-            pl.BlockSpec((4, block, feat), lambda j: (jnp.maximum(j - 2, 0), 0, 0)),
-            pl.BlockSpec((4, block, feat), lambda j: (jnp.minimum(j, 1), 0, 0)),
-        ),
-        compiler_params=params(16),
+        in_specs=[SMEM] + [vmem] * 6,
+        out_specs=(vmem, vmem),
+        scratch_shapes=[pltpu.VMEM((16, block, 2 * rows), BF16)],
+        compiler_params=params(24),
         name="outer_down",
-        cost_estimate=cost(8),
-    )(left, left_o, right, right_o)
+        cost_estimate=cost(0),
+    )(info, first, second, first_o, second_o, right, right_o)
 
 
 def add_first_kernel(keep, got, kept, away):
@@ -1477,41 +1424,44 @@
     up_z = near_z(piece_up, (1, 2, 3))
     (low,) = gather(chain, [zs, send(zs, first_way)])
     high = send(low, second_way)
-    (zs_up,) = gather(chain, [piece_up] + up_z, (), 5)
-    high = gate(chain, high, 0)
-    pieces = (low, high, swap(low), swap(high))
-    first_set, vecs, bias, first, first_t, joint, grad_y, down = enter(
+    (zs,) = gather(chain, [piece_up] + up_z, (), 5)
+    pieces = both_cores(low, gate(chain, high, 0))
+    first_set, vecs, bias, first_t, joint, grad_y, down = enter(
         chain, info, tokens, upstream, down_weight, hidden, pieces
     )
     grad_y_o, first_o = swap(grad_y), swap(first_t)
     first_set = first_set.reshape(2, feat, 3 * third + 128)
-    (low,) = gather(chain, [zs_up, send(zs_up, first_way)])
+    first, second = send(zs, first_way), send(zs, second_way)
+    first = gate(chain, first, 0)
+    pieces = both_cores(zs, first, second, send(first, second_way))
     down_z = near_z(down, (1, 2, 3))
     mixed, mixed_t, stats = mix(chain, info, joint)
     mixed_t = mixed_t.reshape(first_t.shape)
     mixed_o = swap(mixed_t)
+    (zs,) = gather(chain, [down] + down_z, (), 5)
+    proj_set, after, normed, normed_t = rise(chain, info, tokens, mixed, vecs, pieces)
+    normed_o = swap(normed_t)
+    up_a, active_a, slope_a, mine_a, theirs_a = widen(chain, 0, info, normed, bias, pieces[:4])
+    theirs_a = swap(theirs_a)
+    (low,) = gather(chain, [zs, send(zs, first_way)])
     high = send(low, second_way)
-    pieces = (low, high, swap(low), swap(high))
-    (zs_down,) = gather(chain, [down] + down_z, (), 5)
-    proj_set, after, second, second_t = rise(chain, info, tokens, mixed, vecs, pieces)
-    second_o = swap(second_t)
-    (low,) = gather(chain, [zs_down, send(zs_down, first_way)])
-    up_set, active, slope, turned, turned_t = widen(chain, info, second, bias, pieces)
-    up_set = up_set.reshape(2, feat, wide)
+    up_b, active_b, slope_b, mine_b, theirs_b = widen(chain, 1, info, normed, bias, pieces[4:])
     proj_set = proj_set.reshape(2, feat, third)
-    high = gate(chain, send(low, second_way), 5)
-    pieces = (low, high, swap(low), swap(high))
-    down = outer_down(chain, turned, swap(turned_t), grad_y, grad_y_o)
+    down = outer_down(
+        chain, info, mine_a, mine_b, theirs_a, swap(theirs_b), grad_y, grad_y_o
+    )
+    pieces = both_cores(low, gate(chain, high, 0))
+    up_sets = (up_a.reshape(feat, wide), up_b.reshape(feat, wide))
     down_set, hid_theirs, hid_mine, bias_sum, grad_after, at_theirs, at_mine, grad_mixed, sums_a = (
-        fall(chain, info, grad_y, slope, up_set, after, vecs, proj_set, pieces)
+        fall(chain, info, grad_y, (slope_a, slope_b), up_sets, after, vecs, proj_set, pieces)
     )
     hid_o, at_o = swap(hid_theirs), swap(at_theirs)
     down = shift_first(chain, *down, 5)
-    up = outer_up(chain, info, second_t, second_o, hid_mine, hid_o, mixed_t, mixed_o, at_mine, at_o)
+    up = outer_up(chain, info, normed_t, normed_o, hid_mine, hid_o, mixed_t, mixed_o, at_mine, at_o)
     down = shift_second(chain, *down)
     theirs, mine = mix_back(chain, info, joint, grad_mixed, stats)
     theirs_o = swap(theirs)
-    own_down = home_down(chain, *down)
+    down = (down[0], [gate(chain, part, 0) for part in down[1]])
     up = shift_first(chain, *up, 5)
     chain.near(up[1])
     qkv = outer_qkv(chain, info, first_t, first_o, mine, theirs_o)
@@ -1520,8 +1470,11 @@
     )
     up = shift_second(chain, *up)
     qkv = shift_both(chain, *qkv, few_keep, few_away)
-    output = leave(chain, after, active, down_set.reshape(hidden, feat), vecs)
+    output = leave(
+        chain, info, after, active_a, active_b, down_set.reshape(hidden, feat), vecs
+    )
     qkv = shift_second(chain, *qkv)
+    own_down = home_down(chain, *down)
     own_up = home(chain, info, *up)
     own_qkv = home(chain, info, *qkv)
     out_qkv, out_proj, out_up, out_gains, out_shifts, out_bias = finish(

time: 227 us -> 223 us (0.982); the launches traced: 226 us -> 220 us
  waiting for transfers between devices: 51.4 us -> 42.6 us
  starting transfers between devices: 48.8 us -> 52.3 us
  Pallas kernels: 116 us -> 113 us
    ppermute x50 -> x54, waiting for transfers between devices: 51.4 us -> 42.6 us  [send(): return lax.ppermute(array, AXES, pairs(move))]
    ppermute x50 -> x54, starting transfers between devices: 48.8 us -> 52.3 us  [send(): return lax.ppermute(array, AXES, pairs(move))]
    pallas_call x31 -> x35, Pallas kernels: 116 us -> 113 us  [with_token(): *outs, self.token = run(*args, *extra, *([self.token] if held else []))]
    unnamed x28 -> x30, local copies, waits for them, and re-layouts: 6.12 us -> 8.23 us
  transfers between devices with their start and end apart: 50 -> 54, of which waited for: 18 -> 14; matrix products, arithmetic and copies ran while one was open for 1% -> 1% of each run, Pallas kernels for 50% -> 51%
where the time goes in v5:
time: 223 us; the launch traced here: 220 us
  Pallas kernels  113 us (51%)
  starting transfers between devices  52.3 us (23%)
  waiting for transfers between devices  42.6 us (19%)
  local copies, waits for them, and re-layouts  8.47 us (4%)
    pallas_call x35, Pallas kernels, with_token(): *outs, self.token = run(*args, *extra, *([self.token] if held else []))  113 us
    ppermute x54, starting transfers between devices, send(): return lax.ppermute(array, AXES, pairs(move))  52.3 us
    ppermute x54, waiting for transfers between devices, send(): return lax.ppermute(array, AXES, pairs(move))  42.6 us
    unnamed x30, local copies, waits for them, and re-layouts  8.23 us
  transfers between devices with their start and end apart: 54, of which 14 were waited for; matrix products, arithmetic and copies ran while one was open for 1% of the time, Pallas kernels for 51%

profile of v5, /device:TPU:0, one launch (start us, length us, event | category | flops | bytes accessed | tf_op | source)
XLA Modules:
  0.0 219.7 jit_solution(15813973352355198590)
XLA Ops:
  5.2 3.1 %collective-permute-start.1 = (bf16[1,48,1280]{2,1,0:T(8,128)(2,1)S(1)}, bf16[1,48,1280]{2,1,0:T(8,128)(2,1)S(1)}, u32[]{:S(2)}, u32[]{:S(2)}) collective-permute-start(bf16[1,48,1280]{2,1,0:T(8,128)(2,1)S(1)} %get-tuple-element.131.refs_0_), channel_id=1, source_target_pairs={{0,8},{1,9},{2,10},{3,11},{4,12},{5,13},{6,14},{7,15},{8,0},{9,1},... | collective-permute-start | bytes 368648 | tf_op jit(solution)/shard_map/ppermute | solution.py:266
  8.2 2.6 %collective-permute-start.2 = (bf16[1,48,1280]{2,1,0:T(8,128)(2,1)S(1)}, bf16[1,48,1280]{2,1,0:T(8,128)(2,1)S(1)}, u32[]{:S(2)}, u32[]{:S(2)}) collective-permute-start(bf16[1,48,1280]{2,1,0:T(8,128)(2,1)S(1)} %get-tuple-element.131.refs_0_), channel_id=1, source_target_pairs={{0,16},{1,17},{2,18},{3,19},{4,20},{5,21},{6,22},{7,23},{8,24},{9,... | collective-permute-start | bytes 368648 | tf_op jit(solution)/shard_map/ppermute | solution.py:266
  14.5 6.1 %collective-permute-done.2.refs_2_ = bf16[1,48,1280]{2,1,0:T(8,128)(2,1)S(1)} collective-permute-done((bf16[1,48,1280]{2,1,0:T(8,128)(2,1)S(1)}, bf16[1,48,1280]{2,1,0:T(8,128)(2,1)S(1)}, u32[]{:S(2)}, u32[]{:S(2)}) %collective-permute-start.2) | collective-permute-done | bytes 122912 | tf_op jit(solution)/shard_map/ppermute | solution.py:266
  22.2 2.1 collective-permute-start.8
  26.8 2.8 %collective-permute-done.6.refs_1_ = bf16[4,48,1280]{2,1,0:T(8,128)(2,1)S(1)} collective-permute-done((bf16[4,48,1280]{2,1,0:T(8,128)(2,1)S(1)}, bf16[4,48,1280]{2,1,0:T(8,128)(2,1)S(1)}, u32[]{:S(2)}, u32[]{:S(2)}) %collective-permute-start.6) | collective-permute-done | bytes 491552 | tf_op jit(solution)/shard_map/ppermute | solution.py:266
  32.1 8.0 %collective-permute-done.9.refs_2_ = bf16[1,48,1920]{2,1,0:T(8,128)(2,1)S(1)} collective-permute-done((bf16[1,48,1920]{2,1,0:T(8,128)(2,1)S(1)}, bf16[1,48,1920]{2,1,0:T(8,128)(2,1)S(1)}, u32[]{:S(2)}, u32[]{:S(2)}) %collective-permute-start.9) | collective-permute-done | bytes 184352 | tf_op jit(solution)/shard_map/ppermute | solution.py:266
  41.0 4.0 %collective-permute-done.7.refs_0_ = bf16[8,48,1280]{2,1,0:T(8,128)(2,1)} collective-permute-done((bf16[8,48,1280]{2,1,0:T(8,128)(2,1)}, bf16[8,48,1280]{2,1,0:T(8,128)(2,1)}, u32[]{:S(2)}, u32[]{:S(2)}) %collective-permute-start.7) | collective-permute-done | bytes 983072 | tf_op jit(solution)/shard_map/ppermute | solution.py:266
  48.0 6.7 %enter.1 = (bf16[2,16,48,1280]{3,2,1,0:T(8,128)(2,1)S(1)}, f32[8,768]{1,0:T(8,128)S(1)}, f32[1,3072]{1,0:T(1,128)S(1)}, bf16[16,48,512]{2,1,0:T(8,128)(2,1)}, bf...) custom-call(s32[66]{0:T(128)S(1)} %stack.239.refs_0_, ...), custom_call_target="tpu_custom_call", output_to_operand_aliasing={{7}: (8, {})} | custom-call | flops 240000008192 | bytes 1 | tf_op jit(solution)/shard_map/enter/pallas_call | solution.py:345
  54.8 2.1 collective-permute-start.20
  59.4 4.6 %collective-permute-done.13.refs_0_ = bf16[4,48,1920]{2,1,0:T(8,128)(2,1)} collective-permute-done((bf16[4,48,1920]{2,1,0:T(8,128)(2,1)}, bf16[4,48,1920]{2,1,0:T(8,128)(2,1)}, u32[]{:S(2)}, u32[]{:S(2)}) %collective-permute-start.13) | collective-permute-done | bytes 737312 | tf_op jit(solution)/shard_map/ppermute | solution.py:266
  63.9 2.0 collective-permute-start.15
  66.0 7.0 %mix.1 = (bf16[512,768]{1,0:T(8,128)(2,1)S(1)}, bf16[768,512]{1,0:T(8,128)(2,1)}, f32[6,8,512]{2,1,0:T(8,128)S(1)}, f32[8,128]{1,0:T(8,128)S(1)}) custom-call(s32[66]{0:T(128)S(1)} %stack.239.refs_0_, bf16[2,512,1152]{2,1,0:T(8,128)(2,1)S(1)} %get-tuple-element.143.refs_1_.refs_2_.refs_3_, ...), custom_call_target="tpu_custom_call", output_to_operand_aliasing={{3}: (4, {})} | custom-call | flops 299999985664 | bytes 1 | tf_op jit(solution)/shard_map/mix/pallas_call | solution.py:345
  75.7 2.0 gather.8
  79.8 4.4 %rise.1 = (bf16[2,16,48,384]{3,2,1,0:T(8,128)(2,1)S(1)}, f32[512,768]{1,0:T(8,128)S(1)}, bf16[512,768]{1,0:T(8,128)(2,1)S(1)}, bf16[16,48,512]{2,1,0:T(8,128)(2,1)}, f32[8,128]{1,0:T(8,128)S(1)}) custom-call(s32[66]{0:T(128)S(1)} %stack.239.refs_0_, bf16[512,768]{1,0:T(8,128)(2,1)S(1)} %copy-done.5, ...), custom_call_target="tpu_custom_call", output_to_operand_aliasing={{4}: (12, {})} | custom-call | flops 149999992832 | bytes 1 | tf_op jit(solution)/shard_map/rise/pallas_call | solution.py:345
  84.3 7.5 %widen.2 = (bf16[16,48,1536]{2,1,0:T(8,128)(2,1)S(1)}, bf16[512,1536]{1,0:T(8,128)(2,1)S(1)}, bf16[512,1536]{1,0:T(8,128)(2,1)S(1)}, bf16[8,96,512]{2,1,0:T(8,12...) custom-call(s32[66]{0:T(128)S(1)} %stack.239.refs_0_, ...), custom_call_target="tpu_custom_call", output_to_operand_aliasing={{5}: (7, {})} | custom-call | flops 539999993856 | bytes 1 | tf_op jit(solution)/shard_map/widen/pallas_call | solution.py:345
  92.9 2.3 %gather.9 = (bf16[8,96,768]{2,1,0:T(8,128)(2,1)}, f32[8,128]{1,0:T(8,128)S(1)}) custom-call(bf16[4,96,768]{2,1,0:T(8,128)(2,1)} %get-tuple-element.158.refs_0_, bf16[4,96,768]{2,1,0:T(8,128)(2,1)} %collective-permute-done.23.refs_1_, f32[8,128]{1,0:T(8,128)S(1)} %get-tuple-element.159.refs_2_), custom_call_target="tpu_custom_call", output_to_operand_aliasing={{1}: (2, {})} | custom-call | bytes 1 | tf_op jit(solution)/shard_map/gather/pallas_call | solution.py:345
  96.8 7.0 %widen.3 = (bf16[16,48,1536]{2,1,0:T(8,128)(2,1)S(1)}, bf16[512,1536]{1,0:T(8,128)(2,1)S(1)}, bf16[512,1536]{1,0:T(8,128)(2,1)S(1)}, bf16[8,96,512]{2,1,0:T(8,12...) custom-call(s32[66]{0:T(128)S(1)} %stack.239.refs_0_, ...), custom_call_target="tpu_custom_call", output_to_operand_aliasing={{5}: (7, {})} | custom-call | flops 539999993856 | bytes 1 | tf_op jit(solution)/shard_map/widen/pallas_call | solution.py:345
  104.4 2.2 collective-permute-done.26.refs_4_
  106.6 4.6 %outer_down.1 = (f32[8,96,768]{2,1,0:T(8,128)S(1)}, bf16[8,96,768]{2,1,0:T(8,128)(2,1)}, f32[8,128]{1,0:T(8,128)S(1)}) custom-call(s32[66]{0:T(128)S(1)} %stack.239.refs_0_, bf16[8,96,512]{2,1,0:T(8,128)(2,1)S(1)} %get-tuple-element.169.refs_1_, bf16[8,96,512]{2,1,0:T(8,128)(2,1)S(1)} %get-tuple-element.170.refs_2_, ...), custom_call_target="tpu_custom_call", output_to_operand_aliasing={{2}: (7, {})} | custom-call | bytes 1 | tf_op jit(solution)/shard_map/outer_down/pallas_call | solution.py:345
  114.3 2.2 collective-permute-done.29.refs_12_
  117.9 14.1 %fall.1 = (bf16[16,2,96,768]{3,2,1,0:T(8,128)(2,1)}, bf16[512,1536]{1,0:T(8,128)(2,1)}, bf16[512,1536]{1,0:T(8,128)(2,1)S(1)}, f32[1,3072]{1,0:T(1,128)S(1)}, f3...) custom-call(s32[66]{0:T(128)S(1)} %stack.239.refs_0_, ...), custom_call_target="tpu_custom_call", output_to_operand_aliasing={{9}: (13, {})} | custom-call | flops 539999993856 | bytes 1 | tf_op jit(solution)/shard_map/fall/pallas_call | solution.py:345
  132.6 2.3 %shift_first.2 = (f32[4,96,768]{2,1,0:T(8,128)S(1)}, bf16[4,96,768]{2,1,0:T(8,128)(2,1)}, f32[8,128]{1,0:T(8,128)S(1)}) custom-call(f32[8,96,768]{2,1,0:T(8,128)S(1)} %get-tuple-element.181.refs_0_, bf16[8,96,768]{2,1,0:T(8,128)(2,1)} %collective-permute-done.31.refs_1_, f32[8,128]{1,0:T(8,128)S(1)} %get-tuple-element.183.refs_2_), custom_call_target="tpu_custom_call", output_to_operand_aliasing={{2}: (2, {})} | custom-call | flops 149999992832 | bytes 1 | tf_op jit(solution)/shard_map/shift_first/pallas_call | solution.py:345
  136.4 7.4 %outer_up.1 = (f32[8,48,1920]{2,1,0:T(8,128)S(1)}, bf16[8,48,1920]{2,1,0:T(8,128)(2,1)}, f32[8,128]{1,0:T(8,128)S(1)}) custom-call(s32[66]{0:T(128)S(1)} %stack.239.refs_0_, bf16[16,48,512]{2,1,0:T(8,128)(2,1)} %get-tuple-element.186.refs_1_, bf16[16,48,512]{2,1,0:T(8,128)(2,1)} %collective-permute-done.33.refs_2_, ...), custom_call_target="tpu_custom_call", output_to_operand_aliasing={{2}: (9, {})} | custom-call | flops 240000008192 | bytes 1 | tf_op jit(solution)/shard_map/outer_up/pallas_call | solution.py:345
  147.2 2.4 %collective-permute-start.39 = (bf16[96,768]{1,0:T(8,128)(2,1)}, bf16[96,768]{1,0:T(8,128)(2,1)}, u32[]{:S(2)}, u32[]{:S(2)}) collective-permute-start(bf16[96,768]{1,0:T(8,128)(2,1)} %get-tuple-element.199), channel_id=1, source_target_pairs={{0,24},{1,25},{2,26},{3,27},{4,28},{5,29},{6,30},{7,31},{8,16},{9,... | collective-permute-start | bytes 442376 | tf_op jit(solution)/shard_map/ppermute | solution.py:266
  153.2 12.5 %mix_back.1 = (bf16[3,512,384]{2,1,0:T(8,128)(2,1)}, bf16[3,512,384]{2,1,0:T(8,128)(2,1)S(1)}, f32[8,128]{1,0:T(8,128)S(1)}) custom-call(s32[66]{0:T(128)S(1)} %stack.239.refs_0_, bf16[2,512,1152]{2,1,0:T(8,128)(2,1)S(1)} %copy-done.10, bf16[2,512,1152]{2,1,0:T(8,128)(2,1)S(1)} %copy-done.10, ...), custom_call_target="tpu_custom_call", output_to_operand_aliasing={{2}: (6, {})} | custom-call | flops 480000016384 | bytes 1 | tf_op jit(solution)/shard_map/mix_back/pallas_call | solution.py:345
  165.8 2.5 %shift_first.3 = (f32[4,48,1920]{2,1,0:T(8,128)S(1)}, bf16[4,48,1920]{2,1,0:T(8,128)(2,1)}, f32[8,128]{1,0:T(8,128)S(1)}) custom-call(f32[8,48,1920]{2,1,0:T(8,128)S(1)} %get-tuple-element.197.refs_0_, bf16[8,48,1920]{2,1,0:T(8,128)(2,1)} %collective-permute-done.38.refs_1_, f32[8,128]{1,0:T(8,128)S(1)} %get-tuple-element.205.refs_2_), custom_call_target="tpu_custom_call", output_to_operand_aliasing={{2}: (2, {})} | custom-call | flops 149999992832 | bytes 1 | tf_op jit(solution)/shard_map/shift_first/pallas_call | solution.py:345
  169.7 5.4 %outer_qkv.1 = (f32[8,48,1152]{2,1,0:T(8,128)S(1)}, bf16[8,48,1152]{2,1,0:T(8,128)(2,1)}, f32[8,128]{1,0:T(8,128)S(1)}) custom-call(s32[66]{0:T(128)S(1)} %stack.239.refs_0_, bf16[16,48,512]{2,1,0:T(8,128)(2,1)} %get-tuple-element.178.refs_1_, bf16[16,48,512]{2,1,0:T(8,128)(2,1)} %collective-permute-done.30.refs_2_, ...), custom_call_target="tpu_custom_call", output_to_operand_aliasing={{2}: (6, {})} | custom-call | flops 240000008192 | bytes 1 | tf_op jit(solution)/shard_map/outer_qkv/pallas_call | solution.py:345
  175.8 6.4 %exit_back.1 = (bf16[512,768]{1,0:T(8,128)(2,1)}, f32[8,48,128]{2,1,0:T(8,128)S(1)}, bf16[8,48,128]{2,1,0:T(8,128)(2,1)S(1)}, f32[8,128]{1,0:T(8,128)S(1)}) custom-call(s32[66]{0:T(128)S(1)} %stack.239.refs_0_, bf16[512,768]{1,0:T(8,128)(2,1)S(1)} %copy-done.6, ...), custom_call_target="tpu_custom_call", output_to_operand_aliasing={{3}: (9, {})} | custom-call | flops 240000008192 | bytes 1 | tf_op jit(solution)/shard_map/exit_back/pallas_call | solution.py:345
  183.6 2.1 shift_second.4
  190.1 2.1 shift_both.1
  195.0 5.2 %leave.1 = (bf16[512,768]{1,0:T(8,128)(2,1)}, f32[8,128]{1,0:T(8,128)S(1)}) custom-call(s32[66]{0:T(128)S(1)} %stack.239.refs_0_, f32[512,768]{1,0:T(8,128)S(1)} %get-tuple-element.153.refs_6_.refs_1_, bf16[512,1536]{1,0:T(8,128)(2,1)S(1)} %get-tuple-element.157.refs_2_, bf16[512,1536]{1,0:T(8,128)(2,1)S(1)} %copy-done.12, ...), custom_call_target="tpu_custom_call", output_to_operand_aliasing={{1}: (6, {})} | custom-call | flops 210000003072 | bytes 1 | tf_op jit(solution)/shard_map/leave/pallas_call | solution.py:345
  210.1 5.9 %collective-permute-done.47.refs_3_ = bf16[48,1280]{1,0:T(8,128)(2,1)S(1)} collective-permute-done((bf16[48,1280]{1,0:T(8,128)(2,1)S(1)}, bf16[48,1280]{1,0:T(8,128)(2,1)S(1)}, u32[]{:S(2)}, u32[]{:S(2)}) %collective-permute-start.47) | collective-permute-done | bytes 122912 | tf_op jit(solution)/shard_map/ppermute | solution.py:266
  (145 shorter events, 66.0 us)
Async XLA Ops:
  1.2 11.1 %collective-permute-start.4 = (bf16[24,3072]{1,0:T(8,128)(2,1)}, bf16[24,3072]{1,0:T(8,128)(2,1)S(1)}, u32[]{:S(2)}, u32[]{:S(2)}) collective-permute-start(bf16[24,3072]{1,0:T(8,128)(2,1)} %refs_1_.6), channel_id=1, source_target_pairs={{0,1},{1,0},{2,3},{3,2},{4,5},{5,4},{6,7},{7,6},{8,9},{9,8},{10,11... | collective-permute-start | bytes 442376 | tf_op jit(solution)/shard_map/ppermute | solution.py:266
  8.2 12.4 %collective-permute-start.2 = (bf16[1,48,1280]{2,1,0:T(8,128)(2,1)S(1)}, bf16[1,48,1280]{2,1,0:T(8,128)(2,1)S(1)}, u32[]{:S(2)}, u32[]{:S(2)}) collective-permute-start(bf16[1,48,1280]{2,1,0:T(8,128)(2,1)S(1)} %get-tuple-element.131.refs_0_), channel_id=1, source_target_pairs={{0,16},{1,17},{2,18},{3,19},{4,20},{5,21},{6,22},{7,23},{8,24},{9,... | collective-permute-start | bytes 368648 | tf_op jit(solution)/shard_map/ppermute | solution.py:266
  22.2 9.9 %collective-permute-start.8 = (bf16[1,48,1920]{2,1,0:T(8,128)(2,1)S(1)}, bf16[1,48,1920]{2,1,0:T(8,128)(2,1)S(1)}, u32[]{:S(2)}, u32[]{:S(2)}) collective-permute-start(bf16[1,48,1920]{2,1,0:T(8,128)(2,1)S(1)} %get-tuple-element.138.refs_0_), channel_id=1, source_target_pairs={{0,8},{1,9},{2,10},{3,11},{4,12},{5,13},{6,14},{7,15},{8,0},{9,1},... | collective-permute-start | bytes 552968 | tf_op jit(solution)/shard_map/ppermute | solution.py:266
  24.3 15.8 %collective-permute-start.9 = (bf16[1,48,1920]{2,1,0:T(8,128)(2,1)S(1)}, bf16[1,48,1920]{2,1,0:T(8,128)(2,1)S(1)}, u32[]{:S(2)}, u32[]{:S(2)}) collective-permute-start(bf16[1,48,1920]{2,1,0:T(8,128)(2,1)S(1)} %get-tuple-element.138.refs_0_), channel_id=1, source_target_pairs={{0,16},{1,17},{2,18},{3,19},{4,20},{5,21},{6,22},{7,23},{8,24},{9,... | collective-permute-start | bytes 552968 | tf_op jit(solution)/shard_map/ppermute | solution.py:266
  25.3 14.8 %collective-permute-start.10 = (bf16[1,48,1920]{2,1,0:T(8,128)(2,1)S(1)}, bf16[1,48,1920]{2,1,0:T(8,128)(2,1)S(1)}, u32[]{:S(2)}, u32[]{:S(2)}) collective-permute-start(bf16[1,48,1920]{2,1,0:T(8,128)(2,1)S(1)} %get-tuple-element.138.refs_0_), channel_id=1, source_target_pairs={{0,24},{1,25},{2,26},{3,27},{4,28},{5,29},{6,30},{7,31},{8,16},{9,... | collective-permute-start | bytes 552968 | tf_op jit(solution)/shard_map/ppermute | solution.py:266
  30.6 14.4 %collective-permute-start.7 = (bf16[8,48,1280]{2,1,0:T(8,128)(2,1)}, bf16[8,48,1280]{2,1,0:T(8,128)(2,1)}, u32[]{:S(2)}, u32[]{:S(2)}) collective-permute-start(bf16[8,48,1280]{2,1,0:T(8,128)(2,1)} %get-tuple-element.137.refs_4_), channel_id=1, source_target_pairs={{0,4},{1,3},{2,6},{3,1},{4,0},{5,7},{6,2},{7,5},{8,12},{9,11},{10,... | collective-permute-start | bytes 2949128 | tf_op jit(solution)/shard_map/ppermute | solution.py:266
  32.1 15.9 %collective-permute-start.11 = (bf16[8,48,1280]{2,1,0:T(8,128)(2,1)}, bf16[8,48,1280]{2,1,0:T(8,128)(2,1)}, u32[]{:S(2)}, u32[]{:S(2)}) collective-permute-start(bf16[8,48,1280]{2,1,0:T(8,128)(2,1)} %get-tuple-element.137.refs_4_), channel_id=1, source_target_pairs={{0,1},{1,0},{2,3},{3,2},{4,5},{5,4},{6,7},{7,6},{8,9},{9,8},{10,11... | collective-permute-start | bytes 2949128 | tf_op jit(solution)/shard_map/ppermute | solution.py:266
  45.0 18.9 %collective-permute-start.13 = (bf16[4,48,1920]{2,1,0:T(8,128)(2,1)}, bf16[4,48,1920]{2,1,0:T(8,128)(2,1)}, u32[]{:S(2)}, u32[]{:S(2)}) collective-permute-start(bf16[4,48,1920]{2,1,0:T(8,128)(2,1)} %get-tuple-element.144.refs_4_.refs_3_), channel_id=1, source_target_pairs={{0,2},{1,5},{2,0},{3,7},{4,6},{5,1},{6,4},{7,3},{8,10},{9,13},{10,... | collective-permute-start | bytes 2211848 | tf_op jit(solution)/shard_map/ppermute | solution.py:266
  46.5 26.5 %collective-permute-start.14 = (bf16[4,48,1920]{2,1,0:T(8,128)(2,1)}, bf16[4,48,1920]{2,1,0:T(8,128)(2,1)}, u32[]{:S(2)}, u32[]{:S(2)}) collective-permute-start(bf16[4,48,1920]{2,1,0:T(8,128)(2,1)} %get-tuple-element.144.refs_4_.refs_3_), channel_id=1, source_target_pairs={{0,4},{1,3},{2,6},{3,1},{4,0},{5,7},{6,2},{7,5},{8,12},{9,11},{10,... | collective-permute-start | bytes 2211848 | tf_op jit(solution)/shard_map/ppermute | solution.py:266
  54.8 18.2 %collective-permute-start.20 = (bf16[1,96,768]{2,1,0:T(8,128)(2,1)}, bf16[1,96,768]{2,1,0:T(8,128)(2,1)}, u32[]{:S(2)}, u32[]{:S(2)}) collective-permute-start(bf16[1,96,768]{2,1,0:T(8,128)(2,1)} %get-tuple-element.150.refs_0_), channel_id=1, source_target_pairs={{0,8},{1,9},{2,10},{3,11},{4,12},{5,13},{6,14},{7,15},{8,0},{9,1},... | collective-permute-start | bytes 442376 | tf_op jit(solution)/shard_map/ppermute | solution.py:266
  56.9 16.6 %collective-permute-start.21 = (bf16[1,96,768]{2,1,0:T(8,128)(2,1)}, bf16[1,96,768]{2,1,0:T(8,128)(2,1)}, u32[]{:S(2)}, u32[]{:S(2)}) collective-permute-start(bf16[1,96,768]{2,1,0:T(8,128)(2,1)} %get-tuple-element.150.refs_0_), channel_id=1, source_target_pairs={{0,16},{1,17},{2,18},{3,19},{4,20},{5,21},{6,22},{7,23},{8,24},{9,... | collective-permute-start | bytes 442376 | tf_op jit(solution)/shard_map/ppermute | solution.py:266
  58.0 15.6 %collective-permute-start.22 = (bf16[1,96,768]{2,1,0:T(8,128)(2,1)}, bf16[1,96,768]{2,1,0:T(8,128)(2,1)}, u32[]{:S(2)}, u32[]{:S(2)}) collective-permute-start(bf16[1,96,768]{2,1,0:T(8,128)(2,1)} %get-tuple-element.150.refs_0_), channel_id=1, source_target_pairs={{0,24},{1,25},{2,26},{3,27},{4,28},{5,29},{6,30},{7,31},{8,16},{9,... | collective-permute-start | bytes 442376 | tf_op jit(solution)/shard_map/ppermute | solution.py:266
  63.9 11.8 %collective-permute-start.15 = (bf16[4,48,1920]{2,1,0:T(8,128)(2,1)}, bf16[4,48,1920]{2,1,0:T(8,128)(2,1)}, u32[]{:S(2)}, u32[]{:S(2)}) collective-permute-start(bf16[4,48,1920]{2,1,0:T(8,128)(2,1)} %get-tuple-element.149.refs_5_.refs_4_), channel_id=1, source_target_pairs={{0,4},{1,3},{2,6},{3,1},{4,0},{5,7},{6,2},{7,5},{8,12},{9,11},{10,... | collective-permute-start | bytes 2211848 | tf_op jit(solution)/shard_map/ppermute | solution.py:266
  73.6 30.8 %collective-permute-start.27 = (bf16[512,768]{1,0:T(8,128)(2,1)}, bf16[512,768]{1,0:T(8,128)(2,1)}, u32[]{:S(2)}, u32[]{:S(2)}) collective-permute-start(bf16[512,768]{1,0:T(8,128)(2,1)} %get-tuple-element.162.refs_5_.refs_1_), channel_id=1, source_target_pairs={{0,1},{1,0},{2,3},{3,2},{4,5},{5,4},{6,7},{7,6},{8,9},{9,8},{10,11... | collective-permute-start | bytes 2359304 | tf_op jit(solution)/shard_map/ppermute | solution.py:266
  77.8 15.2 %collective-permute-start.23 = (bf16[4,96,768]{2,1,0:T(8,128)(2,1)}, bf16[4,96,768]{2,1,0:T(8,128)(2,1)}, u32[]{:S(2)}, u32[]{:S(2)}) collective-permute-start(bf16[4,96,768]{2,1,0:T(8,128)(2,1)} %get-tuple-element.158.refs_0_), channel_id=1, source_target_pairs={{0,2},{1,5},{2,0},{3,7},{4,6},{5,1},{6,4},{7,3},{8,10},{9,13},{10,... | collective-permute-start | bytes 1769480 | tf_op jit(solution)/shard_map/ppermute | solution.py:266
  95.3 16.5 %collective-permute-start.24 = (bf16[8,96,768]{2,1,0:T(8,128)(2,1)}, bf16[8,96,768]{2,1,0:T(8,128)(2,1)}, u32[]{:S(2)}, u32[]{:S(2)}) collective-permute-start(bf16[8,96,768]{2,1,0:T(8,128)(2,1)} %get-tuple-element.168.refs_9_), channel_id=1, source_target_pairs={{0,4},{1,3},{2,6},{3,1},{4,0},{5,7},{6,2},{7,5},{8,12},{9,11},{10,... | collective-permute-start | bytes 3538952 | tf_op jit(solution)/shard_map/ppermute | solution.py:266
  111.8 57.9 %collective-permute-start.30 = (bf16[16,48,512]{2,1,0:T(8,128)(2,1)}, bf16[16,48,512]{2,1,0:T(8,128)(2,1)}, u32[]{:S(2)}, u32[]{:S(2)}) collective-permute-start(bf16[16,48,512]{2,1,0:T(8,128)(2,1)} %get-tuple-element.178.refs_1_), channel_id=1, source_target_pairs={{0,1},{1,0},{2,3},{3,2},{4,5},{5,4},{6,7},{7,6},{8,9},{9,8},{10,11... | collective-permute-start | bytes 2359304 | tf_op jit(solution)/shard_map/ppermute | solution.py:266
  112.3 22.6 %collective-permute-start.35 = (bf16[16,48,512]{2,1,0:T(8,128)(2,1)}, bf16[16,48,512]{2,1,0:T(8,128)(2,1)}, u32[]{:S(2)}, u32[]{:S(2)}) collective-permute-start(bf16[16,48,512]{2,1,0:T(8,128)(2,1)} %bitcast.62.refs_5_), channel_id=1, source_target_pairs={{0,1},{1,0},{2,3},{3,2},{4,5},{5,4},{6,7},{7,6},{8,9},{9,8},{10,11... | collective-permute-start | bytes 2359304 | tf_op jit(solution)/shard_map/ppermute | solution.py:266
  112.3 24.1 %collective-permute-start.33 = (bf16[16,48,512]{2,1,0:T(8,128)(2,1)}, bf16[16,48,512]{2,1,0:T(8,128)(2,1)}, u32[]{:S(2)}, u32[]{:S(2)}) collective-permute-start(bf16[16,48,512]{2,1,0:T(8,128)(2,1)} %get-tuple-element.186.refs_1_), channel_id=1, source_target_pairs={{0,1},{1,0},{2,3},{3,2},{4,5},{5,4},{6,7},{7,6},{8,9},{9,8},{10,11... | collective-permute-start | bytes 2359304 | tf_op jit(solution)/shard_map/ppermute | solution.py:266
  112.8 19.4 %collective-permute-start.31 = (bf16[8,96,768]{2,1,0:T(8,128)(2,1)}, bf16[8,96,768]{2,1,0:T(8,128)(2,1)}, u32[]{:S(2)}, u32[]{:S(2)}) collective-permute-start(bf16[8,96,768]{2,1,0:T(8,128)(2,1)} %get-tuple-element.182), channel_id=1, source_target_pairs={{0,4},{1,3},{2,6},{3,1},{4,0},{5,7},{6,2},{7,5},{8,12},{9,11},{10,... | collective-permute-start | bytes 3538952 | tf_op jit(solution)/shard_map/ppermute | solution.py:266
  134.9 10.3 %collective-permute-start.32 = (bf16[4,96,768]{2,1,0:T(8,128)(2,1)}, bf16[4,96,768]{2,1,0:T(8,128)(2,1)}, u32[]{:S(2)}, u32[]{:S(2)}) collective-permute-start(bf16[4,96,768]{2,1,0:T(8,128)(2,1)} %get-tuple-element.185), channel_id=1, source_target_pairs={{0,2},{1,5},{2,0},{3,7},{4,6},{5,1},{6,4},{7,3},{8,10},{9,13},{10,... | collective-permute-start | bytes 1769480 | tf_op jit(solution)/shard_map/ppermute | solution.py:266
  143.8 22.0 %collective-permute-start.38 = (bf16[8,48,1920]{2,1,0:T(8,128)(2,1)}, bf16[8,48,1920]{2,1,0:T(8,128)(2,1)}, u32[]{:S(2)}, u32[]{:S(2)}) collective-permute-start(bf16[8,48,1920]{2,1,0:T(8,128)(2,1)} %get-tuple-element.198), channel_id=1, source_target_pairs={{0,4},{1,3},{2,6},{3,1},{4,0},{5,7},{6,2},{7,5},{8,12},{9,11},{10,... | collective-permute-start | bytes 4423688 | tf_op jit(solution)/shard_map/ppermute | solution.py:266
  147.2 18.6 %collective-permute-start.39 = (bf16[96,768]{1,0:T(8,128)(2,1)}, bf16[96,768]{1,0:T(8,128)(2,1)}, u32[]{:S(2)}, u32[]{:S(2)}) collective-permute-start(bf16[96,768]{1,0:T(8,128)(2,1)} %get-tuple-element.199), channel_id=1, source_target_pairs={{0,24},{1,25},{2,26},{3,27},{4,28},{5,29},{6,30},{7,31},{8,16},{9,... | collective-permute-start | bytes 442376 | tf_op jit(solution)/shard_map/ppermute | solution.py:266
  149.6 16.2 %collective-permute-start.40 = (bf16[96,768]{1,0:T(8,128)(2,1)}, bf16[96,768]{1,0:T(8,128)(2,1)}, u32[]{:S(2)}, u32[]{:S(2)}) collective-permute-start(bf16[96,768]{1,0:T(8,128)(2,1)} %get-tuple-element.200), channel_id=1, source_target_pairs={{0,16},{1,17},{2,18},{3,19},{4,20},{5,21},{6,22},{7,23},{8,24},{9,... | collective-permute-start | bytes 442376 | tf_op jit(solution)/shard_map/ppermute | solution.py:266
  150.7 15.0 %collective-permute-start.41 = (bf16[96,768]{1,0:T(8,128)(2,1)}, bf16[96,768]{1,0:T(8,128)(2,1)}, u32[]{:S(2)}, u32[]{:S(2)}) collective-permute-start(bf16[96,768]{1,0:T(8,128)(2,1)} %get-tuple-element.201), channel_id=1, source_target_pairs={{0,8},{1,9},{2,10},{3,11},{4,12},{5,13},{6,14},{7,15},{8,0},{9,1},... | collective-permute-start | bytes 442376 | tf_op jit(solution)/shard_map/ppermute | solution.py:266
  168.3 15.2 %collective-permute-start.44 = (bf16[4,48,1920]{2,1,0:T(8,128)(2,1)}, bf16[4,48,1920]{2,1,0:T(8,128)(2,1)}, u32[]{:S(2)}, u32[]{:S(2)}) collective-permute-start(bf16[4,48,1920]{2,1,0:T(8,128)(2,1)} %get-tuple-element.206.refs_5_), channel_id=1, source_target_pairs={{0,2},{1,5},{2,0},{3,7},{4,6},{5,1},{6,4},{7,3},{8,10},{9,13},{10,... | collective-permute-start | bytes 2211848 | tf_op jit(solution)/shard_map/ppermute | solution.py:266
  175.1 14.9 %collective-permute-start.42 = (bf16[8,48,1152]{2,1,0:T(8,128)(2,1)}, bf16[8,48,1152]{2,1,0:T(8,128)(2,1)}, u32[]{:S(2)}, u32[]{:S(2)}) collective-permute-start(bf16[8,48,1152]{2,1,0:T(8,128)(2,1)} %get-tuple-element.209), channel_id=1, source_target_pairs={{0,4},{1,3},{2,6},{3,1},{4,0},{5,7},{6,2},{7,5},{8,12},{9,11},{10,... | collective-permute-start | bytes 2654216 | tf_op jit(solution)/shard_map/ppermute | solution.py:266
  185.7 19.9 %collective-permute-start.49 = (bf16[48,1920]{1,0:T(8,128)(2,1)}, bf16[48,1920]{1,0:T(8,128)(2,1)}, u32[]{:S(2)}, u32[]{:S(2)}) collective-permute-start(bf16[48,1920]{1,0:T(8,128)(2,1)} %get-tuple-element.231), channel_id=1, source_target_pairs={{0,8},{1,9},{2,10},{3,11},{4,12},{5,13},{6,14},{7,15},{8,0},{9,1},... | collective-permute-start | bytes 552968 | tf_op jit(solution)/shard_map/ppermute | solution.py:266
  186.8 21.9 %collective-permute-start.50 = (bf16[48,1920]{1,0:T(8,128)(2,1)}, bf16[48,1920]{1,0:T(8,128)(2,1)}, u32[]{:S(2)}, u32[]{:S(2)}) collective-permute-start(bf16[48,1920]{1,0:T(8,128)(2,1)} %get-tuple-element.232), channel_id=1, source_target_pairs={{0,16},{1,17},{2,18},{3,19},{4,20},{5,21},{6,22},{7,23},{8,24},{9,... | collective-permute-start | bytes 552968 | tf_op jit(solution)/shard_map/ppermute | solution.py:266
  188.6 20.1 %collective-permute-start.51 = (bf16[48,1920]{1,0:T(8,128)(2,1)}, bf16[48,1920]{1,0:T(8,128)(2,1)}, u32[]{:S(2)}, u32[]{:S(2)}) collective-permute-start(bf16[48,1920]{1,0:T(8,128)(2,1)} %get-tuple-element.233), channel_id=1, source_target_pairs={{0,24},{1,25},{2,26},{3,27},{4,28},{5,29},{6,30},{7,31},{8,16},{9,... | collective-permute-start | bytes 552968 | tf_op jit(solution)/shard_map/ppermute | solution.py:266
  203.7 12.3 %collective-permute-start.47 = (bf16[48,1280]{1,0:T(8,128)(2,1)S(1)}, bf16[48,1280]{1,0:T(8,128)(2,1)S(1)}, u32[]{:S(2)}, u32[]{:S(2)}) collective-permute-start(bf16[48,1280]{1,0:T(8,128)(2,1)S(1)} %get-tuple-element.228), channel_id=1, source_target_pairs={{0,16},{1,17},{2,18},{3,19},{4,20},{5,21},{6,22},{7,23},{8,24},{9,... | collective-permute-start | bytes 368648 | tf_op jit(solution)/shard_map/ppermute | solution.py:266
  205.5 10.5 %collective-permute-start.48 = (bf16[48,1280]{1,0:T(8,128)(2,1)S(1)}, bf16[48,1280]{1,0:T(8,128)(2,1)S(1)}, u32[]{:S(2)}, u32[]{:S(2)}) collective-permute-start(bf16[48,1280]{1,0:T(8,128)(2,1)S(1)} %get-tuple-element.229), channel_id=1, source_target_pairs={{0,24},{1,25},{2,26},{3,27},{4,28},{5,29},{6,30},{7,31},{8,16},{9,... | collective-permute-start | bytes 368648 | tf_op jit(solution)/shard_map/ppermute | solution.py:266
  (37 other events, 203.4 us)

commit v6 on v5

--- a/solution.py
+++ b/solution.py
@@ -447,22 +447,22 @@
     )(info, up, up_o, proj, proj_o)
 
 
-def gather_kernel(n_in, n_held, *refs):
-    out, at = refs[n_in + n_held], 0
-    for part in refs[:n_in]:
+def gather_kernel(n_in, n_held, order, *refs):
+    out = refs[n_in + n_held]
+    for i, part in enumerate(refs[:n_in]):
+        at = part.shape[0] * (i if order is None else order[i])
         out[at : at + part.shape[0]] = part[...]
-        at += part.shape[0]
     for i in range(n_held):
         refs[n_in + n_held + 1 + i][...] = refs[n_in + i][...]
 
 
-def gather(chain, parts, held=(), micros=0):
+def gather(chain, parts, held=(), micros=0, order=None):
     vmem = pl.BlockSpec(memory_space=pltpu.VMEM)
     _, rows, cols = parts[0].shape
     count = sum(part.shape[0] for part in parts)
     n, n_held = len(parts), len(held)
     return chain.call(
-        partial(gather_kernel, n, n_held),
+        partial(gather_kernel, n, n_held, order),
         out_shape=(shape((count, rows, cols), BF16),) + tuple(shape(h.shape, h.dtype) for h in held),
         in_specs=[vmem] * (n + n_held),
         out_specs=(vmem,) * (1 + n_held),
@@ -504,8 +504,8 @@
     down,
     *refs,
 ):
-    pieces = refs[:4]
-    kept, vecs, bias, flipped, joint, grad_y, piece_down, weights, sem = refs[4:]
+    pieces = refs[:8]
+    kept, vecs, bias, flipped, joint, grad_y, piece_down, weights, sem = refs[8:]
     feat = tokens.shape[1]
     third = feat // 2
     piece_down[0] = down[...]
@@ -552,7 +552,7 @@
             shape((rows, feat), BF16),
             shape((1,) + down.shape, BF16),
         ),
-        in_specs=[SMEM] + [vmem] * 7,
+        in_specs=[SMEM] + [vmem] * 11,
         out_specs=(ANY,) + (vmem,) * 6,
         scratch_shapes=[pltpu.VMEM(sets, BF16), pltpu.SemaphoreType.DMA],
         compiler_params=params(20),
@@ -1129,12 +1129,19 @@
 
 
 def outer_up_kernel(
-    info, left, left_o, right, right_o, low, low_o, attn, attn_o, keep, away, turned
+    info, left, left_o, right, right_o, low, low_o, attn, attn_o, keep, away, turned, *late
 ):
     step, last = pl.program_id(0), pl.num_programs(0) - 1
+    buffers, sems = late[:4], late[4]
+    copies = [
+        pltpu.make_async_copy(src, dst, sems.at[i])
+        for i, (src, dst) in enumerate(zip((low, low_o, attn, attn_o), buffers))
+    ]
 
     @pl.when(step == 0)
     def _():
+        for copy in copies:
+            copy.start()
         line_up(info, left, left_o, turned)
 
     @pl.when(step < last)
@@ -1145,8 +1152,10 @@
 
     @pl.when(step == last)
     def _():
-        line_up(info, low, low_o, turned)
-        total = outer_tile(turned, attn[...], attn_o[...])
+        for copy in copies:
+            copy.wait()
+        line_up(info, buffers[0], buffers[1], turned)
+        total = outer_tile(turned, buffers[2][...], buffers[3][...])
         keep[:, :, : attn.shape[1]] = total[:8]
         away[:, :, : attn.shape[1]] = total[8:].astype(BF16)
 
@@ -1162,13 +1171,12 @@
         outer_up_kernel,
         grid=(n + 1,),
         out_shape=(shape((8, block, cols), F32), shape((8, block, cols), BF16)),
-        in_specs=[SMEM]
-        + [full(left.shape)] * 2
-        + [strip] * 2
-        + [full(left.shape)] * 2
-        + [full(attn.shape)] * 2,
+        in_specs=[SMEM] + [full(left.shape)] * 2 + [strip] * 2 + [ANY] * 4,
         out_specs=(out, out),
-        scratch_shapes=[pltpu.VMEM((16, block, 2 * rows), BF16)],
+        scratch_shapes=[pltpu.VMEM((16, block, 2 * rows), BF16)]
+        + [pltpu.VMEM(left.shape, BF16)] * 2
+        + [pltpu.VMEM(attn.shape, BF16)] * 2
+        + [pltpu.SemaphoreType.DMA((4,))],
         compiler_params=params(20),
         name="outer_up",
         cost_estimate=cost(8),
@@ -1420,12 +1428,13 @@
     small = small + jnp.pad(up_bias[None], ((0, rows - 1), (128 - up_bias.shape[0], 0)))
     piece = first_piece(chain, info, qkv_weight, swap(qkv_weight), small)
     piece_up = up_piece(chain, info, up_weight, swap(up_weight), proj_weight, swap(proj_weight))
-    zs, piece_up = gather(chain, [piece] + near_z(piece, (1, 2, 3)), (piece_up,))
+    zs, piece_up = gather(chain, [piece] + near_z(piece, (3, 2, 1)), (piece_up,), 0, (0, 3, 2, 1))
     up_z = near_z(piece_up, (1, 2, 3))
-    (low,) = gather(chain, [zs, send(zs, first_way)])
-    high = send(low, second_way)
-    (zs,) = gather(chain, [piece_up] + up_z, (), 5)
-    pieces = both_cores(low, gate(chain, high, 0))
+    first = gate(chain, send(zs, first_way), 0)
+    second, both = send(zs, second_way), send(first, second_way)
+    (zs_up,) = gather(chain, [piece_up] + up_z, (), 5)
+    pieces = both_cores(zs, first, gate(chain, second, 0), gate(chain, both, 0))
+    zs = zs_up
     first_set, vecs, bias, first_t, joint, grad_y, down = enter(
         chain, info, tokens, upstream, down_weight, hidden, pieces
     )

time: 223 us -> 221 us (level)
  waiting for transfers between devices: 42.6 us -> 35.7 us
  starting transfers between devices: 52.3 us -> 56.7 us
    ppermute x54 -> x57, waiting for transfers between devices: 42.6 us -> 35.7 us  [send(): return lax.ppermute(array, AXES, pairs(move))]
    ppermute x54 -> x57, starting transfers between devices: 52.3 us -> 56.7 us  [send(): return lax.ppermute(array, AXES, pairs(move))]
    pallas_call x35 -> x36, Pallas kernels: 113 us -> 112 us  [with_token(): *outs, self.token = run(*args, *extra, *([self.token] if held else []))]
  transfers between devices with their start and end apart: 54 -> 57, of which waited for: 14 -> 15; matrix products, arithmetic and copies ran while one was open for 1% -> 1% of each run, Pallas kernels for 51% -> 51%
where the time goes in v6:
time: 221 us; the launch traced here: 217 us
  Pallas kernels  112 us (51%)
  starting transfers between devices  56.7 us (26%)
  waiting for transfers between devices  35.7 us (16%)
  local copies, waits for them, and re-layouts  8.47 us (4%)
    pallas_call x36, Pallas kernels, with_token(): *outs, self.token = run(*args, *extra, *([self.token] if held else []))  112 us
    ppermute x57, starting transfers between devices, send(): return lax.ppermute(array, AXES, pairs(move))  56.7 us
    ppermute x57, waiting for transfers between devices, send(): return lax.ppermute(array, AXES, pairs(move))  35.7 us
    unnamed x30, local copies, waits for them, and re-layouts  8.23 us
  transfers between devices with their start and end apart: 57, of which 15 were waited for; matrix products, arithmetic and copies ran while one was open for 1% of the time, Pallas kernels for 51%

profile of v6, /device:TPU:0, one launch (start us, length us, event | category | flops | bytes accessed | tf_op | source)
XLA Modules:
  0.0 216.8 jit_solution(16330744410944736969)
XLA Ops:
  5.2 5.1 %collective-permute-start.1 = (bf16[1,48,1280]{2,1,0:T(8,128)(2,1)S(1)}, bf16[1,48,1280]{2,1,0:T(8,128)(2,1)S(1)}, u32[]{:S(2)}, u32[]{:S(2)}) collective-permute-start(bf16[1,48,1280]{2,1,0:T(8,128)(2,1)S(1)} %get-tuple-element.133.refs_0_), channel_id=1, source_target_pairs={{0,24},{1,25},{2,26},{3,27},{4,28},{5,29},{6,30},{7,31},{8,16},{9,... | collective-permute-start | bytes 368648 | tf_op jit(solution)/shard_map/ppermute | solution.py:266
  14.6 6.3 %collective-permute-done.2.refs_2_ = bf16[1,48,1280]{2,1,0:T(8,128)(2,1)S(1)} collective-permute-done((bf16[1,48,1280]{2,1,0:T(8,128)(2,1)S(1)}, bf16[1,48,1280]{2,1,0:T(8,128)(2,1)S(1)}, u32[]{:S(2)}, u32[]{:S(2)}) %collective-permute-start.2) | collective-permute-done | bytes 122912 | tf_op jit(solution)/shard_map/ppermute | solution.py:266
  23.2 3.0 %collective-permute-start.9 = (bf16[1,48,1920]{2,1,0:T(8,128)(2,1)S(1)}, bf16[1,48,1920]{2,1,0:T(8,128)(2,1)S(1)}, u32[]{:S(2)}, u32[]{:S(2)}) collective-permute-start(bf16[1,48,1920]{2,1,0:T(8,128)(2,1)S(1)} %get-tuple-element.140.refs_0_), channel_id=1, source_target_pairs={{0,16},{1,17},{2,18},{3,19},{4,20},{5,21},{6,22},{7,23},{8,24},{9,... | collective-permute-start | bytes 552968 | tf_op jit(solution)/shard_map/ppermute | solution.py:266
  29.1 3.9 %collective-permute-done.6.refs_0_ = bf16[4,48,1280]{2,1,0:T(8,128)(2,1)} collective-permute-done((bf16[4,48,1280]{2,1,0:T(8,128)(2,1)}, bf16[4,48,1280]{2,1,0:T(8,128)(2,1)}, u32[]{:S(2)}, u32[]{:S(2)}) %collective-permute-start.6) | collective-permute-done | bytes 491552 | tf_op jit(solution)/shard_map/ppermute | solution.py:266
  33.0 2.6 %collective-permute-start.11 = (bf16[4,48,1280]{2,1,0:T(8,128)(2,1)}, bf16[4,48,1280]{2,1,0:T(8,128)(2,1)}, u32[]{:S(2)}, u32[]{:S(2)}) collective-permute-start(bf16[4,48,1280]{2,1,0:T(8,128)(2,1)} %get-tuple-element.139.refs_5_), channel_id=1, source_target_pairs={{0,4},{1,3},{2,6},{3,1},{4,0},{5,7},{6,2},{7,5},{8,12},{9,11},{10,... | collective-permute-start | bytes 1474568 | tf_op jit(solution)/shard_map/ppermute | solution.py:266
  35.6 4.1 %collective-permute-done.9.refs_2_ = bf16[1,48,1920]{2,1,0:T(8,128)(2,1)S(1)} collective-permute-done((bf16[1,48,1920]{2,1,0:T(8,128)(2,1)S(1)}, bf16[1,48,1920]{2,1,0:T(8,128)(2,1)S(1)}, u32[]{:S(2)}, u32[]{:S(2)}) %collective-permute-start.9) | collective-permute-done | bytes 184352 | tf_op jit(solution)/shard_map/ppermute | solution.py:266
  46.3 6.7 %enter.1 = (bf16[2,16,48,1280]{3,2,1,0:T(8,128)(2,1)S(1)}, f32[8,768]{1,0:T(8,128)S(1)}, f32[1,3072]{1,0:T(1,128)S(1)}, bf16[16,48,512]{2,1,0:T(8,128)(2,1)}, bf...) custom-call(s32[66]{0:T(128)S(1)} %stack.239.refs_0_, ...), custom_call_target="tpu_custom_call", output_to_operand_aliasing={{7}: (12, {})} | custom-call | flops 240000008192 | bytes 1 | tf_op jit(solution)/shard_map/enter/pallas_call | solution.py:345
  53.6 2.5 %collective-permute-start.24 = (bf16[1,96,768]{2,1,0:T(8,128)(2,1)}, bf16[1,96,768]{2,1,0:T(8,128)(2,1)}, u32[]{:S(2)}, u32[]{:S(2)}) collective-permute-start(bf16[1,96,768]{2,1,0:T(8,128)(2,1)} %get-tuple-element.154.refs_0_), channel_id=1, source_target_pairs={{0,16},{1,17},{2,18},{3,19},{4,20},{5,21},{6,22},{7,23},{8,24},{9,... | collective-permute-start | bytes 442376 | tf_op jit(solution)/shard_map/ppermute | solution.py:266
  57.4 3.6 %collective-permute-done.16.refs_0_ = bf16[4,48,1920]{2,1,0:T(8,128)(2,1)} collective-permute-done((bf16[4,48,1920]{2,1,0:T(8,128)(2,1)}, bf16[4,48,1920]{2,1,0:T(8,128)(2,1)}, u32[]{:S(2)}, u32[]{:S(2)}) %collective-permute-start.16) | collective-permute-done | bytes 737312 | tf_op jit(solution)/shard_map/ppermute | solution.py:266
  61.1 2.9 %collective-permute-start.18 = (bf16[4,48,1920]{2,1,0:T(8,128)(2,1)}, bf16[4,48,1920]{2,1,0:T(8,128)(2,1)}, u32[]{:S(2)}, u32[]{:S(2)}) collective-permute-start(bf16[4,48,1920]{2,1,0:T(8,128)(2,1)} %get-tuple-element.153.refs_5_.refs_4_), channel_id=1, source_target_pairs={{0,4},{1,3},{2,6},{3,1},{4,0},{5,7},{6,2},{7,5},{8,12},{9,11},{10,... | collective-permute-start | bytes 2211848 | tf_op jit(solution)/shard_map/ppermute | solution.py:266
  64.0 7.0 %mix.1 = (bf16[512,768]{1,0:T(8,128)(2,1)S(1)}, bf16[768,512]{1,0:T(8,128)(2,1)}, f32[6,8,512]{2,1,0:T(8,128)S(1)}, f32[8,128]{1,0:T(8,128)S(1)}) custom-call(s32[66]{0:T(128)S(1)} %stack.239.refs_0_, bf16[2,512,1152]{2,1,0:T(8,128)(2,1)S(1)} %get-tuple-element.147.refs_1_.refs_2_.refs_3_, ...), custom_call_target="tpu_custom_call", output_to_operand_aliasing={{3}: (4, {})} | custom-call | flops 299999985664 | bytes 1 | tf_op jit(solution)/shard_map/mix/pallas_call | solution.py:345
  77.8 4.4 %rise.1 = (bf16[2,16,48,384]{3,2,1,0:T(8,128)(2,1)S(1)}, f32[512,768]{1,0:T(8,128)S(1)}, bf16[512,768]{1,0:T(8,128)(2,1)S(1)}, bf16[16,48,512]{2,1,0:T(8,128)(2,1)}, f32[8,128]{1,0:T(8,128)S(1)}) custom-call(s32[66]{0:T(128)S(1)} %stack.239.refs_0_, bf16[512,768]{1,0:T(8,128)(2,1)S(1)} %copy-done.5, ...), custom_call_target="tpu_custom_call", output_to_operand_aliasing={{4}: (12, {})} | custom-call | flops 149999992832 | bytes 1 | tf_op jit(solution)/shard_map/rise/pallas_call | solution.py:345
  82.2 7.5 %widen.2 = (bf16[16,48,1536]{2,1,0:T(8,128)(2,1)S(1)}, bf16[512,1536]{1,0:T(8,128)(2,1)S(1)}, bf16[512,1536]{1,0:T(8,128)(2,1)S(1)}, bf16[8,96,512]{2,1,0:T(8,12...) custom-call(s32[66]{0:T(128)S(1)} %stack.239.refs_0_, ...), custom_call_target="tpu_custom_call", output_to_operand_aliasing={{5}: (7, {})} | custom-call | flops 539999993856 | bytes 1 | tf_op jit(solution)/shard_map/widen/pallas_call | solution.py:345
  90.9 2.3 %gather.7 = (bf16[8,96,768]{2,1,0:T(8,128)(2,1)}, f32[8,128]{1,0:T(8,128)S(1)}) custom-call(bf16[4,96,768]{2,1,0:T(8,128)(2,1)} %get-tuple-element.162.refs_0_, bf16[4,96,768]{2,1,0:T(8,128)(2,1)} %collective-permute-done.26.refs_1_, f32[8,128]{1,0:T(8,128)S(1)} %get-tuple-element.163.refs_2_), custom_call_target="tpu_custom_call", output_to_operand_aliasing={{1}: (2, {})} | custom-call | bytes 1 | tf_op jit(solution)/shard_map/gather/pallas_call | solution.py:345
  94.8 7.0 %widen.3 = (bf16[16,48,1536]{2,1,0:T(8,128)(2,1)S(1)}, bf16[512,1536]{1,0:T(8,128)(2,1)S(1)}, bf16[512,1536]{1,0:T(8,128)(2,1)S(1)}, bf16[8,96,512]{2,1,0:T(8,12...) custom-call(s32[66]{0:T(128)S(1)} %stack.239.refs_0_, ...), custom_call_target="tpu_custom_call", output_to_operand_aliasing={{5}: (7, {})} | custom-call | flops 539999993856 | bytes 1 | tf_op jit(solution)/shard_map/widen/pallas_call | solution.py:345
  102.4 2.2 collective-permute-done.29.refs_4_
  104.6 4.6 %outer_down.1 = (f32[8,96,768]{2,1,0:T(8,128)S(1)}, bf16[8,96,768]{2,1,0:T(8,128)(2,1)}, f32[8,128]{1,0:T(8,128)S(1)}) custom-call(s32[66]{0:T(128)S(1)} %stack.239.refs_0_, bf16[8,96,512]{2,1,0:T(8,128)(2,1)S(1)} %get-tuple-element.173.refs_1_, bf16[8,96,512]{2,1,0:T(8,128)(2,1)S(1)} %get-tuple-element.174.refs_2_, ...), custom_call_target="tpu_custom_call", output_to_operand_aliasing={{2}: (7, {})} | custom-call | bytes 1 | tf_op jit(solution)/shard_map/outer_down/pallas_call | solution.py:345
  112.3 2.2 collective-permute-done.32.refs_12_
  115.9 14.1 %fall.1 = (bf16[16,2,96,768]{3,2,1,0:T(8,128)(2,1)}, bf16[512,1536]{1,0:T(8,128)(2,1)}, bf16[512,1536]{1,0:T(8,128)(2,1)S(1)}, f32[1,3072]{1,0:T(1,128)S(1)}, f3...) custom-call(s32[66]{0:T(128)S(1)} %stack.239.refs_0_, ...), custom_call_target="tpu_custom_call", output_to_operand_aliasing={{9}: (13, {})} | custom-call | flops 539999993856 | bytes 1 | tf_op jit(solution)/shard_map/fall/pallas_call | solution.py:345
  130.6 2.3 %shift_first.2 = (f32[4,96,768]{2,1,0:T(8,128)S(1)}, bf16[4,96,768]{2,1,0:T(8,128)(2,1)}, f32[8,128]{1,0:T(8,128)S(1)}) custom-call(f32[8,96,768]{2,1,0:T(8,128)S(1)} %get-tuple-element.185.refs_0_, bf16[8,96,768]{2,1,0:T(8,128)(2,1)} %collective-permute-done.34.refs_1_, f32[8,128]{1,0:T(8,128)S(1)} %get-tuple-element.187.refs_2_), custom_call_target="tpu_custom_call", output_to_operand_aliasing={{2}: (2, {})} | custom-call | flops 149999992832 | bytes 1 | tf_op jit(solution)/shard_map/shift_first/pallas_call | solution.py:345
  134.5 7.1 %outer_up.1 = (f32[8,48,1920]{2,1,0:T(8,128)S(1)}, bf16[8,48,1920]{2,1,0:T(8,128)(2,1)}, f32[8,128]{1,0:T(8,128)S(1)}) custom-call(s32[66]{0:T(128)S(1)} %stack.239.refs_0_, bf16[16,48,512]{2,1,0:T(8,128)(2,1)} %get-tuple-element.190.refs_1_, bf16[16,48,512]{2,1,0:T(8,128)(2,1)} %collective-permute-done.36.refs_2_, ...), custom_call_target="tpu_custom_call", output_to_operand_aliasing={{2}: (9, {})} | custom-call | flops 240000008192 | bytes 1 | tf_op jit(solution)/shard_map/outer_up/pallas_call | solution.py:345
  145.1 2.5 %collective-permute-start.42 = (bf16[96,768]{1,0:T(8,128)(2,1)}, bf16[96,768]{1,0:T(8,128)(2,1)}, u32[]{:S(2)}, u32[]{:S(2)}) collective-permute-start(bf16[96,768]{1,0:T(8,128)(2,1)} %get-tuple-element.203), channel_id=1, source_target_pairs={{0,24},{1,25},{2,26},{3,27},{4,28},{5,29},{6,30},{7,31},{8,16},{9,... | collective-permute-start | bytes 442376 | tf_op jit(solution)/shard_map/ppermute | solution.py:266
  151.1 12.5 %mix_back.1 = (bf16[3,512,384]{2,1,0:T(8,128)(2,1)}, bf16[3,512,384]{2,1,0:T(8,128)(2,1)S(1)}, f32[8,128]{1,0:T(8,128)S(1)}) custom-call(s32[66]{0:T(128)S(1)} %stack.239.refs_0_, bf16[2,512,1152]{2,1,0:T(8,128)(2,1)S(1)} %copy-done.10, bf16[2,512,1152]{2,1,0:T(8,128)(2,1)S(1)} %copy-done.10, ...), custom_call_target="tpu_custom_call", output_to_operand_aliasing={{2}: (6, {})} | custom-call | flops 480000016384 | bytes 1 | tf_op jit(solution)/shard_map/mix_back/pallas_call | solution.py:345
  163.7 2.5 %shift_first.3 = (f32[4,48,1920]{2,1,0:T(8,128)S(1)}, bf16[4,48,1920]{2,1,0:T(8,128)(2,1)}, f32[8,128]{1,0:T(8,128)S(1)}) custom-call(f32[8,48,1920]{2,1,0:T(8,128)S(1)} %get-tuple-element.201.refs_0_, bf16[8,48,1920]{2,1,0:T(8,128)(2,1)} %collective-permute-done.41.refs_1_, f32[8,128]{1,0:T(8,128)S(1)} %get-tuple-element.209.refs_2_), custom_call_target="tpu_custom_call", output_to_operand_aliasing={{2}: (2, {})} | custom-call | flops 149999992832 | bytes 1 | tf_op jit(solution)/shard_map/shift_first/pallas_call | solution.py:345
  167.7 5.4 %outer_qkv.1 = (f32[8,48,1152]{2,1,0:T(8,128)S(1)}, bf16[8,48,1152]{2,1,0:T(8,128)(2,1)}, f32[8,128]{1,0:T(8,128)S(1)}) custom-call(s32[66]{0:T(128)S(1)} %stack.239.refs_0_, bf16[16,48,512]{2,1,0:T(8,128)(2,1)} %get-tuple-element.182.refs_1_, bf16[16,48,512]{2,1,0:T(8,128)(2,1)} %collective-permute-done.33.refs_2_, ...), custom_call_target="tpu_custom_call", output_to_operand_aliasing={{2}: (6, {})} | custom-call | flops 240000008192 | bytes 1 | tf_op jit(solution)/shard_map/outer_qkv/pallas_call | solution.py:345
  173.8 6.4 %exit_back.1 = (bf16[512,768]{1,0:T(8,128)(2,1)}, f32[8,48,128]{2,1,0:T(8,128)S(1)}, bf16[8,48,128]{2,1,0:T(8,128)(2,1)S(1)}, f32[8,128]{1,0:T(8,128)S(1)}) custom-call(s32[66]{0:T(128)S(1)} %stack.239.refs_0_, bf16[512,768]{1,0:T(8,128)(2,1)S(1)} %copy-done.6, ...), custom_call_target="tpu_custom_call", output_to_operand_aliasing={{3}: (9, {})} | custom-call | flops 240000008192 | bytes 1 | tf_op jit(solution)/shard_map/exit_back/pallas_call | solution.py:345
  181.6 2.1 shift_second.4
  183.8 2.9 %collective-permute-start.53 = (bf16[48,1920]{1,0:T(8,128)(2,1)}, bf16[48,1920]{1,0:T(8,128)(2,1)}, u32[]{:S(2)}, u32[]{:S(2)}) collective-permute-start(bf16[48,1920]{1,0:T(8,128)(2,1)} %get-tuple-element.236), channel_id=1, source_target_pairs={{0,16},{1,17},{2,18},{3,19},{4,20},{5,21},{6,22},{7,23},{8,24},{9,... | collective-permute-start | bytes 552968 | tf_op jit(solution)/shard_map/ppermute | solution.py:266
  188.1 2.2 shift_both.1
  193.0 5.2 %leave.1 = (bf16[512,768]{1,0:T(8,128)(2,1)}, f32[8,128]{1,0:T(8,128)S(1)}) custom-call(s32[66]{0:T(128)S(1)} %stack.239.refs_0_, f32[512,768]{1,0:T(8,128)S(1)} %get-tuple-element.157.refs_6_.refs_1_, bf16[512,1536]{1,0:T(8,128)(2,1)S(1)} %get-tuple-element.161.refs_2_, bf16[512,1536]{1,0:T(8,128)(2,1)S(1)} %copy-done.12, ...), custom_call_target="tpu_custom_call", output_to_operand_aliasing={{1}: (6, {})} | custom-call | flops 210000003072 | bytes 1 | tf_op jit(solution)/shard_map/leave/pallas_call | solution.py:345
  200.6 3.1 %collective-permute-start.50 = (bf16[48,1280]{1,0:T(8,128)(2,1)S(1)}, bf16[48,1280]{1,0:T(8,128)(2,1)S(1)}, u32[]{:S(2)}, u32[]{:S(2)}) collective-permute-start(bf16[48,1280]{1,0:T(8,128)(2,1)S(1)} %get-tuple-element.232), channel_id=1, source_target_pairs={{0,16},{1,17},{2,18},{3,19},{4,20},{5,21},{6,22},{7,23},{8,24},{9,... | collective-permute-start | bytes 368648 | tf_op jit(solution)/shard_map/ppermute | solution.py:266
  208.1 5.0 %collective-permute-done.50.refs_3_ = bf16[48,1280]{1,0:T(8,128)(2,1)S(1)} collective-permute-done((bf16[48,1280]{1,0:T(8,128)(2,1)S(1)}, bf16[48,1280]{1,0:T(8,128)(2,1)S(1)}, u32[]{:S(2)}, u32[]{:S(2)}) %collective-permute-start.50) | collective-permute-done | bytes 122912 | tf_op jit(solution)/shard_map/ppermute | solution.py:266
  (152 shorter events, 63.7 us)
Async XLA Ops:
  1.2 11.2 %collective-permute-start.4 = (bf16[24,3072]{1,0:T(8,128)(2,1)}, bf16[24,3072]{1,0:T(8,128)(2,1)S(1)}, u32[]{:S(2)}, u32[]{:S(2)}) collective-permute-start(bf16[24,3072]{1,0:T(8,128)(2,1)} %refs_1_.6), channel_id=1, source_target_pairs={{0,1},{1,0},{2,3},{3,2},{4,5},{5,4},{6,7},{7,6},{8,9},{9,8},{10,11... | collective-permute-start | bytes 442376 | tf_op jit(solution)/shard_map/ppermute | solution.py:266
  10.3 10.6 %collective-permute-start.2 = (bf16[1,48,1280]{2,1,0:T(8,128)(2,1)S(1)}, bf16[1,48,1280]{2,1,0:T(8,128)(2,1)S(1)}, u32[]{:S(2)}, u32[]{:S(2)}) collective-permute-start(bf16[1,48,1280]{2,1,0:T(8,128)(2,1)S(1)} %get-tuple-element.133.refs_0_), channel_id=1, source_target_pairs={{0,16},{1,17},{2,18},{3,19},{4,20},{5,21},{6,22},{7,23},{8,24},{9,... | collective-permute-start | bytes 368648 | tf_op jit(solution)/shard_map/ppermute | solution.py:266
  10.3 10.6 %collective-permute-start.3 = (bf16[1,48,1280]{2,1,0:T(8,128)(2,1)S(1)}, bf16[1,48,1280]{2,1,0:T(8,128)(2,1)S(1)}, u32[]{:S(2)}, u32[]{:S(2)}) collective-permute-start(bf16[1,48,1280]{2,1,0:T(8,128)(2,1)S(1)} %get-tuple-element.133.refs_0_), channel_id=1, source_target_pairs={{0,8},{1,9},{2,10},{3,11},{4,12},{5,13},{6,14},{7,15},{8,0},{9,1},... | collective-permute-start | bytes 368648 | tf_op jit(solution)/shard_map/ppermute | solution.py:266
  21.7 11.3 %collective-permute-start.6 = (bf16[4,48,1280]{2,1,0:T(8,128)(2,1)}, bf16[4,48,1280]{2,1,0:T(8,128)(2,1)}, u32[]{:S(2)}, u32[]{:S(2)}) collective-permute-start(bf16[4,48,1280]{2,1,0:T(8,128)(2,1)} %get-tuple-element.137.refs_4_), channel_id=1, source_target_pairs={{0,2},{1,5},{2,0},{3,7},{4,6},{5,1},{6,4},{7,3},{8,10},{9,13},{10,... | collective-permute-start | bytes 1474568 | tf_op jit(solution)/shard_map/ppermute | solution.py:266
  23.2 16.4 %collective-permute-start.9 = (bf16[1,48,1920]{2,1,0:T(8,128)(2,1)S(1)}, bf16[1,48,1920]{2,1,0:T(8,128)(2,1)S(1)}, u32[]{:S(2)}, u32[]{:S(2)}) collective-permute-start(bf16[1,48,1920]{2,1,0:T(8,128)(2,1)S(1)} %get-tuple-element.140.refs_0_), channel_id=1, source_target_pairs={{0,16},{1,17},{2,18},{3,19},{4,20},{5,21},{6,22},{7,23},{8,24},{9,... | collective-permute-start | bytes 552968 | tf_op jit(solution)/shard_map/ppermute | solution.py:266
  26.3 13.4 %collective-permute-start.10 = (bf16[1,48,1920]{2,1,0:T(8,128)(2,1)S(1)}, bf16[1,48,1920]{2,1,0:T(8,128)(2,1)S(1)}, u32[]{:S(2)}, u32[]{:S(2)}) collective-permute-start(bf16[1,48,1920]{2,1,0:T(8,128)(2,1)S(1)} %get-tuple-element.140.refs_0_), channel_id=1, source_target_pairs={{0,24},{1,25},{2,26},{3,27},{4,28},{5,29},{6,30},{7,31},{8,16},{9,... | collective-permute-start | bytes 552968 | tf_op jit(solution)/shard_map/ppermute | solution.py:266
  27.6 13.0 %collective-permute-start.7 = (bf16[4,48,1280]{2,1,0:T(8,128)(2,1)}, bf16[4,48,1280]{2,1,0:T(8,128)(2,1)}, u32[]{:S(2)}, u32[]{:S(2)}) collective-permute-start(bf16[4,48,1280]{2,1,0:T(8,128)(2,1)} %get-tuple-element.137.refs_4_), channel_id=1, source_target_pairs={{0,4},{1,3},{2,6},{3,1},{4,0},{5,7},{6,2},{7,5},{8,12},{9,11},{10,... | collective-permute-start | bytes 1474568 | tf_op jit(solution)/shard_map/ppermute | solution.py:266
  33.0 11.2 %collective-permute-start.12 = (bf16[4,48,1280]{2,1,0:T(8,128)(2,1)}, bf16[4,48,1280]{2,1,0:T(8,128)(2,1)}, u32[]{:S(2)}, u32[]{:S(2)}) collective-permute-start(bf16[4,48,1280]{2,1,0:T(8,128)(2,1)} %get-tuple-element.137.refs_4_), channel_id=1, source_target_pairs={{0,1},{1,0},{2,3},{3,2},{4,5},{5,4},{6,7},{7,6},{8,9},{9,8},{10,11... | collective-permute-start | bytes 1474568 | tf_op jit(solution)/shard_map/ppermute | solution.py:266
  42.7 18.4 %collective-permute-start.16 = (bf16[4,48,1920]{2,1,0:T(8,128)(2,1)}, bf16[4,48,1920]{2,1,0:T(8,128)(2,1)}, u32[]{:S(2)}, u32[]{:S(2)}) collective-permute-start(bf16[4,48,1920]{2,1,0:T(8,128)(2,1)} %get-tuple-element.148.refs_4_.refs_3_), channel_id=1, source_target_pairs={{0,2},{1,5},{2,0},{3,7},{4,6},{5,1},{6,4},{7,3},{8,10},{9,13},{10,... | collective-permute-start | bytes 2211848 | tf_op jit(solution)/shard_map/ppermute | solution.py:266
  44.2 26.7 %collective-permute-start.17 = (bf16[4,48,1920]{2,1,0:T(8,128)(2,1)}, bf16[4,48,1920]{2,1,0:T(8,128)(2,1)}, u32[]{:S(2)}, u32[]{:S(2)}) collective-permute-start(bf16[4,48,1920]{2,1,0:T(8,128)(2,1)} %get-tuple-element.148.refs_4_.refs_3_), channel_id=1, source_target_pairs={{0,4},{1,3},{2,6},{3,1},{4,0},{5,7},{6,2},{7,5},{8,12},{9,11},{10,... | collective-permute-start | bytes 2211848 | tf_op jit(solution)/shard_map/ppermute | solution.py:266
  53.0 18.0 %collective-permute-start.23 = (bf16[1,96,768]{2,1,0:T(8,128)(2,1)}, bf16[1,96,768]{2,1,0:T(8,128)(2,1)}, u32[]{:S(2)}, u32[]{:S(2)}) collective-permute-start(bf16[1,96,768]{2,1,0:T(8,128)(2,1)} %get-tuple-element.154.refs_0_), channel_id=1, source_target_pairs={{0,8},{1,9},{2,10},{3,11},{4,12},{5,13},{6,14},{7,15},{8,0},{9,1},... | collective-permute-start | bytes 442376 | tf_op jit(solution)/shard_map/ppermute | solution.py:266
  53.6 17.9 %collective-permute-start.24 = (bf16[1,96,768]{2,1,0:T(8,128)(2,1)}, bf16[1,96,768]{2,1,0:T(8,128)(2,1)}, u32[]{:S(2)}, u32[]{:S(2)}) collective-permute-start(bf16[1,96,768]{2,1,0:T(8,128)(2,1)} %get-tuple-element.154.refs_0_), channel_id=1, source_target_pairs={{0,16},{1,17},{2,18},{3,19},{4,20},{5,21},{6,22},{7,23},{8,24},{9,... | collective-permute-start | bytes 442376 | tf_op jit(solution)/shard_map/ppermute | solution.py:266
  56.1 15.4 %collective-permute-start.25 = (bf16[1,96,768]{2,1,0:T(8,128)(2,1)}, bf16[1,96,768]{2,1,0:T(8,128)(2,1)}, u32[]{:S(2)}, u32[]{:S(2)}) collective-permute-start(bf16[1,96,768]{2,1,0:T(8,128)(2,1)} %get-tuple-element.154.refs_0_), channel_id=1, source_target_pairs={{0,24},{1,25},{2,26},{3,27},{4,28},{5,29},{6,30},{7,31},{8,16},{9,... | collective-permute-start | bytes 442376 | tf_op jit(solution)/shard_map/ppermute | solution.py:266
  61.1 12.6 %collective-permute-start.18 = (bf16[4,48,1920]{2,1,0:T(8,128)(2,1)}, bf16[4,48,1920]{2,1,0:T(8,128)(2,1)}, u32[]{:S(2)}, u32[]{:S(2)}) collective-permute-start(bf16[4,48,1920]{2,1,0:T(8,128)(2,1)} %get-tuple-element.153.refs_5_.refs_4_), channel_id=1, source_target_pairs={{0,4},{1,3},{2,6},{3,1},{4,0},{5,7},{6,2},{7,5},{8,12},{9,11},{10,... | collective-permute-start | bytes 2211848 | tf_op jit(solution)/shard_map/ppermute | solution.py:266
  71.6 30.9 %collective-permute-start.30 = (bf16[512,768]{1,0:T(8,128)(2,1)}, bf16[512,768]{1,0:T(8,128)(2,1)}, u32[]{:S(2)}, u32[]{:S(2)}) collective-permute-start(bf16[512,768]{1,0:T(8,128)(2,1)} %get-tuple-element.166.refs_5_.refs_1_), channel_id=1, source_target_pairs={{0,1},{1,0},{2,3},{3,2},{4,5},{5,4},{6,7},{7,6},{8,9},{9,8},{10,11... | collective-permute-start | bytes 2359304 | tf_op jit(solution)/shard_map/ppermute | solution.py:266
  75.8 15.1 %collective-permute-start.26 = (bf16[4,96,768]{2,1,0:T(8,128)(2,1)}, bf16[4,96,768]{2,1,0:T(8,128)(2,1)}, u32[]{:S(2)}, u32[]{:S(2)}) collective-permute-start(bf16[4,96,768]{2,1,0:T(8,128)(2,1)} %get-tuple-element.162.refs_0_), channel_id=1, source_target_pairs={{0,2},{1,5},{2,0},{3,7},{4,6},{5,1},{6,4},{7,3},{8,10},{9,13},{10,... | collective-permute-start | bytes 1769480 | tf_op jit(solution)/shard_map/ppermute | solution.py:266
  93.3 16.5 %collective-permute-start.27 = (bf16[8,96,768]{2,1,0:T(8,128)(2,1)}, bf16[8,96,768]{2,1,0:T(8,128)(2,1)}, u32[]{:S(2)}, u32[]{:S(2)}) collective-permute-start(bf16[8,96,768]{2,1,0:T(8,128)(2,1)} %get-tuple-element.172.refs_9_), channel_id=1, source_target_pairs={{0,4},{1,3},{2,6},{3,1},{4,0},{5,7},{6,2},{7,5},{8,12},{9,11},{10,... | collective-permute-start | bytes 3538952 | tf_op jit(solution)/shard_map/ppermute | solution.py:266
  109.8 57.9 %collective-permute-start.33 = (bf16[16,48,512]{2,1,0:T(8,128)(2,1)}, bf16[16,48,512]{2,1,0:T(8,128)(2,1)}, u32[]{:S(2)}, u32[]{:S(2)}) collective-permute-start(bf16[16,48,512]{2,1,0:T(8,128)(2,1)} %get-tuple-element.182.refs_1_), channel_id=1, source_target_pairs={{0,1},{1,0},{2,3},{3,2},{4,5},{5,4},{6,7},{7,6},{8,9},{9,8},{10,11... | collective-permute-start | bytes 2359304 | tf_op jit(solution)/shard_map/ppermute | solution.py:266
  110.3 22.7 %collective-permute-start.38 = (bf16[16,48,512]{2,1,0:T(8,128)(2,1)}, bf16[16,48,512]{2,1,0:T(8,128)(2,1)}, u32[]{:S(2)}, u32[]{:S(2)}) collective-permute-start(bf16[16,48,512]{2,1,0:T(8,128)(2,1)} %bitcast.62.refs_5_), channel_id=1, source_target_pairs={{0,1},{1,0},{2,3},{3,2},{4,5},{5,4},{6,7},{7,6},{8,9},{9,8},{10,11... | collective-permute-start | bytes 2359304 | tf_op jit(solution)/shard_map/ppermute | solution.py:266
  110.3 24.2 %collective-permute-start.36 = (bf16[16,48,512]{2,1,0:T(8,128)(2,1)}, bf16[16,48,512]{2,1,0:T(8,128)(2,1)}, u32[]{:S(2)}, u32[]{:S(2)}) collective-permute-start(bf16[16,48,512]{2,1,0:T(8,128)(2,1)} %get-tuple-element.190.refs_1_), channel_id=1, source_target_pairs={{0,1},{1,0},{2,3},{3,2},{4,5},{5,4},{6,7},{7,6},{8,9},{9,8},{10,11... | collective-permute-start | bytes 2359304 | tf_op jit(solution)/shard_map/ppermute | solution.py:266
  110.8 19.4 %collective-permute-start.34 = (bf16[8,96,768]{2,1,0:T(8,128)(2,1)}, bf16[8,96,768]{2,1,0:T(8,128)(2,1)}, u32[]{:S(2)}, u32[]{:S(2)}) collective-permute-start(bf16[8,96,768]{2,1,0:T(8,128)(2,1)} %get-tuple-element.186), channel_id=1, source_target_pairs={{0,4},{1,3},{2,6},{3,1},{4,0},{5,7},{6,2},{7,5},{8,12},{9,11},{10,... | collective-permute-start | bytes 3538952 | tf_op jit(solution)/shard_map/ppermute | solution.py:266
  133.0 10.2 %collective-permute-start.35 = (bf16[4,96,768]{2,1,0:T(8,128)(2,1)}, bf16[4,96,768]{2,1,0:T(8,128)(2,1)}, u32[]{:S(2)}, u32[]{:S(2)}) collective-permute-start(bf16[4,96,768]{2,1,0:T(8,128)(2,1)} %get-tuple-element.189), channel_id=1, source_target_pairs={{0,2},{1,5},{2,0},{3,7},{4,6},{5,1},{6,4},{7,3},{8,10},{9,13},{10,... | collective-permute-start | bytes 1769480 | tf_op jit(solution)/shard_map/ppermute | solution.py:266
  141.5 22.1 %collective-permute-start.41 = (bf16[8,48,1920]{2,1,0:T(8,128)(2,1)}, bf16[8,48,1920]{2,1,0:T(8,128)(2,1)}, u32[]{:S(2)}, u32[]{:S(2)}) collective-permute-start(bf16[8,48,1920]{2,1,0:T(8,128)(2,1)} %get-tuple-element.202), channel_id=1, source_target_pairs={{0,4},{1,3},{2,6},{3,1},{4,0},{5,7},{6,2},{7,5},{8,12},{9,11},{10,... | collective-permute-start | bytes 4423688 | tf_op jit(solution)/shard_map/ppermute | solution.py:266
  145.1 18.6 %collective-permute-start.42 = (bf16[96,768]{1,0:T(8,128)(2,1)}, bf16[96,768]{1,0:T(8,128)(2,1)}, u32[]{:S(2)}, u32[]{:S(2)}) collective-permute-start(bf16[96,768]{1,0:T(8,128)(2,1)} %get-tuple-element.203), channel_id=1, source_target_pairs={{0,24},{1,25},{2,26},{3,27},{4,28},{5,29},{6,30},{7,31},{8,16},{9,... | collective-permute-start | bytes 442376 | tf_op jit(solution)/shard_map/ppermute | solution.py:266
  147.6 16.1 %collective-permute-start.43 = (bf16[96,768]{1,0:T(8,128)(2,1)}, bf16[96,768]{1,0:T(8,128)(2,1)}, u32[]{:S(2)}, u32[]{:S(2)}) collective-permute-start(bf16[96,768]{1,0:T(8,128)(2,1)} %get-tuple-element.204), channel_id=1, source_target_pairs={{0,16},{1,17},{2,18},{3,19},{4,20},{5,21},{6,22},{7,23},{8,24},{9,... | collective-permute-start | bytes 442376 | tf_op jit(solution)/shard_map/ppermute | solution.py:266
  147.6 16.1 %collective-permute-start.44 = (bf16[96,768]{1,0:T(8,128)(2,1)}, bf16[96,768]{1,0:T(8,128)(2,1)}, u32[]{:S(2)}, u32[]{:S(2)}) collective-permute-start(bf16[96,768]{1,0:T(8,128)(2,1)} %get-tuple-element.205), channel_id=1, source_target_pairs={{0,8},{1,9},{2,10},{3,11},{4,12},{5,13},{6,14},{7,15},{8,0},{9,1},... | collective-permute-start | bytes 442376 | tf_op jit(solution)/shard_map/ppermute | solution.py:266
  166.2 15.4 %collective-permute-start.47 = (bf16[4,48,1920]{2,1,0:T(8,128)(2,1)}, bf16[4,48,1920]{2,1,0:T(8,128)(2,1)}, u32[]{:S(2)}, u32[]{:S(2)}) collective-permute-start(bf16[4,48,1920]{2,1,0:T(8,128)(2,1)} %get-tuple-element.210.refs_5_), channel_id=1, source_target_pairs={{0,2},{1,5},{2,0},{3,7},{4,6},{5,1},{6,4},{7,3},{8,10},{9,13},{10,... | collective-permute-start | bytes 2211848 | tf_op jit(solution)/shard_map/ppermute | solution.py:266
  173.1 14.9 %collective-permute-start.45 = (bf16[8,48,1152]{2,1,0:T(8,128)(2,1)}, bf16[8,48,1152]{2,1,0:T(8,128)(2,1)}, u32[]{:S(2)}, u32[]{:S(2)}) collective-permute-start(bf16[8,48,1152]{2,1,0:T(8,128)(2,1)} %get-tuple-element.213), channel_id=1, source_target_pairs={{0,4},{1,3},{2,6},{3,1},{4,0},{5,7},{6,2},{7,5},{8,12},{9,11},{10,... | collective-permute-start | bytes 2654216 | tf_op jit(solution)/shard_map/ppermute | solution.py:266
  183.7 20.0 %collective-permute-start.52 = (bf16[48,1920]{1,0:T(8,128)(2,1)}, bf16[48,1920]{1,0:T(8,128)(2,1)}, u32[]{:S(2)}, u32[]{:S(2)}) collective-permute-start(bf16[48,1920]{1,0:T(8,128)(2,1)} %get-tuple-element.235), channel_id=1, source_target_pairs={{0,8},{1,9},{2,10},{3,11},{4,12},{5,13},{6,14},{7,15},{8,0},{9,1},... | collective-permute-start | bytes 552968 | tf_op jit(solution)/shard_map/ppermute | solution.py:266
  183.8 23.0 %collective-permute-start.53 = (bf16[48,1920]{1,0:T(8,128)(2,1)}, bf16[48,1920]{1,0:T(8,128)(2,1)}, u32[]{:S(2)}, u32[]{:S(2)}) collective-permute-start(bf16[48,1920]{1,0:T(8,128)(2,1)} %get-tuple-element.236), channel_id=1, source_target_pairs={{0,16},{1,17},{2,18},{3,19},{4,20},{5,21},{6,22},{7,23},{8,24},{9,... | collective-permute-start | bytes 552968 | tf_op jit(solution)/shard_map/ppermute | solution.py:266
  186.7 20.0 %collective-permute-start.54 = (bf16[48,1920]{1,0:T(8,128)(2,1)}, bf16[48,1920]{1,0:T(8,128)(2,1)}, u32[]{:S(2)}, u32[]{:S(2)}) collective-permute-start(bf16[48,1920]{1,0:T(8,128)(2,1)} %get-tuple-element.237), channel_id=1, source_target_pairs={{0,24},{1,25},{2,26},{3,27},{4,28},{5,29},{6,30},{7,31},{8,16},{9,... | collective-permute-start | bytes 552968 | tf_op jit(solution)/shard_map/ppermute | solution.py:266
  200.6 12.5 %collective-permute-start.50 = (bf16[48,1280]{1,0:T(8,128)(2,1)S(1)}, bf16[48,1280]{1,0:T(8,128)(2,1)S(1)}, u32[]{:S(2)}, u32[]{:S(2)}) collective-permute-start(bf16[48,1280]{1,0:T(8,128)(2,1)S(1)} %get-tuple-element.232), channel_id=1, source_target_pairs={{0,16},{1,17},{2,18},{3,19},{4,20},{5,21},{6,22},{7,23},{8,24},{9,... | collective-permute-start | bytes 368648 | tf_op jit(solution)/shard_map/ppermute | solution.py:266
  (40 other events, 221.4 us)

commit v7 on v6

--- a/solution.py
+++ b/solution.py
@@ -1147,7 +1147,7 @@
     @pl.when(step < last)
     def _():
         total = outer_tile(turned, right[...], right_o[...])
-        keep[...] = total[:8]
+        keep[...] = total[:8].astype(BF16)
         away[...] = total[8:].astype(BF16)
 
     @pl.when(step == last)
@@ -1156,7 +1156,7 @@
             copy.wait()
         line_up(info, buffers[0], buffers[1], turned)
         total = outer_tile(turned, buffers[2][...], buffers[3][...])
-        keep[:, :, : attn.shape[1]] = total[:8]
+        keep[:, :, : attn.shape[1]] = total[:8].astype(BF16)
         away[:, :, : attn.shape[1]] = total[8:].astype(BF16)
 
 
@@ -1170,7 +1170,7 @@
     return chain.call(
         outer_up_kernel,
         grid=(n + 1,),
-        out_shape=(shape((8, block, cols), F32), shape((8, block, cols), BF16)),
+        out_shape=(shape((8, block, cols), BF16), shape((8, block, cols), BF16)),
         in_specs=[SMEM] + [full(left.shape)] * 2 + [strip] * 2 + [ANY] * 4,
         out_specs=(out, out),
         scratch_shapes=[pltpu.VMEM((16, block, 2 * rows), BF16)]
@@ -1233,7 +1233,7 @@
     vmem = pl.BlockSpec(memory_space=pltpu.VMEM)
     return chain.call(
         outer_down_kernel,
-        out_shape=(shape((8, block, feat), F32), shape((8, block, feat), BF16)),
+        out_shape=(shape((8, block, feat), BF16), shape((8, block, feat), BF16)),
         in_specs=[SMEM] + [vmem] * 6,
         out_specs=(vmem, vmem),
         scratch_shapes=[pltpu.VMEM((16, block, 2 * rows), BF16)],
@@ -1243,9 +1243,18 @@
     )(info, first, second, first_o, second_o, right, right_o)
 
 
-def add_first_kernel(keep, got, kept, away):
-    kept[...] = keep[:4] + got[:4].astype(F32)
-    away[...] = (keep[4:] + got[4:].astype(F32)).astype(BF16)
+def add_first_kernel(keep, got, kept, away, raw, low, sems):
+    far = pltpu.make_async_copy(got.at[pl.ds(4, 4)], raw.at[1], sems.at[0])
+    near = pltpu.make_async_copy(got.at[pl.ds(0, 4)], raw.at[0], sems.at[1])
+    out = pltpu.make_async_copy(low, away, sems.at[2])
+    far.start()
+    near.start()
+    far.wait()
+    low[...] = (keep[4:].astype(F32) + raw[1].astype(F32)).astype(BF16)
+    out.start()
+    near.wait()
+    kept[...] = keep[:4].astype(F32) + raw[0].astype(F32)
+    out.wait()
 
 
 def shift_first(chain, keep, away, micros=0):
@@ -1254,8 +1263,13 @@
     return chain.call(
         add_first_kernel,
         out_shape=(shape((4, rows, cols), F32), shape((4, rows, cols), BF16)),
-        in_specs=[vmem, vmem],
-        out_specs=(vmem, vmem),
+        in_specs=[vmem, ANY],
+        out_specs=(vmem, ANY),
+        scratch_shapes=[
+            pltpu.VMEM((2, 4, rows, cols), BF16),
+            pltpu.VMEM((4, rows, cols), BF16),
+            pltpu.SemaphoreType.DMA((3,)),
+        ],
         compiler_params=params(12),
         name="shift_first",
         cost_estimate=cost(micros),

time: 221 us -> 219 us (level)
  starting transfers between devices: 56.7 us -> 52.2 us
  waiting for transfers between devices: 35.7 us -> 39.2 us
    ppermute x57, starting transfers between devices: 56.7 us -> 52.2 us  [send(): return lax.ppermute(array, AXES, pairs(move))]
    ppermute x57, waiting for transfers between devices: 35.7 us -> 39.2 us  [send(): return lax.ppermute(array, AXES, pairs(move))]
  transfers between devices with their start and end apart: 57 -> 57, of which waited for: 15 -> 17; matrix products, arithmetic and copies ran while one was open for 1% -> 1% of each run, Pallas kernels for 51% -> 51%
where the time goes in v7:
time: 219 us; the launch traced here: 215 us
  Pallas kernels  112 us (51%)
  starting transfers between devices  52.2 us (24%)
  waiting for transfers between devices  39.2 us (18%)
  local copies, waits for them, and re-layouts  8.25 us (4%)
    pallas_call x36, Pallas kernels, with_token(): *outs, self.token = run(*args, *extra, *([self.token] if held else []))  112 us
    ppermute x57, starting transfers between devices, send(): return lax.ppermute(array, AXES, pairs(move))  52.2 us
    ppermute x57, waiting for transfers between devices, send(): return lax.ppermute(array, AXES, pairs(move))  39.2 us
    unnamed x30, local copies, waits for them, and re-layouts  8.01 us
  transfers between devices with their start and end apart: 57, of which 17 were waited for; matrix products, arithmetic and copies ran while one was open for 1% of the time, Pallas kernels for 51%

profile of v7, /device:TPU:0, one launch (start us, length us, event | category | flops | bytes accessed | tf_op | source)
XLA Modules:
  0.0 214.9 jit_solution(7004734297522086000)
XLA Ops:
  5.2 5.1 %collective-permute-start.1 = (bf16[1,48,1280]{2,1,0:T(8,128)(2,1)S(1)}, bf16[1,48,1280]{2,1,0:T(8,128)(2,1)S(1)}, u32[]{:S(2)}, u32[]{:S(2)}) collective-permute-start(bf16[1,48,1280]{2,1,0:T(8,128)(2,1)S(1)} %get-tuple-element.133.refs_0_), channel_id=1, source_target_pairs={{0,24},{1,25},{2,26},{3,27},{4,28},{5,29},{6,30},{7,31},{8,16},{9,... | collective-permute-start | bytes 368648 | tf_op jit(solution)/shard_map/ppermute | solution.py:266
  14.6 6.3 %collective-permute-done.2.refs_2_ = bf16[1,48,1280]{2,1,0:T(8,128)(2,1)S(1)} collective-permute-done((bf16[1,48,1280]{2,1,0:T(8,128)(2,1)S(1)}, bf16[1,48,1280]{2,1,0:T(8,128)(2,1)S(1)}, u32[]{:S(2)}, u32[]{:S(2)}) %collective-permute-start.2) | collective-permute-done | bytes 122912 | tf_op jit(solution)/shard_map/ppermute | solution.py:266
  23.2 3.0 %collective-permute-start.9 = (bf16[1,48,1920]{2,1,0:T(8,128)(2,1)S(1)}, bf16[1,48,1920]{2,1,0:T(8,128)(2,1)S(1)}, u32[]{:S(2)}, u32[]{:S(2)}) collective-permute-start(bf16[1,48,1920]{2,1,0:T(8,128)(2,1)S(1)} %get-tuple-element.140.refs_0_), channel_id=1, source_target_pairs={{0,16},{1,17},{2,18},{3,19},{4,20},{5,21},{6,22},{7,23},{8,24},{9,... | collective-permute-start | bytes 552968 | tf_op jit(solution)/shard_map/ppermute | solution.py:266
  29.1 3.9 %collective-permute-done.6.refs_0_ = bf16[4,48,1280]{2,1,0:T(8,128)(2,1)} collective-permute-done((bf16[4,48,1280]{2,1,0:T(8,128)(2,1)}, bf16[4,48,1280]{2,1,0:T(8,128)(2,1)}, u32[]{:S(2)}, u32[]{:S(2)}) %collective-permute-start.6) | collective-permute-done | bytes 491552 | tf_op jit(solution)/shard_map/ppermute | solution.py:266
  33.0 2.6 %collective-permute-start.11 = (bf16[4,48,1280]{2,1,0:T(8,128)(2,1)}, bf16[4,48,1280]{2,1,0:T(8,128)(2,1)}, u32[]{:S(2)}, u32[]{:S(2)}) collective-permute-start(bf16[4,48,1280]{2,1,0:T(8,128)(2,1)} %get-tuple-element.139.refs_5_), channel_id=1, source_target_pairs={{0,4},{1,3},{2,6},{3,1},{4,0},{5,7},{6,2},{7,5},{8,12},{9,11},{10,... | collective-permute-start | bytes 1474568 | tf_op jit(solution)/shard_map/ppermute | solution.py:266
  35.6 4.1 %collective-permute-done.9.refs_2_ = bf16[1,48,1920]{2,1,0:T(8,128)(2,1)S(1)} collective-permute-done((bf16[1,48,1920]{2,1,0:T(8,128)(2,1)S(1)}, bf16[1,48,1920]{2,1,0:T(8,128)(2,1)S(1)}, u32[]{:S(2)}, u32[]{:S(2)}) %collective-permute-start.9) | collective-permute-done | bytes 184352 | tf_op jit(solution)/shard_map/ppermute | solution.py:266
  46.3 6.7 %enter.1 = (bf16[2,16,48,1280]{3,2,1,0:T(8,128)(2,1)S(1)}, f32[8,768]{1,0:T(8,128)S(1)}, f32[1,3072]{1,0:T(1,128)S(1)}, bf16[16,48,512]{2,1,0:T(8,128)(2,1)}, bf...) custom-call(s32[66]{0:T(128)S(1)} %stack.239.refs_0_, ...), custom_call_target="tpu_custom_call", output_to_operand_aliasing={{7}: (12, {})} | custom-call | flops 240000008192 | bytes 1 | tf_op jit(solution)/shard_map/enter/pallas_call | solution.py:345
  53.6 2.5 %collective-permute-start.24 = (bf16[1,96,768]{2,1,0:T(8,128)(2,1)}, bf16[1,96,768]{2,1,0:T(8,128)(2,1)}, u32[]{:S(2)}, u32[]{:S(2)}) collective-permute-start(bf16[1,96,768]{2,1,0:T(8,128)(2,1)} %get-tuple-element.154.refs_0_), channel_id=1, source_target_pairs={{0,16},{1,17},{2,18},{3,19},{4,20},{5,21},{6,22},{7,23},{8,24},{9,... | collective-permute-start | bytes 442376 | tf_op jit(solution)/shard_map/ppermute | solution.py:266
  57.4 3.6 %collective-permute-done.16.refs_0_ = bf16[4,48,1920]{2,1,0:T(8,128)(2,1)} collective-permute-done((bf16[4,48,1920]{2,1,0:T(8,128)(2,1)}, bf16[4,48,1920]{2,1,0:T(8,128)(2,1)}, u32[]{:S(2)}, u32[]{:S(2)}) %collective-permute-start.16) | collective-permute-done | bytes 737312 | tf_op jit(solution)/shard_map/ppermute | solution.py:266
  61.1 2.9 %collective-permute-start.18 = (bf16[4,48,1920]{2,1,0:T(8,128)(2,1)}, bf16[4,48,1920]{2,1,0:T(8,128)(2,1)}, u32[]{:S(2)}, u32[]{:S(2)}) collective-permute-start(bf16[4,48,1920]{2,1,0:T(8,128)(2,1)} %get-tuple-element.153.refs_5_.refs_4_), channel_id=1, source_target_pairs={{0,4},{1,3},{2,6},{3,1},{4,0},{5,7},{6,2},{7,5},{8,12},{9,11},{10,... | collective-permute-start | bytes 2211848 | tf_op jit(solution)/shard_map/ppermute | solution.py:266
  64.0 7.0 %mix.1 = (bf16[512,768]{1,0:T(8,128)(2,1)S(1)}, bf16[768,512]{1,0:T(8,128)(2,1)}, f32[6,8,512]{2,1,0:T(8,128)S(1)}, f32[8,128]{1,0:T(8,128)S(1)}) custom-call(s32[66]{0:T(128)S(1)} %stack.239.refs_0_, bf16[2,512,1152]{2,1,0:T(8,128)(2,1)S(1)} %get-tuple-element.147.refs_1_.refs_2_.refs_3_, ...), custom_call_target="tpu_custom_call", output_to_operand_aliasing={{3}: (4, {})} | custom-call | flops 299999985664 | bytes 1 | tf_op jit(solution)/shard_map/mix/pallas_call | solution.py:345
  73.7 2.1 gather.6
  77.8 4.5 %rise.1 = (bf16[2,16,48,384]{3,2,1,0:T(8,128)(2,1)S(1)}, f32[512,768]{1,0:T(8,128)S(1)}, bf16[512,768]{1,0:T(8,128)(2,1)S(1)}, bf16[16,48,512]{2,1,0:T(8,128)(2,1)}, f32[8,128]{1,0:T(8,128)S(1)}) custom-call(s32[66]{0:T(128)S(1)} %stack.239.refs_0_, bf16[512,768]{1,0:T(8,128)(2,1)S(1)} %copy-done.5, ...), custom_call_target="tpu_custom_call", output_to_operand_aliasing={{4}: (12, {})} | custom-call | flops 149999992832 | bytes 1 | tf_op jit(solution)/shard_map/rise/pallas_call | solution.py:345
  82.3 7.5 %widen.2 = (bf16[16,48,1536]{2,1,0:T(8,128)(2,1)S(1)}, bf16[512,1536]{1,0:T(8,128)(2,1)S(1)}, bf16[512,1536]{1,0:T(8,128)(2,1)S(1)}, bf16[8,96,512]{2,1,0:T(8,12...) custom-call(s32[66]{0:T(128)S(1)} %stack.239.refs_0_, ...), custom_call_target="tpu_custom_call", output_to_operand_aliasing={{5}: (7, {})} | custom-call | flops 539999993856 | bytes 1 | tf_op jit(solution)/shard_map/widen/pallas_call | solution.py:345
  90.9 2.3 %gather.7 = (bf16[8,96,768]{2,1,0:T(8,128)(2,1)}, f32[8,128]{1,0:T(8,128)S(1)}) custom-call(bf16[4,96,768]{2,1,0:T(8,128)(2,1)} %get-tuple-element.162.refs_0_, bf16[4,96,768]{2,1,0:T(8,128)(2,1)} %collective-permute-done.26.refs_1_, f32[8,128]{1,0:T(8,128)S(1)} %get-tuple-element.163.refs_2_), custom_call_target="tpu_custom_call", output_to_operand_aliasing={{1}: (2, {})} | custom-call | bytes 1 | tf_op jit(solution)/shard_map/gather/pallas_call | solution.py:345
  94.8 7.0 %widen.3 = (bf16[16,48,1536]{2,1,0:T(8,128)(2,1)S(1)}, bf16[512,1536]{1,0:T(8,128)(2,1)S(1)}, bf16[512,1536]{1,0:T(8,128)(2,1)S(1)}, bf16[8,96,512]{2,1,0:T(8,12...) custom-call(s32[66]{0:T(128)S(1)} %stack.239.refs_0_, ...), custom_call_target="tpu_custom_call", output_to_operand_aliasing={{5}: (7, {})} | custom-call | flops 539999993856 | bytes 1 | tf_op jit(solution)/shard_map/widen/pallas_call | solution.py:345
  103.5 3.0 %collective-permute-done.29.refs_4_ = bf16[8,96,512]{2,1,0:T(8,128)(2,1)S(1)} collective-permute-done((bf16[8,96,512]{2,1,0:T(8,128)(2,1)S(1)}, bf16[8,96,512]{2,1,0:T(8,128)(2,1)S(1)}, u32[]{:S(2)}, u32[]{:S(2)}) %collective-permute-start.29) | collective-permute-done | bytes 786464 | tf_op jit(solution)/shard_map/ppermute | solution.py:266
  106.5 4.7 %outer_down.1 = (bf16[8,96,768]{2,1,0:T(8,128)(2,1)S(1)}, bf16[8,96,768]{2,1,0:T(8,128)(2,1)}, f32[8,128]{1,0:T(8,128)S(1)}) custom-call(s32[66]{0:T(128)S(1)} %stack.239.refs_0_, bf16[8,96,512]{2,1,0:T(8,128)(2,1)S(1)} %get-tuple-element.173.refs_1_, bf16[8,96,512]{2,1,0:T(8,128)(2,1)S(1)} %get-tuple-element.174.refs_2_, ...), custom_call_target="tpu_custom_call", output_to_operand_aliasing={{2}: (7, {})} | custom-call | bytes 1 | tf_op jit(solution)/shard_map/outer_down/pallas_call | solution.py:345
  114.6 14.1 %fall.1 = (bf16[16,2,96,768]{3,2,1,0:T(8,128)(2,1)}, bf16[512,1536]{1,0:T(8,128)(2,1)}, bf16[512,1536]{1,0:T(8,128)(2,1)S(1)}, f32[1,3072]{1,0:T(1,128)S(1)}, f3...) custom-call(s32[66]{0:T(128)S(1)} %stack.239.refs_0_, ...), custom_call_target="tpu_custom_call", output_to_operand_aliasing={{9}: (13, {})} | custom-call | flops 539999993856 | bytes 1 | tf_op jit(solution)/shard_map/fall/pallas_call | solution.py:345
  129.3 2.0 shift_first.2
  133.1 6.9 %outer_up.1 = (bf16[8,48,1920]{2,1,0:T(8,128)(2,1)S(1)}, bf16[8,48,1920]{2,1,0:T(8,128)(2,1)}, f32[8,128]{1,0:T(8,128)S(1)}) custom-call(s32[66]{0:T(128)S(1)} %stack.239.refs_0_, bf16[16,48,512]{2,1,0:T(8,128)(2,1)} %get-tuple-element.190.refs_1_, bf16[16,48,512]{2,1,0:T(8,128)(2,1)} %collective-permute-done.36.refs_2_, ...), custom_call_target="tpu_custom_call", output_to_operand_aliasing={{2}: (9, {})} | custom-call | flops 240000008192 | bytes 1 | tf_op jit(solution)/shard_map/outer_up/pallas_call | solution.py:345
  143.6 2.5 %collective-permute-start.42 = (bf16[96,768]{1,0:T(8,128)(2,1)}, bf16[96,768]{1,0:T(8,128)(2,1)}, u32[]{:S(2)}, u32[]{:S(2)}) collective-permute-start(bf16[96,768]{1,0:T(8,128)(2,1)} %get-tuple-element.203), channel_id=1, source_target_pairs={{0,24},{1,25},{2,26},{3,27},{4,28},{5,29},{6,30},{7,31},{8,16},{9,... | collective-permute-start | bytes 442376 | tf_op jit(solution)/shard_map/ppermute | solution.py:266
  149.6 12.5 %mix_back.1 = (bf16[3,512,384]{2,1,0:T(8,128)(2,1)}, bf16[3,512,384]{2,1,0:T(8,128)(2,1)S(1)}, f32[8,128]{1,0:T(8,128)S(1)}) custom-call(s32[66]{0:T(128)S(1)} %stack.239.refs_0_, bf16[2,512,1152]{2,1,0:T(8,128)(2,1)S(1)} %copy-done.10, bf16[2,512,1152]{2,1,0:T(8,128)(2,1)S(1)} %copy-done.10, ...), custom_call_target="tpu_custom_call", output_to_operand_aliasing={{2}: (6, {})} | custom-call | flops 480000016384 | bytes 1 | tf_op jit(solution)/shard_map/mix_back/pallas_call | solution.py:345
  162.2 2.2 %shift_first.3 = (f32[4,48,1920]{2,1,0:T(8,128)S(1)}, bf16[4,48,1920]{2,1,0:T(8,128)(2,1)}, f32[8,128]{1,0:T(8,128)S(1)}) custom-call(bf16[8,48,1920]{2,1,0:T(8,128)(2,1)S(1)} %get-tuple-element.201.refs_0_, bf16[8,48,1920]{2,1,0:T(8,128)(2,1)} %collective-permute-done.41.refs_1_, ...), custom_call_target="tpu_custom_call", output_to_operand_aliasing={{2}: (2, {})} | custom-call | flops 149999992832 | bytes 1 | tf_op jit(solution)/shard_map/shift_first/pallas_call | solution.py:345
  165.3 5.4 %outer_qkv.1 = (f32[8,48,1152]{2,1,0:T(8,128)S(1)}, bf16[8,48,1152]{2,1,0:T(8,128)(2,1)}, f32[8,128]{1,0:T(8,128)S(1)}) custom-call(s32[66]{0:T(128)S(1)} %stack.239.refs_0_, bf16[16,48,512]{2,1,0:T(8,128)(2,1)} %get-tuple-element.182.refs_1_, bf16[16,48,512]{2,1,0:T(8,128)(2,1)} %collective-permute-done.33.refs_2_, ...), custom_call_target="tpu_custom_call", output_to_operand_aliasing={{2}: (6, {})} | custom-call | flops 240000008192 | bytes 1 | tf_op jit(solution)/shard_map/outer_qkv/pallas_call | solution.py:345
  171.9 6.4 %exit_back.1 = (bf16[512,768]{1,0:T(8,128)(2,1)}, f32[8,48,128]{2,1,0:T(8,128)S(1)}, bf16[8,48,128]{2,1,0:T(8,128)(2,1)S(1)}, f32[8,128]{1,0:T(8,128)S(1)}) custom-call(s32[66]{0:T(128)S(1)} %stack.239.refs_0_, bf16[512,768]{1,0:T(8,128)(2,1)S(1)} %copy-done.6, ...), custom_call_target="tpu_custom_call", output_to_operand_aliasing={{3}: (9, {})} | custom-call | flops 240000008192 | bytes 1 | tf_op jit(solution)/shard_map/exit_back/pallas_call | solution.py:345
  179.2 2.1 shift_second.4
  181.4 2.9 %collective-permute-start.53 = (bf16[48,1920]{1,0:T(8,128)(2,1)}, bf16[48,1920]{1,0:T(8,128)(2,1)}, u32[]{:S(2)}, u32[]{:S(2)}) collective-permute-start(bf16[48,1920]{1,0:T(8,128)(2,1)} %get-tuple-element.236), channel_id=1, source_target_pairs={{0,16},{1,17},{2,18},{3,19},{4,20},{5,21},{6,22},{7,23},{8,24},{9,... | collective-permute-start | bytes 552968 | tf_op jit(solution)/shard_map/ppermute | solution.py:266
  186.2 2.2 %shift_both.1 = (f32[4,48,1280]{2,1,0:T(8,128)S(1)}, bf16[4,48,1280]{2,1,0:T(8,128)(2,1)}, f32[8,128]{1,0:T(8,128)S(1)}) custom-call(f32[8,48,1152]{2,1,0:T(8,128)S(1)} %get-tuple-element.212.refs_0_, bf16[8,48,1152]{2,1,0:T(8,128)(2,1)} %collective-permute-done.45.refs_1_, ...), custom_call_target="tpu_custom_call", output_to_operand_aliasing={{2}: (4, {})} | custom-call | bytes 1 | tf_op jit(solution)/shard_map/shift_both/pallas_call | solution.py:345
  190.4 5.2 %leave.1 = (bf16[512,768]{1,0:T(8,128)(2,1)}, f32[8,128]{1,0:T(8,128)S(1)}) custom-call(s32[66]{0:T(128)S(1)} %stack.239.refs_0_, f32[512,768]{1,0:T(8,128)S(1)} %get-tuple-element.157.refs_6_.refs_1_, bf16[512,1536]{1,0:T(8,128)(2,1)S(1)} %get-tuple-element.161.refs_2_, bf16[512,1536]{1,0:T(8,128)(2,1)S(1)} %copy-done.12, ...), custom_call_target="tpu_custom_call", output_to_operand_aliasing={{1}: (6, {})} | custom-call | flops 210000003072 | bytes 1 | tf_op jit(solution)/shard_map/leave/pallas_call | solution.py:345
  198.8 2.9 %collective-permute-start.50 = (bf16[48,1280]{1,0:T(8,128)(2,1)S(1)}, bf16[48,1280]{1,0:T(8,128)(2,1)S(1)}, u32[]{:S(2)}, u32[]{:S(2)}) collective-permute-start(bf16[48,1280]{1,0:T(8,128)(2,1)S(1)} %get-tuple-element.232), channel_id=1, source_target_pairs={{0,16},{1,17},{2,18},{3,19},{4,20},{5,21},{6,22},{7,23},{8,24},{9,... | collective-permute-start | bytes 368648 | tf_op jit(solution)/shard_map/ppermute | solution.py:266
  206.2 4.9 %collective-permute-done.50.refs_3_ = bf16[48,1280]{1,0:T(8,128)(2,1)S(1)} collective-permute-done((bf16[48,1280]{1,0:T(8,128)(2,1)S(1)}, bf16[48,1280]{1,0:T(8,128)(2,1)S(1)}, u32[]{:S(2)}, u32[]{:S(2)}) %collective-permute-start.50) | collective-permute-done | bytes 122912 | tf_op jit(solution)/shard_map/ppermute | solution.py:266
  (152 shorter events, 61.8 us)
Async XLA Ops:
  1.2 11.2 %collective-permute-start.4 = (bf16[24,3072]{1,0:T(8,128)(2,1)}, bf16[24,3072]{1,0:T(8,128)(2,1)S(1)}, u32[]{:S(2)}, u32[]{:S(2)}) collective-permute-start(bf16[24,3072]{1,0:T(8,128)(2,1)} %refs_1_.6), channel_id=1, source_target_pairs={{0,1},{1,0},{2,3},{3,2},{4,5},{5,4},{6,7},{7,6},{8,9},{9,8},{10,11... | collective-permute-start | bytes 442376 | tf_op jit(solution)/shard_map/ppermute | solution.py:266
  10.3 10.6 %collective-permute-start.2 = (bf16[1,48,1280]{2,1,0:T(8,128)(2,1)S(1)}, bf16[1,48,1280]{2,1,0:T(8,128)(2,1)S(1)}, u32[]{:S(2)}, u32[]{:S(2)}) collective-permute-start(bf16[1,48,1280]{2,1,0:T(8,128)(2,1)S(1)} %get-tuple-element.133.refs_0_), channel_id=1, source_target_pairs={{0,16},{1,17},{2,18},{3,19},{4,20},{5,21},{6,22},{7,23},{8,24},{9,... | collective-permute-start | bytes 368648 | tf_op jit(solution)/shard_map/ppermute | solution.py:266
  10.3 10.6 %collective-permute-start.3 = (bf16[1,48,1280]{2,1,0:T(8,128)(2,1)S(1)}, bf16[1,48,1280]{2,1,0:T(8,128)(2,1)S(1)}, u32[]{:S(2)}, u32[]{:S(2)}) collective-permute-start(bf16[1,48,1280]{2,1,0:T(8,128)(2,1)S(1)} %get-tuple-element.133.refs_0_), channel_id=1, source_target_pairs={{0,8},{1,9},{2,10},{3,11},{4,12},{5,13},{6,14},{7,15},{8,0},{9,1},... | collective-permute-start | bytes 368648 | tf_op jit(solution)/shard_map/ppermute | solution.py:266
  21.7 11.3 %collective-permute-start.6 = (bf16[4,48,1280]{2,1,0:T(8,128)(2,1)}, bf16[4,48,1280]{2,1,0:T(8,128)(2,1)}, u32[]{:S(2)}, u32[]{:S(2)}) collective-permute-start(bf16[4,48,1280]{2,1,0:T(8,128)(2,1)} %get-tuple-element.137.refs_4_), channel_id=1, source_target_pairs={{0,2},{1,5},{2,0},{3,7},{4,6},{5,1},{6,4},{7,3},{8,10},{9,13},{10,... | collective-permute-start | bytes 1474568 | tf_op jit(solution)/shard_map/ppermute | solution.py:266
  23.2 16.4 %collective-permute-start.9 = (bf16[1,48,1920]{2,1,0:T(8,128)(2,1)S(1)}, bf16[1,48,1920]{2,1,0:T(8,128)(2,1)S(1)}, u32[]{:S(2)}, u32[]{:S(2)}) collective-permute-start(bf16[1,48,1920]{2,1,0:T(8,128)(2,1)S(1)} %get-tuple-element.140.refs_0_), channel_id=1, source_target_pairs={{0,16},{1,17},{2,18},{3,19},{4,20},{5,21},{6,22},{7,23},{8,24},{9,... | collective-permute-start | bytes 552968 | tf_op jit(solution)/shard_map/ppermute | solution.py:266
  26.3 13.4 %collective-permute-start.10 = (bf16[1,48,1920]{2,1,0:T(8,128)(2,1)S(1)}, bf16[1,48,1920]{2,1,0:T(8,128)(2,1)S(1)}, u32[]{:S(2)}, u32[]{:S(2)}) collective-permute-start(bf16[1,48,1920]{2,1,0:T(8,128)(2,1)S(1)} %get-tuple-element.140.refs_0_), channel_id=1, source_target_pairs={{0,24},{1,25},{2,26},{3,27},{4,28},{5,29},{6,30},{7,31},{8,16},{9,... | collective-permute-start | bytes 552968 | tf_op jit(solution)/shard_map/ppermute | solution.py:266
  27.6 13.0 %collective-permute-start.7 = (bf16[4,48,1280]{2,1,0:T(8,128)(2,1)}, bf16[4,48,1280]{2,1,0:T(8,128)(2,1)}, u32[]{:S(2)}, u32[]{:S(2)}) collective-permute-start(bf16[4,48,1280]{2,1,0:T(8,128)(2,1)} %get-tuple-element.137.refs_4_), channel_id=1, source_target_pairs={{0,4},{1,3},{2,6},{3,1},{4,0},{5,7},{6,2},{7,5},{8,12},{9,11},{10,... | collective-permute-start | bytes 1474568 | tf_op jit(solution)/shard_map/ppermute | solution.py:266
  33.0 11.2 %collective-permute-start.12 = (bf16[4,48,1280]{2,1,0:T(8,128)(2,1)}, bf16[4,48,1280]{2,1,0:T(8,128)(2,1)}, u32[]{:S(2)}, u32[]{:S(2)}) collective-permute-start(bf16[4,48,1280]{2,1,0:T(8,128)(2,1)} %get-tuple-element.137.refs_4_), channel_id=1, source_target_pairs={{0,1},{1,0},{2,3},{3,2},{4,5},{5,4},{6,7},{7,6},{8,9},{9,8},{10,11... | collective-permute-start | bytes 1474568 | tf_op jit(solution)/shard_map/ppermute | solution.py:266
  42.7 18.4 %collective-permute-start.16 = (bf16[4,48,1920]{2,1,0:T(8,128)(2,1)}, bf16[4,48,1920]{2,1,0:T(8,128)(2,1)}, u32[]{:S(2)}, u32[]{:S(2)}) collective-permute-start(bf16[4,48,1920]{2,1,0:T(8,128)(2,1)} %get-tuple-element.148.refs_4_.refs_3_), channel_id=1, source_target_pairs={{0,2},{1,5},{2,0},{3,7},{4,6},{5,1},{6,4},{7,3},{8,10},{9,13},{10,... | collective-permute-start | bytes 2211848 | tf_op jit(solution)/shard_map/ppermute | solution.py:266
  44.2 26.7 %collective-permute-start.17 = (bf16[4,48,1920]{2,1,0:T(8,128)(2,1)}, bf16[4,48,1920]{2,1,0:T(8,128)(2,1)}, u32[]{:S(2)}, u32[]{:S(2)}) collective-permute-start(bf16[4,48,1920]{2,1,0:T(8,128)(2,1)} %get-tuple-element.148.refs_4_.refs_3_), channel_id=1, source_target_pairs={{0,4},{1,3},{2,6},{3,1},{4,0},{5,7},{6,2},{7,5},{8,12},{9,11},{10,... | collective-permute-start | bytes 2211848 | tf_op jit(solution)/shard_map/ppermute | solution.py:266
  53.0 18.0 %collective-permute-start.23 = (bf16[1,96,768]{2,1,0:T(8,128)(2,1)}, bf16[1,96,768]{2,1,0:T(8,128)(2,1)}, u32[]{:S(2)}, u32[]{:S(2)}) collective-permute-start(bf16[1,96,768]{2,1,0:T(8,128)(2,1)} %get-tuple-element.154.refs_0_), channel_id=1, source_target_pairs={{0,8},{1,9},{2,10},{3,11},{4,12},{5,13},{6,14},{7,15},{8,0},{9,1},... | collective-permute-start | bytes 442376 | tf_op jit(solution)/shard_map/ppermute | solution.py:266
  53.6 17.9 %collective-permute-start.24 = (bf16[1,96,768]{2,1,0:T(8,128)(2,1)}, bf16[1,96,768]{2,1,0:T(8,128)(2,1)}, u32[]{:S(2)}, u32[]{:S(2)}) collective-permute-start(bf16[1,96,768]{2,1,0:T(8,128)(2,1)} %get-tuple-element.154.refs_0_), channel_id=1, source_target_pairs={{0,16},{1,17},{2,18},{3,19},{4,20},{5,21},{6,22},{7,23},{8,24},{9,... | collective-permute-start | bytes 442376 | tf_op jit(solution)/shard_map/ppermute | solution.py:266
  56.1 15.4 %collective-permute-start.25 = (bf16[1,96,768]{2,1,0:T(8,128)(2,1)}, bf16[1,96,768]{2,1,0:T(8,128)(2,1)}, u32[]{:S(2)}, u32[]{:S(2)}) collective-permute-start(bf16[1,96,768]{2,1,0:T(8,128)(2,1)} %get-tuple-element.154.refs_0_), channel_id=1, source_target_pairs={{0,24},{1,25},{2,26},{3,27},{4,28},{5,29},{6,30},{7,31},{8,16},{9,... | collective-permute-start | bytes 442376 | tf_op jit(solution)/shard_map/ppermute | solution.py:266
  61.1 12.6 %collective-permute-start.18 = (bf16[4,48,1920]{2,1,0:T(8,128)(2,1)}, bf16[4,48,1920]{2,1,0:T(8,128)(2,1)}, u32[]{:S(2)}, u32[]{:S(2)}) collective-permute-start(bf16[4,48,1920]{2,1,0:T(8,128)(2,1)} %get-tuple-element.153.refs_5_.refs_4_), channel_id=1, source_target_pairs={{0,4},{1,3},{2,6},{3,1},{4,0},{5,7},{6,2},{7,5},{8,12},{9,11},{10,... | collective-permute-start | bytes 2211848 | tf_op jit(solution)/shard_map/ppermute | solution.py:266
  71.6 32.0 %collective-permute-start.30 = (bf16[512,768]{1,0:T(8,128)(2,1)}, bf16[512,768]{1,0:T(8,128)(2,1)}, u32[]{:S(2)}, u32[]{:S(2)}) collective-permute-start(bf16[512,768]{1,0:T(8,128)(2,1)} %get-tuple-element.166.refs_5_.refs_1_), channel_id=1, source_target_pairs={{0,1},{1,0},{2,3},{3,2},{4,5},{5,4},{6,7},{7,6},{8,9},{9,8},{10,11... | collective-permute-start | bytes 2359304 | tf_op jit(solution)/shard_map/ppermute | solution.py:266
  75.8 15.2 %collective-permute-start.26 = (bf16[4,96,768]{2,1,0:T(8,128)(2,1)}, bf16[4,96,768]{2,1,0:T(8,128)(2,1)}, u32[]{:S(2)}, u32[]{:S(2)}) collective-permute-start(bf16[4,96,768]{2,1,0:T(8,128)(2,1)} %get-tuple-element.162.refs_0_), channel_id=1, source_target_pairs={{0,2},{1,5},{2,0},{3,7},{4,6},{5,1},{6,4},{7,3},{8,10},{9,13},{10,... | collective-permute-start | bytes 1769480 | tf_op jit(solution)/shard_map/ppermute | solution.py:266
  93.3 18.0 %collective-permute-start.27 = (bf16[8,96,768]{2,1,0:T(8,128)(2,1)}, bf16[8,96,768]{2,1,0:T(8,128)(2,1)}, u32[]{:S(2)}, u32[]{:S(2)}) collective-permute-start(bf16[8,96,768]{2,1,0:T(8,128)(2,1)} %get-tuple-element.172.refs_9_), channel_id=1, source_target_pairs={{0,4},{1,3},{2,6},{3,1},{4,0},{5,7},{6,2},{7,5},{8,12},{9,11},{10,... | collective-permute-start | bytes 3538952 | tf_op jit(solution)/shard_map/ppermute | solution.py:266
  111.6 53.4 %collective-permute-start.33 = (bf16[16,48,512]{2,1,0:T(8,128)(2,1)}, bf16[16,48,512]{2,1,0:T(8,128)(2,1)}, u32[]{:S(2)}, u32[]{:S(2)}) collective-permute-start(bf16[16,48,512]{2,1,0:T(8,128)(2,1)} %get-tuple-element.182.refs_1_), channel_id=1, source_target_pairs={{0,1},{1,0},{2,3},{3,2},{4,5},{5,4},{6,7},{7,6},{8,9},{9,8},{10,11... | collective-permute-start | bytes 2359304 | tf_op jit(solution)/shard_map/ppermute | solution.py:266
  111.8 19.6 %collective-permute-start.38 = (bf16[16,48,512]{2,1,0:T(8,128)(2,1)}, bf16[16,48,512]{2,1,0:T(8,128)(2,1)}, u32[]{:S(2)}, u32[]{:S(2)}) collective-permute-start(bf16[16,48,512]{2,1,0:T(8,128)(2,1)} %bitcast.62.refs_5_), channel_id=1, source_target_pairs={{0,1},{1,0},{2,3},{3,2},{4,5},{5,4},{6,7},{7,6},{8,9},{9,8},{10,11... | collective-permute-start | bytes 2359304 | tf_op jit(solution)/shard_map/ppermute | solution.py:266
  112.1 19.9 %collective-permute-start.36 = (bf16[16,48,512]{2,1,0:T(8,128)(2,1)}, bf16[16,48,512]{2,1,0:T(8,128)(2,1)}, u32[]{:S(2)}, u32[]{:S(2)}) collective-permute-start(bf16[16,48,512]{2,1,0:T(8,128)(2,1)} %get-tuple-element.190.refs_1_), channel_id=1, source_target_pairs={{0,1},{1,0},{2,3},{3,2},{4,5},{5,4},{6,7},{7,6},{8,9},{9,8},{10,11... | collective-permute-start | bytes 2359304 | tf_op jit(solution)/shard_map/ppermute | solution.py:266
  112.3 16.9 %collective-permute-start.34 = (bf16[8,96,768]{2,1,0:T(8,128)(2,1)}, bf16[8,96,768]{2,1,0:T(8,128)(2,1)}, u32[]{:S(2)}, u32[]{:S(2)}) collective-permute-start(bf16[8,96,768]{2,1,0:T(8,128)(2,1)} %get-tuple-element.186), channel_id=1, source_target_pairs={{0,4},{1,3},{2,6},{3,1},{4,0},{5,7},{6,2},{7,5},{8,12},{9,11},{10,... | collective-permute-start | bytes 3538952 | tf_op jit(solution)/shard_map/ppermute | solution.py:266
  131.4 10.3 %collective-permute-start.35 = (bf16[4,96,768]{2,1,0:T(8,128)(2,1)}, bf16[4,96,768]{2,1,0:T(8,128)(2,1)}, u32[]{:S(2)}, u32[]{:S(2)}) collective-permute-start(bf16[4,96,768]{2,1,0:T(8,128)(2,1)} %get-tuple-element.189), channel_id=1, source_target_pairs={{0,2},{1,5},{2,0},{3,7},{4,6},{5,1},{6,4},{7,3},{8,10},{9,13},{10,... | collective-permute-start | bytes 1769480 | tf_op jit(solution)/shard_map/ppermute | solution.py:266
  140.1 22.1 %collective-permute-start.41 = (bf16[8,48,1920]{2,1,0:T(8,128)(2,1)}, bf16[8,48,1920]{2,1,0:T(8,128)(2,1)}, u32[]{:S(2)}, u32[]{:S(2)}) collective-permute-start(bf16[8,48,1920]{2,1,0:T(8,128)(2,1)} %get-tuple-element.202), channel_id=1, source_target_pairs={{0,4},{1,3},{2,6},{3,1},{4,0},{5,7},{6,2},{7,5},{8,12},{9,11},{10,... | collective-permute-start | bytes 4423688 | tf_op jit(solution)/shard_map/ppermute | solution.py:266
  143.6 18.6 %collective-permute-start.42 = (bf16[96,768]{1,0:T(8,128)(2,1)}, bf16[96,768]{1,0:T(8,128)(2,1)}, u32[]{:S(2)}, u32[]{:S(2)}) collective-permute-start(bf16[96,768]{1,0:T(8,128)(2,1)} %get-tuple-element.203), channel_id=1, source_target_pairs={{0,24},{1,25},{2,26},{3,27},{4,28},{5,29},{6,30},{7,31},{8,16},{9,... | collective-permute-start | bytes 442376 | tf_op jit(solution)/shard_map/ppermute | solution.py:266
  146.1 16.1 %collective-permute-start.43 = (bf16[96,768]{1,0:T(8,128)(2,1)}, bf16[96,768]{1,0:T(8,128)(2,1)}, u32[]{:S(2)}, u32[]{:S(2)}) collective-permute-start(bf16[96,768]{1,0:T(8,128)(2,1)} %get-tuple-element.204), channel_id=1, source_target_pairs={{0,16},{1,17},{2,18},{3,19},{4,20},{5,21},{6,22},{7,23},{8,24},{9,... | collective-permute-start | bytes 442376 | tf_op jit(solution)/shard_map/ppermute | solution.py:266
  146.1 16.0 %collective-permute-start.44 = (bf16[96,768]{1,0:T(8,128)(2,1)}, bf16[96,768]{1,0:T(8,128)(2,1)}, u32[]{:S(2)}, u32[]{:S(2)}) collective-permute-start(bf16[96,768]{1,0:T(8,128)(2,1)} %get-tuple-element.205), channel_id=1, source_target_pairs={{0,8},{1,9},{2,10},{3,11},{4,12},{5,13},{6,14},{7,15},{8,0},{9,1},... | collective-permute-start | bytes 442376 | tf_op jit(solution)/shard_map/ppermute | solution.py:266
  164.4 14.8 %collective-permute-start.47 = (bf16[4,48,1920]{2,1,0:T(8,128)(2,1)}, bf16[4,48,1920]{2,1,0:T(8,128)(2,1)}, u32[]{:S(2)}, u32[]{:S(2)}) collective-permute-start(bf16[4,48,1920]{2,1,0:T(8,128)(2,1)} %get-tuple-element.210.refs_5_), channel_id=1, source_target_pairs={{0,2},{1,5},{2,0},{3,7},{4,6},{5,1},{6,4},{7,3},{8,10},{9,13},{10,... | collective-permute-start | bytes 2211848 | tf_op jit(solution)/shard_map/ppermute | solution.py:266
  170.7 15.4 %collective-permute-start.45 = (bf16[8,48,1152]{2,1,0:T(8,128)(2,1)}, bf16[8,48,1152]{2,1,0:T(8,128)(2,1)}, u32[]{:S(2)}, u32[]{:S(2)}) collective-permute-start(bf16[8,48,1152]{2,1,0:T(8,128)(2,1)} %get-tuple-element.213), channel_id=1, source_target_pairs={{0,4},{1,3},{2,6},{3,1},{4,0},{5,7},{6,2},{7,5},{8,12},{9,11},{10,... | collective-permute-start | bytes 2654216 | tf_op jit(solution)/shard_map/ppermute | solution.py:266
  181.3 20.5 %collective-permute-start.52 = (bf16[48,1920]{1,0:T(8,128)(2,1)}, bf16[48,1920]{1,0:T(8,128)(2,1)}, u32[]{:S(2)}, u32[]{:S(2)}) collective-permute-start(bf16[48,1920]{1,0:T(8,128)(2,1)} %get-tuple-element.235), channel_id=1, source_target_pairs={{0,8},{1,9},{2,10},{3,11},{4,12},{5,13},{6,14},{7,15},{8,0},{9,1},... | collective-permute-start | bytes 552968 | tf_op jit(solution)/shard_map/ppermute | solution.py:266
  181.4 23.5 %collective-permute-start.53 = (bf16[48,1920]{1,0:T(8,128)(2,1)}, bf16[48,1920]{1,0:T(8,128)(2,1)}, u32[]{:S(2)}, u32[]{:S(2)}) collective-permute-start(bf16[48,1920]{1,0:T(8,128)(2,1)} %get-tuple-element.236), channel_id=1, source_target_pairs={{0,16},{1,17},{2,18},{3,19},{4,20},{5,21},{6,22},{7,23},{8,24},{9,... | collective-permute-start | bytes 552968 | tf_op jit(solution)/shard_map/ppermute | solution.py:266
  184.3 20.6 %collective-permute-start.54 = (bf16[48,1920]{1,0:T(8,128)(2,1)}, bf16[48,1920]{1,0:T(8,128)(2,1)}, u32[]{:S(2)}, u32[]{:S(2)}) collective-permute-start(bf16[48,1920]{1,0:T(8,128)(2,1)} %get-tuple-element.237), channel_id=1, source_target_pairs={{0,24},{1,25},{2,26},{3,27},{4,28},{5,29},{6,30},{7,31},{8,16},{9,... | collective-permute-start | bytes 552968 | tf_op jit(solution)/shard_map/ppermute | solution.py:266
  198.8 12.4 %collective-permute-start.50 = (bf16[48,1280]{1,0:T(8,128)(2,1)S(1)}, bf16[48,1280]{1,0:T(8,128)(2,1)S(1)}, u32[]{:S(2)}, u32[]{:S(2)}) collective-permute-start(bf16[48,1280]{1,0:T(8,128)(2,1)S(1)} %get-tuple-element.232), channel_id=1, source_target_pairs={{0,16},{1,17},{2,18},{3,19},{4,20},{5,21},{6,22},{7,23},{8,24},{9,... | collective-permute-start | bytes 368648 | tf_op jit(solution)/shard_map/ppermute | solution.py:266
  (40 other events, 221.6 us)

commit v8 on v7

--- a/solution.py
+++ b/solution.py
@@ -1253,7 +1253,7 @@
     low[...] = (keep[4:].astype(F32) + raw[1].astype(F32)).astype(BF16)
     out.start()
     near.wait()
-    kept[...] = keep[:4].astype(F32) + raw[0].astype(F32)
+    kept[...] = (keep[:4].astype(F32) + raw[0].astype(F32)).astype(BF16)
     out.wait()
 
 
@@ -1262,7 +1262,7 @@
     vmem = pl.BlockSpec(memory_space=pltpu.VMEM)
     return chain.call(
         add_first_kernel,
-        out_shape=(shape((4, rows, cols), F32), shape((4, rows, cols), BF16)),
+        out_shape=(shape((4, rows, cols), BF16), shape((4, rows, cols), BF16)),
         in_specs=[vmem, ANY],
         out_specs=(vmem, ANY),
         scratch_shapes=[
@@ -1300,9 +1300,9 @@
 
 
 def add_second_kernel(keep, got, base, one, two, three):
-    base[...] = keep[0] + got[0].astype(F32)
+    base[...] = keep[0].astype(F32) + got[0].astype(F32)
     for s, out in ((1, one), (2, two), (3, three)):
-        out[...] = (keep[s] + got[s].astype(F32)).astype(BF16)
+        out[...] = (keep[s].astype(F32) + got[s].astype(F32)).astype(BF16)
 
 
 def shift_second(chain, keep, away):

time: 219 us -> 217 us (level)
  no operation moved by 1% of the time
where the time goes in v8:
time: 217 us; the launch traced here: 213 us
  Pallas kernels  112 us (52%)
  starting transfers between devices  52.2 us (24%)
  waiting for transfers between devices  38.2 us (18%)
  local copies, waits for them, and re-layouts  7.52 us (3%)
    pallas_call x36, Pallas kernels, with_token(): *outs, self.token = run(*args, *extra, *([self.token] if held else []))  112 us
    ppermute x57, starting transfers between devices, send(): return lax.ppermute(array, AXES, pairs(move))  52.2 us
    ppermute x57, waiting for transfers between devices, send(): return lax.ppermute(array, AXES, pairs(move))  38.2 us
    unnamed x30, local copies, waits for them, and re-layouts  7.28 us
  transfers between devices with their start and end apart: 57, of which 17 were waited for; matrix products, arithmetic and copies ran while one was open for 1% of the time, Pallas kernels for 51%

profile of v8, /device:TPU:0, one launch (start us, length us, event | category | flops | bytes accessed | tf_op | source)
XLA Modules:
  0.0 213.2 jit_solution(7101587649535982591)
XLA Ops:
  5.2 5.1 %collective-permute-start.1 = (bf16[1,48,1280]{2,1,0:T(8,128)(2,1)S(1)}, bf16[1,48,1280]{2,1,0:T(8,128)(2,1)S(1)}, u32[]{:S(2)}, u32[]{:S(2)}) collective-permute-start(bf16[1,48,1280]{2,1,0:T(8,128)(2,1)S(1)} %get-tuple-element.133.refs_0_), channel_id=1, source_target_pairs={{0,24},{1,25},{2,26},{3,27},{4,28},{5,29},{6,30},{7,31},{8,16},{9,... | collective-permute-start | bytes 368648 | tf_op jit(solution)/shard_map/ppermute | solution.py:266
  14.6 6.3 %collective-permute-done.2.refs_2_ = bf16[1,48,1280]{2,1,0:T(8,128)(2,1)S(1)} collective-permute-done((bf16[1,48,1280]{2,1,0:T(8,128)(2,1)S(1)}, bf16[1,48,1280]{2,1,0:T(8,128)(2,1)S(1)}, u32[]{:S(2)}, u32[]{:S(2)}) %collective-permute-start.2) | collective-permute-done | bytes 122912 | tf_op jit(solution)/shard_map/ppermute | solution.py:266
  23.2 3.0 %collective-permute-start.9 = (bf16[1,48,1920]{2,1,0:T(8,128)(2,1)S(1)}, bf16[1,48,1920]{2,1,0:T(8,128)(2,1)S(1)}, u32[]{:S(2)}, u32[]{:S(2)}) collective-permute-start(bf16[1,48,1920]{2,1,0:T(8,128)(2,1)S(1)} %get-tuple-element.140.refs_0_), channel_id=1, source_target_pairs={{0,16},{1,17},{2,18},{3,19},{4,20},{5,21},{6,22},{7,23},{8,24},{9,... | collective-permute-start | bytes 552968 | tf_op jit(solution)/shard_map/ppermute | solution.py:266
  29.1 3.9 %collective-permute-done.6.refs_0_ = bf16[4,48,1280]{2,1,0:T(8,128)(2,1)} collective-permute-done((bf16[4,48,1280]{2,1,0:T(8,128)(2,1)}, bf16[4,48,1280]{2,1,0:T(8,128)(2,1)}, u32[]{:S(2)}, u32[]{:S(2)}) %collective-permute-start.6) | collective-permute-done | bytes 491552 | tf_op jit(solution)/shard_map/ppermute | solution.py:266
  33.0 2.6 %collective-permute-start.11 = (bf16[4,48,1280]{2,1,0:T(8,128)(2,1)}, bf16[4,48,1280]{2,1,0:T(8,128)(2,1)}, u32[]{:S(2)}, u32[]{:S(2)}) collective-permute-start(bf16[4,48,1280]{2,1,0:T(8,128)(2,1)} %get-tuple-element.139.refs_5_), channel_id=1, source_target_pairs={{0,4},{1,3},{2,6},{3,1},{4,0},{5,7},{6,2},{7,5},{8,12},{9,11},{10,... | collective-permute-start | bytes 1474568 | tf_op jit(solution)/shard_map/ppermute | solution.py:266
  35.6 4.1 %collective-permute-done.9.refs_2_ = bf16[1,48,1920]{2,1,0:T(8,128)(2,1)S(1)} collective-permute-done((bf16[1,48,1920]{2,1,0:T(8,128)(2,1)S(1)}, bf16[1,48,1920]{2,1,0:T(8,128)(2,1)S(1)}, u32[]{:S(2)}, u32[]{:S(2)}) %collective-permute-start.9) | collective-permute-done | bytes 184352 | tf_op jit(solution)/shard_map/ppermute | solution.py:266
  46.3 6.7 %enter.1 = (bf16[2,16,48,1280]{3,2,1,0:T(8,128)(2,1)S(1)}, f32[8,768]{1,0:T(8,128)S(1)}, f32[1,3072]{1,0:T(1,128)S(1)}, bf16[16,48,512]{2,1,0:T(8,128)(2,1)}, bf...) custom-call(s32[66]{0:T(128)S(1)} %stack.239.refs_0_, ...), custom_call_target="tpu_custom_call", output_to_operand_aliasing={{7}: (12, {})} | custom-call | flops 240000008192 | bytes 1 | tf_op jit(solution)/shard_map/enter/pallas_call | solution.py:345
  53.6 2.5 %collective-permute-start.24 = (bf16[1,96,768]{2,1,0:T(8,128)(2,1)}, bf16[1,96,768]{2,1,0:T(8,128)(2,1)}, u32[]{:S(2)}, u32[]{:S(2)}) collective-permute-start(bf16[1,96,768]{2,1,0:T(8,128)(2,1)} %get-tuple-element.154.refs_0_), channel_id=1, source_target_pairs={{0,16},{1,17},{2,18},{3,19},{4,20},{5,21},{6,22},{7,23},{8,24},{9,... | collective-permute-start | bytes 442376 | tf_op jit(solution)/shard_map/ppermute | solution.py:266
  57.4 3.6 %collective-permute-done.16.refs_0_ = bf16[4,48,1920]{2,1,0:T(8,128)(2,1)} collective-permute-done((bf16[4,48,1920]{2,1,0:T(8,128)(2,1)}, bf16[4,48,1920]{2,1,0:T(8,128)(2,1)}, u32[]{:S(2)}, u32[]{:S(2)}) %collective-permute-start.16) | collective-permute-done | bytes 737312 | tf_op jit(solution)/shard_map/ppermute | solution.py:266
  61.1 2.9 %collective-permute-start.18 = (bf16[4,48,1920]{2,1,0:T(8,128)(2,1)}, bf16[4,48,1920]{2,1,0:T(8,128)(2,1)}, u32[]{:S(2)}, u32[]{:S(2)}) collective-permute-start(bf16[4,48,1920]{2,1,0:T(8,128)(2,1)} %get-tuple-element.153.refs_5_.refs_4_), channel_id=1, source_target_pairs={{0,4},{1,3},{2,6},{3,1},{4,0},{5,7},{6,2},{7,5},{8,12},{9,11},{10,... | collective-permute-start | bytes 2211848 | tf_op jit(solution)/shard_map/ppermute | solution.py:266
  64.0 7.0 %mix.1 = (bf16[512,768]{1,0:T(8,128)(2,1)S(1)}, bf16[768,512]{1,0:T(8,128)(2,1)}, f32[6,8,512]{2,1,0:T(8,128)S(1)}, f32[8,128]{1,0:T(8,128)S(1)}) custom-call(s32[66]{0:T(128)S(1)} %stack.239.refs_0_, bf16[2,512,1152]{2,1,0:T(8,128)(2,1)S(1)} %get-tuple-element.147.refs_1_.refs_2_.refs_3_, ...), custom_call_target="tpu_custom_call", output_to_operand_aliasing={{3}: (4, {})} | custom-call | flops 299999985664 | bytes 1 | tf_op jit(solution)/shard_map/mix/pallas_call | solution.py:345
  73.7 2.1 gather.6
  77.8 4.5 %rise.1 = (bf16[2,16,48,384]{3,2,1,0:T(8,128)(2,1)S(1)}, f32[512,768]{1,0:T(8,128)S(1)}, bf16[512,768]{1,0:T(8,128)(2,1)S(1)}, bf16[16,48,512]{2,1,0:T(8,128)(2,1)}, f32[8,128]{1,0:T(8,128)S(1)}) custom-call(s32[66]{0:T(128)S(1)} %stack.239.refs_0_, bf16[512,768]{1,0:T(8,128)(2,1)S(1)} %copy-done.5, ...), custom_call_target="tpu_custom_call", output_to_operand_aliasing={{4}: (12, {})} | custom-call | flops 149999992832 | bytes 1 | tf_op jit(solution)/shard_map/rise/pallas_call | solution.py:345
  82.3 7.5 %widen.2 = (bf16[16,48,1536]{2,1,0:T(8,128)(2,1)S(1)}, bf16[512,1536]{1,0:T(8,128)(2,1)S(1)}, bf16[512,1536]{1,0:T(8,128)(2,1)S(1)}, bf16[8,96,512]{2,1,0:T(8,12...) custom-call(s32[66]{0:T(128)S(1)} %stack.239.refs_0_, ...), custom_call_target="tpu_custom_call", output_to_operand_aliasing={{5}: (7, {})} | custom-call | flops 539999993856 | bytes 1 | tf_op jit(solution)/shard_map/widen/pallas_call | solution.py:345
  90.9 2.3 %gather.7 = (bf16[8,96,768]{2,1,0:T(8,128)(2,1)}, f32[8,128]{1,0:T(8,128)S(1)}) custom-call(bf16[4,96,768]{2,1,0:T(8,128)(2,1)} %get-tuple-element.162.refs_0_, bf16[4,96,768]{2,1,0:T(8,128)(2,1)} %collective-permute-done.26.refs_1_, f32[8,128]{1,0:T(8,128)S(1)} %get-tuple-element.163.refs_2_), custom_call_target="tpu_custom_call", output_to_operand_aliasing={{1}: (2, {})} | custom-call | bytes 1 | tf_op jit(solution)/shard_map/gather/pallas_call | solution.py:345
  94.8 7.0 %widen.3 = (bf16[16,48,1536]{2,1,0:T(8,128)(2,1)S(1)}, bf16[512,1536]{1,0:T(8,128)(2,1)S(1)}, bf16[512,1536]{1,0:T(8,128)(2,1)S(1)}, bf16[8,96,512]{2,1,0:T(8,12...) custom-call(s32[66]{0:T(128)S(1)} %stack.239.refs_0_, ...), custom_call_target="tpu_custom_call", output_to_operand_aliasing={{5}: (7, {})} | custom-call | flops 539999993856 | bytes 1 | tf_op jit(solution)/shard_map/widen/pallas_call | solution.py:345
  103.5 3.0 %collective-permute-done.29.refs_4_ = bf16[8,96,512]{2,1,0:T(8,128)(2,1)S(1)} collective-permute-done((bf16[8,96,512]{2,1,0:T(8,128)(2,1)S(1)}, bf16[8,96,512]{2,1,0:T(8,128)(2,1)S(1)}, u32[]{:S(2)}, u32[]{:S(2)}) %collective-permute-start.29) | collective-permute-done | bytes 786464 | tf_op jit(solution)/shard_map/ppermute | solution.py:266
  106.5 4.7 %outer_down.1 = (bf16[8,96,768]{2,1,0:T(8,128)(2,1)S(1)}, bf16[8,96,768]{2,1,0:T(8,128)(2,1)}, f32[8,128]{1,0:T(8,128)S(1)}) custom-call(s32[66]{0:T(128)S(1)} %stack.239.refs_0_, bf16[8,96,512]{2,1,0:T(8,128)(2,1)S(1)} %get-tuple-element.173.refs_1_, bf16[8,96,512]{2,1,0:T(8,128)(2,1)S(1)} %get-tuple-element.174.refs_2_, ...), custom_call_target="tpu_custom_call", output_to_operand_aliasing={{2}: (7, {})} | custom-call | bytes 1 | tf_op jit(solution)/shard_map/outer_down/pallas_call | solution.py:345
  114.6 14.1 %fall.1 = (bf16[16,2,96,768]{3,2,1,0:T(8,128)(2,1)}, bf16[512,1536]{1,0:T(8,128)(2,1)}, bf16[512,1536]{1,0:T(8,128)(2,1)S(1)}, f32[1,3072]{1,0:T(1,128)S(1)}, f3...) custom-call(s32[66]{0:T(128)S(1)} %stack.239.refs_0_, ...), custom_call_target="tpu_custom_call", output_to_operand_aliasing={{9}: (13, {})} | custom-call | flops 539999993856 | bytes 1 | tf_op jit(solution)/shard_map/fall/pallas_call | solution.py:345
  129.3 2.0 shift_first.2
  133.1 7.1 %outer_up.1 = (bf16[8,48,1920]{2,1,0:T(8,128)(2,1)S(1)}, bf16[8,48,1920]{2,1,0:T(8,128)(2,1)}, f32[8,128]{1,0:T(8,128)S(1)}) custom-call(s32[66]{0:T(128)S(1)} %stack.239.refs_0_, bf16[16,48,512]{2,1,0:T(8,128)(2,1)} %get-tuple-element.190.refs_1_, bf16[16,48,512]{2,1,0:T(8,128)(2,1)} %collective-permute-done.36.refs_2_, ...), custom_call_target="tpu_custom_call", output_to_operand_aliasing={{2}: (9, {})} | custom-call | flops 240000008192 | bytes 1 | tf_op jit(solution)/shard_map/outer_up/pallas_call | solution.py:345
  143.5 2.5 %collective-permute-start.42 = (bf16[96,768]{1,0:T(8,128)(2,1)}, bf16[96,768]{1,0:T(8,128)(2,1)}, u32[]{:S(2)}, u32[]{:S(2)}) collective-permute-start(bf16[96,768]{1,0:T(8,128)(2,1)} %get-tuple-element.203), channel_id=1, source_target_pairs={{0,24},{1,25},{2,26},{3,27},{4,28},{5,29},{6,30},{7,31},{8,16},{9,... | collective-permute-start | bytes 442376 | tf_op jit(solution)/shard_map/ppermute | solution.py:266
  147.9 12.5 %mix_back.1 = (bf16[3,512,384]{2,1,0:T(8,128)(2,1)}, bf16[3,512,384]{2,1,0:T(8,128)(2,1)S(1)}, f32[8,128]{1,0:T(8,128)S(1)}) custom-call(s32[66]{0:T(128)S(1)} %stack.239.refs_0_, bf16[2,512,1152]{2,1,0:T(8,128)(2,1)S(1)} %copy-done.10, bf16[2,512,1152]{2,1,0:T(8,128)(2,1)S(1)} %copy-done.10, ...), custom_call_target="tpu_custom_call", output_to_operand_aliasing={{2}: (6, {})} | custom-call | flops 480000016384 | bytes 1 | tf_op jit(solution)/shard_map/mix_back/pallas_call | solution.py:345
  160.5 2.2 %shift_first.3 = (bf16[4,48,1920]{2,1,0:T(8,128)(2,1)S(1)}, bf16[4,48,1920]{2,1,0:T(8,128)(2,1)}, f32[8,128]{1,0:T(8,128)S(1)}) custom-call(bf16[8,48,1920]{2,1,0:T(8,128)(2,1)S(1)} %get-tuple-element.201.refs_0_, bf16[8,48,1920]{2,1,0:T(8,128)(2,1)} %collective-permute-done.41.refs_1_, ...), custom_call_target="tpu_custom_call", output_to_operand_aliasing={{2}: (2, {})} | custom-call | flops 149999992832 | bytes 1 | tf_op jit(solution)/shard_map/shift_first/pallas_call | solution.py:345
  163.6 5.4 %outer_qkv.1 = (f32[8,48,1152]{2,1,0:T(8,128)S(1)}, bf16[8,48,1152]{2,1,0:T(8,128)(2,1)}, f32[8,128]{1,0:T(8,128)S(1)}) custom-call(s32[66]{0:T(128)S(1)} %stack.239.refs_0_, bf16[16,48,512]{2,1,0:T(8,128)(2,1)} %get-tuple-element.182.refs_1_, bf16[16,48,512]{2,1,0:T(8,128)(2,1)} %collective-permute-done.33.refs_2_, ...), custom_call_target="tpu_custom_call", output_to_operand_aliasing={{2}: (6, {})} | custom-call | flops 240000008192 | bytes 1 | tf_op jit(solution)/shard_map/outer_qkv/pallas_call | solution.py:345
  170.2 6.4 %exit_back.1 = (bf16[512,768]{1,0:T(8,128)(2,1)}, f32[8,48,128]{2,1,0:T(8,128)S(1)}, bf16[8,48,128]{2,1,0:T(8,128)(2,1)S(1)}, f32[8,128]{1,0:T(8,128)S(1)}) custom-call(s32[66]{0:T(128)S(1)} %stack.239.refs_0_, bf16[512,768]{1,0:T(8,128)(2,1)S(1)} %copy-done.6, ...), custom_call_target="tpu_custom_call", output_to_operand_aliasing={{3}: (9, {})} | custom-call | flops 240000008192 | bytes 1 | tf_op jit(solution)/shard_map/exit_back/pallas_call | solution.py:345
  179.6 2.9 %collective-permute-start.53 = (bf16[48,1920]{1,0:T(8,128)(2,1)}, bf16[48,1920]{1,0:T(8,128)(2,1)}, u32[]{:S(2)}, u32[]{:S(2)}) collective-permute-start(bf16[48,1920]{1,0:T(8,128)(2,1)} %get-tuple-element.236), channel_id=1, source_target_pairs={{0,16},{1,17},{2,18},{3,19},{4,20},{5,21},{6,22},{7,23},{8,24},{9,... | collective-permute-start | bytes 552968 | tf_op jit(solution)/shard_map/ppermute | solution.py:266
  184.5 2.2 %shift_both.1 = (f32[4,48,1280]{2,1,0:T(8,128)S(1)}, bf16[4,48,1280]{2,1,0:T(8,128)(2,1)}, f32[8,128]{1,0:T(8,128)S(1)}) custom-call(f32[8,48,1152]{2,1,0:T(8,128)S(1)} %get-tuple-element.212.refs_0_, bf16[8,48,1152]{2,1,0:T(8,128)(2,1)} %collective-permute-done.45.refs_1_, ...), custom_call_target="tpu_custom_call", output_to_operand_aliasing={{2}: (4, {})} | custom-call | bytes 1 | tf_op jit(solution)/shard_map/shift_both/pallas_call | solution.py:345
  187.3 2.3 %copy-done.8 = bf16[16,2,96,768]{3,2,1,0:T(8,128)(2,1)S(1)} copy-done((bf16[16,2,96,768]{3,2,1,0:T(8,128)(2,1)S(1)}, bf16[16,2,96,768]{3,2,1,0:T(8,128)(2,1)}, u32[]{:S(2)}) %copy-start.8) | copy-done | bytes 4718616
  189.6 5.2 %leave.1 = (bf16[512,768]{1,0:T(8,128)(2,1)}, f32[8,128]{1,0:T(8,128)S(1)}) custom-call(s32[66]{0:T(128)S(1)} %stack.239.refs_0_, f32[512,768]{1,0:T(8,128)S(1)} %get-tuple-element.157.refs_6_.refs_1_, bf16[512,1536]{1,0:T(8,128)(2,1)S(1)} %get-tuple-element.161.refs_2_, bf16[512,1536]{1,0:T(8,128)(2,1)S(1)} %copy-done.12, ...), custom_call_target="tpu_custom_call", output_to_operand_aliasing={{1}: (6, {})} | custom-call | flops 210000003072 | bytes 1 | tf_op jit(solution)/shard_map/leave/pallas_call | solution.py:345
  197.1 2.9 %collective-permute-start.50 = (bf16[48,1280]{1,0:T(8,128)(2,1)S(1)}, bf16[48,1280]{1,0:T(8,128)(2,1)S(1)}, u32[]{:S(2)}, u32[]{:S(2)}) collective-permute-start(bf16[48,1280]{1,0:T(8,128)(2,1)S(1)} %get-tuple-element.232), channel_id=1, source_target_pairs={{0,16},{1,17},{2,18},{3,19},{4,20},{5,21},{6,22},{7,23},{8,24},{9,... | collective-permute-start | bytes 368648 | tf_op jit(solution)/shard_map/ppermute | solution.py:266
  204.5 4.9 %collective-permute-done.50.refs_3_ = bf16[48,1280]{1,0:T(8,128)(2,1)S(1)} collective-permute-done((bf16[48,1280]{1,0:T(8,128)(2,1)S(1)}, bf16[48,1280]{1,0:T(8,128)(2,1)S(1)}, u32[]{:S(2)}, u32[]{:S(2)}) %collective-permute-start.50) | collective-permute-done | bytes 122912 | tf_op jit(solution)/shard_map/ppermute | solution.py:266
  (152 shorter events, 59.7 us)
Async XLA Ops:
  1.2 11.2 %collective-permute-start.4 = (bf16[24,3072]{1,0:T(8,128)(2,1)}, bf16[24,3072]{1,0:T(8,128)(2,1)S(1)}, u32[]{:S(2)}, u32[]{:S(2)}) collective-permute-start(bf16[24,3072]{1,0:T(8,128)(2,1)} %refs_1_.6), channel_id=1, source_target_pairs={{0,1},{1,0},{2,3},{3,2},{4,5},{5,4},{6,7},{7,6},{8,9},{9,8},{10,11... | collective-permute-start | bytes 442376 | tf_op jit(solution)/shard_map/ppermute | solution.py:266
  10.3 10.6 %collective-permute-start.2 = (bf16[1,48,1280]{2,1,0:T(8,128)(2,1)S(1)}, bf16[1,48,1280]{2,1,0:T(8,128)(2,1)S(1)}, u32[]{:S(2)}, u32[]{:S(2)}) collective-permute-start(bf16[1,48,1280]{2,1,0:T(8,128)(2,1)S(1)} %get-tuple-element.133.refs_0_), channel_id=1, source_target_pairs={{0,16},{1,17},{2,18},{3,19},{4,20},{5,21},{6,22},{7,23},{8,24},{9,... | collective-permute-start | bytes 368648 | tf_op jit(solution)/shard_map/ppermute | solution.py:266
  10.3 10.6 %collective-permute-start.3 = (bf16[1,48,1280]{2,1,0:T(8,128)(2,1)S(1)}, bf16[1,48,1280]{2,1,0:T(8,128)(2,1)S(1)}, u32[]{:S(2)}, u32[]{:S(2)}) collective-permute-start(bf16[1,48,1280]{2,1,0:T(8,128)(2,1)S(1)} %get-tuple-element.133.refs_0_), channel_id=1, source_target_pairs={{0,8},{1,9},{2,10},{3,11},{4,12},{5,13},{6,14},{7,15},{8,0},{9,1},... | collective-permute-start | bytes 368648 | tf_op jit(solution)/shard_map/ppermute | solution.py:266
  21.7 11.3 %collective-permute-start.6 = (bf16[4,48,1280]{2,1,0:T(8,128)(2,1)}, bf16[4,48,1280]{2,1,0:T(8,128)(2,1)}, u32[]{:S(2)}, u32[]{:S(2)}) collective-permute-start(bf16[4,48,1280]{2,1,0:T(8,128)(2,1)} %get-tuple-element.137.refs_4_), channel_id=1, source_target_pairs={{0,2},{1,5},{2,0},{3,7},{4,6},{5,1},{6,4},{7,3},{8,10},{9,13},{10,... | collective-permute-start | bytes 1474568 | tf_op jit(solution)/shard_map/ppermute | solution.py:266
  23.2 16.4 %collective-permute-start.9 = (bf16[1,48,1920]{2,1,0:T(8,128)(2,1)S(1)}, bf16[1,48,1920]{2,1,0:T(8,128)(2,1)S(1)}, u32[]{:S(2)}, u32[]{:S(2)}) collective-permute-start(bf16[1,48,1920]{2,1,0:T(8,128)(2,1)S(1)} %get-tuple-element.140.refs_0_), channel_id=1, source_target_pairs={{0,16},{1,17},{2,18},{3,19},{4,20},{5,21},{6,22},{7,23},{8,24},{9,... | collective-permute-start | bytes 552968 | tf_op jit(solution)/shard_map/ppermute | solution.py:266
  26.3 13.4 %collective-permute-start.10 = (bf16[1,48,1920]{2,1,0:T(8,128)(2,1)S(1)}, bf16[1,48,1920]{2,1,0:T(8,128)(2,1)S(1)}, u32[]{:S(2)}, u32[]{:S(2)}) collective-permute-start(bf16[1,48,1920]{2,1,0:T(8,128)(2,1)S(1)} %get-tuple-element.140.refs_0_), channel_id=1, source_target_pairs={{0,24},{1,25},{2,26},{3,27},{4,28},{5,29},{6,30},{7,31},{8,16},{9,... | collective-permute-start | bytes 552968 | tf_op jit(solution)/shard_map/ppermute | solution.py:266
  27.6 13.0 %collective-permute-start.7 = (bf16[4,48,1280]{2,1,0:T(8,128)(2,1)}, bf16[4,48,1280]{2,1,0:T(8,128)(2,1)}, u32[]{:S(2)}, u32[]{:S(2)}) collective-permute-start(bf16[4,48,1280]{2,1,0:T(8,128)(2,1)} %get-tuple-element.137.refs_4_), channel_id=1, source_target_pairs={{0,4},{1,3},{2,6},{3,1},{4,0},{5,7},{6,2},{7,5},{8,12},{9,11},{10,... | collective-permute-start | bytes 1474568 | tf_op jit(solution)/shard_map/ppermute | solution.py:266
  33.0 11.2 %collective-permute-start.12 = (bf16[4,48,1280]{2,1,0:T(8,128)(2,1)}, bf16[4,48,1280]{2,1,0:T(8,128)(2,1)}, u32[]{:S(2)}, u32[]{:S(2)}) collective-permute-start(bf16[4,48,1280]{2,1,0:T(8,128)(2,1)} %get-tuple-element.137.refs_4_), channel_id=1, source_target_pairs={{0,1},{1,0},{2,3},{3,2},{4,5},{5,4},{6,7},{7,6},{8,9},{9,8},{10,11... | collective-permute-start | bytes 1474568 | tf_op jit(solution)/shard_map/ppermute | solution.py:266
  42.7 18.4 %collective-permute-start.16 = (bf16[4,48,1920]{2,1,0:T(8,128)(2,1)}, bf16[4,48,1920]{2,1,0:T(8,128)(2,1)}, u32[]{:S(2)}, u32[]{:S(2)}) collective-permute-start(bf16[4,48,1920]{2,1,0:T(8,128)(2,1)} %get-tuple-element.148.refs_4_.refs_3_), channel_id=1, source_target_pairs={{0,2},{1,5},{2,0},{3,7},{4,6},{5,1},{6,4},{7,3},{8,10},{9,13},{10,... | collective-permute-start | bytes 2211848 | tf_op jit(solution)/shard_map/ppermute | solution.py:266
  44.2 26.7 %collective-permute-start.17 = (bf16[4,48,1920]{2,1,0:T(8,128)(2,1)}, bf16[4,48,1920]{2,1,0:T(8,128)(2,1)}, u32[]{:S(2)}, u32[]{:S(2)}) collective-permute-start(bf16[4,48,1920]{2,1,0:T(8,128)(2,1)} %get-tuple-element.148.refs_4_.refs_3_), channel_id=1, source_target_pairs={{0,4},{1,3},{2,6},{3,1},{4,0},{5,7},{6,2},{7,5},{8,12},{9,11},{10,... | collective-permute-start | bytes 2211848 | tf_op jit(solution)/shard_map/ppermute | solution.py:266
  53.0 18.0 %collective-permute-start.23 = (bf16[1,96,768]{2,1,0:T(8,128)(2,1)}, bf16[1,96,768]{2,1,0:T(8,128)(2,1)}, u32[]{:S(2)}, u32[]{:S(2)}) collective-permute-start(bf16[1,96,768]{2,1,0:T(8,128)(2,1)} %get-tuple-element.154.refs_0_), channel_id=1, source_target_pairs={{0,8},{1,9},{2,10},{3,11},{4,12},{5,13},{6,14},{7,15},{8,0},{9,1},... | collective-permute-start | bytes 442376 | tf_op jit(solution)/shard_map/ppermute | solution.py:266
  53.6 17.9 %collective-permute-start.24 = (bf16[1,96,768]{2,1,0:T(8,128)(2,1)}, bf16[1,96,768]{2,1,0:T(8,128)(2,1)}, u32[]{:S(2)}, u32[]{:S(2)}) collective-permute-start(bf16[1,96,768]{2,1,0:T(8,128)(2,1)} %get-tuple-element.154.refs_0_), channel_id=1, source_target_pairs={{0,16},{1,17},{2,18},{3,19},{4,20},{5,21},{6,22},{7,23},{8,24},{9,... | collective-permute-start | bytes 442376 | tf_op jit(solution)/shard_map/ppermute | solution.py:266
  56.1 15.4 %collective-permute-start.25 = (bf16[1,96,768]{2,1,0:T(8,128)(2,1)}, bf16[1,96,768]{2,1,0:T(8,128)(2,1)}, u32[]{:S(2)}, u32[]{:S(2)}) collective-permute-start(bf16[1,96,768]{2,1,0:T(8,128)(2,1)} %get-tuple-element.154.refs_0_), channel_id=1, source_target_pairs={{0,24},{1,25},{2,26},{3,27},{4,28},{5,29},{6,30},{7,31},{8,16},{9,... | collective-permute-start | bytes 442376 | tf_op jit(solution)/shard_map/ppermute | solution.py:266
  61.1 12.6 %collective-permute-start.18 = (bf16[4,48,1920]{2,1,0:T(8,128)(2,1)}, bf16[4,48,1920]{2,1,0:T(8,128)(2,1)}, u32[]{:S(2)}, u32[]{:S(2)}) collective-permute-start(bf16[4,48,1920]{2,1,0:T(8,128)(2,1)} %get-tuple-element.153.refs_5_.refs_4_), channel_id=1, source_target_pairs={{0,4},{1,3},{2,6},{3,1},{4,0},{5,7},{6,2},{7,5},{8,12},{9,11},{10,... | collective-permute-start | bytes 2211848 | tf_op jit(solution)/shard_map/ppermute | solution.py:266
  71.6 32.0 %collective-permute-start.30 = (bf16[512,768]{1,0:T(8,128)(2,1)}, bf16[512,768]{1,0:T(8,128)(2,1)}, u32[]{:S(2)}, u32[]{:S(2)}) collective-permute-start(bf16[512,768]{1,0:T(8,128)(2,1)} %get-tuple-element.166.refs_5_.refs_1_), channel_id=1, source_target_pairs={{0,1},{1,0},{2,3},{3,2},{4,5},{5,4},{6,7},{7,6},{8,9},{9,8},{10,11... | collective-permute-start | bytes 2359304 | tf_op jit(solution)/shard_map/ppermute | solution.py:266
  75.8 15.2 %collective-permute-start.26 = (bf16[4,96,768]{2,1,0:T(8,128)(2,1)}, bf16[4,96,768]{2,1,0:T(8,128)(2,1)}, u32[]{:S(2)}, u32[]{:S(2)}) collective-permute-start(bf16[4,96,768]{2,1,0:T(8,128)(2,1)} %get-tuple-element.162.refs_0_), channel_id=1, source_target_pairs={{0,2},{1,5},{2,0},{3,7},{4,6},{5,1},{6,4},{7,3},{8,10},{9,13},{10,... | collective-permute-start | bytes 1769480 | tf_op jit(solution)/shard_map/ppermute | solution.py:266
  93.3 18.0 %collective-permute-start.27 = (bf16[8,96,768]{2,1,0:T(8,128)(2,1)}, bf16[8,96,768]{2,1,0:T(8,128)(2,1)}, u32[]{:S(2)}, u32[]{:S(2)}) collective-permute-start(bf16[8,96,768]{2,1,0:T(8,128)(2,1)} %get-tuple-element.172.refs_9_), channel_id=1, source_target_pairs={{0,4},{1,3},{2,6},{3,1},{4,0},{5,7},{6,2},{7,5},{8,12},{9,11},{10,... | collective-permute-start | bytes 3538952 | tf_op jit(solution)/shard_map/ppermute | solution.py:266
  111.6 51.8 %collective-permute-start.33 = (bf16[16,48,512]{2,1,0:T(8,128)(2,1)}, bf16[16,48,512]{2,1,0:T(8,128)(2,1)}, u32[]{:S(2)}, u32[]{:S(2)}) collective-permute-start(bf16[16,48,512]{2,1,0:T(8,128)(2,1)} %get-tuple-element.182.refs_1_), channel_id=1, source_target_pairs={{0,1},{1,0},{2,3},{3,2},{4,5},{5,4},{6,7},{7,6},{8,9},{9,8},{10,11... | collective-permute-start | bytes 2359304 | tf_op jit(solution)/shard_map/ppermute | solution.py:266
  111.8 19.6 %collective-permute-start.38 = (bf16[16,48,512]{2,1,0:T(8,128)(2,1)}, bf16[16,48,512]{2,1,0:T(8,128)(2,1)}, u32[]{:S(2)}, u32[]{:S(2)}) collective-permute-start(bf16[16,48,512]{2,1,0:T(8,128)(2,1)} %bitcast.62.refs_5_), channel_id=1, source_target_pairs={{0,1},{1,0},{2,3},{3,2},{4,5},{5,4},{6,7},{7,6},{8,9},{9,8},{10,11... | collective-permute-start | bytes 2359304 | tf_op jit(solution)/shard_map/ppermute | solution.py:266
  112.1 19.9 %collective-permute-start.36 = (bf16[16,48,512]{2,1,0:T(8,128)(2,1)}, bf16[16,48,512]{2,1,0:T(8,128)(2,1)}, u32[]{:S(2)}, u32[]{:S(2)}) collective-permute-start(bf16[16,48,512]{2,1,0:T(8,128)(2,1)} %get-tuple-element.190.refs_1_), channel_id=1, source_target_pairs={{0,1},{1,0},{2,3},{3,2},{4,5},{5,4},{6,7},{7,6},{8,9},{9,8},{10,11... | collective-permute-start | bytes 2359304 | tf_op jit(solution)/shard_map/ppermute | solution.py:266
  112.3 16.9 %collective-permute-start.34 = (bf16[8,96,768]{2,1,0:T(8,128)(2,1)}, bf16[8,96,768]{2,1,0:T(8,128)(2,1)}, u32[]{:S(2)}, u32[]{:S(2)}) collective-permute-start(bf16[8,96,768]{2,1,0:T(8,128)(2,1)} %get-tuple-element.186), channel_id=1, source_target_pairs={{0,4},{1,3},{2,6},{3,1},{4,0},{5,7},{6,2},{7,5},{8,12},{9,11},{10,... | collective-permute-start | bytes 3538952 | tf_op jit(solution)/shard_map/ppermute | solution.py:266
  131.4 10.3 %collective-permute-start.35 = (bf16[4,96,768]{2,1,0:T(8,128)(2,1)}, bf16[4,96,768]{2,1,0:T(8,128)(2,1)}, u32[]{:S(2)}, u32[]{:S(2)}) collective-permute-start(bf16[4,96,768]{2,1,0:T(8,128)(2,1)} %get-tuple-element.189), channel_id=1, source_target_pairs={{0,2},{1,5},{2,0},{3,7},{4,6},{5,1},{6,4},{7,3},{8,10},{9,13},{10,... | collective-permute-start | bytes 1769480 | tf_op jit(solution)/shard_map/ppermute | solution.py:266
  140.3 20.2 %collective-permute-start.41 = (bf16[8,48,1920]{2,1,0:T(8,128)(2,1)}, bf16[8,48,1920]{2,1,0:T(8,128)(2,1)}, u32[]{:S(2)}, u32[]{:S(2)}) collective-permute-start(bf16[8,48,1920]{2,1,0:T(8,128)(2,1)} %get-tuple-element.202), channel_id=1, source_target_pairs={{0,4},{1,3},{2,6},{3,1},{4,0},{5,7},{6,2},{7,5},{8,12},{9,11},{10,... | collective-permute-start | bytes 4423688 | tf_op jit(solution)/shard_map/ppermute | solution.py:266
  143.5 16.9 %collective-permute-start.42 = (bf16[96,768]{1,0:T(8,128)(2,1)}, bf16[96,768]{1,0:T(8,128)(2,1)}, u32[]{:S(2)}, u32[]{:S(2)}) collective-permute-start(bf16[96,768]{1,0:T(8,128)(2,1)} %get-tuple-element.203), channel_id=1, source_target_pairs={{0,24},{1,25},{2,26},{3,27},{4,28},{5,29},{6,30},{7,31},{8,16},{9,... | collective-permute-start | bytes 442376 | tf_op jit(solution)/shard_map/ppermute | solution.py:266
  146.0 14.4 %collective-permute-start.43 = (bf16[96,768]{1,0:T(8,128)(2,1)}, bf16[96,768]{1,0:T(8,128)(2,1)}, u32[]{:S(2)}, u32[]{:S(2)}) collective-permute-start(bf16[96,768]{1,0:T(8,128)(2,1)} %get-tuple-element.204), channel_id=1, source_target_pairs={{0,16},{1,17},{2,18},{3,19},{4,20},{5,21},{6,22},{7,23},{8,24},{9,... | collective-permute-start | bytes 442376 | tf_op jit(solution)/shard_map/ppermute | solution.py:266
  146.0 14.4 %collective-permute-start.44 = (bf16[96,768]{1,0:T(8,128)(2,1)}, bf16[96,768]{1,0:T(8,128)(2,1)}, u32[]{:S(2)}, u32[]{:S(2)}) collective-permute-start(bf16[96,768]{1,0:T(8,128)(2,1)} %get-tuple-element.205), channel_id=1, source_target_pairs={{0,8},{1,9},{2,10},{3,11},{4,12},{5,13},{6,14},{7,15},{8,0},{9,1},... | collective-permute-start | bytes 442376 | tf_op jit(solution)/shard_map/ppermute | solution.py:266
  162.7 14.8 %collective-permute-start.47 = (bf16[4,48,1920]{2,1,0:T(8,128)(2,1)}, bf16[4,48,1920]{2,1,0:T(8,128)(2,1)}, u32[]{:S(2)}, u32[]{:S(2)}) collective-permute-start(bf16[4,48,1920]{2,1,0:T(8,128)(2,1)} %get-tuple-element.210.refs_5_), channel_id=1, source_target_pairs={{0,2},{1,5},{2,0},{3,7},{4,6},{5,1},{6,4},{7,3},{8,10},{9,13},{10,... | collective-permute-start | bytes 2211848 | tf_op jit(solution)/shard_map/ppermute | solution.py:266
  169.0 15.4 %collective-permute-start.45 = (bf16[8,48,1152]{2,1,0:T(8,128)(2,1)}, bf16[8,48,1152]{2,1,0:T(8,128)(2,1)}, u32[]{:S(2)}, u32[]{:S(2)}) collective-permute-start(bf16[8,48,1152]{2,1,0:T(8,128)(2,1)} %get-tuple-element.213), channel_id=1, source_target_pairs={{0,4},{1,3},{2,6},{3,1},{4,0},{5,7},{6,2},{7,5},{8,12},{9,11},{10,... | collective-permute-start | bytes 2654216 | tf_op jit(solution)/shard_map/ppermute | solution.py:266
  179.4 20.6 %collective-permute-start.52 = (bf16[48,1920]{1,0:T(8,128)(2,1)}, bf16[48,1920]{1,0:T(8,128)(2,1)}, u32[]{:S(2)}, u32[]{:S(2)}) collective-permute-start(bf16[48,1920]{1,0:T(8,128)(2,1)} %get-tuple-element.235), channel_id=1, source_target_pairs={{0,8},{1,9},{2,10},{3,11},{4,12},{5,13},{6,14},{7,15},{8,0},{9,1},... | collective-permute-start | bytes 552968 | tf_op jit(solution)/shard_map/ppermute | solution.py:266
  179.6 23.6 %collective-permute-start.53 = (bf16[48,1920]{1,0:T(8,128)(2,1)}, bf16[48,1920]{1,0:T(8,128)(2,1)}, u32[]{:S(2)}, u32[]{:S(2)}) collective-permute-start(bf16[48,1920]{1,0:T(8,128)(2,1)} %get-tuple-element.236), channel_id=1, source_target_pairs={{0,16},{1,17},{2,18},{3,19},{4,20},{5,21},{6,22},{7,23},{8,24},{9,... | collective-permute-start | bytes 552968 | tf_op jit(solution)/shard_map/ppermute | solution.py:266
  182.5 20.7 %collective-permute-start.54 = (bf16[48,1920]{1,0:T(8,128)(2,1)}, bf16[48,1920]{1,0:T(8,128)(2,1)}, u32[]{:S(2)}, u32[]{:S(2)}) collective-permute-start(bf16[48,1920]{1,0:T(8,128)(2,1)} %get-tuple-element.237), channel_id=1, source_target_pairs={{0,24},{1,25},{2,26},{3,27},{4,28},{5,29},{6,30},{7,31},{8,16},{9,... | collective-permute-start | bytes 552968 | tf_op jit(solution)/shard_map/ppermute | solution.py:266
  197.1 12.4 %collective-permute-start.50 = (bf16[48,1280]{1,0:T(8,128)(2,1)S(1)}, bf16[48,1280]{1,0:T(8,128)(2,1)S(1)}, u32[]{:S(2)}, u32[]{:S(2)}) collective-permute-start(bf16[48,1280]{1,0:T(8,128)(2,1)S(1)} %get-tuple-element.232), channel_id=1, source_target_pairs={{0,16},{1,17},{2,18},{3,19},{4,20},{5,21},{6,22},{7,23},{8,24},{9,... | collective-permute-start | bytes 368648 | tf_op jit(solution)/shard_map/ppermute | solution.py:266
  (40 other events, 233.7 us)
